TPU v7x, 128 devices: a whole 4x4x4 slice. The times are simulated.
128 devices in a mesh: gx: 16 (over y_hi, z, core), gy: 8 (over y_lo, x).
Axes of the slice: x: 4, y: 4 (y_hi: 2, y_lo: 2; y = y_hi * 2 + y_lo), z: 4, core: 2. Of those that a mesh axis runs over, the one named last changes fastest.
Arguments:
- grad_pressure: float32 [128, 256, 1024], P('gx', 'gy'), may hold values from -6 to 6
- beta: float32 [3, 128, 256, 1024], P(None, 'gx', 'gy'), may hold values from 0.25 to 4
- tile_rows: int32 [32768], P(('gx', 'gy')), may hold values from 0 to 2047
- tile_owner: int32 [32768, 1], P(('gx', 'gy')), may hold values from 0 to 127; in each aligned block of 256 rows (0 to 255, 256 to 511, ...) at most 8 rows name the same one
- tile_slot: int32 [32768], P(('gx', 'gy')), may hold values from 0 to 255
- face_mask: int32 [32768, 128], P(('gx', 'gy')), may hold values 0 or 1
- heights: float32 [3, 32768, 128], P(None, ('gx', 'gy')), may hold values from -6 to 6
Outputs:
- grad_rhs: float32 [128, 256, 1024], P('gx', 'gy')
- grad_heights: float32 [3, 32768, 128], P(None, ('gx', 'gy'))
Inputs may be any that keep to these rules, and one draw needn't show every extreme that they name: `tile_rows`: each entry indexes a row of 128 cells inside its own device's block. `tile_owner`: among the 256 tiles of one device no owner is named more than 8 times.
All inputs are finite; a program needn't handle non-finite values. No bound on the sum of `face_mask` on one device may be relied on, other than what follows from the above.
Results may differ from a plain program's by a relative error of at most 0.000025.
Values sent between devices are 32-bit elements; how exact they have to be, the bound alone decides.
No kernel may reach another device: no remote copies, remote signals or barrier semaphores. Data moves between devices by JAX's collectives and lax.ppermute only.
A program may use at most 192 MiB of HBM per device.

v0:
```python
import math

import jax
import jax.numpy as jnp
from jax import lax
from jax.sharding import PartitionSpec as P

ITERS = 3
STEPS = 4
CAP = 8


LOW_BOUND = 0.1
HIGH_BOUND = 1.9


def from_behind(array, axis, by):
    size = lax.axis_size(axis)
    pairs = [(i, i + by) for i in range(size) if 0 <= i + by < size]
    return lax.ppermute(array, axis, pairs)


def with_halo(array, sides, width):
    edges = {}
    for axis, dim in sides:
        size, length = (lax.axis_size(axis), array.shape[dim])
        up = [(i, (i + 1) % size) for i in range(size - 1)]
        last = lax.slice_in_dim(array, length - width, length, axis=dim)
        initial = lax.slice_in_dim(array, 0, width, axis=dim)
        edges[dim] = (
            lax.ppermute(last, axis, up),
            lax.ppermute(initial, axis, [(b, a) for a, b in up]),
        )
    done = []
    for _, dim in sides:
        low, high = edges[dim]
        around = [(width, width) if d in done else (0, 0) for d in range(array.ndim)]
        array = jnp.concatenate([jnp.pad(low, around), array, jnp.pad(high, around)], axis=dim)
        done.append(dim)
    return array


def sent_together(arrays, axis, split_dim, concat_dim, along):
    columns = [a.reshape(*a.shape[:along], -1) for a in arrays]
    both = jnp.concatenate(columns, axis=along)
    result, at, outs = (
        lax.all_to_all(both, axis, split_axis=split_dim, concat_axis=concat_dim, tiled=True),
        0,
        [],
    )
    for a, column in zip(arrays, columns):
        section = result[..., at : at + column.shape[along]]
        outs.append(section.reshape(*section.shape[:along], *a.shape[along:]))
        at += column.shape[along]
    return tuple(outs)


def omega_of(step_index):
    theta = 0.5 * (HIGH_BOUND + LOW_BOUND) + 0.5 * (HIGH_BOUND - LOW_BOUND) * math.cos(
        math.pi * (2 * step_index + 1) / (2 * STEPS)
    )
    return 1.0 / theta


def z_low(field):
    return jnp.concatenate([jnp.zeros_like(field[:, :, :1]), field[:, :, :-1]], axis=2)


def stencil(scaled, padded, coeffs):
    beta_x, low_x, beta_y, low_y, beta_z, low_z, diagonal = coeffs
    up_z = jnp.concatenate([scaled[:, :, 1:], jnp.zeros_like(scaled[:, :, :1])], axis=2)
    beside = beta_x * padded[2:, 1:-1] + low_x * padded[:-2, 1:-1]
    beside = beside + beta_y * padded[1:-1, 2:] + low_y * padded[1:-1, :-2]
    beside = beside + beta_z * up_z + low_z * z_low(scaled)
    return diagonal * scaled - beside


def near_coeffs(beta):
    beta_x, beta_y, beta_z = (beta[0], beta[1], beta[2])
    rim_x = from_behind(beta_x[-1:], "gx", 1)
    low_x = jnp.concatenate([rim_x, beta_x[:-1]], axis=0)
    rim_y = from_behind(beta_y[:, -1:], "gy", 1)
    low_y = jnp.concatenate([rim_y, beta_y[:, :-1]], axis=1)
    low_z = z_low(beta_z)
    diagonal = beta_x + low_x + beta_y + low_y + beta_z + low_z
    return ((beta_x, low_x, beta_y, low_y, beta_z, low_z, diagonal), 1.0 / diagonal)


def cycle_near(adjoint, coeffs, inv_diag):
    increment = jnp.zeros_like(adjoint)
    for step_index in reversed(range(STEPS)):
        scaled = omega_of(step_index) * inv_diag * adjoint
        increment = increment + scaled
        padded = with_halo(scaled, (("gx", 0), ("gy", 1)), 1)
        adjoint = adjoint - stencil(scaled, padded, coeffs)
    return (adjoint, increment)


def pack_jumps(gradient, tile_rows, owner_ids, tile_slot, face_mask, peers):
    flat_rows = gradient.reshape(-1, 128)
    picked = flat_rows[tile_rows] * face_mask.astype(jnp.float32)
    onehot = (owner_ids[:, None] == jnp.arange(peers, dtype=jnp.int32)[None, :]).astype(jnp.int32)
    position = jnp.sum(jnp.cumsum(onehot, axis=0) * onehot, axis=1) - 1
    target = owner_ids * CAP + position
    send_rows = (
        jnp.zeros((peers * CAP, 128), jnp.float32).at[target].set(picked).reshape(peers, CAP, 128)
    )
    send_slots = (
        jnp.zeros((peers * CAP,), jnp.float32)
        .at[target]
        .set(tile_slot.astype(jnp.float32))
        .reshape(peers, CAP)
    )
    return (send_rows, send_slots)


def add_jumps(slot_table, recv_rows, recv_slots):
    slot_ids = recv_slots.reshape(-1).astype(jnp.int32)
    return slot_table.at[slot_ids].add(recv_rows.reshape(-1, 128))


def curvature_back(slot_table, heights):
    slope = 0.5 * (heights[2] - heights[0])
    bend = heights[2] - 2.0 * heights[1] + heights[0]
    denom = 1.0 + slope * slope
    factor = denom ** (-1.5)
    skew_term = -3.0 * slope * bend * denom ** (-2.5)
    return jnp.stack(
        [
            slot_table * (factor - 0.5 * skew_term),
            -2.0 * slot_table * factor,
            slot_table * (factor + 0.5 * skew_term),
        ]
    )


def shards(grad_pressure, beta, tile_rows, tile_owner, tile_slot, face_mask, heights):
    peers = lax.axis_size("gx") * lax.axis_size("gy")
    owner_ids = tile_owner[:, 0]
    coeffs, inv_diag = near_coeffs(beta)
    adjoint = grad_pressure
    grad_rhs = jnp.zeros_like(grad_pressure)
    slot_table = jnp.zeros((heights.shape[1], 128), jnp.float32)
    for cycle_index in range(ITERS):
        adjoint, increment = cycle_near(adjoint, coeffs, inv_diag)
        grad_rhs = grad_rhs + increment
    send_rows, send_slots = pack_jumps(grad_rhs, tile_rows, owner_ids, tile_slot, face_mask, peers)
    recv_rows, recv_slots = sent_together((send_rows, send_slots), ("gx", "gy"), 0, 0, 2)
    slot_table = add_jumps(slot_table, recv_rows, recv_slots)
    grad_heights = curvature_back(slot_table, heights)
    return (grad_rhs, grad_heights)


def solution(mesh):
    in_specs = (
        P("gx", "gy", None),
        P(None, "gx", "gy", None),
        P(("gx", "gy")),
        P(("gx", "gy"), None),
        P(("gx", "gy")),
        P(("gx", "gy"), None),
        P(None, ("gx", "gy"), None),
    )
    out_specs = (P("gx", "gy", None), P(None, ("gx", "gy"), None))
    return jax.shard_map(shards, mesh=mesh, in_specs=in_specs, out_specs=out_specs, check_vma=False)
```

profile of v0, /device:TPU:1, one launch (start us, length us, event | category | flops | bytes accessed | tf_op | source)
XLA Modules:
  0.0 308.2 jit_solution(3027342508971789906)
XLA Ops:
  0.7 2.9 slice_bitcast_fusion.1
  4.5 3.9 %collective-permute-start.1 = (f32[8,1,1024]{2,1,0:T(1,128)S(1)}, f32[8,1,1024]{2,1,0:T(1,128)S(1)}, u32[]{:S(2)}, u32[]{:S(2)}) collective-permute-start(f32[8,1,1024]{2,1,0:T(1,128)S(1)} %slice.558), channel_id=1, source_target_pairs={{0,1},{1,2},{2,3},{3,4},{4,5},{5,6},{6,7},{8,9},{9,10},{10,11},{11... | collective-permute-start | bytes 98312 | tf_op jit(solution)/shard_map/ppermute | solution.py:20
  9.2 4.4 %collective-permute-start = (f32[1,32,1024]{2,1,0:T(8,128)}, f32[1,32,1024]{2,1,0:T(8,128)S(1)}, u32[]{:S(2)}, u32[]{:S(2)}) collective-permute-start(f32[1,32,1024]{2,1,0:T(8,128)} %slice_bitcast_fusion.5), channel_id=1, source_target_pairs={{0,8},{8,16},{16,24},{24,32},{32,40},{40,48},{48,56},{56,64},{64,7... | collective-permute-start | bytes 393224 | tf_op jit(solution)/shard_map/ppermute | solution.py:20
  15.3 1.4 scatter_custom_fusion.1
  17.8 2.9 fusion.179
  20.9 2.2 collective-permute-start.2
  23.1 3.6 %collective-permute-start.3 = (f32[1,32,1024]{2,1,0:T(8,128)S(1)}, f32[1,32,1024]{2,1,0:T(8,128)S(1)}, u32[]{:S(2)}, u32[]{:S(2)}) collective-permute-start(f32[1,32,1024]{2,1,0:T(8,128)S(1)} %get-tuple-element.79), channel_id=1, source_target_pairs={{0,8},{8,16},{16,24},{24,32},{32,40},{40,48},{48,56},{56,64},{64,7... | collective-permute-start | bytes 393224 | tf_op jit(solution)/shard_map/ppermute | solution.py:31
  26.8 1.3 collective-permute-start.4
  28.1 4.0 %collective-permute-start.5 = (f32[8,1,1024]{2,1,0:T(1,128)S(1)}, f32[8,1,1024]{2,1,0:T(1,128)S(1)}, u32[]{:S(2)}, u32[]{:S(2)}) collective-permute-start(f32[8,1,1024]{2,1,0:T(1,128)S(1)} %get-tuple-element.78), channel_id=1, source_target_pairs={{0,1},{1,2},{2,3},{3,4},{4,5},{5,6},{6,7},{8,9},{9,10},{10,11},{11... | collective-permute-start | bytes 98312 | tf_op jit(solution)/shard_map/ppermute | solution.py:31
  33.1 2.0 fusion.177
  35.2 1.9 collective-permute-start.6
  37.2 3.6 %collective-permute-start.7 = (f32[1,32,1024]{2,1,0:T(8,128)S(1)}, f32[1,32,1024]{2,1,0:T(8,128)S(1)}, u32[]{:S(2)}, u32[]{:S(2)}) collective-permute-start(f32[1,32,1024]{2,1,0:T(8,128)S(1)} %get-tuple-element.73), channel_id=1, source_target_pairs={{0,8},{8,16},{16,24},{24,32},{32,40},{40,48},{48,56},{56,64},{64,7... | collective-permute-start | bytes 393224 | tf_op jit(solution)/shard_map/ppermute | solution.py:31
  40.8 1.3 collective-permute-start.8
  42.1 4.3 %collective-permute-start.9 = (f32[8,1,1024]{2,1,0:T(1,128)S(1)}, f32[8,1,1024]{2,1,0:T(1,128)S(1)}, u32[]{:S(2)}, u32[]{:S(2)}) collective-permute-start(f32[8,1,1024]{2,1,0:T(1,128)S(1)} %get-tuple-element.72), channel_id=1, source_target_pairs={{0,1},{1,2},{2,3},{3,4},{4,5},{5,6},{6,7},{8,9},{9,10},{10,11},{11... | collective-permute-start | bytes 98312 | tf_op jit(solution)/shard_map/ppermute | solution.py:31
  47.4 1.9 multiply_multiply_fusion.4
  49.4 1.9 collective-permute-start.10
  51.4 3.6 %collective-permute-start.11 = (f32[1,32,1024]{2,1,0:T(8,128)S(1)}, f32[1,32,1024]{2,1,0:T(8,128)S(1)}, u32[]{:S(2)}, u32[]{:S(2)}) collective-permute-start(f32[1,32,1024]{2,1,0:T(8,128)S(1)} %get-tuple-element.67), channel_id=1, source_target_pairs={{0,8},{8,16},{16,24},{24,32},{32,40},{40,48},{48,56},{56,64},{64,7... | collective-permute-start | bytes 393224 | tf_op jit(solution)/shard_map/ppermute | solution.py:31
  55.0 1.3 collective-permute-start.12
  56.3 4.3 %collective-permute-start.13 = (f32[8,1,1024]{2,1,0:T(1,128)S(1)}, f32[8,1,1024]{2,1,0:T(1,128)S(1)}, u32[]{:S(2)}, u32[]{:S(2)}) collective-permute-start(f32[8,1,1024]{2,1,0:T(1,128)S(1)} %get-tuple-element.66), channel_id=1, source_target_pairs={{0,1},{1,2},{2,3},{3,4},{4,5},{5,6},{6,7},{8,9},{9,10},{10,11},{11... | collective-permute-start | bytes 98312 | tf_op jit(solution)/shard_map/ppermute | solution.py:31
  61.6 3.4 %multiply_multiply_fusion.1 = f32[8,32,1024]{2,1,0:T(8,128)S(1)} fusion(f32[8,32,1023]{2,1,0:T(8,128)S(1)} %get-tuple-element.70, f32[8,32,1023]{2,1,0:T(8,128)S(1)} %get-tuple-element.69, f32[1,32,1024]{2,1,0:T(8,128)S(1)} %collective-permute-done.10, f32[8,32,1024]{2,1,0:T(8,128)S(1)} %multiply_multiply_fusion.4, ...), kind=kLoop, calls=%fused_computation.251 | loop fusion | flops 16252928 | bytes 15330304 | tf_op jit(solution)/shard_map/mul | solution.py:92
  65.1 1.9 collective-permute-start.14
  67.1 3.6 %collective-permute-start.15 = (f32[1,32,1024]{2,1,0:T(8,128)S(1)}, f32[1,32,1024]{2,1,0:T(8,128)S(1)}, u32[]{:S(2)}, u32[]{:S(2)}) collective-permute-start(f32[1,32,1024]{2,1,0:T(8,128)S(1)} %get-tuple-element.61), channel_id=1, source_target_pairs={{0,8},{8,16},{16,24},{24,32},{32,40},{40,48},{48,56},{56,64},{64,7... | collective-permute-start | bytes 393224 | tf_op jit(solution)/shard_map/ppermute | solution.py:31
  70.7 1.3 collective-permute-start.16
  72.0 4.5 %collective-permute-start.17 = (f32[8,1,1024]{2,1,0:T(1,128)S(1)}, f32[8,1,1024]{2,1,0:T(1,128)S(1)}, u32[]{:S(2)}, u32[]{:S(2)}) collective-permute-start(f32[8,1,1024]{2,1,0:T(1,128)S(1)} %get-tuple-element.60), channel_id=1, source_target_pairs={{0,1},{1,2},{2,3},{3,4},{4,5},{5,6},{6,7},{8,9},{9,10},{10,11},{11... | collective-permute-start | bytes 98312 | tf_op jit(solution)/shard_map/ppermute | solution.py:31
  76.5 1.7 fusion.203
  79.0 6.8 %fusion.175 = (f32[8,32,1024]{2,1,0:T(8,128)S(1)}, f32[8,32,1024]{2,1,0:T(8,128)}) fusion(f32[8,32,1024]{2,1,0:T(8,128)S(1)} %get-tuple-element.14, f32[8,32,1023]{2,1,0:T(8,128)} %get-tuple-element.64, f32[8,32,1023]{2,1,0:T(8,128)} %get-tuple-element.63, f32[1,32,1024]{2,1,0:T(8,128)} %copy-done.35, f32[8,32,1024]{2,1,0:T(8,128)S(1)} %multiply_multiply_fusion.1, ...), kind=kLoop, calls=%fused_computation.300 | loop fusion | flops 22020096 | bytes 20898816 | tf_op jit(solution)/shard_map/mul | solution.py:92
  85.9 2.1 collective-permute-start.18
  88.0 3.6 %collective-permute-start.19 = (f32[1,32,1024]{2,1,0:T(8,128)S(1)}, f32[1,32,1024]{2,1,0:T(8,128)S(1)}, u32[]{:S(2)}, u32[]{:S(2)}) collective-permute-start(f32[1,32,1024]{2,1,0:T(8,128)S(1)} %get-tuple-element.55), channel_id=1, source_target_pairs={{0,8},{8,16},{16,24},{24,32},{32,40},{40,48},{48,56},{56,64},{64,7... | collective-permute-start | bytes 393224 | tf_op jit(solution)/shard_map/ppermute | solution.py:31
  91.6 1.3 collective-permute-start.20
  92.9 6.6 %collective-permute-start.21 = (f32[8,1,1024]{2,1,0:T(1,128)S(1)}, f32[8,1,1024]{2,1,0:T(1,128)S(1)}, u32[]{:S(2)}, u32[]{:S(2)}) collective-permute-start(f32[8,1,1024]{2,1,0:T(1,128)S(1)} %get-tuple-element.54), channel_id=1, source_target_pairs={{0,1},{1,2},{2,3},{3,4},{4,5},{5,6},{6,7},{8,9},{9,10},{10,11},{11... | collective-permute-start | bytes 98312 | tf_op jit(solution)/shard_map/ppermute | solution.py:31
  100.4 2.0 fusion.173
  102.5 1.9 collective-permute-start.22
  104.4 3.6 %collective-permute-start.23 = (f32[1,32,1024]{2,1,0:T(8,128)S(1)}, f32[1,32,1024]{2,1,0:T(8,128)S(1)}, u32[]{:S(2)}, u32[]{:S(2)}) collective-permute-start(f32[1,32,1024]{2,1,0:T(8,128)S(1)} %get-tuple-element.49), channel_id=1, source_target_pairs={{0,8},{8,16},{16,24},{24,32},{32,40},{40,48},{48,56},{56,64},{64,7... | collective-permute-start | bytes 393224 | tf_op jit(solution)/shard_map/ppermute | solution.py:31
  108.1 1.3 collective-permute-start.24
  109.4 6.4 %collective-permute-start.25 = (f32[8,1,1024]{2,1,0:T(1,128)S(1)}, f32[8,1,1024]{2,1,0:T(1,128)S(1)}, u32[]{:S(2)}, u32[]{:S(2)}) collective-permute-start(f32[8,1,1024]{2,1,0:T(1,128)S(1)} %get-tuple-element.48), channel_id=1, source_target_pairs={{0,1},{1,2},{2,3},{3,4},{4,5},{5,6},{6,7},{8,9},{9,10},{10,11},{11... | collective-permute-start | bytes 98312 | tf_op jit(solution)/shard_map/ppermute | solution.py:31
  116.8 2.0 multiply_multiply_fusion.3
  118.8 1.9 collective-permute-start.26
  120.8 4.6 %collective-permute-start.27 = (f32[1,32,1024]{2,1,0:T(8,128)S(1)}, f32[1,32,1024]{2,1,0:T(8,128)S(1)}, u32[]{:S(2)}, u32[]{:S(2)}) collective-permute-start(f32[1,32,1024]{2,1,0:T(8,128)S(1)} %get-tuple-element.43), channel_id=1, source_target_pairs={{0,8},{8,16},{16,24},{24,32},{32,40},{40,48},{48,56},{56,64},{64,7... | collective-permute-start | bytes 393224 | tf_op jit(solution)/shard_map/ppermute | solution.py:31
  126.6 6.4 %collective-permute-start.29 = (f32[8,1,1024]{2,1,0:T(1,128)S(1)}, f32[8,1,1024]{2,1,0:T(1,128)S(1)}, u32[]{:S(2)}, u32[]{:S(2)}) collective-permute-start(f32[8,1,1024]{2,1,0:T(1,128)S(1)} %get-tuple-element.42), channel_id=1, source_target_pairs={{0,1},{1,2},{2,3},{3,4},{4,5},{5,6},{6,7},{8,9},{9,10},{10,11},{11... | collective-permute-start | bytes 98312 | tf_op jit(solution)/shard_map/ppermute | solution.py:31
  134.1 3.4 %multiply_multiply_fusion = f32[8,32,1024]{2,1,0:T(8,128)S(1)} fusion(f32[8,32,1023]{2,1,0:T(8,128)S(1)} %get-tuple-element.46, f32[8,32,1023]{2,1,0:T(8,128)S(1)} %get-tuple-element.45, f32[1,32,1024]{2,1,0:T(8,128)S(1)} %collective-permute-done.26, f32[8,32,1024]{2,1,0:T(8,128)S(1)} %multiply_multiply_fusion.3, ...), kind=kLoop, calls=%fused_computation.250 | loop fusion | flops 16252928 | bytes 15330304 | tf_op jit(solution)/shard_map/mul | solution.py:92
  137.7 1.9 collective-permute-start.30
  139.6 7.8 %collective-permute-start.31 = (f32[1,32,1024]{2,1,0:T(8,128)S(1)}, f32[1,32,1024]{2,1,0:T(8,128)S(1)}, u32[]{:S(2)}, u32[]{:S(2)}) collective-permute-start(f32[1,32,1024]{2,1,0:T(8,128)S(1)} %get-tuple-element.37), channel_id=1, source_target_pairs={{0,8},{8,16},{16,24},{24,32},{32,40},{40,48},{48,56},{56,64},{64,7... | collective-permute-start | bytes 393224 | tf_op jit(solution)/shard_map/ppermute | solution.py:31
  148.7 6.4 %collective-permute-start.33 = (f32[8,1,1024]{2,1,0:T(1,128)S(1)}, f32[8,1,1024]{2,1,0:T(1,128)S(1)}, u32[]{:S(2)}, u32[]{:S(2)}) collective-permute-start(f32[8,1,1024]{2,1,0:T(1,128)S(1)} %get-tuple-element.36), channel_id=1, source_target_pairs={{0,1},{1,2},{2,3},{3,4},{4,5},{5,6},{6,7},{8,9},{9,10},{10,11},{11... | collective-permute-start | bytes 98312 | tf_op jit(solution)/shard_map/ppermute | solution.py:31
  155.1 1.7 fusion.191
  157.6 8.4 %fusion.171 = (f32[8,32,1024]{2,1,0:T(8,128)S(1)}, f32[8,32,1024]{2,1,0:T(8,128)}) fusion(f32[8,32,1024]{2,1,0:T(8,128)} %copy-done.12, f32[8,32,1023]{2,1,0:T(8,128)} %get-tuple-element.40, f32[8,32,1023]{2,1,0:T(8,128)} %get-tuple-element.39, f32[1,32,1024]{2,1,0:T(8,128)} %copy-done.36, f32[8,32,1024]{2,1,0:T(8,128)} %copy-done.7, ...), kind=kLoop, calls=%fused_computation.298 | loop fusion | flops 22020096 | bytes 20898816 | tf_op jit(solution)/shard_map/mul | solution.py:92
  166.1 2.1 collective-permute-start.34
  168.1 6.0 %collective-permute-start.35 = (f32[1,32,1024]{2,1,0:T(8,128)S(1)}, f32[1,32,1024]{2,1,0:T(8,128)S(1)}, u32[]{:S(2)}, u32[]{:S(2)}) collective-permute-start(f32[1,32,1024]{2,1,0:T(8,128)S(1)} %get-tuple-element.31), channel_id=1, source_target_pairs={{0,8},{8,16},{16,24},{24,32},{32,40},{40,48},{48,56},{56,64},{64,7... | collective-permute-start | bytes 393224 | tf_op jit(solution)/shard_map/ppermute | solution.py:31
  174.1 1.3 collective-permute-start.36
  175.4 6.4 %collective-permute-start.37 = (f32[8,1,1024]{2,1,0:T(1,128)S(1)}, f32[8,1,1024]{2,1,0:T(1,128)S(1)}, u32[]{:S(2)}, u32[]{:S(2)}) collective-permute-start(f32[8,1,1024]{2,1,0:T(1,128)S(1)} %get-tuple-element.30), channel_id=1, source_target_pairs={{0,1},{1,2},{2,3},{3,4},{4,5},{5,6},{6,7},{8,9},{9,10},{10,11},{11... | collective-permute-start | bytes 98312 | tf_op jit(solution)/shard_map/ppermute | solution.py:31
  182.8 2.1 fusion.169
  185.0 1.9 collective-permute-start.38
  186.9 8.5 %collective-permute-start.39 = (f32[1,32,1024]{2,1,0:T(8,128)S(1)}, f32[1,32,1024]{2,1,0:T(8,128)S(1)}, u32[]{:S(2)}, u32[]{:S(2)}) collective-permute-start(f32[1,32,1024]{2,1,0:T(8,128)S(1)} %get-tuple-element.25), channel_id=1, source_target_pairs={{0,8},{8,16},{16,24},{24,32},{32,40},{40,48},{48,56},{56,64},{64,7... | collective-permute-start | bytes 393224 | tf_op jit(solution)/shard_map/ppermute | solution.py:31
  196.8 6.6 %collective-permute-start.41 = (f32[8,1,1024]{2,1,0:T(1,128)S(1)}, f32[8,1,1024]{2,1,0:T(1,128)S(1)}, u32[]{:S(2)}, u32[]{:S(2)}) collective-permute-start(f32[8,1,1024]{2,1,0:T(1,128)S(1)} %get-tuple-element.24), channel_id=1, source_target_pairs={{0,1},{1,2},{2,3},{3,4},{4,5},{5,6},{6,7},{8,9},{9,10},{10,11},{11... | collective-permute-start | bytes 98312 | tf_op jit(solution)/shard_map/ppermute | solution.py:31
  204.8 2.0 multiply_multiply_fusion.2
  206.9 2.1 collective-permute-start.42
  209.0 5.9 %collective-permute-start.43 = (f32[1,32,1024]{2,1,0:T(8,128)S(1)}, f32[1,32,1024]{2,1,0:T(8,128)}, u32[]{:S(2)}, u32[]{:S(2)}) collective-permute-start(f32[1,32,1024]{2,1,0:T(8,128)S(1)} %get-tuple-element.21), channel_id=1, source_target_pairs={{0,8},{8,16},{16,24},{24,32},{32,40},{40,48},{48,56},{56,64},{64,7... | collective-permute-start | bytes 393224 | tf_op jit(solution)/shard_map/ppermute | solution.py:31
  216.2 6.4 %collective-permute-start.45 = (f32[8,1,1024]{2,1,0:T(1,128)S(1)}, f32[8,1,1024]{2,1,0:T(1,128)S(1)}, u32[]{:S(2)}, u32[]{:S(2)}) collective-permute-start(f32[8,1,1024]{2,1,0:T(1,128)S(1)} %get-tuple-element.20), channel_id=1, source_target_pairs={{0,1},{1,2},{2,3},{3,4},{4,5},{5,6},{6,7},{8,9},{9,10},{10,11},{11... | collective-permute-start | bytes 98312 | tf_op jit(solution)/shard_map/ppermute | solution.py:31
  222.6 1.7 fusion.180
  224.9 11.6 %fusion.9 = f32[8,32,1024]{2,1,0:T(8,128)} fusion(f32[8,1,1024]{2,1,0:T(1,128)} %copy-done.42, f32[1,32,1024]{2,1,0:T(8,128)} %collective-permute-done.42, f32[8,32,1024]{2,1,0:T(8,128)S(1)} %multiply_multiply_fusion.2, f32[1,32,1024]{2,1,0:T(8,128)} %collective-permute-done.43, f32[8,1,1024]{2,1,0:T(1,128)} %copy-done.41, ...), kind=kLoop, calls=%fused_computation.14 | loop fusion | flops 44826624 | bytes 34458624 | tf_op jit(solution)/shard_map/add | solution.py:146
  236.5 1.4 reshape.63
  238.0 2.4 scatter_custom_fusion
  240.5 58.3 %all_to_all.5 = f32[128,8,129]{2,1,0:T(8,128)S(1)} all-to-all(f32[128,8,129]{2,1,0:T(8,128)S(1)} %pad_maximum_fusion.68), channel_id=1, replica_groups=mesh['gx'=16,'gy'=8] {'gx','gy'}, dimensions={0} | all-to-all | bytes 1056768 | tf_op jit(solution)/shard_map/all_to_all | solution.py:47
  298.8 2.2 fusion.151
  301.1 6.1 %scatter_custom_fusion.2 = f32[256,128]{1,0:T(8,128)S(1)} fusion(s32[1024]{0:T(1024)S(1)} %bitcast.259, f32[128,8,129]{2,1,0:T(8,128)S(1)} %all_to_all.5, f32[]{:T(128)} %constant.18.clone.1), kind=kCustom, calls=%fused_computation.259 | custom fusion | flops 131072 | bytes 655364 | tf_op jit(solution)/shard_map/scatter-add | solution.py:119
  (203 shorter events, 21.7 us)
Async XLA Ops:
  0.7 14.5 %copy-start.48 = (s32[256]{0:T(256)S(1)}, s32[256]{0:T(256)}, u32[]{:S(2)}) copy-start(s32[256]{0:T(256)} %param.9) | copy-start | bytes 3076
  0.7 14.6 %copy-start.49 = (s32[256]{0:T(256)S(1)}, s32[256]{0:T(256)}, u32[]{:S(2)}) copy-start(s32[256]{0:T(256)} %param.11) | copy-start | bytes 3076
  4.5 13.3 %collective-permute-start.1 = (f32[8,1,1024]{2,1,0:T(1,128)S(1)}, f32[8,1,1024]{2,1,0:T(1,128)S(1)}, u32[]{:S(2)}, u32[]{:S(2)}) collective-permute-start(f32[8,1,1024]{2,1,0:T(1,128)S(1)} %slice.558), channel_id=1, source_target_pairs={{0,1},{1,2},{2,3},{3,4},{4,5},{5,6},{6,7},{8,9},{9,10},{10,11},{11... | collective-permute-start | bytes 98312 | tf_op jit(solution)/shard_map/ppermute | solution.py:20
  9.2 8.7 %collective-permute-start = (f32[1,32,1024]{2,1,0:T(8,128)}, f32[1,32,1024]{2,1,0:T(8,128)S(1)}, u32[]{:S(2)}, u32[]{:S(2)}) collective-permute-start(f32[1,32,1024]{2,1,0:T(8,128)} %slice_bitcast_fusion.5), channel_id=1, source_target_pairs={{0,8},{8,16},{16,24},{24,32},{32,40},{40,48},{48,56},{56,64},{64,7... | collective-permute-start | bytes 393224 | tf_op jit(solution)/shard_map/ppermute | solution.py:20
  20.8 58.2 %copy-start.12 = (f32[8,32,1024]{2,1,0:T(8,128)}, f32[8,32,1024]{2,1,0:T(8,128)S(1)}, u32[]{:S(2)}) copy-start(f32[8,32,1024]{2,1,0:T(8,128)S(1)} %get-tuple-element.14) | copy-start | bytes 3145732
  20.9 12.1 %collective-permute-start.2 = (f32[1,32,1024]{2,1,0:T(8,128)S(1)}, f32[1,32,1024]{2,1,0:T(8,128)S(1)}, u32[]{:S(2)}, u32[]{:S(2)}) collective-permute-start(f32[1,32,1024]{2,1,0:T(8,128)S(1)} %get-tuple-element.80), channel_id=1, source_target_pairs={{8,0},{16,8},{24,16},{32,24},{40,32},{48,40},{56,48},{64,56},{72,6... | collective-permute-start | bytes 393224 | tf_op jit(solution)/shard_map/ppermute | solution.py:32
  23.1 10.0 %collective-permute-start.3 = (f32[1,32,1024]{2,1,0:T(8,128)S(1)}, f32[1,32,1024]{2,1,0:T(8,128)S(1)}, u32[]{:S(2)}, u32[]{:S(2)}) collective-permute-start(f32[1,32,1024]{2,1,0:T(8,128)S(1)} %get-tuple-element.79), channel_id=1, source_target_pairs={{0,8},{8,16},{16,24},{24,32},{32,40},{40,48},{48,56},{56,64},{64,7... | collective-permute-start | bytes 393224 | tf_op jit(solution)/shard_map/ppermute | solution.py:31
  26.8 5.7 %collective-permute-start.4 = (f32[8,1,1024]{2,1,0:T(1,128)S(1)}, f32[8,1,1024]{2,1,0:T(1,128)S(1)}, u32[]{:S(2)}, u32[]{:S(2)}) collective-permute-start(f32[8,1,1024]{2,1,0:T(1,128)S(1)} %get-tuple-element.77), channel_id=1, source_target_pairs={{1,0},{2,1},{3,2},{4,3},{5,4},{6,5},{7,6},{9,8},{10,9},{11,10},{12... | collective-permute-start | bytes 98312 | tf_op jit(solution)/shard_map/ppermute | solution.py:32
  28.1 5.0 %collective-permute-start.5 = (f32[8,1,1024]{2,1,0:T(1,128)S(1)}, f32[8,1,1024]{2,1,0:T(1,128)S(1)}, u32[]{:S(2)}, u32[]{:S(2)}) collective-permute-start(f32[8,1,1024]{2,1,0:T(1,128)S(1)} %get-tuple-element.78), channel_id=1, source_target_pairs={{0,1},{1,2},{2,3},{3,4},{4,5},{5,6},{6,7},{8,9},{9,10},{10,11},{11... | collective-permute-start | bytes 98312 | tf_op jit(solution)/shard_map/ppermute | solution.py:31
  35.1 65.2 %copy-start.16 = (f32[8,32,1024]{2,1,0:T(8,128)}, f32[8,32,1024]{2,1,0:T(8,128)S(1)}, u32[]{:S(2)}) copy-start(f32[8,32,1024]{2,1,0:T(8,128)S(1)} %get-tuple-element.11) | copy-start | bytes 3145732
  35.2 12.2 %collective-permute-start.6 = (f32[1,32,1024]{2,1,0:T(8,128)S(1)}, f32[1,32,1024]{2,1,0:T(8,128)S(1)}, u32[]{:S(2)}, u32[]{:S(2)}) collective-permute-start(f32[1,32,1024]{2,1,0:T(8,128)S(1)} %get-tuple-element.74), channel_id=1, source_target_pairs={{8,0},{16,8},{24,16},{32,24},{40,32},{48,40},{56,48},{64,56},{72,6... | collective-permute-start | bytes 393224 | tf_op jit(solution)/shard_map/ppermute | solution.py:32
  37.2 10.2 %collective-permute-start.7 = (f32[1,32,1024]{2,1,0:T(8,128)S(1)}, f32[1,32,1024]{2,1,0:T(8,128)S(1)}, u32[]{:S(2)}, u32[]{:S(2)}) collective-permute-start(f32[1,32,1024]{2,1,0:T(8,128)S(1)} %get-tuple-element.73), channel_id=1, source_target_pairs={{0,8},{8,16},{16,24},{24,32},{32,40},{40,48},{48,56},{56,64},{64,7... | collective-permute-start | bytes 393224 | tf_op jit(solution)/shard_map/ppermute | solution.py:31
  40.8 6.0 %collective-permute-start.8 = (f32[8,1,1024]{2,1,0:T(1,128)S(1)}, f32[8,1,1024]{2,1,0:T(1,128)S(1)}, u32[]{:S(2)}, u32[]{:S(2)}) collective-permute-start(f32[8,1,1024]{2,1,0:T(1,128)S(1)} %get-tuple-element.71), channel_id=1, source_target_pairs={{1,0},{2,1},{3,2},{4,3},{5,4},{6,5},{7,6},{9,8},{10,9},{11,10},{12... | collective-permute-start | bytes 98312 | tf_op jit(solution)/shard_map/ppermute | solution.py:32
  42.1 5.3 %collective-permute-start.9 = (f32[8,1,1024]{2,1,0:T(1,128)S(1)}, f32[8,1,1024]{2,1,0:T(1,128)S(1)}, u32[]{:S(2)}, u32[]{:S(2)}) collective-permute-start(f32[8,1,1024]{2,1,0:T(1,128)S(1)} %get-tuple-element.72), channel_id=1, source_target_pairs={{0,1},{1,2},{2,3},{3,4},{4,5},{5,6},{6,7},{8,9},{9,10},{10,11},{11... | collective-permute-start | bytes 98312 | tf_op jit(solution)/shard_map/ppermute | solution.py:31
  49.4 12.2 %collective-permute-start.10 = (f32[1,32,1024]{2,1,0:T(8,128)S(1)}, f32[1,32,1024]{2,1,0:T(8,128)S(1)}, u32[]{:S(2)}, u32[]{:S(2)}) collective-permute-start(f32[1,32,1024]{2,1,0:T(8,128)S(1)} %get-tuple-element.68), channel_id=1, source_target_pairs={{8,0},{16,8},{24,16},{32,24},{40,32},{48,40},{56,48},{64,56},{72,6... | collective-permute-start | bytes 393224 | tf_op jit(solution)/shard_map/ppermute | solution.py:32
  51.4 10.2 %collective-permute-start.11 = (f32[1,32,1024]{2,1,0:T(8,128)S(1)}, f32[1,32,1024]{2,1,0:T(8,128)S(1)}, u32[]{:S(2)}, u32[]{:S(2)}) collective-permute-start(f32[1,32,1024]{2,1,0:T(8,128)S(1)} %get-tuple-element.67), channel_id=1, source_target_pairs={{0,8},{8,16},{16,24},{24,32},{32,40},{40,48},{48,56},{56,64},{64,7... | collective-permute-start | bytes 393224 | tf_op jit(solution)/shard_map/ppermute | solution.py:31
  55.0 6.0 %collective-permute-start.12 = (f32[8,1,1024]{2,1,0:T(1,128)S(1)}, f32[8,1,1024]{2,1,0:T(1,128)S(1)}, u32[]{:S(2)}, u32[]{:S(2)}) collective-permute-start(f32[8,1,1024]{2,1,0:T(1,128)S(1)} %get-tuple-element.65), channel_id=1, source_target_pairs={{1,0},{2,1},{3,2},{4,3},{5,4},{6,5},{7,6},{9,8},{10,9},{11,10},{12... | collective-permute-start | bytes 98312 | tf_op jit(solution)/shard_map/ppermute | solution.py:32
  56.3 5.3 %collective-permute-start.13 = (f32[8,1,1024]{2,1,0:T(1,128)S(1)}, f32[8,1,1024]{2,1,0:T(1,128)S(1)}, u32[]{:S(2)}, u32[]{:S(2)}) collective-permute-start(f32[8,1,1024]{2,1,0:T(1,128)S(1)} %get-tuple-element.66), channel_id=1, source_target_pairs={{0,1},{1,2},{2,3},{3,4},{4,5},{5,6},{6,7},{8,9},{9,10},{10,11},{11... | collective-permute-start | bytes 98312 | tf_op jit(solution)/shard_map/ppermute | solution.py:31
  61.0 18.0 %copy-start.8 = (f32[8,32,1023]{2,1,0:T(8,128)}, f32[8,32,1023]{2,1,0:T(8,128)S(1)}, u32[]{:S(2)}) copy-start(f32[8,32,1023]{2,1,0:T(8,128)S(1)} %get-tuple-element.69) | copy-start | bytes 3142660
  61.0 18.0 %copy-start.9 = (f32[8,32,1023]{2,1,0:T(8,128)}, f32[8,32,1023]{2,1,0:T(8,128)S(1)}, u32[]{:S(2)}) copy-start(f32[8,32,1023]{2,1,0:T(8,128)S(1)} %get-tuple-element.70) | copy-start | bytes 3142660
  61.0 18.0 %copy-start.31 = (f32[8,1,1024]{2,1,0:T(1,128)}, f32[8,1,1024]{2,1,0:T(1,128)S(1)}, u32[]{:S(2)}) copy-start(f32[8,1,1024]{2,1,0:T(1,128)S(1)} %collective-permute-done.12) | copy-start | bytes 98308
  61.6 17.4 %copy-start.23 = (f32[1,32,1024]{2,1,0:T(8,128)}, f32[1,32,1024]{2,1,0:T(8,128)S(1)}, u32[]{:S(2)}) copy-start(f32[1,32,1024]{2,1,0:T(8,128)S(1)} %collective-permute-done.10) | copy-start | bytes 393220
  65.1 13.1 %collective-permute-start.14 = (f32[1,32,1024]{2,1,0:T(8,128)S(1)}, f32[1,32,1024]{2,1,0:T(8,128)S(1)}, u32[]{:S(2)}, u32[]{:S(2)}) collective-permute-start(f32[1,32,1024]{2,1,0:T(8,128)S(1)} %get-tuple-element.62), channel_id=1, source_target_pairs={{8,0},{16,8},{24,16},{32,24},{40,32},{48,40},{56,48},{64,56},{72,6... | collective-permute-start | bytes 393224 | tf_op jit(solution)/shard_map/ppermute | solution.py:32
  67.1 11.2 %collective-permute-start.15 = (f32[1,32,1024]{2,1,0:T(8,128)S(1)}, f32[1,32,1024]{2,1,0:T(8,128)S(1)}, u32[]{:S(2)}, u32[]{:S(2)}) collective-permute-start(f32[1,32,1024]{2,1,0:T(8,128)S(1)} %get-tuple-element.61), channel_id=1, source_target_pairs={{0,8},{8,16},{16,24},{24,32},{32,40},{40,48},{48,56},{56,64},{64,7... | collective-permute-start | bytes 393224 | tf_op jit(solution)/shard_map/ppermute | solution.py:31
  70.7 7.5 %collective-permute-start.16 = (f32[8,1,1024]{2,1,0:T(1,128)S(1)}, f32[8,1,1024]{2,1,0:T(1,128)S(1)}, u32[]{:S(2)}, u32[]{:S(2)}) collective-permute-start(f32[8,1,1024]{2,1,0:T(1,128)S(1)} %get-tuple-element.59), channel_id=1, source_target_pairs={{1,0},{2,1},{3,2},{4,3},{5,4},{6,5},{7,6},{9,8},{10,9},{11,10},{12... | collective-permute-start | bytes 98312 | tf_op jit(solution)/shard_map/ppermute | solution.py:32
  72.0 6.2 %collective-permute-start.17 = (f32[8,1,1024]{2,1,0:T(1,128)S(1)}, f32[8,1,1024]{2,1,0:T(1,128)S(1)}, u32[]{:S(2)}, u32[]{:S(2)}) collective-permute-start(f32[8,1,1024]{2,1,0:T(1,128)S(1)} %get-tuple-element.60), channel_id=1, source_target_pairs={{0,1},{1,2},{2,3},{3,4},{4,5},{5,6},{6,7},{8,9},{9,10},{10,11},{11... | collective-permute-start | bytes 98312 | tf_op jit(solution)/shard_map/ppermute | solution.py:31
  85.8 14.5 %copy-start.20 = (f32[8,32,1024]{2,1,0:T(8,128)S(1)}, f32[8,32,1024]{2,1,0:T(8,128)}, u32[]{:S(2)}) copy-start(f32[8,32,1024]{2,1,0:T(8,128)} %get-tuple-element.9) | copy-start | bytes 3145732
  85.9 14.4 %collective-permute-start.18 = (f32[1,32,1024]{2,1,0:T(8,128)S(1)}, f32[1,32,1024]{2,1,0:T(8,128)S(1)}, u32[]{:S(2)}, u32[]{:S(2)}) collective-permute-start(f32[1,32,1024]{2,1,0:T(8,128)S(1)} %get-tuple-element.56), channel_id=1, source_target_pairs={{8,0},{16,8},{24,16},{32,24},{40,32},{48,40},{56,48},{64,56},{72,6... | collective-permute-start | bytes 393224 | tf_op jit(solution)/shard_map/ppermute | solution.py:32
  88.0 12.4 %collective-permute-start.19 = (f32[1,32,1024]{2,1,0:T(8,128)S(1)}, f32[1,32,1024]{2,1,0:T(8,128)S(1)}, u32[]{:S(2)}, u32[]{:S(2)}) collective-permute-start(f32[1,32,1024]{2,1,0:T(8,128)S(1)} %get-tuple-element.55), channel_id=1, source_target_pairs={{0,8},{8,16},{16,24},{24,32},{32,40},{40,48},{48,56},{56,64},{64,7... | collective-permute-start | bytes 393224 | tf_op jit(solution)/shard_map/ppermute | solution.py:31
  91.6 8.3 %collective-permute-start.20 = (f32[8,1,1024]{2,1,0:T(1,128)S(1)}, f32[8,1,1024]{2,1,0:T(1,128)S(1)}, u32[]{:S(2)}, u32[]{:S(2)}) collective-permute-start(f32[8,1,1024]{2,1,0:T(1,128)S(1)} %get-tuple-element.53), channel_id=1, source_target_pairs={{1,0},{2,1},{3,2},{4,3},{5,4},{6,5},{7,6},{9,8},{10,9},{11,10},{12... | collective-permute-start | bytes 98312 | tf_op jit(solution)/shard_map/ppermute | solution.py:32
  92.9 7.4 %collective-permute-start.21 = (f32[8,1,1024]{2,1,0:T(1,128)S(1)}, f32[8,1,1024]{2,1,0:T(1,128)S(1)}, u32[]{:S(2)}, u32[]{:S(2)}) collective-permute-start(f32[8,1,1024]{2,1,0:T(1,128)S(1)} %get-tuple-element.54), channel_id=1, source_target_pairs={{0,1},{1,2},{2,3},{3,4},{4,5},{5,6},{6,7},{8,9},{9,10},{10,11},{11... | collective-permute-start | bytes 98312 | tf_op jit(solution)/shard_map/ppermute | solution.py:31
  102.4 31.6 %copy-start.5 = (f32[8,32,1024]{2,1,0:T(8,128)}, f32[8,32,1024]{2,1,0:T(8,128)S(1)}, u32[]{:S(2)}) copy-start(f32[8,32,1024]{2,1,0:T(8,128)S(1)} %get-tuple-element.7) | copy-start | bytes 3145732
  102.5 14.3 %collective-permute-start.22 = (f32[1,32,1024]{2,1,0:T(8,128)S(1)}, f32[1,32,1024]{2,1,0:T(8,128)S(1)}, u32[]{:S(2)}, u32[]{:S(2)}) collective-permute-start(f32[1,32,1024]{2,1,0:T(8,128)S(1)} %get-tuple-element.50), channel_id=1, source_target_pairs={{8,0},{16,8},{24,16},{32,24},{40,32},{48,40},{56,48},{64,56},{72,6... | collective-permute-start | bytes 393224 | tf_op jit(solution)/shard_map/ppermute | solution.py:32
  104.4 12.4 %collective-permute-start.23 = (f32[1,32,1024]{2,1,0:T(8,128)S(1)}, f32[1,32,1024]{2,1,0:T(8,128)S(1)}, u32[]{:S(2)}, u32[]{:S(2)}) collective-permute-start(f32[1,32,1024]{2,1,0:T(8,128)S(1)} %get-tuple-element.49), channel_id=1, source_target_pairs={{0,8},{8,16},{16,24},{24,32},{32,40},{40,48},{48,56},{56,64},{64,7... | collective-permute-start | bytes 393224 | tf_op jit(solution)/shard_map/ppermute | solution.py:31
  108.1 8.1 %collective-permute-start.24 = (f32[8,1,1024]{2,1,0:T(1,128)S(1)}, f32[8,1,1024]{2,1,0:T(1,128)S(1)}, u32[]{:S(2)}, u32[]{:S(2)}) collective-permute-start(f32[8,1,1024]{2,1,0:T(1,128)S(1)} %get-tuple-element.47), channel_id=1, source_target_pairs={{1,0},{2,1},{3,2},{4,3},{5,4},{6,5},{7,6},{9,8},{10,9},{11,10},{12... | collective-permute-start | bytes 98312 | tf_op jit(solution)/shard_map/ppermute | solution.py:32
  109.4 7.4 %collective-permute-start.25 = (f32[8,1,1024]{2,1,0:T(1,128)S(1)}, f32[8,1,1024]{2,1,0:T(1,128)S(1)}, u32[]{:S(2)}, u32[]{:S(2)}) collective-permute-start(f32[8,1,1024]{2,1,0:T(1,128)S(1)} %get-tuple-element.48), channel_id=1, source_target_pairs={{0,1},{1,2},{2,3},{3,4},{4,5},{5,6},{6,7},{8,9},{9,10},{10,11},{11... | collective-permute-start | bytes 98312 | tf_op jit(solution)/shard_map/ppermute | solution.py:31
  116.8 17.3 %copy-start.29 = (f32[8,1,1024]{2,1,0:T(1,128)}, f32[8,1,1024]{2,1,0:T(1,128)S(1)}, u32[]{:S(2)}) copy-start(f32[8,1,1024]{2,1,0:T(1,128)S(1)} %collective-permute-done.25) | copy-start | bytes 98308
  116.8 17.3 %copy-start.21 = (f32[1,32,1024]{2,1,0:T(8,128)}, f32[1,32,1024]{2,1,0:T(8,128)S(1)}, u32[]{:S(2)}) copy-start(f32[1,32,1024]{2,1,0:T(8,128)S(1)} %collective-permute-done.23) | copy-start | bytes 393220
  118.8 15.2 %collective-permute-start.26 = (f32[1,32,1024]{2,1,0:T(8,128)S(1)}, f32[1,32,1024]{2,1,0:T(8,128)S(1)}, u32[]{:S(2)}, u32[]{:S(2)}) collective-permute-start(f32[1,32,1024]{2,1,0:T(8,128)S(1)} %get-tuple-element.44), channel_id=1, source_target_pairs={{8,0},{16,8},{24,16},{32,24},{40,32},{48,40},{56,48},{64,56},{72,6... | collective-permute-start | bytes 393224 | tf_op jit(solution)/shard_map/ppermute | solution.py:32
  120.8 13.3 %collective-permute-start.27 = (f32[1,32,1024]{2,1,0:T(8,128)S(1)}, f32[1,32,1024]{2,1,0:T(8,128)S(1)}, u32[]{:S(2)}, u32[]{:S(2)}) collective-permute-start(f32[1,32,1024]{2,1,0:T(8,128)S(1)} %get-tuple-element.43), channel_id=1, source_target_pairs={{0,8},{8,16},{16,24},{24,32},{32,40},{40,48},{48,56},{56,64},{64,7... | collective-permute-start | bytes 393224 | tf_op jit(solution)/shard_map/ppermute | solution.py:31
  125.3 8.1 %collective-permute-start.28 = (f32[8,1,1024]{2,1,0:T(1,128)S(1)}, f32[8,1,1024]{2,1,0:T(1,128)S(1)}, u32[]{:S(2)}, u32[]{:S(2)}) collective-permute-start(f32[8,1,1024]{2,1,0:T(1,128)S(1)} %get-tuple-element.41), channel_id=1, source_target_pairs={{1,0},{2,1},{3,2},{4,3},{5,4},{6,5},{7,6},{9,8},{10,9},{11,10},{12... | collective-permute-start | bytes 98312 | tf_op jit(solution)/shard_map/ppermute | solution.py:32
  126.6 7.4 %collective-permute-start.29 = (f32[8,1,1024]{2,1,0:T(1,128)S(1)}, f32[8,1,1024]{2,1,0:T(1,128)S(1)}, u32[]{:S(2)}, u32[]{:S(2)}) collective-permute-start(f32[8,1,1024]{2,1,0:T(1,128)S(1)} %get-tuple-element.42), channel_id=1, source_target_pairs={{0,1},{1,2},{2,3},{3,4},{4,5},{5,6},{6,7},{8,9},{9,10},{10,11},{11... | collective-permute-start | bytes 98312 | tf_op jit(solution)/shard_map/ppermute | solution.py:31
  137.6 19.4 %copy-start.7 = (f32[8,32,1024]{2,1,0:T(8,128)}, f32[8,32,1024]{2,1,0:T(8,128)S(1)}, u32[]{:S(2)}) copy-start(f32[8,32,1024]{2,1,0:T(8,128)S(1)} %multiply_multiply_fusion) | copy-start | bytes 3145732
  137.7 19.2 %collective-permute-start.30 = (f32[1,32,1024]{2,1,0:T(8,128)S(1)}, f32[1,32,1024]{2,1,0:T(8,128)S(1)}, u32[]{:S(2)}, u32[]{:S(2)}) collective-permute-start(f32[1,32,1024]{2,1,0:T(8,128)S(1)} %get-tuple-element.38), channel_id=1, source_target_pairs={{8,0},{16,8},{24,16},{32,24},{40,32},{48,40},{56,48},{64,56},{72,6... | collective-permute-start | bytes 393224 | tf_op jit(solution)/shard_map/ppermute | solution.py:32
  139.6 17.3 %collective-permute-start.31 = (f32[1,32,1024]{2,1,0:T(8,128)S(1)}, f32[1,32,1024]{2,1,0:T(8,128)S(1)}, u32[]{:S(2)}, u32[]{:S(2)}) collective-permute-start(f32[1,32,1024]{2,1,0:T(8,128)S(1)} %get-tuple-element.37), channel_id=1, source_target_pairs={{0,8},{8,16},{16,24},{24,32},{32,40},{40,48},{48,56},{56,64},{64,7... | collective-permute-start | bytes 393224 | tf_op jit(solution)/shard_map/ppermute | solution.py:31
  147.4 9.4 %collective-permute-start.32 = (f32[8,1,1024]{2,1,0:T(1,128)S(1)}, f32[8,1,1024]{2,1,0:T(1,128)S(1)}, u32[]{:S(2)}, u32[]{:S(2)}) collective-permute-start(f32[8,1,1024]{2,1,0:T(1,128)S(1)} %get-tuple-element.35), channel_id=1, source_target_pairs={{1,0},{2,1},{3,2},{4,3},{5,4},{6,5},{7,6},{9,8},{10,9},{11,10},{12... | collective-permute-start | bytes 98312 | tf_op jit(solution)/shard_map/ppermute | solution.py:32
  148.7 8.1 %collective-permute-start.33 = (f32[8,1,1024]{2,1,0:T(1,128)S(1)}, f32[8,1,1024]{2,1,0:T(1,128)S(1)}, u32[]{:S(2)}, u32[]{:S(2)}) collective-permute-start(f32[8,1,1024]{2,1,0:T(1,128)S(1)} %get-tuple-element.36), channel_id=1, source_target_pairs={{0,1},{1,2},{2,3},{3,4},{4,5},{5,6},{6,7},{8,9},{9,10},{10,11},{11... | collective-permute-start | bytes 98312 | tf_op jit(solution)/shard_map/ppermute | solution.py:31
  166.0 16.8 %copy-start.17 = (f32[8,32,1024]{2,1,0:T(8,128)S(1)}, f32[8,32,1024]{2,1,0:T(8,128)}, u32[]{:S(2)}) copy-start(f32[8,32,1024]{2,1,0:T(8,128)} %copy-done.16) | copy-start | bytes 3145732
  166.0 16.8 %copy-start.19 = (f32[8,32,1024]{2,1,0:T(8,128)S(1)}, f32[8,32,1024]{2,1,0:T(8,128)}, u32[]{:S(2)}) copy-start(f32[8,32,1024]{2,1,0:T(8,128)} %get-tuple-element.5) | copy-start | bytes 3145732
  166.1 16.7 %collective-permute-start.34 = (f32[1,32,1024]{2,1,0:T(8,128)S(1)}, f32[1,32,1024]{2,1,0:T(8,128)S(1)}, u32[]{:S(2)}, u32[]{:S(2)}) collective-permute-start(f32[1,32,1024]{2,1,0:T(8,128)S(1)} %get-tuple-element.32), channel_id=1, source_target_pairs={{8,0},{16,8},{24,16},{32,24},{40,32},{48,40},{56,48},{64,56},{72,6... | collective-permute-start | bytes 393224 | tf_op jit(solution)/shard_map/ppermute | solution.py:32
  168.1 14.7 %collective-permute-start.35 = (f32[1,32,1024]{2,1,0:T(8,128)S(1)}, f32[1,32,1024]{2,1,0:T(8,128)S(1)}, u32[]{:S(2)}, u32[]{:S(2)}) collective-permute-start(f32[1,32,1024]{2,1,0:T(8,128)S(1)} %get-tuple-element.31), channel_id=1, source_target_pairs={{0,8},{8,16},{16,24},{24,32},{32,40},{40,48},{48,56},{56,64},{64,7... | collective-permute-start | bytes 393224 | tf_op jit(solution)/shard_map/ppermute | solution.py:31
  174.1 8.1 %collective-permute-start.36 = (f32[8,1,1024]{2,1,0:T(1,128)S(1)}, f32[8,1,1024]{2,1,0:T(1,128)S(1)}, u32[]{:S(2)}, u32[]{:S(2)}) collective-permute-start(f32[8,1,1024]{2,1,0:T(1,128)S(1)} %get-tuple-element.29), channel_id=1, source_target_pairs={{1,0},{2,1},{3,2},{4,3},{5,4},{6,5},{7,6},{9,8},{10,9},{11,10},{12... | collective-permute-start | bytes 98312 | tf_op jit(solution)/shard_map/ppermute | solution.py:32
  175.4 7.4 %collective-permute-start.37 = (f32[8,1,1024]{2,1,0:T(1,128)S(1)}, f32[8,1,1024]{2,1,0:T(1,128)S(1)}, u32[]{:S(2)}, u32[]{:S(2)}) collective-permute-start(f32[8,1,1024]{2,1,0:T(1,128)S(1)} %get-tuple-element.30), channel_id=1, source_target_pairs={{0,1},{1,2},{2,3},{3,4},{4,5},{5,6},{6,7},{8,9},{9,10},{10,11},{11... | collective-permute-start | bytes 98312 | tf_op jit(solution)/shard_map/ppermute | solution.py:31
  184.9 21.8 %copy-start.15 = (f32[8,32,1024]{2,1,0:T(8,128)}, f32[8,32,1024]{2,1,0:T(8,128)S(1)}, u32[]{:S(2)}) copy-start(f32[8,32,1024]{2,1,0:T(8,128)S(1)} %get-tuple-element.3) | copy-start | bytes 3145732
  185.0 19.2 %collective-permute-start.38 = (f32[1,32,1024]{2,1,0:T(8,128)S(1)}, f32[1,32,1024]{2,1,0:T(8,128)S(1)}, u32[]{:S(2)}, u32[]{:S(2)}) collective-permute-start(f32[1,32,1024]{2,1,0:T(8,128)S(1)} %get-tuple-element.26), channel_id=1, source_target_pairs={{8,0},{16,8},{24,16},{32,24},{40,32},{48,40},{56,48},{64,56},{72,6... | collective-permute-start | bytes 393224 | tf_op jit(solution)/shard_map/ppermute | solution.py:32
  186.9 17.3 %collective-permute-start.39 = (f32[1,32,1024]{2,1,0:T(8,128)S(1)}, f32[1,32,1024]{2,1,0:T(8,128)S(1)}, u32[]{:S(2)}, u32[]{:S(2)}) collective-permute-start(f32[1,32,1024]{2,1,0:T(8,128)S(1)} %get-tuple-element.25), channel_id=1, source_target_pairs={{0,8},{8,16},{16,24},{24,32},{32,40},{40,48},{48,56},{56,64},{64,7... | collective-permute-start | bytes 393224 | tf_op jit(solution)/shard_map/ppermute | solution.py:31
  195.5 8.3 %collective-permute-start.40 = (f32[8,1,1024]{2,1,0:T(1,128)S(1)}, f32[8,1,1024]{2,1,0:T(1,128)S(1)}, u32[]{:S(2)}, u32[]{:S(2)}) collective-permute-start(f32[8,1,1024]{2,1,0:T(1,128)S(1)} %get-tuple-element.23), channel_id=1, source_target_pairs={{1,0},{2,1},{3,2},{4,3},{5,4},{6,5},{7,6},{9,8},{10,9},{11,10},{12... | collective-permute-start | bytes 98312 | tf_op jit(solution)/shard_map/ppermute | solution.py:32
  196.8 7.4 %collective-permute-start.41 = (f32[8,1,1024]{2,1,0:T(1,128)S(1)}, f32[8,1,1024]{2,1,0:T(1,128)S(1)}, u32[]{:S(2)}, u32[]{:S(2)}) collective-permute-start(f32[8,1,1024]{2,1,0:T(1,128)S(1)} %get-tuple-element.24), channel_id=1, source_target_pairs={{0,1},{1,2},{2,3},{3,4},{4,5},{5,6},{6,7},{8,9},{9,10},{10,11},{11... | collective-permute-start | bytes 98312 | tf_op jit(solution)/shard_map/ppermute | solution.py:31
  206.8 18.1 %copy-start.6 = (f32[8,32,1024]{2,1,0:T(8,128)S(1)}, f32[8,32,1024]{2,1,0:T(8,128)}, u32[]{:S(2)}) copy-start(f32[8,32,1024]{2,1,0:T(8,128)} %copy-done.5) | copy-start | bytes 3145732
  206.9 17.4 %collective-permute-start.42 = (f32[1,32,1024]{2,1,0:T(8,128)S(1)}, f32[1,32,1024]{2,1,0:T(8,128)}, u32[]{:S(2)}, u32[]{:S(2)}) collective-permute-start(f32[1,32,1024]{2,1,0:T(8,128)S(1)} %get-tuple-element.22), channel_id=1, source_target_pairs={{8,0},{16,8},{24,16},{32,24},{40,32},{48,40},{56,48},{64,56},{72,6... | collective-permute-start | bytes 393224 | tf_op jit(solution)/shard_map/ppermute | solution.py:32
  209.0 15.3 %collective-permute-start.43 = (f32[1,32,1024]{2,1,0:T(8,128)S(1)}, f32[1,32,1024]{2,1,0:T(8,128)}, u32[]{:S(2)}, u32[]{:S(2)}) collective-permute-start(f32[1,32,1024]{2,1,0:T(8,128)S(1)} %get-tuple-element.21), channel_id=1, source_target_pairs={{0,8},{8,16},{16,24},{24,32},{32,40},{40,48},{48,56},{56,64},{64,7... | collective-permute-start | bytes 393224 | tf_op jit(solution)/shard_map/ppermute | solution.py:31
  214.9 9.4 %collective-permute-start.44 = (f32[8,1,1024]{2,1,0:T(1,128)S(1)}, f32[8,1,1024]{2,1,0:T(1,128)S(1)}, u32[]{:S(2)}, u32[]{:S(2)}) collective-permute-start(f32[8,1,1024]{2,1,0:T(1,128)S(1)} %get-tuple-element.19), channel_id=1, source_target_pairs={{1,0},{2,1},{3,2},{4,3},{5,4},{6,5},{7,6},{9,8},{10,9},{11,10},{12... | collective-permute-start | bytes 98312 | tf_op jit(solution)/shard_map/ppermute | solution.py:32
  216.2 8.1 %collective-permute-start.45 = (f32[8,1,1024]{2,1,0:T(1,128)S(1)}, f32[8,1,1024]{2,1,0:T(1,128)S(1)}, u32[]{:S(2)}, u32[]{:S(2)}) collective-permute-start(f32[8,1,1024]{2,1,0:T(1,128)S(1)} %get-tuple-element.20), channel_id=1, source_target_pairs={{0,1},{1,2},{2,3},{3,4},{4,5},{5,6},{6,7},{8,9},{9,10},{10,11},{11... | collective-permute-start | bytes 98312 | tf_op jit(solution)/shard_map/ppermute | solution.py:31
  240.4 66.9 %copy-start.30 = (f32[3,256,128]{2,1,0:T(8,128)S(1)}, f32[3,256,128]{2,1,0:T(8,128)}, u32[]{:S(2)}) copy-start(f32[3,256,128]{2,1,0:T(8,128)} %param.13) | copy-start | bytes 1179652
  (32 other events, 126.6 us)
where the time goes:
time: 310 us; the launch traced here: 308 us
  starting transfers between devices  161 us (52%)
  other arithmetic  60.8 us (20%)
  blocking collectives  58.3 us (19%)
  local copies, waits for them, and re-layouts  21.5 us (7%)
  waiting for transfers between devices  4.42 us (1%)
    ppermute x22, starting transfers between devices, with_halo(): lax.ppermute(last, axis, up)  117 us
    all_to_all x1, blocking collectives, sent_together(): lax.all_to_all(both, axis, split_axis=split_dim, concat_axis=concat_dim,...  58.3 us
    mul x11, other arithmetic, cycle_near(): scaled = omega_of(step_index) * inv_diag * adjoint  37 us
    ppermute x22, starting transfers between devices, with_halo(): lax.ppermute(initial, axis, [(b, a) for a, b in up])  36 us
    add x1, other arithmetic, shards(): grad_rhs = grad_rhs + increment  11.6 us
    ppermute x2, starting transfers between devices, from_behind(): return lax.ppermute(array, axis, pairs)  8.32 us
    slice x11, local copies, waits for them, and re-layouts, stencil(): scaled[:, :, 1:]  8.24 us
  transfers between devices with their start and end apart: 46, of which 8 were waited for; matrix products, arithmetic and copies ran while one was open for 4% of the time, Pallas kernels for 0%

commit v1 on v0

v1 whole, which is shorter than its diff:
```python
import functools
import math

import jax
import jax.numpy as jnp
from jax import lax
from jax.experimental import pallas as pl
from jax.experimental.pallas import tpu as pltpu
from jax.sharding import PartitionSpec as P

STEPS = 4
CAP = 8
LOW_BOUND = 0.1
HIGH_BOUND = 1.9

ROUNDS = (3, 4, 4)
K = max(ROUNDS)
C = K - 1
NX, NY = 8, 32
EX, EY = NX + 2 * K, NY + 2 * K
TILE = (8, 128)
ANY = pl.BlockSpec(memory_space=pl.ANY)
SMEM = pl.BlockSpec(memory_space=pltpu.SMEM)
VMEM = pl.BlockSpec(memory_space=pltpu.VMEM)
F32 = jnp.float32
MIB = 1 << 20


def omega_of(step):
    j = STEPS - 1 - step % STEPS
    theta = 0.5 * (HIGH_BOUND + LOW_BOUND) + 0.5 * (HIGH_BOUND - LOW_BOUND) * math.cos(
        math.pi * (2 * j + 1) / (2 * STEPS)
    )
    return 1.0 / theta


def rows_shape(*lead):
    return jax.ShapeDtypeStruct((*lead, *TILE), F32)


def z_up(v):
    r = pltpu.roll(v, 127, 2)
    lane = lax.broadcasted_iota(jnp.int32, v.shape, 2)
    return jnp.where(lane == 127, pltpu.roll(r, 7, 1), r)


def z_down(v):
    r = pltpu.roll(v, 1, 2)
    lane = lax.broadcasted_iota(jnp.int32, v.shape, 2)
    return jnp.where(lane == 0, pltpu.roll(r, 1, 1), r)


class Sides:
    def __init__(self):
        self.above = {
            (axis, ab): (lax.axis_index(axis) % 2) == (0 if ab == "a" else 1)
            for axis in ("gx", "gy")
            for ab in ("a", "b")
        }

    def send(self, axis, ab, n):
        return jnp.where(self.above[axis, ab], (NX if axis == "gx" else NY) - n, 0)

    def land(self, axis, ab, n):
        return jnp.where(self.above[axis, ab], K + (NX if axis == "gx" else NY), K - n)


class Copies:
    def __init__(self, sems):
        self.sems = sems
        self.all = []

    def start(self, src, dst):
        copy = pltpu.make_async_copy(src, dst, self.sems.at[len(self.all)])
        copy.start()
        self.all.append(copy)

    def wait(self):
        for copy in self.all:
            copy.wait()


def fields_of(k):
    return (("g", k, k), ("bx", k + 1, k), ("by", k, k + 1), ("bz", k, k))


def pack_kernel(k, g, beta, g_rows, b_rows, xa, xb, ya, yb, nat, rows, in_sems, out_sems):
    sides = Sides()
    copies = []
    for x in range(NX):
        copies.append(
            (
                pltpu.make_async_copy(g.at[x], nat.at[0, x], in_sems.at[0, x]),
                pltpu.make_async_copy(beta.at[:, x], nat.at[1:4, x], in_sems.at[1, x]),
            )
        )
        for c in copies[-1]:
            c.start()
    flat = rows.reshape(4 * NX * NY * 8, 128)
    for x in range(NX):
        for c in copies[x]:
            c.wait()

        @pl.loop(0, 4)
        def _(a, x=x):
            for yc in range(0, NY, 8):
                for s in range(8):
                    at = ((a * NX + x) * NY + yc) * 8 + s
                    flat[pl.ds(at, 8, stride=8), :] = nat[a, x, yc : yc + 8, 128 * s : 128 * s + 128]

    out = Copies(out_sems)
    for axis, ab, strip in (("gy", "a", ya), ("gy", "b", yb), ("gx", "b", xb), ("gx", "a", xa)):
        at = 0
        for i, (_, in_x, in_y) in enumerate(fields_of(k)):
            n = in_x if axis == "gx" else in_y
            first = sides.send(axis, ab, n)
            if axis == "gx":
                out.start(rows.at[i, pl.ds(first, n)], strip.at[at : at + n])
            else:
                out.start(rows.at[i, :, pl.ds(first, n)], strip.at[:, at : at + n])
            at += n
    out.start(rows.at[0], g_rows)
    out.start(rows.at[1:4], b_rows)
    out.wait()


def pack(k, g, beta):
    n = 4 * k + 1
    return pl.pallas_call(
        functools.partial(pack_kernel, k),
        out_shape=(
            rows_shape(NX, NY),
            rows_shape(3, NX, NY),
            rows_shape(n, NY),
            rows_shape(n, NY),
            rows_shape(NX, n),
            rows_shape(NX, n),
        ),
        in_specs=[ANY] * 2,
        out_specs=(ANY,) * 6,
        scratch_shapes=[
            pltpu.VMEM((4, NX, NY, 1024), F32),
            pltpu.VMEM((4, NX, NY, *TILE), F32),
            pltpu.SemaphoreType.DMA((2, NX)),
            pltpu.SemaphoreType.DMA((18,)),
        ],
        compiler_params=pltpu.CompilerParams(vmem_limit_bytes=12 * MIB),
        name="pack",
    )(g, beta)


def corner_kernel(planes, ya, yb, ca, cb, sems):
    sides = Sides()
    out = Copies(sems)
    for ab, corner in (("b", cb), ("a", ca)):
        first = sides.send("gx", ab, planes)
        out.start(ya.at[pl.ds(first, planes)], corner.at[0])
        out.start(yb.at[pl.ds(first, planes)], corner.at[1])
    out.wait()


def corners(planes, ya, yb):
    shape = rows_shape(2, planes, ya.shape[1])
    return pl.pallas_call(
        functools.partial(corner_kernel, planes),
        out_shape=(shape, shape),
        in_specs=[ANY] * 2,
        out_specs=(ANY,) * 2,
        scratch_shapes=[pltpu.SemaphoreType.DMA((4,))],
        compiler_params=pltpu.CompilerParams(vmem_limit_bytes=MIB),
        name="corners",
    )(ya, yb)


def swap(array, axis, ab):
    size = lax.axis_size(axis)
    pairs = [(i, i ^ 1 if ab == "a" else ((i + 1) ^ 1) - 1) for i in range(size)]
    return lax.ppermute(array, axis, [(i, j) for i, j in pairs if 0 <= j < size])


def exchange(planes, xa, xb, ya, yb):
    ya, yb = swap(ya, "gy", "a"), swap(yb, "gy", "b")
    xb, xa = swap(xb, "gx", "b"), swap(xa, "gx", "a")
    ca, cb = corners(planes, ya, yb)
    cb, ca = swap(cb, "gx", "b"), swap(ca, "gx", "a")
    return xa, xb, ya, yb, ca, cb


def land_first(k, sides, into, g_rows, b_rows, xs, ys, cs, fields):
    for i, field in enumerate(fields):
        src = g_rows if i == 0 else b_rows.at[i - 1]
        into.start(src, field.at[K : K + NX, K : K + NY])
    at_x = at_y = 0
    for i, (_, in_x, in_y) in enumerate(fields_of(k)):
        for ab in ("a", "b"):
            x, y = sides.land("gx", ab, in_x), sides.land("gy", ab, in_y)
            into.start(xs[ab].at[at_x : at_x + in_x], fields[i].at[pl.ds(x, in_x), K : K + NY])
            into.start(ys[ab].at[:, at_y : at_y + in_y], fields[i].at[K : K + NX, pl.ds(y, in_y)])
            x = sides.land("gx", ab, k)
            for j, other in enumerate(("a", "b")):
                y = sides.land("gy", other, in_y)
                into.start(
                    cs[ab].at[j, :, at_y : at_y + in_y],
                    fields[i].at[pl.ds(x, k), pl.ds(y, in_y)],
                )
        at_x, at_y = at_x + in_x, at_y + in_y


def land_later(k, sides, into, w_rows, xs, ys, cs, w):
    into.start(w_rows, w.at[K : K + NX, K : K + NY])
    for ab in ("a", "b"):
        x, y = sides.land("gx", ab, k), sides.land("gy", ab, k)
        into.start(xs[ab], w.at[pl.ds(x, k), K : K + NY])
        into.start(ys[ab], w.at[K : K + NX, pl.ds(y, k)])
        x = sides.land("gx", ab, k - 1)
        for j, other in enumerate(("a", "b")):
            y = sides.land("gy", other, k)
            into.start(cs[ab].at[j], w.at[pl.ds(x, k - 1), pl.ds(y, k)])


def chunks(low, high, size=8):
    return [(y, min(size, high - y)) for y in range(low, high, size)]


def scale(w, bx, by, bz, inv):
    @pl.loop(K - C, K + NX + C)
    def _(x):
        for y, n in chunks(K - C, K + NY + C):
            b = bz[x, y : y + n]
            sub = lax.broadcasted_iota(jnp.int32, b.shape, 1)
            lane = lax.broadcasted_iota(jnp.int32, b.shape, 2)
            inner = jnp.where((sub == 7) & (lane == 127), 0.0, b)
            beside = by[x, y - 1 : y + n]
            diagonal = bx[x, y : y + n] + bx[x - 1, y : y + n] + beside[1:] + beside[:-1] + b + z_down(inner)
            inverse = jnp.where(b > 0.0, 1.0 / jnp.where(b > 0.0, diagonal, 1.0), 0.0)
            inv[x, y : y + n] = inverse
            w[x, y : y + n] = w[x, y : y + n] * inverse
            bz[x, y : y + n] = inner


def one_step(step, reach, last, w, new, bx, by, bz, inv, acc):
    omega = omega_of(step)

    def run(x, y, n, inside):
        around = w[x, y - 1 : y + n + 1]
        centre = around[1:-1]
        beside = by[x, y - 1 : y + n]
        along = bz[x, y : y + n]
        total = bx[x, y : y + n] * w[x + 1, y : y + n] + bx[x - 1, y : y + n] * w[x - 1, y : y + n]
        total = total + beside[1:] * around[2:] + beside[:-1] * around[:-2]
        total = total + along * z_up(centre) + z_down(along * centre)
        moved = centre + omega * (inv[x, y : y + n] * total - centre)
        if not last:
            new[x, y : y + n] = moved
        if inside:
            at = (x - K, slice(y - K, y - K + n))
            term = omega * centre
            if last:
                term = term + omega_of(step + 1) * moved
            acc[at] = term if step == 0 else acc[at] + term

    if reach:

        @pl.loop(0, 2 * reach)
        def _(i):
            x = jnp.where(i < reach, K - reach + i, K + NX - reach + i)
            for y, n in chunks(K - reach, K + NY + reach):
                run(x, y, n, False)

    @pl.loop(K, K + NX)
    def _(x):
        if reach:
            run(x, K - reach, reach, False)
            run(x, K + NY, reach, False)
        for y, n in chunks(K, K + NY):
            run(x, y, n, True)


def steps_of(first, k, last, w, bx, by, bz, inv, acc):
    for i in range(k):
        end = last and i == k - 1
        one_step(first + i, k - 1 - i, end, w[i % 2], w[1 - i % 2], bx, by, bz, inv, acc)
    return w[k % 2]


def leave(k, sides, out, w, w_rows, xa, xb, ya, yb):
    for axis, ab, strip in (("gy", "a", ya), ("gy", "b", yb), ("gx", "b", xb), ("gx", "a", xa)):
        first = sides.send(axis, ab, k) + K
        if axis == "gx":
            out.start(w.at[pl.ds(first, k), K : K + NY], strip)
        else:
            out.start(w.at[K : K + NX, pl.ds(first, k)], strip)
    out.start(w.at[K : K + NX, K : K + NY], w_rows)


def first_kernel(
    k, k_next,
    g_rows, b_rows, xa, xb, ya, yb, ca, cb,
    bx_out, by_out, bz_out, inv_out, acc_out, w_out, xa_out, xb_out, ya_out, yb_out,
    w0, w1, bx, by, bz, inv, acc, in_sems, out_sems,
):
    sides = Sides()
    into = Copies(in_sems)
    land_first(k, sides, into, g_rows, b_rows, {"a": xa, "b": xb}, {"a": ya, "b": yb}, {"a": ca, "b": cb}, (w0, bx, by, bz))
    into.wait()
    scale(w0, bx, by, bz, inv)
    out = Copies(out_sems)
    for src, dst in ((bx, bx_out), (by, by_out), (bz, bz_out), (inv, inv_out)):
        out.start(src, dst)
    w = steps_of(0, k, False, (w0, w1), bx, by, bz, inv, acc)
    leave(k_next, sides, out, w, w_out, xa_out, xb_out, ya_out, yb_out)
    out.start(acc, acc_out)
    out.wait()


EXT = pltpu.VMEM((EX, EY, *TILE), F32)
ACC = pltpu.VMEM((NX, NY, *TILE), F32)


def first_round(k, k_next, *arrays):
    ext, core = rows_shape(EX, EY), rows_shape(NX, NY)
    x, y = rows_shape(k_next, NY), rows_shape(NX, k_next)
    return pl.pallas_call(
        functools.partial(first_kernel, k, k_next),
        out_shape=(ext,) * 4 + (core, core, x, x, y, y),
        in_specs=[ANY] * 8,
        out_specs=(ANY,) * 10,
        scratch_shapes=[EXT] * 6 + [ACC, pltpu.SemaphoreType.DMA((36,)), pltpu.SemaphoreType.DMA((10,))],
        compiler_params=pltpu.CompilerParams(vmem_limit_bytes=22 * MIB),
        name="first_round",
    )(*arrays)


def later_kernel(
    first, k, k_next,
    bx_in, by_in, bz_in, inv_in, acc_in, w_in, xa, xb, ya, yb, ca, cb,
    acc_out, w_out, xa_out, xb_out, ya_out, yb_out,
    w0, w1, bx, by, bz, inv, acc, in_sems, out_sems,
):
    sides = Sides()
    into = Copies(in_sems)
    for src, dst in ((bx_in, bx), (by_in, by), (bz_in, bz), (inv_in, inv), (acc_in, acc)):
        into.start(src, dst)
    land_later(k, sides, into, w_in, {"a": xa, "b": xb}, {"a": ya, "b": yb}, {"a": ca, "b": cb}, w0)
    into.wait()
    w = steps_of(first, k, False, (w0, w1), bx, by, bz, inv, acc)
    out = Copies(out_sems)
    leave(k_next, sides, out, w, w_out, xa_out, xb_out, ya_out, yb_out)
    out.start(acc, acc_out)
    out.wait()


def later_round(first, k, k_next, *arrays):
    core = rows_shape(NX, NY)
    x, y = rows_shape(k_next, NY), rows_shape(NX, k_next)
    return pl.pallas_call(
        functools.partial(later_kernel, first, k, k_next),
        out_shape=(core, core, x, x, y, y),
        in_specs=[ANY] * 12,
        out_specs=(ANY,) * 6,
        scratch_shapes=[EXT] * 6 + [ACC, pltpu.SemaphoreType.DMA((14,)), pltpu.SemaphoreType.DMA((6,))],
        compiler_params=pltpu.CompilerParams(vmem_limit_bytes=22 * MIB),
        name="later_round",
    )(*arrays)


def last_kernel(
    first, k,
    tile_rows, targets, mask, slots,
    bx_in, by_in, bz_in, inv_in, acc_in, w_in, xa, xb, ya, yb, ca, cb,
    grad, sent,
    w0, w1, bx, by, bz, inv, acc, in_sems,
):
    sides = Sides()
    into = Copies(in_sems)
    for src, dst in ((bx_in, bx), (by_in, by), (bz_in, bz), (inv_in, inv), (acc_in, acc)):
        into.start(src, dst)
    land_later(k, sides, into, w_in, {"a": xa, "b": xb}, {"a": ya, "b": yb}, {"a": ca, "b": cb}, w0)
    sent[...] = jnp.zeros_like(sent)
    peers = slots.shape[0]
    sent[pl.ds(CAP, peers, stride=CAP + 1), :] = slots[...]
    into.wait()
    steps_of(first, k, True, (w0, w1), bx, by, bz, inv, acc)
    flat = acc.reshape(NX * NY * 8, 128)

    @pl.loop(0, mask.shape[0] // 8)
    def _(t8):
        for t in range(8):
            at = t8 * 8 + t
            row = flat[pl.ds(tile_rows[at], 1), :] * mask[pl.ds(at, 1), :].astype(F32)
            sent[pl.ds(targets[at], 1), :] = row

    @pl.loop(0, NX)
    def _(x):
        for yc in range(0, NY, 8):
            for s in range(8):
                at = (x * NY + yc) * 8 + s
                grad[x, yc : yc + 8, 128 * s : 128 * s + 128] = flat[pl.ds(at, 8, stride=8), :]


def last_round(first, k, peers, *arrays):
    return pl.pallas_call(
        functools.partial(last_kernel, first, k),
        out_shape=(
            jax.ShapeDtypeStruct((NX, NY, 1024), F32),
            jax.ShapeDtypeStruct((peers * (CAP + 1), 128), F32),
        ),
        in_specs=[SMEM, SMEM, VMEM, VMEM] + [ANY] * 12,
        out_specs=(VMEM, VMEM),
        scratch_shapes=[EXT] * 6 + [ACC, pltpu.SemaphoreType.DMA((14,))],
        compiler_params=pltpu.CompilerParams(vmem_limit_bytes=26 * MIB),
        name="last_round",
    )(*arrays)


def finish_kernel(received, heights, out):
    peers = received.shape[0] // (CAP + 1)
    slots = received[pl.ds(CAP, peers, stride=CAP + 1), :].T
    n_slots = heights.shape[1]
    ids = lax.broadcasted_iota(jnp.int32, (n_slots, peers), 0).astype(F32)
    table = jnp.zeros((n_slots, 128), F32)
    for p in range(CAP):
        named = (ids == slots[p : p + 1, :]).astype(jnp.bfloat16)
        rest = received[pl.ds(p, peers, stride=CAP + 1), :]
        for _ in range(3):
            part = rest.astype(jnp.bfloat16)
            rest = rest - part.astype(F32)
            table = table + jnp.dot(named, part, preferred_element_type=F32)
    slope = 0.5 * (heights[2] - heights[0])
    bend = heights[2] - 2.0 * heights[1] + heights[0]
    denom = 1.0 + slope * slope
    factor = 1.0 / (denom * jnp.sqrt(denom))
    skew_half = -1.5 * slope * bend * factor / denom
    out[0] = table * (factor - skew_half)
    out[1] = -2.0 * table * factor
    out[2] = table * (factor + skew_half)


def finish(received, heights):
    return pl.pallas_call(
        finish_kernel,
        out_shape=jax.ShapeDtypeStruct(heights.shape, F32),
        in_specs=[VMEM, VMEM],
        out_specs=VMEM,
        compiler_params=pltpu.CompilerParams(vmem_limit_bytes=8 * MIB),
        name="finish",
    )(received, heights)


def routes(tile_owner, tile_slot, peers):
    owner = tile_owner[:, 0]
    order = jnp.arange(owner.shape[0])
    before = (owner[:, None] == owner[None, :]) & (order[None, :] < order[:, None])
    position = jnp.sum(before.astype(jnp.int32), axis=1)
    is_owner = (owner[None, :] == jnp.arange(peers)[:, None]).astype(F32)
    placed = jnp.where(position[:, None] == jnp.arange(128)[None, :], tile_slot[:, None].astype(F32), 0.0)
    slots = jnp.dot(is_owner, placed, precision=lax.Precision.HIGHEST)
    return owner * (CAP + 1) + position, slots


def shards(grad_pressure, beta, tile_rows, tile_owner, tile_slot, face_mask, heights):
    peers = lax.axis_size("gx") * lax.axis_size("gy")
    targets, slots = routes(tile_owner, tile_slot, peers)
    k = ROUNDS[0]
    g_rows, b_rows, *strips = pack(k, grad_pressure, beta)
    out = first_round(k, ROUNDS[1], g_rows, b_rows, *exchange(k, *strips))
    coeffs, state, strips = out[:4], out[4:6], out[6:]
    done = k
    for k, k_next in zip(ROUNDS[1:-1], ROUNDS[2:]):
        out = later_round(done, k, k_next, *coeffs, *state, *exchange(k - 1, *strips))
        state, strips = out[:2], out[2:]
        done += k
    k = ROUNDS[-1]
    grad_rhs, sent = last_round(
        done, k, peers, tile_rows, targets, face_mask, slots, *coeffs, *state, *exchange(k - 1, *strips)
    )
    sent = sent.reshape(peers, 1, (CAP + 1) * 128)
    received = lax.all_to_all(sent, ("gx", "gy"), split_axis=0, concat_axis=0, tiled=True)
    return grad_rhs, finish(received.reshape(peers * (CAP + 1), 128), heights)


def solution(mesh):
    in_specs = (
        P("gx", "gy", None),
        P(None, "gx", "gy", None),
        P(("gx", "gy")),
        P(("gx", "gy"), None),
        P(("gx", "gy")),
        P(("gx", "gy"), None),
        P(None, ("gx", "gy"), None),
    )
    out_specs = (P("gx", "gy", None), P(None, ("gx", "gy"), None))
    return jax.shard_map(shards, mesh=mesh, in_specs=in_specs, out_specs=out_specs, check_vma=False)
```

time: 310 us -> 144 us (0.46)
  starting transfers between devices: 161 us -> 47.9 us
  other arithmetic: 60.8 us -> 0.19 us
  Pallas kernels: 0 us -> 34.7 us
  blocking collectives: 58.3 us -> 34.4 us
  local copies, waits for them, and re-layouts: 21.5 us -> 3.13 us
  waiting for transfers between devices: 4.42 us -> 22.3 us
    ppermute x46 -> x18, starting transfers between devices: 161 us -> 47.9 us  [swap(): lax.ppermute(array, axis, [(i, j) for i, j in pairs if 0 <= j < size])]
    mul x11 -> x0, other arithmetic: 37 us -> none  [cycle_near(): scaled = omega_of(step_index) * inv_diag * adjoint]
    pallas_call x0 -> x8, Pallas kernels: none -> 34.7 us  [the longest x1 10.2 us: last_round(): pl.pallas_call(functools.partial(last_kernel, first, k), out_shape=(jax.S...]
    all_to_all x1, blocking collectives: 58.3 us -> 34.4 us  [shards(): lax.all_to_all(sent, ('gx', 'gy'), split_axis=0, concat_axis=0, tiled=True)]
    ppermute x46 -> x18, waiting for transfers between devices: 4.42 us -> 22.3 us  [swap(): lax.ppermute(array, axis, [(i, j) for i, j in pairs if 0 <= j < size])]
    add x1, other arithmetic: 11.6 us -> 0.01 us  [routes(): return (owner * (CAP + 1) + position, slots)]
    slice x36 -> x0, local copies, waits for them, and re-layouts: 10.7 us -> none  [the longest x11 8.24 us: stencil(): scaled[:, :, 1:]]
    scatter-add x1 -> x0, other arithmetic: 6.1 us -> none  [add_jumps(): return slot_table.at[slot_ids].add(recv_rows.reshape(-1, 128))]
  transfers between devices with their start and end apart: 46 -> 18, of which waited for: 8 -> 6; matrix products, arithmetic and copies ran while one was open for 4% -> 0% of each run, Pallas kernels for 0% -> 1%
where the time goes in v1:
time: 144 us
  starting transfers between devices  47.9 us (33%)
  Pallas kernels  34.7 us (24%)
  blocking collectives  34.4 us (24%)
  waiting for transfers between devices  22.3 us (15%)
  local copies, waits for them, and re-layouts  3.13 us (2%)
    ppermute x18, starting transfers between devices, swap(): lax.ppermute(array, axis, [(i, j) for i, j in pairs if 0 <= j < size])  47.9 us
    all_to_all x1, blocking collectives, shards(): lax.all_to_all(sent, ('gx', 'gy'), split_axis=0, concat_axis=0, tiled=True)  34.4 us
    ppermute x18, waiting for transfers between devices, swap(): lax.ppermute(array, axis, [(i, j) for i, j in pairs if 0 <= j < size])  22.3 us
    pallas_call x1, Pallas kernels, last_round(): pl.pallas_call(functools.partial(last_kernel, first, k), out_shape=(jax.S...  10.2 us
    pallas_call x1, Pallas kernels, first_round(): pl.pallas_call(functools.partial(first_kernel, k, k_next), out_shape=(ext...  8.88 us
    pallas_call x1, Pallas kernels, later_round(): pl.pallas_call(functools.partial(later_kernel, first, k, k_next), out_sha...  8.22 us
    pallas_call x1, Pallas kernels, pack(): pl.pallas_call(functools.partial(pack_kernel, k), out_shape=(rows_shape(N...  4.55 us
    unnamed x14, local copies, waits for them, and re-layouts  3.13 us
  transfers between devices with their start and end apart: 18, of which 6 were waited for; matrix products, arithmetic and copies ran while one was open for 0% of the time, Pallas kernels for 1%

profile of v1, /device:TPU:1, one launch (start us, length us, event | category | flops | bytes accessed | tf_op | source)
XLA Modules:
  0.0 143.9 jit_solution(16701901042819468760)
XLA Ops:
  0.6 0.0 copy-start
  0.6 1.9 %copy-done = f32[3,8,32,1024]{3,2,1,0:T(8,128)S(1)} copy-done((f32[3,8,32,1024]{3,2,1,0:T(8,128)S(1)}, f32[3,8,32,1024]{3,2,1,0:T(8,128)}, u32[]{:S(2)}) %copy-start) | copy-done | bytes 3145752
  2.5 0.0 copy-start.1
  2.5 1.2 copy-done.1
  3.7 4.5 %pack.1 = (f32[8,32,8,128]{3,2,1,0:T(8,128)S(1)}, f32[3,8,32,8,128]{4,3,2,1,0:T(8,128)S(1)}, f32[13,32,8,128]{3,2,1,0:T(8,128)S(1)}, f32[13,32,8,128]{3,2,1,0:T(...) custom-call(f32[8,32,1024]{2,1,0:T(8,128)S(1)} %copy-done.1, f32[3,8,32,1024]{3,2,1,0:T(8,128)S(1)} %copy-done), custom_call_target="tpu_custom_call" | custom-call | tf_op jit(solution)/shard_map/pack/pallas_call | solution.py:129
  8.3 1.5 %collective-permute-start = (f32[13,32,8,128]{3,2,1,0:T(8,128)S(1)}, f32[13,32,8,128]{3,2,1,0:T(8,128)S(1)}, u32[]{:S(2)}, u32[]{:S(2)}) collective-permute-start(f32[13,32,8,128]{3,2,1,0:T(8,128)S(1)} %get-tuple-element.34), channel_id=1, source_target_pairs={{0,8},{8,0},{16,24},{24,16},{32,40},{40,32},{48,56},{56,48},{64,72... | collective-permute-start | bytes 5111816 | tf_op jit(solution)/shard_map/ppermute | solution.py:178
  9.8 3.5 %collective-permute-start.1 = (f32[13,32,8,128]{3,2,1,0:T(8,128)S(1)}, f32[13,32,8,128]{3,2,1,0:T(8,128)S(1)}, u32[]{:S(2)}, u32[]{:S(2)}) collective-permute-start(f32[13,32,8,128]{3,2,1,0:T(8,128)S(1)} %get-tuple-element.35), channel_id=1, source_target_pairs={{8,16},{16,8},{24,32},{32,24},{40,48},{48,40},{56,64},{64,56},{72,... | collective-permute-start | bytes 5111816 | tf_op jit(solution)/shard_map/ppermute | solution.py:178
  13.3 1.3 collective-permute-start.2
  14.6 0.7 collective-permute-start.3
  15.3 7.4 %collective-permute-done.2.ya = f32[8,13,8,128]{3,2,1,0:T(8,128)S(1)} collective-permute-done((f32[8,13,8,128]{3,2,1,0:T(8,128)S(1)}, f32[8,13,8,128]{3,2,1,0:T(8,128)S(1)}, u32[]{:S(2)}, u32[]{:S(2)}) %collective-permute-start.2) | collective-permute-done | bytes 426016 | tf_op jit(solution)/shard_map/ppermute | solution.py:178
  22.7 0.0 collective-permute-done.3.yb
  22.7 0.8 corners.3
  23.5 0.1 collective-permute-start.4
  23.6 5.5 %collective-permute-start.5 = (f32[2,3,13,8,128]{4,3,2,1,0:T(8,128)S(1)}, f32[2,3,13,8,128]{4,3,2,1,0:T(8,128)S(1)}, u32[]{:S(2)}, u32[]{:S(2)}) collective-permute-start(f32[2,3,13,8,128]{4,3,2,1,0:T(8,128)S(1)} %get-tuple-element.39), channel_id=1, source_target_pairs={{8,16},{16,8},{24,32},{32,24},{40,48},{48,40},{56,64},{64,56},{72,... | collective-permute-start | bytes 958472 | tf_op jit(solution)/shard_map/ppermute | solution.py:178
  29.2 0.0 collective-permute-done.4.ca
  29.2 7.2 %collective-permute-done.5.cb = f32[2,3,13,8,128]{4,3,2,1,0:T(8,128)S(1)} collective-permute-done((f32[2,3,13,8,128]{4,3,2,1,0:T(8,128)S(1)}, f32[2,3,13,8,128]{4,3,2,1,0:T(8,128)S(1)}, u32[]{:S(2)}, u32[]{:S(2)}) %collective-permute-start.5) | collective-permute-done | bytes 319520 | tf_op jit(solution)/shard_map/ppermute | solution.py:178
  36.4 0.0 collective-permute-done.xa
  36.4 0.0 collective-permute-done.1.xb
  36.4 0.0 copy-start.6
  36.4 8.9 %first_round.1 = (f32[16,40,8,128]{3,2,1,0:T(8,128)S(1)}, f32[16,40,8,128]{3,2,1,0:T(8,128)S(1)}, f32[16,40,8,128]{3,2,1,0:T(8,128)S(1)}, f32[16,40,8,128]{3,2,1...) custom-call(f32[8,32,8,128]{3,2,1,0:T(8,128)S(1)} %get-tuple-element, ...), custom_call_target="tpu_custom_call" | custom-call | tf_op jit(solution)/shard_map/first_round/pallas_call | solution.py:323
  45.3 0.1 collective-permute-start.6
  45.4 4.0 %collective-permute-start.7 = (f32[4,32,8,128]{3,2,1,0:T(8,128)S(1)}, f32[4,32,8,128]{3,2,1,0:T(8,128)S(1)}, u32[]{:S(2)}, u32[]{:S(2)}) collective-permute-start(f32[4,32,8,128]{3,2,1,0:T(8,128)S(1)} %get-tuple-element.47), channel_id=1, source_target_pairs={{8,16},{16,8},{24,32},{32,24},{40,48},{48,40},{56,64},{64,56},{72,... | collective-permute-start | bytes 1572872 | tf_op jit(solution)/shard_map/ppermute | solution.py:178
  49.4 1.3 collective-permute-start.8
  50.7 0.7 collective-permute-start.9
  51.3 1.9 %collective-permute-done.8.ya = f32[8,4,8,128]{3,2,1,0:T(8,128)S(1)} collective-permute-done((f32[8,4,8,128]{3,2,1,0:T(8,128)S(1)}, f32[8,4,8,128]{3,2,1,0:T(8,128)S(1)}, u32[]{:S(2)}, u32[]{:S(2)}) %collective-permute-start.8) | collective-permute-done | bytes 131104 | tf_op jit(solution)/shard_map/ppermute | solution.py:178
  53.3 0.0 collective-permute-done.9.yb
  53.3 0.3 corners.4
  53.5 0.1 collective-permute-start.10
  53.6 4.6 %collective-permute-start.11 = (f32[2,3,4,8,128]{4,3,2,1,0:T(8,128)S(1)}, f32[2,3,4,8,128]{4,3,2,1,0:T(8,128)S(1)}, u32[]{:S(2)}, u32[]{:S(2)}) collective-permute-start(f32[2,3,4,8,128]{4,3,2,1,0:T(8,128)S(1)} %get-tuple-element.51), channel_id=1, source_target_pairs={{8,16},{16,8},{24,32},{32,24},{40,48},{48,40},{56,64},{64,56},{72,... | collective-permute-start | bytes 294920 | tf_op jit(solution)/shard_map/ppermute | solution.py:178
  58.2 0.0 copy-done.6
  58.2 0.0 collective-permute-done.10.ca
  58.2 2.3 %collective-permute-done.11.cb = f32[2,3,4,8,128]{4,3,2,1,0:T(8,128)S(1)} collective-permute-done((f32[2,3,4,8,128]{4,3,2,1,0:T(8,128)S(1)}, f32[2,3,4,8,128]{4,3,2,1,0:T(8,128)S(1)}, u32[]{:S(2)}, u32[]{:S(2)}) %collective-permute-start.11) | collective-permute-done | bytes 98336 | tf_op jit(solution)/shard_map/ppermute | solution.py:178
  60.5 0.0 collective-permute-done.6.xa
  60.5 0.0 collective-permute-done.7.xb
  60.5 0.0 copy-start.5
  60.5 0.0 copy-start.3
  60.5 0.0 copy-start.4
  60.5 8.2 %later_round.1 = (f32[8,32,8,128]{3,2,1,0:T(8,128)S(1)}, f32[8,32,8,128]{3,2,1,0:T(8,128)S(1)}, f32[4,32,8,128]{3,2,1,0:T(8,128)S(1)}, f32[4,32,8,128]{3,2,1,0:T...) custom-call(f32[16,40,8,128]{3,2,1,0:T(8,128)S(1)} %get-tuple-element.40.bx_in, ...), custom_call_target="tpu_custom_call" | custom-call | tf_op jit(solution)/shard_map/later_round/pallas_call | solution.py:356
  68.8 0.1 collective-permute-start.12
  68.9 15.7 %collective-permute-start.13 = (f32[4,32,8,128]{3,2,1,0:T(8,128)S(1)}, f32[4,32,8,128]{3,2,1,0:T(8,128)S(1)}, u32[]{:S(2)}, u32[]{:S(2)}) collective-permute-start(f32[4,32,8,128]{3,2,1,0:T(8,128)S(1)} %get-tuple-element.55), channel_id=1, source_target_pairs={{8,16},{16,8},{24,32},{32,24},{40,48},{48,40},{56,64},{64,56},{72,... | collective-permute-start | bytes 1572872 | tf_op jit(solution)/shard_map/ppermute | solution.py:178
  84.6 0.0 copy-done.5
  84.6 0.2 convert_reduce_fusion
  84.8 3.4 %collective-permute-start.14 = (f32[8,4,8,128]{3,2,1,0:T(8,128)S(1)}, f32[8,4,8,128]{3,2,1,0:T(8,128)S(1)}, u32[]{:S(2)}, u32[]{:S(2)}) collective-permute-start(f32[8,4,8,128]{3,2,1,0:T(8,128)S(1)} %get-tuple-element.56), channel_id=1, source_target_pairs={{0,1},{1,0},{2,3},{3,2},{4,5},{5,4},{6,7},{7,6},{8,9},{9,8},{10,11... | collective-permute-start | bytes 393224 | tf_op jit(solution)/shard_map/ppermute | solution.py:178
  88.2 0.7 collective-permute-start.15
  88.8 0.3 fusion.1.slots
  89.2 1.4 collective-permute-done.14.ya
  90.5 0.0 collective-permute-done.15.yb
  90.5 0.3 corners.5
  90.8 0.1 collective-permute-start.16
  90.9 4.6 %collective-permute-start.17 = (f32[2,3,4,8,128]{4,3,2,1,0:T(8,128)S(1)}, f32[2,3,4,8,128]{4,3,2,1,0:T(8,128)S(1)}, u32[]{:S(2)}, u32[]{:S(2)}) collective-permute-start(f32[2,3,4,8,128]{4,3,2,1,0:T(8,128)S(1)} %get-tuple-element.59), channel_id=1, source_target_pairs={{8,16},{16,8},{24,32},{32,24},{40,48},{48,40},{56,64},{64,56},{72,... | collective-permute-start | bytes 294920 | tf_op jit(solution)/shard_map/ppermute | solution.py:178
  95.6 0.0 collective-permute-done.16.ca
  95.6 2.3 %collective-permute-done.17.cb = f32[2,3,4,8,128]{4,3,2,1,0:T(8,128)S(1)} collective-permute-done((f32[2,3,4,8,128]{4,3,2,1,0:T(8,128)S(1)}, f32[2,3,4,8,128]{4,3,2,1,0:T(8,128)S(1)}, u32[]{:S(2)}, u32[]{:S(2)}) %collective-permute-start.17) | collective-permute-done | bytes 98336 | tf_op jit(solution)/shard_map/ppermute | solution.py:178
  97.8 0.0 collective-permute-done.12.xa
  97.8 0.0 collective-permute-done.13.xb
  97.8 0.0 copy-done.3
  97.9 0.0 copy-done.4
  97.9 0.0 copy-start.2
  97.9 10.2 %last_round.1 = (f32[8,32,1024]{2,1,0:T(8,128)}, f32[1152,128]{1,0:T(8,128)S(1)}) custom-call(s32[256]{0:T(256)S(1)} %copy-done.4, s32[256]{0:T(256)S(1)} %multiply_add_fusion.targets, s32[256,128]{1,0:T(8,128)S(1)} %copy-done.3, f32[128,128]{1,0:T(8,128)S(1)} %fusion.1.slots, f32[16,40,8,128]{3,2,1,0:T(8,128)S(1)} %get-tuple-element.40.bx_in, ...), custom_call_target="tpu_custom_call" | custom-call | tf_op jit(solution)/shard_map/last_round/pallas_call | solution.py:402
  108.1 34.4 %all_to_all.5 = f32[128,1,1152]{2,1,0:T(1,128)S(1)} all-to-all(f32[128,1,1152]{2,1,0:T(1,128)S(1)} %bitcast.4), channel_id=1, replica_groups=mesh['gx'=16,'gy'=8] {'gx','gy'}, dimensions={0} | all-to-all | bytes 1179648 | tf_op jit(solution)/shard_map/all_to_all | solution.py:478
  142.5 0.0 copy-done.2
  142.5 1.4 finish.1
  (2 shorter events, 0.0 us)
Async XLA Ops:
  0.6 1.9 %copy-start = (f32[3,8,32,1024]{3,2,1,0:T(8,128)S(1)}, f32[3,8,32,1024]{3,2,1,0:T(8,128)}, u32[]{:S(2)}) copy-start(f32[3,8,32,1024]{3,2,1,0:T(8,128)} %beta.1) | copy-start | bytes 9437188
  2.5 1.2 copy-start.1
  8.3 28.1 %collective-permute-start = (f32[13,32,8,128]{3,2,1,0:T(8,128)S(1)}, f32[13,32,8,128]{3,2,1,0:T(8,128)S(1)}, u32[]{:S(2)}, u32[]{:S(2)}) collective-permute-start(f32[13,32,8,128]{3,2,1,0:T(8,128)S(1)} %get-tuple-element.34), channel_id=1, source_target_pairs={{0,8},{8,0},{16,24},{24,16},{32,40},{40,32},{48,56},{56,48},{64,72... | collective-permute-start | bytes 5111816 | tf_op jit(solution)/shard_map/ppermute | solution.py:178
  9.8 26.6 %collective-permute-start.1 = (f32[13,32,8,128]{3,2,1,0:T(8,128)S(1)}, f32[13,32,8,128]{3,2,1,0:T(8,128)S(1)}, u32[]{:S(2)}, u32[]{:S(2)}) collective-permute-start(f32[13,32,8,128]{3,2,1,0:T(8,128)S(1)} %get-tuple-element.35), channel_id=1, source_target_pairs={{8,16},{16,8},{24,32},{32,24},{40,48},{48,40},{56,64},{64,56},{72,... | collective-permute-start | bytes 5111816 | tf_op jit(solution)/shard_map/ppermute | solution.py:178
  13.3 9.3 %collective-permute-start.2 = (f32[8,13,8,128]{3,2,1,0:T(8,128)S(1)}, f32[8,13,8,128]{3,2,1,0:T(8,128)S(1)}, u32[]{:S(2)}, u32[]{:S(2)}) collective-permute-start(f32[8,13,8,128]{3,2,1,0:T(8,128)S(1)} %get-tuple-element.36), channel_id=1, source_target_pairs={{0,1},{1,0},{2,3},{3,2},{4,5},{5,4},{6,7},{7,6},{8,9},{9,8},{10,11... | collective-permute-start | bytes 1277960 | tf_op jit(solution)/shard_map/ppermute | solution.py:178
  14.6 8.1 %collective-permute-start.3 = (f32[8,13,8,128]{3,2,1,0:T(8,128)S(1)}, f32[8,13,8,128]{3,2,1,0:T(8,128)S(1)}, u32[]{:S(2)}, u32[]{:S(2)}) collective-permute-start(f32[8,13,8,128]{3,2,1,0:T(8,128)S(1)} %get-tuple-element.37), channel_id=1, source_target_pairs={{1,2},{2,1},{3,4},{4,3},{5,6},{6,5},{9,10},{10,9},{11,12},{12,11},... | collective-permute-start | bytes 1277960 | tf_op jit(solution)/shard_map/ppermute | solution.py:178
  23.5 5.7 %collective-permute-start.4 = (f32[2,3,13,8,128]{4,3,2,1,0:T(8,128)S(1)}, f32[2,3,13,8,128]{4,3,2,1,0:T(8,128)S(1)}, u32[]{:S(2)}, u32[]{:S(2)}) collective-permute-start(f32[2,3,13,8,128]{4,3,2,1,0:T(8,128)S(1)} %get-tuple-element.38), channel_id=1, source_target_pairs={{0,8},{8,0},{16,24},{24,16},{32,40},{40,32},{48,56},{56,48},{64,72... | collective-permute-start | bytes 958472 | tf_op jit(solution)/shard_map/ppermute | solution.py:178
  23.6 12.7 %collective-permute-start.5 = (f32[2,3,13,8,128]{4,3,2,1,0:T(8,128)S(1)}, f32[2,3,13,8,128]{4,3,2,1,0:T(8,128)S(1)}, u32[]{:S(2)}, u32[]{:S(2)}) collective-permute-start(f32[2,3,13,8,128]{4,3,2,1,0:T(8,128)S(1)} %get-tuple-element.39), channel_id=1, source_target_pairs={{8,16},{16,8},{24,32},{32,24},{40,48},{48,40},{56,64},{64,56},{72,... | collective-permute-start | bytes 958472 | tf_op jit(solution)/shard_map/ppermute | solution.py:178
  36.4 21.9 %copy-start.6 = (s32[256]{0:T(256)S(1)}, s32[256]{0:T(256)}, u32[]{:S(2)}) copy-start(s32[256]{0:T(256)} %param.11) | copy-start | bytes 3076
  45.3 15.2 %collective-permute-start.6 = (f32[4,32,8,128]{3,2,1,0:T(8,128)S(1)}, f32[4,32,8,128]{3,2,1,0:T(8,128)S(1)}, u32[]{:S(2)}, u32[]{:S(2)}) collective-permute-start(f32[4,32,8,128]{3,2,1,0:T(8,128)S(1)} %get-tuple-element.46), channel_id=1, source_target_pairs={{0,8},{8,0},{16,24},{24,16},{32,40},{40,32},{48,56},{56,48},{64,72... | collective-permute-start | bytes 1572872 | tf_op jit(solution)/shard_map/ppermute | solution.py:178
  45.4 15.2 %collective-permute-start.7 = (f32[4,32,8,128]{3,2,1,0:T(8,128)S(1)}, f32[4,32,8,128]{3,2,1,0:T(8,128)S(1)}, u32[]{:S(2)}, u32[]{:S(2)}) collective-permute-start(f32[4,32,8,128]{3,2,1,0:T(8,128)S(1)} %get-tuple-element.47), channel_id=1, source_target_pairs={{8,16},{16,8},{24,32},{32,24},{40,48},{48,40},{56,64},{64,56},{72,... | collective-permute-start | bytes 1572872 | tf_op jit(solution)/shard_map/ppermute | solution.py:178
  49.4 3.9 %collective-permute-start.8 = (f32[8,4,8,128]{3,2,1,0:T(8,128)S(1)}, f32[8,4,8,128]{3,2,1,0:T(8,128)S(1)}, u32[]{:S(2)}, u32[]{:S(2)}) collective-permute-start(f32[8,4,8,128]{3,2,1,0:T(8,128)S(1)} %get-tuple-element.48), channel_id=1, source_target_pairs={{0,1},{1,0},{2,3},{3,2},{4,5},{5,4},{6,7},{7,6},{8,9},{9,8},{10,11... | collective-permute-start | bytes 393224 | tf_op jit(solution)/shard_map/ppermute | solution.py:178
  50.7 2.6 %collective-permute-start.9 = (f32[8,4,8,128]{3,2,1,0:T(8,128)S(1)}, f32[8,4,8,128]{3,2,1,0:T(8,128)S(1)}, u32[]{:S(2)}, u32[]{:S(2)}) collective-permute-start(f32[8,4,8,128]{3,2,1,0:T(8,128)S(1)} %get-tuple-element.49), channel_id=1, source_target_pairs={{1,2},{2,1},{3,4},{4,3},{5,6},{6,5},{9,10},{10,9},{11,12},{12,11},... | collective-permute-start | bytes 393224 | tf_op jit(solution)/shard_map/ppermute | solution.py:178
  53.5 4.7 %collective-permute-start.10 = (f32[2,3,4,8,128]{4,3,2,1,0:T(8,128)S(1)}, f32[2,3,4,8,128]{4,3,2,1,0:T(8,128)S(1)}, u32[]{:S(2)}, u32[]{:S(2)}) collective-permute-start(f32[2,3,4,8,128]{4,3,2,1,0:T(8,128)S(1)} %get-tuple-element.50), channel_id=1, source_target_pairs={{0,8},{8,0},{16,24},{24,16},{32,40},{40,32},{48,56},{56,48},{64,72... | collective-permute-start | bytes 294920 | tf_op jit(solution)/shard_map/ppermute | solution.py:178
  53.6 6.9 %collective-permute-start.11 = (f32[2,3,4,8,128]{4,3,2,1,0:T(8,128)S(1)}, f32[2,3,4,8,128]{4,3,2,1,0:T(8,128)S(1)}, u32[]{:S(2)}, u32[]{:S(2)}) collective-permute-start(f32[2,3,4,8,128]{4,3,2,1,0:T(8,128)S(1)} %get-tuple-element.51), channel_id=1, source_target_pairs={{8,16},{16,8},{24,32},{32,24},{40,48},{48,40},{56,64},{64,56},{72,... | collective-permute-start | bytes 294920 | tf_op jit(solution)/shard_map/ppermute | solution.py:178
  60.5 24.1 %copy-start.5 = (s32[256,1]{0,1:T(1,128)S(1)}, s32[256,1]{0,1:T(1,128)}, u32[]{:S(2)}) copy-start(s32[256,1]{0,1:T(1,128)} %param.10) | copy-start | bytes 3076
  60.5 37.3 %copy-start.3 = (s32[256,128]{1,0:T(8,128)S(1)}, s32[256,128]{1,0:T(8,128)}, u32[]{:S(2)}) copy-start(s32[256,128]{1,0:T(8,128)} %mask.1) | copy-start | bytes 393220
  60.5 37.3 %copy-start.4 = (s32[256]{0:T(256)S(1)}, s32[256]{0:T(256)}, u32[]{:S(2)}) copy-start(s32[256]{0:T(256)} %tile_rows.1) | copy-start | bytes 3076
  68.8 29.1 %collective-permute-start.12 = (f32[4,32,8,128]{3,2,1,0:T(8,128)S(1)}, f32[4,32,8,128]{3,2,1,0:T(8,128)S(1)}, u32[]{:S(2)}, u32[]{:S(2)}) collective-permute-start(f32[4,32,8,128]{3,2,1,0:T(8,128)S(1)} %get-tuple-element.54), channel_id=1, source_target_pairs={{0,8},{8,0},{16,24},{24,16},{32,40},{40,32},{48,56},{56,48},{64,72... | collective-permute-start | bytes 1572872 | tf_op jit(solution)/shard_map/ppermute | solution.py:178
  68.9 29.0 %collective-permute-start.13 = (f32[4,32,8,128]{3,2,1,0:T(8,128)S(1)}, f32[4,32,8,128]{3,2,1,0:T(8,128)S(1)}, u32[]{:S(2)}, u32[]{:S(2)}) collective-permute-start(f32[4,32,8,128]{3,2,1,0:T(8,128)S(1)} %get-tuple-element.55), channel_id=1, source_target_pairs={{8,16},{16,8},{24,32},{32,24},{40,48},{48,40},{56,64},{64,56},{72,... | collective-permute-start | bytes 1572872 | tf_op jit(solution)/shard_map/ppermute | solution.py:178
  84.8 5.8 %collective-permute-start.14 = (f32[8,4,8,128]{3,2,1,0:T(8,128)S(1)}, f32[8,4,8,128]{3,2,1,0:T(8,128)S(1)}, u32[]{:S(2)}, u32[]{:S(2)}) collective-permute-start(f32[8,4,8,128]{3,2,1,0:T(8,128)S(1)} %get-tuple-element.56), channel_id=1, source_target_pairs={{0,1},{1,0},{2,3},{3,2},{4,5},{5,4},{6,7},{7,6},{8,9},{9,8},{10,11... | collective-permute-start | bytes 393224 | tf_op jit(solution)/shard_map/ppermute | solution.py:178
  88.2 2.4 %collective-permute-start.15 = (f32[8,4,8,128]{3,2,1,0:T(8,128)S(1)}, f32[8,4,8,128]{3,2,1,0:T(8,128)S(1)}, u32[]{:S(2)}, u32[]{:S(2)}) collective-permute-start(f32[8,4,8,128]{3,2,1,0:T(8,128)S(1)} %get-tuple-element.57), channel_id=1, source_target_pairs={{1,2},{2,1},{3,4},{4,3},{5,6},{6,5},{9,10},{10,9},{11,12},{12,11},... | collective-permute-start | bytes 393224 | tf_op jit(solution)/shard_map/ppermute | solution.py:178
  90.8 4.7 %collective-permute-start.16 = (f32[2,3,4,8,128]{4,3,2,1,0:T(8,128)S(1)}, f32[2,3,4,8,128]{4,3,2,1,0:T(8,128)S(1)}, u32[]{:S(2)}, u32[]{:S(2)}) collective-permute-start(f32[2,3,4,8,128]{4,3,2,1,0:T(8,128)S(1)} %get-tuple-element.58), channel_id=1, source_target_pairs={{0,8},{8,0},{16,24},{24,16},{32,40},{40,32},{48,56},{56,48},{64,72... | collective-permute-start | bytes 294920 | tf_op jit(solution)/shard_map/ppermute | solution.py:178
  90.9 6.9 %collective-permute-start.17 = (f32[2,3,4,8,128]{4,3,2,1,0:T(8,128)S(1)}, f32[2,3,4,8,128]{4,3,2,1,0:T(8,128)S(1)}, u32[]{:S(2)}, u32[]{:S(2)}) collective-permute-start(f32[2,3,4,8,128]{4,3,2,1,0:T(8,128)S(1)} %get-tuple-element.59), channel_id=1, source_target_pairs={{8,16},{16,8},{24,32},{32,24},{40,48},{48,40},{56,64},{64,56},{72,... | collective-permute-start | bytes 294920 | tf_op jit(solution)/shard_map/ppermute | solution.py:178
  97.9 44.7 %copy-start.2 = (f32[3,256,128]{2,1,0:T(8,128)S(1)}, f32[3,256,128]{2,1,0:T(8,128)}, u32[]{:S(2)}) copy-start(f32[3,256,128]{2,1,0:T(8,128)} %heights.1) | copy-start | bytes 1179652

commit v2 on v1

--- a/solution.py
+++ b/solution.py
@@ -22,8 +22,11 @@
 ANY = pl.BlockSpec(memory_space=pl.ANY)
 SMEM = pl.BlockSpec(memory_space=pltpu.SMEM)
 VMEM = pl.BlockSpec(memory_space=pltpu.VMEM)
+HBM = pl.BlockSpec(memory_space=pltpu.HBM)
 F32 = jnp.float32
 MIB = 1 << 20
+EXT = pltpu.VMEM((EX, EY, *TILE), F32)
+ACC = pltpu.VMEM((NX, NY, *TILE), F32)
 
 
 def omega_of(step):
@@ -84,7 +87,7 @@
     return (("g", k, k), ("bx", k + 1, k), ("by", k, k + 1), ("bz", k, k))
 
 
-def pack_kernel(k, g, beta, g_rows, b_rows, xa, xb, ya, yb, nat, rows, in_sems, out_sems):
+def pack_kernel(k, g, beta, w, bx, by, bz, xa, xb, ya, yb, nat, in_sems, out_sems):
     sides = Sides()
     copies = []
     for x in range(NX):
@@ -96,31 +99,31 @@
         )
         for c in copies[-1]:
             c.start()
-    flat = rows.reshape(4 * NX * NY * 8, 128)
+    fields = (w, bx, by, bz)
     for x in range(NX):
         for c in copies[x]:
             c.wait()
-
-        @pl.loop(0, 4)
-        def _(a, x=x):
-            for yc in range(0, NY, 8):
+        for a, field in enumerate(fields):
+            flat = field.reshape(EX * EY * 8, 128)
+
+            @pl.loop(0, NY // 8)
+            def _(yc, x=x, a=a, flat=flat):
+                y = pl.multiple_of(yc * 8, 8)
                 for s in range(8):
-                    at = ((a * NX + x) * NY + yc) * 8 + s
-                    flat[pl.ds(at, 8, stride=8), :] = nat[a, x, yc : yc + 8, 128 * s : 128 * s + 128]
+                    at = ((x + K) * EY + K + y) * 8 + s
+                    flat[pl.ds(at, 8, stride=8), :] = nat[a, x, pl.ds(y, 8), 128 * s : 128 * s + 128]
 
     out = Copies(out_sems)
     for axis, ab, strip in (("gy", "a", ya), ("gy", "b", yb), ("gx", "b", xb), ("gx", "a", xa)):
         at = 0
-        for i, (_, in_x, in_y) in enumerate(fields_of(k)):
+        for field, (_, in_x, in_y) in zip(fields, fields_of(k)):
             n = in_x if axis == "gx" else in_y
-            first = sides.send(axis, ab, n)
+            first = sides.send(axis, ab, n) + K
             if axis == "gx":
-                out.start(rows.at[i, pl.ds(first, n)], strip.at[at : at + n])
+                out.start(field.at[pl.ds(first, n), K : K + NY], strip.at[at : at + n])
             else:
-                out.start(rows.at[i, :, pl.ds(first, n)], strip.at[:, at : at + n])
+                out.start(field.at[K : K + NX, pl.ds(first, n)], strip.at[:, at : at + n])
             at += n
-    out.start(rows.at[0], g_rows)
-    out.start(rows.at[1:4], b_rows)
     out.wait()
 
 
@@ -128,25 +131,17 @@
     n = 4 * k + 1
     return pl.pallas_call(
         functools.partial(pack_kernel, k),
-        out_shape=(
-            rows_shape(NX, NY),
-            rows_shape(3, NX, NY),
-            rows_shape(n, NY),
-            rows_shape(n, NY),
-            rows_shape(NX, n),
-            rows_shape(NX, n),
-        ),
-        in_specs=[ANY] * 2,
-        out_specs=(ANY,) * 6,
+        out_shape=(EXT,) * 4 + (rows_shape(n, NY), rows_shape(n, NY), rows_shape(NX, n), rows_shape(NX, n)),
+        in_specs=[HBM] * 2,
+        out_specs=(VMEM,) * 4 + (ANY,) * 4,
         scratch_shapes=[
             pltpu.VMEM((4, NX, NY, 1024), F32),
-            pltpu.VMEM((4, NX, NY, *TILE), F32),
             pltpu.SemaphoreType.DMA((2, NX)),
-            pltpu.SemaphoreType.DMA((18,)),
+            pltpu.SemaphoreType.DMA((16,)),
         ],
-        compiler_params=pltpu.CompilerParams(vmem_limit_bytes=12 * MIB),
+        compiler_params=pltpu.CompilerParams(vmem_limit_bytes=8 * MIB),
         name="pack",
-    )(g, beta)
+    )(*(pltpu.with_memory_space_constraint(array, pltpu.HBM) for array in (g, beta)))
 
 
 def corner_kernel(planes, ya, yb, ca, cb, sems):
@@ -186,10 +181,7 @@
     return xa, xb, ya, yb, ca, cb
 
 
-def land_first(k, sides, into, g_rows, b_rows, xs, ys, cs, fields):
-    for i, field in enumerate(fields):
-        src = g_rows if i == 0 else b_rows.at[i - 1]
-        into.start(src, field.at[K : K + NX, K : K + NY])
+def land_first(k, sides, into, xs, ys, cs, fields):
     at_x = at_y = 0
     for i, (_, in_x, in_y) in enumerate(fields_of(k)):
         for ab in ("a", "b"):
@@ -206,8 +198,7 @@
         at_x, at_y = at_x + in_x, at_y + in_y
 
 
-def land_later(k, sides, into, w_rows, xs, ys, cs, w):
-    into.start(w_rows, w.at[K : K + NX, K : K + NY])
+def land_later(k, sides, into, xs, ys, cs, w):
     for ab in ("a", "b"):
         x, y = sides.land("gx", ab, k), sides.land("gy", ab, k)
         into.start(xs[ab], w.at[pl.ds(x, k), K : K + NY])
@@ -283,99 +274,92 @@
     return w[k % 2]
 
 
-def leave(k, sides, out, w, w_rows, xa, xb, ya, yb):
+def leave(k, sides, out, w, xa, xb, ya, yb):
     for axis, ab, strip in (("gy", "a", ya), ("gy", "b", yb), ("gx", "b", xb), ("gx", "a", xa)):
         first = sides.send(axis, ab, k) + K
         if axis == "gx":
             out.start(w.at[pl.ds(first, k), K : K + NY], strip)
         else:
             out.start(w.at[K : K + NX, pl.ds(first, k)], strip)
-    out.start(w.at[K : K + NX, K : K + NY], w_rows)
 
 
 def first_kernel(
     k, k_next,
-    g_rows, b_rows, xa, xb, ya, yb, ca, cb,
-    bx_out, by_out, bz_out, inv_out, acc_out, w_out, xa_out, xb_out, ya_out, yb_out,
-    w0, w1, bx, by, bz, inv, acc, in_sems, out_sems,
+    w_in, bx_in, by_in, bz_in, xa, xb, ya, yb, ca, cb,
+    w0, bx, by, bz, inv, acc, w1, xa_out, xb_out, ya_out, yb_out,
+    in_sems, out_sems,
 ):
     sides = Sides()
     into = Copies(in_sems)
-    land_first(k, sides, into, g_rows, b_rows, {"a": xa, "b": xb}, {"a": ya, "b": yb}, {"a": ca, "b": cb}, (w0, bx, by, bz))
+    land_first(k, sides, into, {"a": xa, "b": xb}, {"a": ya, "b": yb}, {"a": ca, "b": cb}, (w0, bx, by, bz))
     into.wait()
     scale(w0, bx, by, bz, inv)
+    w = steps_of(0, k, False, (w0, w1), bx, by, bz, inv, acc)
     out = Copies(out_sems)
-    for src, dst in ((bx, bx_out), (by, by_out), (bz, bz_out), (inv, inv_out)):
-        out.start(src, dst)
-    w = steps_of(0, k, False, (w0, w1), bx, by, bz, inv, acc)
-    leave(k_next, sides, out, w, w_out, xa_out, xb_out, ya_out, yb_out)
-    out.start(acc, acc_out)
+    leave(k_next, sides, out, w, xa_out, xb_out, ya_out, yb_out)
     out.wait()
 
 
-EXT = pltpu.VMEM((EX, EY, *TILE), F32)
-ACC = pltpu.VMEM((NX, NY, *TILE), F32)
+def strips_shape(k):
+    x, y = rows_shape(k, NY), rows_shape(NX, k)
+    return (x, x, y, y)
 
 
 def first_round(k, k_next, *arrays):
-    ext, core = rows_shape(EX, EY), rows_shape(NX, NY)
-    x, y = rows_shape(k_next, NY), rows_shape(NX, k_next)
-    return pl.pallas_call(
+    assert k % 2 == 1
+    _, bx, by, bz, inv, acc, w, *strips = pl.pallas_call(
         functools.partial(first_kernel, k, k_next),
-        out_shape=(ext,) * 4 + (core, core, x, x, y, y),
-        in_specs=[ANY] * 8,
-        out_specs=(ANY,) * 10,
-        scratch_shapes=[EXT] * 6 + [ACC, pltpu.SemaphoreType.DMA((36,)), pltpu.SemaphoreType.DMA((10,))],
-        compiler_params=pltpu.CompilerParams(vmem_limit_bytes=22 * MIB),
+        out_shape=(EXT,) * 5 + (ACC, EXT) + strips_shape(k_next),
+        in_specs=[VMEM] * 4 + [ANY] * 6,
+        out_specs=(VMEM,) * 7 + (ANY,) * 4,
+        scratch_shapes=[pltpu.SemaphoreType.DMA((32,)), pltpu.SemaphoreType.DMA((4,))],
+        input_output_aliases={i: i for i in range(4)},
+        compiler_params=pltpu.CompilerParams(vmem_limit_bytes=2 * MIB),
         name="first_round",
     )(*arrays)
+    return (bx, by, bz, inv), (w, acc), strips
 
 
 def later_kernel(
     first, k, k_next,
-    bx_in, by_in, bz_in, inv_in, acc_in, w_in, xa, xb, ya, yb, ca, cb,
-    acc_out, w_out, xa_out, xb_out, ya_out, yb_out,
-    w0, w1, bx, by, bz, inv, acc, in_sems, out_sems,
+    bx, by, bz, inv, w_in, acc_in, xa, xb, ya, yb, ca, cb,
+    w0, acc, xa_out, xb_out, ya_out, yb_out,
+    w1, in_sems, out_sems,
 ):
     sides = Sides()
     into = Copies(in_sems)
-    for src, dst in ((bx_in, bx), (by_in, by), (bz_in, bz), (inv_in, inv), (acc_in, acc)):
-        into.start(src, dst)
-    land_later(k, sides, into, w_in, {"a": xa, "b": xb}, {"a": ya, "b": yb}, {"a": ca, "b": cb}, w0)
+    land_later(k, sides, into, {"a": xa, "b": xb}, {"a": ya, "b": yb}, {"a": ca, "b": cb}, w0)
     into.wait()
     w = steps_of(first, k, False, (w0, w1), bx, by, bz, inv, acc)
     out = Copies(out_sems)
-    leave(k_next, sides, out, w, w_out, xa_out, xb_out, ya_out, yb_out)
-    out.start(acc, acc_out)
+    leave(k_next, sides, out, w, xa_out, xb_out, ya_out, yb_out)
     out.wait()
 
 
 def later_round(first, k, k_next, *arrays):
-    core = rows_shape(NX, NY)
-    x, y = rows_shape(k_next, NY), rows_shape(NX, k_next)
-    return pl.pallas_call(
+    assert k % 2 == 0
+    w, acc, *strips = pl.pallas_call(
         functools.partial(later_kernel, first, k, k_next),
-        out_shape=(core, core, x, x, y, y),
-        in_specs=[ANY] * 12,
-        out_specs=(ANY,) * 6,
-        scratch_shapes=[EXT] * 6 + [ACC, pltpu.SemaphoreType.DMA((14,)), pltpu.SemaphoreType.DMA((6,))],
-        compiler_params=pltpu.CompilerParams(vmem_limit_bytes=22 * MIB),
+        out_shape=(EXT, ACC) + strips_shape(k_next),
+        in_specs=[VMEM] * 6 + [ANY] * 6,
+        out_specs=(VMEM,) * 2 + (ANY,) * 4,
+        scratch_shapes=[EXT, pltpu.SemaphoreType.DMA((8,)), pltpu.SemaphoreType.DMA((4,))],
+        input_output_aliases={4: 0, 5: 1},
+        compiler_params=pltpu.CompilerParams(vmem_limit_bytes=6 * MIB),
         name="later_round",
     )(*arrays)
+    return (w, acc), strips
 
 
 def last_kernel(
     first, k,
-    tile_rows, targets, mask, slots,
-    bx_in, by_in, bz_in, inv_in, acc_in, w_in, xa, xb, ya, yb, ca, cb,
-    grad, sent,
-    w0, w1, bx, by, bz, inv, acc, in_sems,
+    tile_rows, targets, mask, slots, bx, by, bz, inv, w_in, acc_in, xa, xb, ya, yb, ca, cb,
+    grad, sent, w0, acc,
+    w1, in_sems,
 ):
     sides = Sides()
     into = Copies(in_sems)
-    for src, dst in ((bx_in, bx), (by_in, by), (bz_in, bz), (inv_in, inv), (acc_in, acc)):
-        into.start(src, dst)
-    land_later(k, sides, into, w_in, {"a": xa, "b": xb}, {"a": ya, "b": yb}, {"a": ca, "b": cb}, w0)
+    land_later(k, sides, into, {"a": xa, "b": xb}, {"a": ya, "b": yb}, {"a": ca, "b": cb}, w0)
     sent[...] = jnp.zeros_like(sent)
     peers = slots.shape[0]
     sent[pl.ds(CAP, peers, stride=CAP + 1), :] = slots[...]
@@ -404,13 +388,16 @@
         out_shape=(
             jax.ShapeDtypeStruct((NX, NY, 1024), F32),
             jax.ShapeDtypeStruct((peers * (CAP + 1), 128), F32),
+            EXT,
+            ACC,
         ),
-        in_specs=[SMEM, SMEM, VMEM, VMEM] + [ANY] * 12,
-        out_specs=(VMEM, VMEM),
-        scratch_shapes=[EXT] * 6 + [ACC, pltpu.SemaphoreType.DMA((14,))],
-        compiler_params=pltpu.CompilerParams(vmem_limit_bytes=26 * MIB),
+        in_specs=[SMEM, SMEM] + [VMEM] * 8 + [ANY] * 6,
+        out_specs=(VMEM,) * 4,
+        scratch_shapes=[EXT, pltpu.SemaphoreType.DMA((8,))],
+        input_output_aliases={8: 2, 9: 3},
+        compiler_params=pltpu.CompilerParams(vmem_limit_bytes=10 * MIB),
         name="last_round",
-    )(*arrays)
+    )(*arrays)[:2]
 
 
 def finish_kernel(received, heights, out):
@@ -462,13 +449,11 @@
     peers = lax.axis_size("gx") * lax.axis_size("gy")
     targets, slots = routes(tile_owner, tile_slot, peers)
     k = ROUNDS[0]
-    g_rows, b_rows, *strips = pack(k, grad_pressure, beta)
-    out = first_round(k, ROUNDS[1], g_rows, b_rows, *exchange(k, *strips))
-    coeffs, state, strips = out[:4], out[4:6], out[6:]
+    packed = pack(k, grad_pressure, beta)
+    coeffs, state, strips = first_round(k, ROUNDS[1], *packed[:4], *exchange(k, *packed[4:]))
     done = k
     for k, k_next in zip(ROUNDS[1:-1], ROUNDS[2:]):
-        out = later_round(done, k, k_next, *coeffs, *state, *exchange(k - 1, *strips))
-        state, strips = out[:2], out[2:]
+        state, strips = later_round(done, k, k_next, *coeffs, *state, *exchange(k - 1, *strips))
         done += k
     k = ROUNDS[-1]
     grad_rhs, sent = last_round(

time: 144 us -> 139 us (0.965)
  local copies, waits for them, and re-layouts: 3.13 us -> 0.03 us
  Pallas kernels: 34.7 us -> 32.1 us
    unnamed x14 -> x10, local copies, waits for them, and re-layouts: 3.13 us -> 0.03 us
    pallas_call x2, Pallas kernels: 13.4 us -> 11.5 us  [the longest x1 8.29 us: first_round(): pl.pallas_call(functools.partial(first_kernel, k, k_next), out_shape=(EXT...]
where the time goes in v2:
time: 139 us; the launch traced here: 138 us
  starting transfers between devices  47.9 us (34%)
  blocking collectives  34.4 us (25%)
  Pallas kernels  32.1 us (23%)
  waiting for transfers between devices  22.3 us (16%)
    ppermute x18, starting transfers between devices, swap(): lax.ppermute(array, axis, [(i, j) for i, j in pairs if 0 <= j < size])  47.9 us
    all_to_all x1, blocking collectives, shards(): lax.all_to_all(sent, ('gx', 'gy'), split_axis=0, concat_axis=0, tiled=True)  34.4 us
    ppermute x18, waiting for transfers between devices, swap(): lax.ppermute(array, axis, [(i, j) for i, j in pairs if 0 <= j < size])  22.3 us
    pallas_call x1, Pallas kernels, last_round(): pl.pallas_call(functools.partial(last_kernel, first, k), out_shape=(jax.S...  9.97 us
    pallas_call x1, Pallas kernels, first_round(): pl.pallas_call(functools.partial(first_kernel, k, k_next), out_shape=(EXT...  8.29 us
    pallas_call x1, Pallas kernels, later_round(): pl.pallas_call(functools.partial(later_kernel, first, k, k_next), out_sha...  7.8 us
    pallas_call x1, Pallas kernels, pack(): pl.pallas_call(functools.partial(pack_kernel, k), out_shape=(EXT,) * 4 +...  3.22 us
  transfers between devices with their start and end apart: 18, of which 6 were waited for; matrix products, arithmetic and copies ran while one was open for 0% of the time, Pallas kernels for 1%

profile of v2, /device:TPU:1, one launch (start us, length us, event | category | flops | bytes accessed | tf_op | source)
XLA Modules:
  0.0 138.2 jit_solution(17568844824635635701)
XLA Ops:
  0.6 3.2 %pack.1 = (f32[16,40,8,128]{3,2,1,0:T(8,128)S(1)}, f32[16,40,8,128]{3,2,1,0:T(8,128)S(1)}, f32[16,40,8,128]{3,2,1,0:T(8,128)S(1)}, f32[16,40,8,128]{3,2,1,0:T(8,...) custom-call(f32[8,32,1024]{2,1,0:T(8,128)} %g.1, ...), custom_call_target="tpu_custom_call" | custom-call | tf_op jit(solution)/shard_map/pack/pallas_call | solution.py:132
  3.9 1.5 %collective-permute-start = (f32[13,32,8,128]{3,2,1,0:T(8,128)S(1)}, f32[13,32,8,128]{3,2,1,0:T(8,128)S(1)}, u32[]{:S(2)}, u32[]{:S(2)}) collective-permute-start(f32[13,32,8,128]{3,2,1,0:T(8,128)S(1)} %get-tuple-element.38), channel_id=1, source_target_pairs={{0,8},{8,0},{16,24},{24,16},{32,40},{40,32},{48,56},{56,48},{64,72... | collective-permute-start | bytes 5111816 | tf_op jit(solution)/shard_map/ppermute | solution.py:173
  5.4 3.5 %collective-permute-start.1 = (f32[13,32,8,128]{3,2,1,0:T(8,128)S(1)}, f32[13,32,8,128]{3,2,1,0:T(8,128)S(1)}, u32[]{:S(2)}, u32[]{:S(2)}) collective-permute-start(f32[13,32,8,128]{3,2,1,0:T(8,128)S(1)} %get-tuple-element.39), channel_id=1, source_target_pairs={{8,16},{16,8},{24,32},{32,24},{40,48},{48,40},{56,64},{64,56},{72,... | collective-permute-start | bytes 5111816 | tf_op jit(solution)/shard_map/ppermute | solution.py:173
  8.9 1.3 collective-permute-start.2
  10.2 0.7 collective-permute-start.3
  10.9 7.4 %collective-permute-done.2.ya = f32[8,13,8,128]{3,2,1,0:T(8,128)S(1)} collective-permute-done((f32[8,13,8,128]{3,2,1,0:T(8,128)S(1)}, f32[8,13,8,128]{3,2,1,0:T(8,128)S(1)}, u32[]{:S(2)}, u32[]{:S(2)}) %collective-permute-start.2) | collective-permute-done | bytes 426016 | tf_op jit(solution)/shard_map/ppermute | solution.py:173
  18.2 0.0 collective-permute-done.3.yb
  18.2 0.8 corners.3
  19.1 0.1 collective-permute-start.4
  19.2 5.5 %collective-permute-start.5 = (f32[2,3,13,8,128]{4,3,2,1,0:T(8,128)S(1)}, f32[2,3,13,8,128]{4,3,2,1,0:T(8,128)S(1)}, u32[]{:S(2)}, u32[]{:S(2)}) collective-permute-start(f32[2,3,13,8,128]{4,3,2,1,0:T(8,128)S(1)} %get-tuple-element.43), channel_id=1, source_target_pairs={{8,16},{16,8},{24,32},{32,24},{40,48},{48,40},{56,64},{64,56},{72,... | collective-permute-start | bytes 958472 | tf_op jit(solution)/shard_map/ppermute | solution.py:173
  24.7 0.0 collective-permute-done.4.ca
  24.7 7.2 %collective-permute-done.5.cb = f32[2,3,13,8,128]{4,3,2,1,0:T(8,128)S(1)} collective-permute-done((f32[2,3,13,8,128]{4,3,2,1,0:T(8,128)S(1)}, f32[2,3,13,8,128]{4,3,2,1,0:T(8,128)S(1)}, u32[]{:S(2)}, u32[]{:S(2)}) %collective-permute-start.5) | collective-permute-done | bytes 319520 | tf_op jit(solution)/shard_map/ppermute | solution.py:173
  31.9 0.0 collective-permute-done.xa
  31.9 0.0 collective-permute-done.1.xb
  31.9 0.0 copy-start.4
  31.9 8.3 %first_round.1 = (f32[16,40,8,128]{3,2,1,0:T(8,128)S(1)}, f32[16,40,8,128]{3,2,1,0:T(8,128)S(1)}, f32[16,40,8,128]{3,2,1,0:T(8,128)S(1)}, f32[16,40,8,128]{3,2,1...) custom-call(f32[16,40,8,128]{3,2,1,0:T(8,128)S(1)} %get-tuple-elemen, ...), custom_call_target="tpu_custom_call", output_to_operand_aliasing={{0}: (0, {}), {1}: (1, {}), {2}: (2, {}), {3}: (3, {})} | custom-call | tf_op jit(solution)/shard_map/first_round/pallas_call | solution.py:310
  40.2 0.1 collective-permute-start.6
  40.3 4.0 %collective-permute-start.7 = (f32[4,32,8,128]{3,2,1,0:T(8,128)S(1)}, f32[4,32,8,128]{3,2,1,0:T(8,128)S(1)}, u32[]{:S(2)}, u32[]{:S(2)}) collective-permute-start(f32[4,32,8,128]{3,2,1,0:T(8,128)S(1)} %get-tuple-element.51), channel_id=1, source_target_pairs={{8,16},{16,8},{24,32},{32,24},{40,48},{48,40},{56,64},{64,56},{72,... | collective-permute-start | bytes 1572872 | tf_op jit(solution)/shard_map/ppermute | solution.py:173
  44.3 1.3 collective-permute-start.8
  45.6 0.7 collective-permute-start.9
  46.3 1.9 %collective-permute-done.8.ya = f32[8,4,8,128]{3,2,1,0:T(8,128)S(1)} collective-permute-done((f32[8,4,8,128]{3,2,1,0:T(8,128)S(1)}, f32[8,4,8,128]{3,2,1,0:T(8,128)S(1)}, u32[]{:S(2)}, u32[]{:S(2)}) %collective-permute-start.8) | collective-permute-done | bytes 131104 | tf_op jit(solution)/shard_map/ppermute | solution.py:173
  48.2 0.0 collective-permute-done.9.yb
  48.2 0.3 corners.4
  48.5 0.1 collective-permute-start.10
  48.6 4.6 %collective-permute-start.11 = (f32[2,3,4,8,128]{4,3,2,1,0:T(8,128)S(1)}, f32[2,3,4,8,128]{4,3,2,1,0:T(8,128)S(1)}, u32[]{:S(2)}, u32[]{:S(2)}) collective-permute-start(f32[2,3,4,8,128]{4,3,2,1,0:T(8,128)S(1)} %get-tuple-element.55), channel_id=1, source_target_pairs={{8,16},{16,8},{24,32},{32,24},{40,48},{48,40},{56,64},{64,56},{72,... | collective-permute-start | bytes 294920 | tf_op jit(solution)/shard_map/ppermute | solution.py:173
  53.2 0.0 copy-done.4
  53.2 0.0 collective-permute-done.10.ca
  53.2 2.3 %collective-permute-done.11.cb = f32[2,3,4,8,128]{4,3,2,1,0:T(8,128)S(1)} collective-permute-done((f32[2,3,4,8,128]{4,3,2,1,0:T(8,128)S(1)}, f32[2,3,4,8,128]{4,3,2,1,0:T(8,128)S(1)}, u32[]{:S(2)}, u32[]{:S(2)}) %collective-permute-start.11) | collective-permute-done | bytes 98336 | tf_op jit(solution)/shard_map/ppermute | solution.py:173
  55.5 0.0 collective-permute-done.6.xa
  55.5 0.0 collective-permute-done.7.xb
  55.5 0.0 copy-start.3
  55.5 0.0 copy-start.1
  55.5 0.0 copy-start.2
  55.5 7.8 %later_round.1 = (f32[16,40,8,128]{3,2,1,0:T(8,128)S(1)}, f32[8,32,8,128]{3,2,1,0:T(8,128)S(1)}, f32[4,32,8,128]{3,2,1,0:T(8,128)S(1)}, f32[4,32,8,128]{3,2,1,0:...) custom-call(f32[16,40,8,128]{3,2,1,0:T(8,128)S(1)} %get-tuple-elemen, ...), custom_call_target="tpu_custom_call", output_to_operand_aliasing={{0}: (4, {}), {1}: (5, {})} | custom-call | tf_op jit(solution)/shard_map/later_round/pallas_call | solution.py:341
  63.3 0.1 collective-permute-start.12
  63.4 15.7 %collective-permute-start.13 = (f32[4,32,8,128]{3,2,1,0:T(8,128)S(1)}, f32[4,32,8,128]{3,2,1,0:T(8,128)S(1)}, u32[]{:S(2)}, u32[]{:S(2)}) collective-permute-start(f32[4,32,8,128]{3,2,1,0:T(8,128)S(1)} %get-tuple-element.59), channel_id=1, source_target_pairs={{8,16},{16,8},{24,32},{32,24},{40,48},{48,40},{56,64},{64,56},{72,... | collective-permute-start | bytes 1572872 | tf_op jit(solution)/shard_map/ppermute | solution.py:173
  79.1 0.0 copy-done.3
  79.1 0.2 convert_reduce_fusion
  79.3 3.4 %collective-permute-start.14 = (f32[8,4,8,128]{3,2,1,0:T(8,128)S(1)}, f32[8,4,8,128]{3,2,1,0:T(8,128)S(1)}, u32[]{:S(2)}, u32[]{:S(2)}) collective-permute-start(f32[8,4,8,128]{3,2,1,0:T(8,128)S(1)} %get-tuple-element.60), channel_id=1, source_target_pairs={{0,1},{1,0},{2,3},{3,2},{4,5},{5,4},{6,7},{7,6},{8,9},{9,8},{10,11... | collective-permute-start | bytes 393224 | tf_op jit(solution)/shard_map/ppermute | solution.py:173
  82.7 0.7 collective-permute-start.15
  83.4 0.3 fusion.1.slots
  83.7 1.4 collective-permute-done.14.ya
  85.1 0.0 collective-permute-done.15.yb
  85.1 0.3 corners.5
  85.4 0.1 collective-permute-start.16
  85.5 4.6 %collective-permute-start.17 = (f32[2,3,4,8,128]{4,3,2,1,0:T(8,128)S(1)}, f32[2,3,4,8,128]{4,3,2,1,0:T(8,128)S(1)}, u32[]{:S(2)}, u32[]{:S(2)}) collective-permute-start(f32[2,3,4,8,128]{4,3,2,1,0:T(8,128)S(1)} %get-tuple-element.63), channel_id=1, source_target_pairs={{8,16},{16,8},{24,32},{32,24},{40,48},{48,40},{56,64},{64,56},{72,... | collective-permute-start | bytes 294920 | tf_op jit(solution)/shard_map/ppermute | solution.py:173
  90.1 0.0 collective-permute-done.16.ca
  90.1 2.3 %collective-permute-done.17.cb = f32[2,3,4,8,128]{4,3,2,1,0:T(8,128)S(1)} collective-permute-done((f32[2,3,4,8,128]{4,3,2,1,0:T(8,128)S(1)}, f32[2,3,4,8,128]{4,3,2,1,0:T(8,128)S(1)}, u32[]{:S(2)}, u32[]{:S(2)}) %collective-permute-start.17) | collective-permute-done | bytes 98336 | tf_op jit(solution)/shard_map/ppermute | solution.py:173
  92.4 0.0 collective-permute-done.12.xa
  92.4 0.0 collective-permute-done.13.xb
  92.4 0.0 copy-done.1
  92.4 0.0 copy-done.2
  92.4 0.0 copy-start
  92.4 10.0 %last_round.1 = (f32[8,32,1024]{2,1,0:T(8,128)}, f32[1152,128]{1,0:T(8,128)S(1)}, f32[16,40,8,128]{3,2,1,0:T(8,128)S(1)}, f32[8,32,8,128]{3,2,1,0:T(8,128)S(1)}) custom-call(s32[256]{0:T(256)S(1)} %copy-done.2, s32[256]{0:T(256)S(1)} %multiply_add_fusion.targets, s32[256,128]{1,0:T(8,128)S(1)} %copy-done.1, ...), custom_call_target="tpu_custom_call", output_to_operand_aliasing={{2}: (8, {}), {3}: (9, {})} | custom-call | tf_op jit(solution)/shard_map/last_round/pallas_call | solution.py:386
  102.4 34.4 %all_to_all.5 = f32[128,1,1152]{2,1,0:T(1,128)S(1)} all-to-all(f32[128,1,1152]{2,1,0:T(1,128)S(1)} %bitcast.4), channel_id=1, replica_groups=mesh['gx'=16,'gy'=8] {'gx','gy'}, dimensions={0} | all-to-all | bytes 1179648 | tf_op jit(solution)/shard_map/all_to_all | solution.py:463
  136.8 0.0 copy-done
  136.8 1.4 %finish.1 = f32[3,256,128]{2,1,0:T(8,128)} custom-call(f32[1152,128]{1,0:T(8,128)S(1)} %bitcast.3, f32[3,256,128]{2,1,0:T(8,128)S(1)} %copy-done), custom_call_target="tpu_custom_call" | custom-call | tf_op jit(solution)/shard_map/finish/pallas_call | solution.py:427
  (2 shorter events, 0.0 us)
Async XLA Ops:
  3.9 28.1 %collective-permute-start = (f32[13,32,8,128]{3,2,1,0:T(8,128)S(1)}, f32[13,32,8,128]{3,2,1,0:T(8,128)S(1)}, u32[]{:S(2)}, u32[]{:S(2)}) collective-permute-start(f32[13,32,8,128]{3,2,1,0:T(8,128)S(1)} %get-tuple-element.38), channel_id=1, source_target_pairs={{0,8},{8,0},{16,24},{24,16},{32,40},{40,32},{48,56},{56,48},{64,72... | collective-permute-start | bytes 5111816 | tf_op jit(solution)/shard_map/ppermute | solution.py:173
  5.4 26.6 %collective-permute-start.1 = (f32[13,32,8,128]{3,2,1,0:T(8,128)S(1)}, f32[13,32,8,128]{3,2,1,0:T(8,128)S(1)}, u32[]{:S(2)}, u32[]{:S(2)}) collective-permute-start(f32[13,32,8,128]{3,2,1,0:T(8,128)S(1)} %get-tuple-element.39), channel_id=1, source_target_pairs={{8,16},{16,8},{24,32},{32,24},{40,48},{48,40},{56,64},{64,56},{72,... | collective-permute-start | bytes 5111816 | tf_op jit(solution)/shard_map/ppermute | solution.py:173
  8.9 9.3 %collective-permute-start.2 = (f32[8,13,8,128]{3,2,1,0:T(8,128)S(1)}, f32[8,13,8,128]{3,2,1,0:T(8,128)S(1)}, u32[]{:S(2)}, u32[]{:S(2)}) collective-permute-start(f32[8,13,8,128]{3,2,1,0:T(8,128)S(1)} %get-tuple-element.40), channel_id=1, source_target_pairs={{0,1},{1,0},{2,3},{3,2},{4,5},{5,4},{6,7},{7,6},{8,9},{9,8},{10,11... | collective-permute-start | bytes 1277960 | tf_op jit(solution)/shard_map/ppermute | solution.py:173
  10.2 8.1 %collective-permute-start.3 = (f32[8,13,8,128]{3,2,1,0:T(8,128)S(1)}, f32[8,13,8,128]{3,2,1,0:T(8,128)S(1)}, u32[]{:S(2)}, u32[]{:S(2)}) collective-permute-start(f32[8,13,8,128]{3,2,1,0:T(8,128)S(1)} %get-tuple-element.41), channel_id=1, source_target_pairs={{1,2},{2,1},{3,4},{4,3},{5,6},{6,5},{9,10},{10,9},{11,12},{12,11},... | collective-permute-start | bytes 1277960 | tf_op jit(solution)/shard_map/ppermute | solution.py:173
  19.1 5.7 %collective-permute-start.4 = (f32[2,3,13,8,128]{4,3,2,1,0:T(8,128)S(1)}, f32[2,3,13,8,128]{4,3,2,1,0:T(8,128)S(1)}, u32[]{:S(2)}, u32[]{:S(2)}) collective-permute-start(f32[2,3,13,8,128]{4,3,2,1,0:T(8,128)S(1)} %get-tuple-element.42), channel_id=1, source_target_pairs={{0,8},{8,0},{16,24},{24,16},{32,40},{40,32},{48,56},{56,48},{64,72... | collective-permute-start | bytes 958472 | tf_op jit(solution)/shard_map/ppermute | solution.py:173
  19.2 12.7 %collective-permute-start.5 = (f32[2,3,13,8,128]{4,3,2,1,0:T(8,128)S(1)}, f32[2,3,13,8,128]{4,3,2,1,0:T(8,128)S(1)}, u32[]{:S(2)}, u32[]{:S(2)}) collective-permute-start(f32[2,3,13,8,128]{4,3,2,1,0:T(8,128)S(1)} %get-tuple-element.43), channel_id=1, source_target_pairs={{8,16},{16,8},{24,32},{32,24},{40,48},{48,40},{56,64},{64,56},{72,... | collective-permute-start | bytes 958472 | tf_op jit(solution)/shard_map/ppermute | solution.py:173
  31.9 21.3 %copy-start.4 = (s32[256]{0:T(256)S(1)}, s32[256]{0:T(256)}, u32[]{:S(2)}) copy-start(s32[256]{0:T(256)} %param.11) | copy-start | bytes 3076
  40.2 15.2 %collective-permute-start.6 = (f32[4,32,8,128]{3,2,1,0:T(8,128)S(1)}, f32[4,32,8,128]{3,2,1,0:T(8,128)S(1)}, u32[]{:S(2)}, u32[]{:S(2)}) collective-permute-start(f32[4,32,8,128]{3,2,1,0:T(8,128)S(1)} %get-tuple-element.50), channel_id=1, source_target_pairs={{0,8},{8,0},{16,24},{24,16},{32,40},{40,32},{48,56},{56,48},{64,72... | collective-permute-start | bytes 1572872 | tf_op jit(solution)/shard_map/ppermute | solution.py:173
  40.3 15.2 %collective-permute-start.7 = (f32[4,32,8,128]{3,2,1,0:T(8,128)S(1)}, f32[4,32,8,128]{3,2,1,0:T(8,128)S(1)}, u32[]{:S(2)}, u32[]{:S(2)}) collective-permute-start(f32[4,32,8,128]{3,2,1,0:T(8,128)S(1)} %get-tuple-element.51), channel_id=1, source_target_pairs={{8,16},{16,8},{24,32},{32,24},{40,48},{48,40},{56,64},{64,56},{72,... | collective-permute-start | bytes 1572872 | tf_op jit(solution)/shard_map/ppermute | solution.py:173
  44.3 3.9 %collective-permute-start.8 = (f32[8,4,8,128]{3,2,1,0:T(8,128)S(1)}, f32[8,4,8,128]{3,2,1,0:T(8,128)S(1)}, u32[]{:S(2)}, u32[]{:S(2)}) collective-permute-start(f32[8,4,8,128]{3,2,1,0:T(8,128)S(1)} %get-tuple-element.52), channel_id=1, source_target_pairs={{0,1},{1,0},{2,3},{3,2},{4,5},{5,4},{6,7},{7,6},{8,9},{9,8},{10,11... | collective-permute-start | bytes 393224 | tf_op jit(solution)/shard_map/ppermute | solution.py:173
  45.6 2.6 %collective-permute-start.9 = (f32[8,4,8,128]{3,2,1,0:T(8,128)S(1)}, f32[8,4,8,128]{3,2,1,0:T(8,128)S(1)}, u32[]{:S(2)}, u32[]{:S(2)}) collective-permute-start(f32[8,4,8,128]{3,2,1,0:T(8,128)S(1)} %get-tuple-element.53), channel_id=1, source_target_pairs={{1,2},{2,1},{3,4},{4,3},{5,6},{6,5},{9,10},{10,9},{11,12},{12,11},... | collective-permute-start | bytes 393224 | tf_op jit(solution)/shard_map/ppermute | solution.py:173
  48.5 4.7 %collective-permute-start.10 = (f32[2,3,4,8,128]{4,3,2,1,0:T(8,128)S(1)}, f32[2,3,4,8,128]{4,3,2,1,0:T(8,128)S(1)}, u32[]{:S(2)}, u32[]{:S(2)}) collective-permute-start(f32[2,3,4,8,128]{4,3,2,1,0:T(8,128)S(1)} %get-tuple-element.54), channel_id=1, source_target_pairs={{0,8},{8,0},{16,24},{24,16},{32,40},{40,32},{48,56},{56,48},{64,72... | collective-permute-start | bytes 294920 | tf_op jit(solution)/shard_map/ppermute | solution.py:173
  48.6 6.9 %collective-permute-start.11 = (f32[2,3,4,8,128]{4,3,2,1,0:T(8,128)S(1)}, f32[2,3,4,8,128]{4,3,2,1,0:T(8,128)S(1)}, u32[]{:S(2)}, u32[]{:S(2)}) collective-permute-start(f32[2,3,4,8,128]{4,3,2,1,0:T(8,128)S(1)} %get-tuple-element.55), channel_id=1, source_target_pairs={{8,16},{16,8},{24,32},{32,24},{40,48},{48,40},{56,64},{64,56},{72,... | collective-permute-start | bytes 294920 | tf_op jit(solution)/shard_map/ppermute | solution.py:173
  55.5 23.7 %copy-start.3 = (s32[256,1]{0,1:T(1,128)S(1)}, s32[256,1]{0,1:T(1,128)}, u32[]{:S(2)}) copy-start(s32[256,1]{0,1:T(1,128)} %param.10) | copy-start | bytes 3076
  55.5 36.9 %copy-start.1 = (s32[256,128]{1,0:T(8,128)S(1)}, s32[256,128]{1,0:T(8,128)}, u32[]{:S(2)}) copy-start(s32[256,128]{1,0:T(8,128)} %mask.1) | copy-start | bytes 393220
  55.5 36.9 %copy-start.2 = (s32[256]{0:T(256)S(1)}, s32[256]{0:T(256)}, u32[]{:S(2)}) copy-start(s32[256]{0:T(256)} %tile_rows.1) | copy-start | bytes 3076
  63.3 29.1 %collective-permute-start.12 = (f32[4,32,8,128]{3,2,1,0:T(8,128)S(1)}, f32[4,32,8,128]{3,2,1,0:T(8,128)S(1)}, u32[]{:S(2)}, u32[]{:S(2)}) collective-permute-start(f32[4,32,8,128]{3,2,1,0:T(8,128)S(1)} %get-tuple-element.58), channel_id=1, source_target_pairs={{0,8},{8,0},{16,24},{24,16},{32,40},{40,32},{48,56},{56,48},{64,72... | collective-permute-start | bytes 1572872 | tf_op jit(solution)/shard_map/ppermute | solution.py:173
  63.4 29.0 %collective-permute-start.13 = (f32[4,32,8,128]{3,2,1,0:T(8,128)S(1)}, f32[4,32,8,128]{3,2,1,0:T(8,128)S(1)}, u32[]{:S(2)}, u32[]{:S(2)}) collective-permute-start(f32[4,32,8,128]{3,2,1,0:T(8,128)S(1)} %get-tuple-element.59), channel_id=1, source_target_pairs={{8,16},{16,8},{24,32},{32,24},{40,48},{48,40},{56,64},{64,56},{72,... | collective-permute-start | bytes 1572872 | tf_op jit(solution)/shard_map/ppermute | solution.py:173
  79.3 5.8 %collective-permute-start.14 = (f32[8,4,8,128]{3,2,1,0:T(8,128)S(1)}, f32[8,4,8,128]{3,2,1,0:T(8,128)S(1)}, u32[]{:S(2)}, u32[]{:S(2)}) collective-permute-start(f32[8,4,8,128]{3,2,1,0:T(8,128)S(1)} %get-tuple-element.60), channel_id=1, source_target_pairs={{0,1},{1,0},{2,3},{3,2},{4,5},{5,4},{6,7},{7,6},{8,9},{9,8},{10,11... | collective-permute-start | bytes 393224 | tf_op jit(solution)/shard_map/ppermute | solution.py:173
  82.7 2.4 %collective-permute-start.15 = (f32[8,4,8,128]{3,2,1,0:T(8,128)S(1)}, f32[8,4,8,128]{3,2,1,0:T(8,128)S(1)}, u32[]{:S(2)}, u32[]{:S(2)}) collective-permute-start(f32[8,4,8,128]{3,2,1,0:T(8,128)S(1)} %get-tuple-element.61), channel_id=1, source_target_pairs={{1,2},{2,1},{3,4},{4,3},{5,6},{6,5},{9,10},{10,9},{11,12},{12,11},... | collective-permute-start | bytes 393224 | tf_op jit(solution)/shard_map/ppermute | solution.py:173
  85.4 4.7 %collective-permute-start.16 = (f32[2,3,4,8,128]{4,3,2,1,0:T(8,128)S(1)}, f32[2,3,4,8,128]{4,3,2,1,0:T(8,128)S(1)}, u32[]{:S(2)}, u32[]{:S(2)}) collective-permute-start(f32[2,3,4,8,128]{4,3,2,1,0:T(8,128)S(1)} %get-tuple-element.62), channel_id=1, source_target_pairs={{0,8},{8,0},{16,24},{24,16},{32,40},{40,32},{48,56},{56,48},{64,72... | collective-permute-start | bytes 294920 | tf_op jit(solution)/shard_map/ppermute | solution.py:173
  85.5 6.9 %collective-permute-start.17 = (f32[2,3,4,8,128]{4,3,2,1,0:T(8,128)S(1)}, f32[2,3,4,8,128]{4,3,2,1,0:T(8,128)S(1)}, u32[]{:S(2)}, u32[]{:S(2)}) collective-permute-start(f32[2,3,4,8,128]{4,3,2,1,0:T(8,128)S(1)} %get-tuple-element.63), channel_id=1, source_target_pairs={{8,16},{16,8},{24,32},{32,24},{40,48},{48,40},{56,64},{64,56},{72,... | collective-permute-start | bytes 294920 | tf_op jit(solution)/shard_map/ppermute | solution.py:173
  92.4 44.4 %copy-start = (f32[3,256,128]{2,1,0:T(8,128)S(1)}, f32[3,256,128]{2,1,0:T(8,128)}, u32[]{:S(2)}) copy-start(f32[3,256,128]{2,1,0:T(8,128)} %heights.1) | copy-start | bytes 1179652

commit v3 on v2

--- a/solution.py
+++ b/solution.py
@@ -163,6 +163,7 @@
         out_specs=(ANY,) * 2,
         scratch_shapes=[pltpu.SemaphoreType.DMA((4,))],
         compiler_params=pltpu.CompilerParams(vmem_limit_bytes=MIB),
+        cost_estimate=pl.CostEstimate(flops=10**12, bytes_accessed=MIB, transcendentals=0),
         name="corners",
     )(ya, yb)
 

time: 139 us -> 141 us (1.014)
  Pallas kernels: 32.1 us -> 37.2 us
  starting transfers between devices: 47.9 us -> 43.2 us
    ppermute x18, starting transfers between devices: 47.9 us -> 43.2 us  [swap(): lax.ppermute(array, axis, [(i, j) for i, j in pairs if 0 <= j < size])]
  transfers between devices with their start and end apart: 18 -> 18, of which waited for: 6 -> 4; matrix products, arithmetic and copies ran while one was open for 0% -> 1% of each run, Pallas kernels for 1% -> 1%
where the time goes in v3:
time: 141 us
  starting transfers between devices  43.2 us (31%)
  Pallas kernels  37.2 us (26%)
  blocking collectives  34.2 us (24%)
  waiting for transfers between devices  23 us (16%)
    ppermute x18, starting transfers between devices, swap(): lax.ppermute(array, axis, [(i, j) for i, j in pairs if 0 <= j < size])  43.2 us
    all_to_all x1, blocking collectives, shards(): lax.all_to_all(sent, ('gx', 'gy'), split_axis=0, concat_axis=0, tiled=True)  34.2 us
    ppermute x18, waiting for transfers between devices, swap(): lax.ppermute(array, axis, [(i, j) for i, j in pairs if 0 <= j < size])  23 us
    pallas_call x1, Pallas kernels, last_round(): pl.pallas_call(functools.partial(last_kernel, first, k), out_shape=(jax.S...  11.1 us
    pallas_call x1, Pallas kernels, first_round(): pl.pallas_call(functools.partial(first_kernel, k, k_next), out_shape=(EXT...  9.61 us
    pallas_call x1, Pallas kernels, later_round(): pl.pallas_call(functools.partial(later_kernel, first, k, k_next), out_sha...  9.13 us
    pallas_call x1, Pallas kernels, pack(): pl.pallas_call(functools.partial(pack_kernel, k), out_shape=(EXT,) * 4 +...  4.49 us
  transfers between devices with their start and end apart: 18, of which 4 were waited for; matrix products, arithmetic and copies ran while one was open for 1% of the time, Pallas kernels for 1%

profile of v3, /device:TPU:1, one launch (start us, length us, event | category | flops | bytes accessed | tf_op | source)
XLA Modules:
  0.0 140.9 jit_solution(3244898342930161287)
XLA Ops:
  0.6 4.5 %pack.1 = (f32[16,40,8,128]{3,2,1,0:T(8,128)S(1)}, f32[16,40,8,128]{3,2,1,0:T(8,128)S(1)}, f32[16,40,8,128]{3,2,1,0:T(8,128)S(1)}, f32[16,40,8,128]{3,2,1,0:T(8,...) custom-call(f32[8,32,1024]{2,1,0:T(8,128)} %g.1, ...), custom_call_target="tpu_custom_call" | custom-call | tf_op jit(solution)/shard_map/pack/pallas_call | solution.py:132
  5.1 2.1 %collective-permute-start.2 = (f32[8,13,8,128]{3,2,1,0:T(8,128)S(1)}, f32[8,13,8,128]{3,2,1,0:T(8,128)S(1)}, u32[]{:S(2)}, u32[]{:S(2)}) collective-permute-start(f32[8,13,8,128]{3,2,1,0:T(8,128)S(1)} %get-tuple-element.40), channel_id=1, source_target_pairs={{0,1},{1,0},{2,3},{3,2},{4,5},{5,4},{6,7},{7,6},{8,9},{9,8},{10,11... | collective-permute-start | bytes 1277960 | tf_op jit(solution)/shard_map/ppermute | solution.py:174
  7.2 0.7 collective-permute-start.3
  7.9 1.0 collective-permute-start
  9.0 3.4 %collective-permute-start.1 = (f32[13,32,8,128]{3,2,1,0:T(8,128)}, f32[13,32,8,128]{3,2,1,0:T(8,128)}, u32[]{:S(2)}, u32[]{:S(2)}) collective-permute-start(f32[13,32,8,128]{3,2,1,0:T(8,128)} %get-tuple-element.39), channel_id=1, source_target_pairs={{8,16},{16,8},{24,32},{32,24},{40,48},{48,40},{56,64},{64,56},{72,... | collective-permute-start | bytes 5111816 | tf_op jit(solution)/shard_map/ppermute | solution.py:174
  12.4 3.9 %collective-permute-done.2.ya = f32[8,13,8,128]{3,2,1,0:T(8,128)S(1)} collective-permute-done((f32[8,13,8,128]{3,2,1,0:T(8,128)S(1)}, f32[8,13,8,128]{3,2,1,0:T(8,128)S(1)}, u32[]{:S(2)}, u32[]{:S(2)}) %collective-permute-start.2) | collective-permute-done | bytes 426016 | tf_op jit(solution)/shard_map/ppermute | solution.py:174
  16.3 0.0 collective-permute-done.3.yb
  16.3 0.8 corners.3
  17.1 1.8 %collective-permute-start.4 = (f32[2,3,13,8,128]{4,3,2,1,0:T(8,128)S(1)}, f32[2,3,13,8,128]{4,3,2,1,0:T(8,128)S(1)}, u32[]{:S(2)}, u32[]{:S(2)}) collective-permute-start(f32[2,3,13,8,128]{4,3,2,1,0:T(8,128)S(1)} %get-tuple-element.42), channel_id=1, source_target_pairs={{0,8},{8,0},{16,24},{24,16},{32,40},{40,32},{48,56},{56,48},{64,72... | collective-permute-start | bytes 958472 | tf_op jit(solution)/shard_map/ppermute | solution.py:174
  19.0 3.7 %collective-permute-start.5 = (f32[2,3,13,8,128]{4,3,2,1,0:T(8,128)S(1)}, f32[2,3,13,8,128]{4,3,2,1,0:T(8,128)S(1)}, u32[]{:S(2)}, u32[]{:S(2)}) collective-permute-start(f32[2,3,13,8,128]{4,3,2,1,0:T(8,128)S(1)} %get-tuple-element.43), channel_id=1, source_target_pairs={{8,16},{16,8},{24,32},{32,24},{40,48},{48,40},{56,64},{64,56},{72,... | collective-permute-start | bytes 958472 | tf_op jit(solution)/shard_map/ppermute | solution.py:174
  22.7 0.0 collective-permute-done.4.ca
  22.7 13.4 %collective-permute-done.5.cb = f32[2,3,13,8,128]{4,3,2,1,0:T(8,128)S(1)} collective-permute-done((f32[2,3,13,8,128]{4,3,2,1,0:T(8,128)S(1)}, f32[2,3,13,8,128]{4,3,2,1,0:T(8,128)S(1)}, u32[]{:S(2)}, u32[]{:S(2)}) %collective-permute-start.5) | collective-permute-done | bytes 319520 | tf_op jit(solution)/shard_map/ppermute | solution.py:174
  36.0 0.0 collective-permute-done.xa
  36.0 0.0 collective-permute-done.1.xb
  36.0 9.6 %first_round.1 = (f32[16,40,8,128]{3,2,1,0:T(8,128)S(1)}, f32[16,40,8,128]{3,2,1,0:T(8,128)S(1)}, f32[16,40,8,128]{3,2,1,0:T(8,128)S(1)}, f32[16,40,8,128]{3,2,1...) custom-call(f32[16,40,8,128]{3,2,1,0:T(8,128)S(1)} %get-tuple-elemen, ...), custom_call_target="tpu_custom_call", output_to_operand_aliasing={{0}: (0, {}), {1}: (1, {}), {2}: (2, {}), {3}: (3, {})} | custom-call | tf_op jit(solution)/shard_map/first_round/pallas_call | solution.py:311
  45.7 0.0 copy-start
  45.7 0.0 copy-start.2
  45.7 3.4 %collective-permute-start.8 = (f32[8,4,8,128]{3,2,1,0:T(8,128)S(1)}, f32[8,4,8,128]{3,2,1,0:T(8,128)S(1)}, u32[]{:S(2)}, u32[]{:S(2)}) collective-permute-start(f32[8,4,8,128]{3,2,1,0:T(8,128)S(1)} %get-tuple-element.52), channel_id=1, source_target_pairs={{0,1},{1,0},{2,3},{3,2},{4,5},{5,4},{6,7},{7,6},{8,9},{9,8},{10,11... | collective-permute-start | bytes 393224 | tf_op jit(solution)/shard_map/ppermute | solution.py:174
  49.1 0.7 collective-permute-start.9
  49.8 0.0 copy-done.13
  49.8 0.6 convert_element_type.9
  50.4 0.0 collective-permute-start.6
  50.4 3.9 %collective-permute-start.7 = (f32[4,32,8,128]{3,2,1,0:T(8,128)}, f32[4,32,8,128]{3,2,1,0:T(8,128)}, u32[]{:S(2)}, u32[]{:S(2)}) collective-permute-start(f32[4,32,8,128]{3,2,1,0:T(8,128)} %get-tuple-element.51), channel_id=1, source_target_pairs={{8,16},{16,8},{24,32},{32,24},{40,48},{48,40},{56,64},{64,56},{72,... | collective-permute-start | bytes 1572872 | tf_op jit(solution)/shard_map/ppermute | solution.py:174
  54.3 0.0 collective-permute-done.8.ya
  54.3 0.0 collective-permute-done.9.yb
  54.3 0.0 copy-start.9
  54.3 0.3 corners.4
  54.7 0.1 collective-permute-start.10
  54.7 3.9 %collective-permute-start.11 = (f32[2,3,4,8,128]{4,3,2,1,0:T(8,128)S(1)}, f32[2,3,4,8,128]{4,3,2,1,0:T(8,128)S(1)}, u32[]{:S(2)}, u32[]{:S(2)}) collective-permute-start(f32[2,3,4,8,128]{4,3,2,1,0:T(8,128)S(1)} %get-tuple-element.55), channel_id=1, source_target_pairs={{8,16},{16,8},{24,32},{32,24},{40,48},{48,40},{56,64},{64,56},{72,... | collective-permute-start | bytes 294920 | tf_op jit(solution)/shard_map/ppermute | solution.py:174
  58.7 0.0 copy-done.9
  58.7 0.2 convert_reduce_fusion
  58.9 0.0 copy-start.11
  58.9 0.0 collective-permute-done.10.ca
  58.9 3.5 %collective-permute-done.11.cb = f32[2,3,4,8,128]{4,3,2,1,0:T(8,128)S(1)} collective-permute-done((f32[2,3,4,8,128]{4,3,2,1,0:T(8,128)S(1)}, f32[2,3,4,8,128]{4,3,2,1,0:T(8,128)S(1)}, u32[]{:S(2)}, u32[]{:S(2)}) %collective-permute-start.11) | collective-permute-done | bytes 98336 | tf_op jit(solution)/shard_map/ppermute | solution.py:174
  62.4 0.0 collective-permute-done.6.xa
  62.4 0.0 collective-permute-done.7.xb
  62.4 0.0 copy-done
  62.4 0.0 copy-done.2
  62.4 9.1 %later_round.1 = (f32[16,40,8,128]{3,2,1,0:T(8,128)S(1)}, f32[8,32,8,128]{3,2,1,0:T(8,128)S(1)}, f32[4,32,8,128]{3,2,1,0:T(8,128)}, f32[4,32,8,128]{3,2,1,0:T(8,...) custom-call(f32[16,40,8,128]{3,2,1,0:T(8,128)S(1)} %get-tuple-elemen, ...), custom_call_target="tpu_custom_call", output_to_operand_aliasing={{0}: (4, {}), {1}: (5, {})} | custom-call | tf_op jit(solution)/shard_map/later_round/pallas_call | solution.py:342
  71.6 0.0 copy-start.4
  71.6 1.0 copy-done.4
  72.6 3.7 %collective-permute-start.14 = (f32[8,4,8,128]{3,2,1,0:T(8,128)S(1)}, f32[8,4,8,128]{3,2,1,0:T(8,128)S(1)}, u32[]{:S(2)}, u32[]{:S(2)}) collective-permute-start(f32[8,4,8,128]{3,2,1,0:T(8,128)S(1)} %get-tuple-element.60), channel_id=1, source_target_pairs={{0,1},{1,0},{2,3},{3,2},{4,5},{5,4},{6,7},{7,6},{8,9},{9,8},{10,11... | collective-permute-start | bytes 393224 | tf_op jit(solution)/shard_map/ppermute | solution.py:174
  76.3 0.7 collective-permute-start.15
  77.0 0.3 fusion.1.slots
  77.3 0.1 collective-permute-start.12
  77.4 7.3 %collective-permute-start.13 = (f32[4,32,8,128]{3,2,1,0:T(8,128)}, f32[4,32,8,128]{3,2,1,0:T(8,128)}, u32[]{:S(2)}, u32[]{:S(2)}) collective-permute-start(f32[4,32,8,128]{3,2,1,0:T(8,128)} %get-tuple-element.59), channel_id=1, source_target_pairs={{8,16},{16,8},{24,32},{32,24},{40,48},{48,40},{56,64},{64,56},{72,... | collective-permute-start | bytes 1572872 | tf_op jit(solution)/shard_map/ppermute | solution.py:174
  84.8 0.0 collective-permute-done.14.ya
  84.8 0.0 collective-permute-done.15.yb
  84.8 0.0 copy-start.10
  84.8 0.0 copy-start.12
  84.8 0.0 copy-start.5
  84.8 0.0 copy-start.7
  84.8 0.0 copy-start.8
  84.9 0.3 corners.5
  85.2 0.1 collective-permute-start.16
  85.3 6.6 %collective-permute-start.17 = (f32[2,3,4,8,128]{4,3,2,1,0:T(8,128)S(1)}, f32[2,3,4,8,128]{4,3,2,1,0:T(8,128)S(1)}, u32[]{:S(2)}, u32[]{:S(2)}) collective-permute-start(f32[2,3,4,8,128]{4,3,2,1,0:T(8,128)S(1)} %get-tuple-element.63), channel_id=1, source_target_pairs={{8,16},{16,8},{24,32},{32,24},{40,48},{48,40},{56,64},{64,56},{72,... | collective-permute-start | bytes 294920 | tf_op jit(solution)/shard_map/ppermute | solution.py:174
  91.9 0.0 collective-permute-done.16.ca
  91.9 2.2 %collective-permute-done.17.cb = f32[2,3,4,8,128]{4,3,2,1,0:T(8,128)S(1)} collective-permute-done((f32[2,3,4,8,128]{4,3,2,1,0:T(8,128)S(1)}, f32[2,3,4,8,128]{4,3,2,1,0:T(8,128)S(1)}, u32[]{:S(2)}, u32[]{:S(2)}) %collective-permute-start.17) | collective-permute-done | bytes 98336 | tf_op jit(solution)/shard_map/ppermute | solution.py:174
  94.1 0.0 collective-permute-done.12.xa
  94.1 0.0 collective-permute-done.13.xb
  94.2 0.0 copy-start.6
  94.2 11.1 %last_round.1 = (f32[8,32,1024]{2,1,0:T(8,128)}, f32[1152,128]{1,0:T(8,128)S(1)}, f32[16,40,8,128]{3,2,1,0:T(8,128)S(1)}, f32[8,32,8,128]{3,2,1,0:T(8,128)S(1)}) custom-call(s32[256]{0:T(256)S(1)} %copy-done.8, s32[256]{0:T(256)S(1)} %multiply_add_fusion.targets, s32[256,128]{1,0:T(8,128)S(1)} %copy-done.7, ...), custom_call_target="tpu_custom_call", output_to_operand_aliasing={{2}: (8, {}), {3}: (9, {})} | custom-call | tf_op jit(solution)/shard_map/last_round/pallas_call | solution.py:387
  105.3 34.2 %all_to_all.5 = f32[128,1,1152]{2,1,0:T(1,128)S(1)} all-to-all(f32[128,1,1152]{2,1,0:T(1,128)S(1)} %bitcast.4), channel_id=1, replica_groups=mesh['gx'=16,'gy'=8] {'gx','gy'}, dimensions={0} | all-to-all | bytes 1179648 | tf_op jit(solution)/shard_map/all_to_all | solution.py:464
  139.5 1.4 finish.1
  (15 shorter events, 0.0 us)
Async XLA Ops:
  5.1 11.2 %collective-permute-start.2 = (f32[8,13,8,128]{3,2,1,0:T(8,128)S(1)}, f32[8,13,8,128]{3,2,1,0:T(8,128)S(1)}, u32[]{:S(2)}, u32[]{:S(2)}) collective-permute-start(f32[8,13,8,128]{3,2,1,0:T(8,128)S(1)} %get-tuple-element.40), channel_id=1, source_target_pairs={{0,1},{1,0},{2,3},{3,2},{4,5},{5,4},{6,7},{7,6},{8,9},{9,8},{10,11... | collective-permute-start | bytes 1277960 | tf_op jit(solution)/shard_map/ppermute | solution.py:174
  7.2 9.0 %collective-permute-start.3 = (f32[8,13,8,128]{3,2,1,0:T(8,128)S(1)}, f32[8,13,8,128]{3,2,1,0:T(8,128)S(1)}, u32[]{:S(2)}, u32[]{:S(2)}) collective-permute-start(f32[8,13,8,128]{3,2,1,0:T(8,128)S(1)} %get-tuple-element.41), channel_id=1, source_target_pairs={{1,2},{2,1},{3,4},{4,3},{5,6},{6,5},{9,10},{10,9},{11,12},{12,11},... | collective-permute-start | bytes 1277960 | tf_op jit(solution)/shard_map/ppermute | solution.py:174
  7.9 28.1 %collective-permute-start = (f32[13,32,8,128]{3,2,1,0:T(8,128)}, f32[13,32,8,128]{3,2,1,0:T(8,128)}, u32[]{:S(2)}, u32[]{:S(2)}) collective-permute-start(f32[13,32,8,128]{3,2,1,0:T(8,128)} %get-tuple-element.38), channel_id=1, source_target_pairs={{0,8},{8,0},{16,24},{24,16},{32,40},{40,32},{48,56},{56,48},{64,72... | collective-permute-start | bytes 5111816 | tf_op jit(solution)/shard_map/ppermute | solution.py:174
  9.0 27.1 %collective-permute-start.1 = (f32[13,32,8,128]{3,2,1,0:T(8,128)}, f32[13,32,8,128]{3,2,1,0:T(8,128)}, u32[]{:S(2)}, u32[]{:S(2)}) collective-permute-start(f32[13,32,8,128]{3,2,1,0:T(8,128)} %get-tuple-element.39), channel_id=1, source_target_pairs={{8,16},{16,8},{24,32},{32,24},{40,48},{48,40},{56,64},{64,56},{72,... | collective-permute-start | bytes 5111816 | tf_op jit(solution)/shard_map/ppermute | solution.py:174
  17.1 5.5 %collective-permute-start.4 = (f32[2,3,13,8,128]{4,3,2,1,0:T(8,128)S(1)}, f32[2,3,13,8,128]{4,3,2,1,0:T(8,128)S(1)}, u32[]{:S(2)}, u32[]{:S(2)}) collective-permute-start(f32[2,3,13,8,128]{4,3,2,1,0:T(8,128)S(1)} %get-tuple-element.42), channel_id=1, source_target_pairs={{0,8},{8,0},{16,24},{24,16},{32,40},{40,32},{48,56},{56,48},{64,72... | collective-permute-start | bytes 958472 | tf_op jit(solution)/shard_map/ppermute | solution.py:174
  19.0 17.1 %collective-permute-start.5 = (f32[2,3,13,8,128]{4,3,2,1,0:T(8,128)S(1)}, f32[2,3,13,8,128]{4,3,2,1,0:T(8,128)S(1)}, u32[]{:S(2)}, u32[]{:S(2)}) collective-permute-start(f32[2,3,13,8,128]{4,3,2,1,0:T(8,128)S(1)} %get-tuple-element.43), channel_id=1, source_target_pairs={{8,16},{16,8},{24,32},{32,24},{40,48},{48,40},{56,64},{64,56},{72,... | collective-permute-start | bytes 958472 | tf_op jit(solution)/shard_map/ppermute | solution.py:174
  36.0 13.7 %copy-start.13 = (s32[256]{0:T(256)S(1)}, s32[256]{0:T(256)}, u32[]{:S(2)}) copy-start(s32[256]{0:T(256)} %param.11) | copy-start | bytes 3076
  45.7 16.8 %copy-start = (f32[16,40,8,128]{3,2,1,0:T(8,128)}, f32[16,40,8,128]{3,2,1,0:T(8,128)S(1)}, u32[]{:S(2)}) copy-start(f32[16,40,8,128]{3,2,1,0:T(8,128)S(1)} %get-tuple-element.44.bx) | copy-start | bytes 7864324
  45.7 16.8 %copy-start.2 = (f32[16,40,8,128]{3,2,1,0:T(8,128)}, f32[16,40,8,128]{3,2,1,0:T(8,128)S(1)}, u32[]{:S(2)}) copy-start(f32[16,40,8,128]{3,2,1,0:T(8,128)S(1)} %get-tuple-element.45.by) | copy-start | bytes 7864324
  45.7 8.6 %collective-permute-start.8 = (f32[8,4,8,128]{3,2,1,0:T(8,128)S(1)}, f32[8,4,8,128]{3,2,1,0:T(8,128)S(1)}, u32[]{:S(2)}, u32[]{:S(2)}) collective-permute-start(f32[8,4,8,128]{3,2,1,0:T(8,128)S(1)} %get-tuple-element.52), channel_id=1, source_target_pairs={{0,1},{1,0},{2,3},{3,2},{4,5},{5,4},{6,7},{7,6},{8,9},{9,8},{10,11... | collective-permute-start | bytes 393224 | tf_op jit(solution)/shard_map/ppermute | solution.py:174
  49.1 5.2 %collective-permute-start.9 = (f32[8,4,8,128]{3,2,1,0:T(8,128)S(1)}, f32[8,4,8,128]{3,2,1,0:T(8,128)S(1)}, u32[]{:S(2)}, u32[]{:S(2)}) collective-permute-start(f32[8,4,8,128]{3,2,1,0:T(8,128)S(1)} %get-tuple-element.53), channel_id=1, source_target_pairs={{1,2},{2,1},{3,4},{4,3},{5,6},{6,5},{9,10},{10,9},{11,12},{12,11},... | collective-permute-start | bytes 393224 | tf_op jit(solution)/shard_map/ppermute | solution.py:174
  50.4 12.1 %collective-permute-start.6 = (f32[4,32,8,128]{3,2,1,0:T(8,128)}, f32[4,32,8,128]{3,2,1,0:T(8,128)}, u32[]{:S(2)}, u32[]{:S(2)}) collective-permute-start(f32[4,32,8,128]{3,2,1,0:T(8,128)} %get-tuple-element.50), channel_id=1, source_target_pairs={{0,8},{8,0},{16,24},{24,16},{32,40},{40,32},{48,56},{56,48},{64,72... | collective-permute-start | bytes 1572872 | tf_op jit(solution)/shard_map/ppermute | solution.py:174
  50.4 12.1 %collective-permute-start.7 = (f32[4,32,8,128]{3,2,1,0:T(8,128)}, f32[4,32,8,128]{3,2,1,0:T(8,128)}, u32[]{:S(2)}, u32[]{:S(2)}) collective-permute-start(f32[4,32,8,128]{3,2,1,0:T(8,128)} %get-tuple-element.51), channel_id=1, source_target_pairs={{8,16},{16,8},{24,32},{32,24},{40,48},{48,40},{56,64},{64,56},{72,... | collective-permute-start | bytes 1572872 | tf_op jit(solution)/shard_map/ppermute | solution.py:174
  54.3 4.4 %copy-start.9 = (s32[256,1]{0,1:T(1,128)S(1)}, s32[256,1]{0,1:T(1,128)}, u32[]{:S(2)}) copy-start(s32[256,1]{0,1:T(1,128)} %param.10) | copy-start | bytes 3076
  54.7 4.2 %collective-permute-start.10 = (f32[2,3,4,8,128]{4,3,2,1,0:T(8,128)S(1)}, f32[2,3,4,8,128]{4,3,2,1,0:T(8,128)S(1)}, u32[]{:S(2)}, u32[]{:S(2)}) collective-permute-start(f32[2,3,4,8,128]{4,3,2,1,0:T(8,128)S(1)} %get-tuple-element.54), channel_id=1, source_target_pairs={{0,8},{8,0},{16,24},{24,16},{32,40},{40,32},{48,56},{56,48},{64,72... | collective-permute-start | bytes 294920 | tf_op jit(solution)/shard_map/ppermute | solution.py:174
  54.7 7.7 %collective-permute-start.11 = (f32[2,3,4,8,128]{4,3,2,1,0:T(8,128)S(1)}, f32[2,3,4,8,128]{4,3,2,1,0:T(8,128)S(1)}, u32[]{:S(2)}, u32[]{:S(2)}) collective-permute-start(f32[2,3,4,8,128]{4,3,2,1,0:T(8,128)S(1)} %get-tuple-element.55), channel_id=1, source_target_pairs={{8,16},{16,8},{24,32},{32,24},{40,48},{48,40},{56,64},{64,56},{72,... | collective-permute-start | bytes 294920 | tf_op jit(solution)/shard_map/ppermute | solution.py:174
  58.9 18.1 %copy-start.11 = (s32[256]{0:T(256)}, s32[256]{0:T(256)S(1)}, u32[]{:S(2)}) copy-start(s32[256]{0:T(256)S(1)} %convert_reduce_fusion) | copy-start | bytes 3076
  62.4 14.5 %copy-start.14 = (f32[256]{0:T(256)S(1)}, f32[256]{0:T(256)}, u32[]{:S(2)}) copy-start(f32[256]{0:T(256)} %convert_element_type.9) | copy-start | bytes 3076
  71.6 1.0 copy-start.4
  72.6 12.2 %collective-permute-start.14 = (f32[8,4,8,128]{3,2,1,0:T(8,128)S(1)}, f32[8,4,8,128]{3,2,1,0:T(8,128)S(1)}, u32[]{:S(2)}, u32[]{:S(2)}) collective-permute-start(f32[8,4,8,128]{3,2,1,0:T(8,128)S(1)} %get-tuple-element.60), channel_id=1, source_target_pairs={{0,1},{1,0},{2,3},{3,2},{4,5},{5,4},{6,7},{7,6},{8,9},{9,8},{10,11... | collective-permute-start | bytes 393224 | tf_op jit(solution)/shard_map/ppermute | solution.py:174
  76.3 8.5 %collective-permute-start.15 = (f32[8,4,8,128]{3,2,1,0:T(8,128)S(1)}, f32[8,4,8,128]{3,2,1,0:T(8,128)S(1)}, u32[]{:S(2)}, u32[]{:S(2)}) collective-permute-start(f32[8,4,8,128]{3,2,1,0:T(8,128)S(1)} %get-tuple-element.61), channel_id=1, source_target_pairs={{1,2},{2,1},{3,4},{4,3},{5,6},{6,5},{9,10},{10,9},{11,12},{12,11},... | collective-permute-start | bytes 393224 | tf_op jit(solution)/shard_map/ppermute | solution.py:174
  77.3 16.8 %collective-permute-start.12 = (f32[4,32,8,128]{3,2,1,0:T(8,128)}, f32[4,32,8,128]{3,2,1,0:T(8,128)}, u32[]{:S(2)}, u32[]{:S(2)}) collective-permute-start(f32[4,32,8,128]{3,2,1,0:T(8,128)} %get-tuple-element.58), channel_id=1, source_target_pairs={{0,8},{8,0},{16,24},{24,16},{32,40},{40,32},{48,56},{56,48},{64,72... | collective-permute-start | bytes 1572872 | tf_op jit(solution)/shard_map/ppermute | solution.py:174
  77.4 16.7 %collective-permute-start.13 = (f32[4,32,8,128]{3,2,1,0:T(8,128)}, f32[4,32,8,128]{3,2,1,0:T(8,128)}, u32[]{:S(2)}, u32[]{:S(2)}) collective-permute-start(f32[4,32,8,128]{3,2,1,0:T(8,128)} %get-tuple-element.59), channel_id=1, source_target_pairs={{8,16},{16,8},{24,32},{32,24},{40,48},{48,40},{56,64},{64,56},{72,... | collective-permute-start | bytes 1572872 | tf_op jit(solution)/shard_map/ppermute | solution.py:174
  84.8 7.1 %copy-start.10 = (s32[256,1]{0,1:T(1,128)S(1)}, s32[256,1]{0,1:T(1,128)}, u32[]{:S(2)}) copy-start(s32[256,1]{0,1:T(1,128)} %param.10) | copy-start | bytes 3076
  84.8 7.1 %copy-start.12 = (s32[256]{0:T(256)S(1)}, s32[256]{0:T(256)}, u32[]{:S(2)}) copy-start(s32[256]{0:T(256)} %copy-done.11) | copy-start | bytes 3076
  84.8 9.3 %copy-start.1 = (f32[16,40,8,128]{3,2,1,0:T(8,128)S(1)}, f32[16,40,8,128]{3,2,1,0:T(8,128)}, u32[]{:S(2)}) copy-start(f32[16,40,8,128]{3,2,1,0:T(8,128)} %copy-done) | copy-start | bytes 7864324
  84.8 9.3 %copy-start.3 = (f32[16,40,8,128]{3,2,1,0:T(8,128)S(1)}, f32[16,40,8,128]{3,2,1,0:T(8,128)}, u32[]{:S(2)}) copy-start(f32[16,40,8,128]{3,2,1,0:T(8,128)} %copy-done.2) | copy-start | bytes 7864324
  84.8 9.3 %copy-start.5 = (f32[8,32,8,128]{3,2,1,0:T(8,128)S(1)}, f32[8,32,8,128]{3,2,1,0:T(8,128)}, u32[]{:S(2)}) copy-start(f32[8,32,8,128]{3,2,1,0:T(8,128)} %copy-done.4) | copy-start | bytes 3145732
  84.8 9.3 %copy-start.7 = (s32[256,128]{1,0:T(8,128)S(1)}, s32[256,128]{1,0:T(8,128)}, u32[]{:S(2)}) copy-start(s32[256,128]{1,0:T(8,128)} %mask.1) | copy-start | bytes 393220
  84.8 9.3 %copy-start.8 = (s32[256]{0:T(256)S(1)}, s32[256]{0:T(256)}, u32[]{:S(2)}) copy-start(s32[256]{0:T(256)} %tile_rows.1) | copy-start | bytes 3076
  85.2 6.7 %collective-permute-start.16 = (f32[2,3,4,8,128]{4,3,2,1,0:T(8,128)S(1)}, f32[2,3,4,8,128]{4,3,2,1,0:T(8,128)S(1)}, u32[]{:S(2)}, u32[]{:S(2)}) collective-permute-start(f32[2,3,4,8,128]{4,3,2,1,0:T(8,128)S(1)} %get-tuple-element.62), channel_id=1, source_target_pairs={{0,8},{8,0},{16,24},{24,16},{32,40},{40,32},{48,56},{56,48},{64,72... | collective-permute-start | bytes 294920 | tf_op jit(solution)/shard_map/ppermute | solution.py:174
  85.3 8.8 %collective-permute-start.17 = (f32[2,3,4,8,128]{4,3,2,1,0:T(8,128)S(1)}, f32[2,3,4,8,128]{4,3,2,1,0:T(8,128)S(1)}, u32[]{:S(2)}, u32[]{:S(2)}) collective-permute-start(f32[2,3,4,8,128]{4,3,2,1,0:T(8,128)S(1)} %get-tuple-element.63), channel_id=1, source_target_pairs={{8,16},{16,8},{24,32},{32,24},{40,48},{48,40},{56,64},{64,56},{72,... | collective-permute-start | bytes 294920 | tf_op jit(solution)/shard_map/ppermute | solution.py:174
  94.2 45.3 %copy-start.6 = (f32[3,256,128]{2,1,0:T(8,128)S(1)}, f32[3,256,128]{2,1,0:T(8,128)}, u32[]{:S(2)}) copy-start(f32[3,256,128]{2,1,0:T(8,128)} %heights.1) | copy-start | bytes 1179652

commit v4 on v2

--- a/solution.py
+++ b/solution.py
@@ -84,7 +84,7 @@
 
 
 def fields_of(k):
-    return (("g", k, k), ("bx", k + 1, k), ("by", k, k + 1), ("bz", k, k))
+    return ((k, k, k - 1), (k + 1, k, k), (k, k + 1, k), (k, k, k - 1))
 
 
 def pack_kernel(k, g, beta, w, bx, by, bz, xa, xb, ya, yb, nat, in_sems, out_sems):
@@ -116,7 +116,7 @@
     out = Copies(out_sems)
     for axis, ab, strip in (("gy", "a", ya), ("gy", "b", yb), ("gx", "b", xb), ("gx", "a", xa)):
         at = 0
-        for field, (_, in_x, in_y) in zip(fields, fields_of(k)):
+        for field, (in_x, in_y, _) in zip(fields, fields_of(k)):
             n = in_x if axis == "gx" else in_y
             first = sides.send(axis, ab, n) + K
             if axis == "gx":
@@ -144,25 +144,33 @@
     )(*(pltpu.with_memory_space_constraint(array, pltpu.HBM) for array in (g, beta)))
 
 
-def corner_kernel(planes, ya, yb, ca, cb, sems):
+def corner_kernel(planes, counts, ya, yb, ca, cb, sems):
     sides = Sides()
     out = Copies(sems)
     for ab, corner in (("b", cb), ("a", ca)):
         first = sides.send("gx", ab, planes)
-        out.start(ya.at[pl.ds(first, planes)], corner.at[0])
-        out.start(yb.at[pl.ds(first, planes)], corner.at[1])
+        for j, (other, strip) in enumerate((("a", ya), ("b", yb))):
+            at = done = 0
+            for n, kept in counts:
+                skip = jnp.where(sides.above["gy", other], 0, n - kept)
+                out.start(
+                    strip.at[pl.ds(first, planes), pl.ds(at + skip, kept)],
+                    corner.at[j, :, done : done + kept],
+                )
+                at, done = at + n, done + kept
     out.wait()
 
 
-def corners(planes, ya, yb):
-    shape = rows_shape(2, planes, ya.shape[1])
+def corners(planes, counts, ya, yb):
+    shape = rows_shape(2, planes, sum(kept for _, kept in counts))
     return pl.pallas_call(
-        functools.partial(corner_kernel, planes),
+        functools.partial(corner_kernel, planes, counts),
         out_shape=(shape, shape),
         in_specs=[ANY] * 2,
         out_specs=(ANY,) * 2,
-        scratch_shapes=[pltpu.SemaphoreType.DMA((4,))],
+        scratch_shapes=[pltpu.SemaphoreType.DMA((4 * len(counts),))],
         compiler_params=pltpu.CompilerParams(vmem_limit_bytes=MIB),
+        cost_estimate=pl.CostEstimate(flops=10**10, bytes_accessed=MIB, transcendentals=0),
         name="corners",
     )(ya, yb)
 
@@ -173,29 +181,29 @@
     return lax.ppermute(array, axis, [(i, j) for i, j in pairs if 0 <= j < size])
 
 
-def exchange(planes, xa, xb, ya, yb):
+def exchange(planes, counts, xa, xb, ya, yb):
     ya, yb = swap(ya, "gy", "a"), swap(yb, "gy", "b")
     xb, xa = swap(xb, "gx", "b"), swap(xa, "gx", "a")
-    ca, cb = corners(planes, ya, yb)
+    ca, cb = corners(planes, counts, ya, yb)
     cb, ca = swap(cb, "gx", "b"), swap(ca, "gx", "a")
     return xa, xb, ya, yb, ca, cb
 
 
 def land_first(k, sides, into, xs, ys, cs, fields):
-    at_x = at_y = 0
-    for i, (_, in_x, in_y) in enumerate(fields_of(k)):
+    at_x = at_y = at_c = 0
+    for i, (in_x, in_y, in_c) in enumerate(fields_of(k)):
         for ab in ("a", "b"):
             x, y = sides.land("gx", ab, in_x), sides.land("gy", ab, in_y)
             into.start(xs[ab].at[at_x : at_x + in_x], fields[i].at[pl.ds(x, in_x), K : K + NY])
             into.start(ys[ab].at[:, at_y : at_y + in_y], fields[i].at[K : K + NX, pl.ds(y, in_y)])
             x = sides.land("gx", ab, k)
             for j, other in enumerate(("a", "b")):
-                y = sides.land("gy", other, in_y)
+                y = sides.land("gy", other, in_c)
                 into.start(
-                    cs[ab].at[j, :, at_y : at_y + in_y],
-                    fields[i].at[pl.ds(x, k), pl.ds(y, in_y)],
+                    cs[ab].at[j, :, at_c : at_c + in_c],
+                    fields[i].at[pl.ds(x, k), pl.ds(y, in_c)],
                 )
-        at_x, at_y = at_x + in_x, at_y + in_y
+        at_x, at_y, at_c = at_x + in_x, at_y + in_y, at_c + in_c
 
 
 def land_later(k, sides, into, xs, ys, cs, w):
@@ -205,8 +213,8 @@
         into.start(ys[ab], w.at[K : K + NX, pl.ds(y, k)])
         x = sides.land("gx", ab, k - 1)
         for j, other in enumerate(("a", "b")):
-            y = sides.land("gy", other, k)
-            into.start(cs[ab].at[j], w.at[pl.ds(x, k - 1), pl.ds(y, k)])
+            y = sides.land("gy", other, k - 1)
+            into.start(cs[ab].at[j], w.at[pl.ds(x, k - 1), pl.ds(y, k - 1)])
 
 
 def chunks(low, high, size=8):
@@ -231,40 +239,38 @@
 
 def one_step(step, reach, last, w, new, bx, by, bz, inv, acc):
     omega = omega_of(step)
-
-    def run(x, y, n, inside):
-        around = w[x, y - 1 : y + n + 1]
-        centre = around[1:-1]
-        beside = by[x, y - 1 : y + n]
-        along = bz[x, y : y + n]
-        total = bx[x, y : y + n] * w[x + 1, y : y + n] + bx[x - 1, y : y + n] * w[x - 1, y : y + n]
-        total = total + beside[1:] * around[2:] + beside[:-1] * around[:-2]
-        total = total + along * z_up(centre) + z_down(along * centre)
-        moved = centre + omega * (inv[x, y : y + n] * total - centre)
-        if not last:
-            new[x, y : y + n] = moved
-        if inside:
-            at = (x - K, slice(y - K, y - K + n))
-            term = omega * centre
-            if last:
-                term = term + omega_of(step + 1) * moved
-            acc[at] = term if step == 0 else acc[at] + term
+    low, high = K - reach, K + NX + reach
+
+    def walk(y, n, rows_inside):
+        below = bx[low - 1, pl.ds(y, n)] * w[low - 1, pl.ds(y, n)]
+        around = w[low, pl.ds(y - 1, n + 2)]
+        for x in range(low, high):
+            above = w[x + 1, pl.ds(y - 1, n + 2)]
+            centre = around[1:-1]
+            link = bx[x, pl.ds(y, n)]
+            beside = by[x, pl.ds(y - 1, n + 1)]
+            along = bz[x, pl.ds(y, n)]
+            total = link * above[1:-1] + below
+            total = total + beside[1:] * around[2:] + beside[:-1] * around[:-2]
+            total = total + along * z_up(centre) + z_down(along * centre)
+            moved = centre + omega * (inv[x, pl.ds(y, n)] * total - centre)
+            if not last:
+                new[x, pl.ds(y, n)] = moved
+            if rows_inside and K <= x < K + NX:
+                at = (x - K, pl.ds(y - K, n))
+                term = omega * centre
+                if last:
+                    term = term + omega_of(step + 1) * moved
+                acc[at] = term if step == 0 else acc[at] + term
+            below, around = link * centre, above
 
     if reach:
-
-        @pl.loop(0, 2 * reach)
-        def _(i):
-            x = jnp.where(i < reach, K - reach + i, K + NX - reach + i)
-            for y, n in chunks(K - reach, K + NY + reach):
-                run(x, y, n, False)
-
-    @pl.loop(K, K + NX)
-    def _(x):
-        if reach:
-            run(x, K - reach, reach, False)
-            run(x, K + NY, reach, False)
-        for y, n in chunks(K, K + NY):
-            run(x, y, n, True)
+        walk(K - reach, reach, False)
+        walk(K + NY, reach, False)
+
+    @pl.loop(0, NY // 8)
+    def _(i):
+        walk(K + i * 8, 8, True)
 
 
 def steps_of(first, k, last, w, bx, by, bz, inv, acc):
@@ -450,14 +456,14 @@
     targets, slots = routes(tile_owner, tile_slot, peers)
     k = ROUNDS[0]
     packed = pack(k, grad_pressure, beta)
-    coeffs, state, strips = first_round(k, ROUNDS[1], *packed[:4], *exchange(k, *packed[4:]))
+    coeffs, state, strips = first_round(k, ROUNDS[1], *packed[:4], *exchange(k, [f[1:] for f in fields_of(k)], *packed[4:]))
     done = k
     for k, k_next in zip(ROUNDS[1:-1], ROUNDS[2:]):
-        state, strips = later_round(done, k, k_next, *coeffs, *state, *exchange(k - 1, *strips))
+        state, strips = later_round(done, k, k_next, *coeffs, *state, *exchange(k - 1, [(k, k - 1)], *strips))
         done += k
     k = ROUNDS[-1]
     grad_rhs, sent = last_round(
-        done, k, peers, tile_rows, targets, face_mask, slots, *coeffs, *state, *exchange(k - 1, *strips)
+        done, k, peers, tile_rows, targets, face_mask, slots, *coeffs, *state, *exchange(k - 1, [(k, k - 1)], *strips)
     )
     sent = sent.reshape(peers, 1, (CAP + 1) * 128)
     received = lax.all_to_all(sent, ("gx", "gy"), split_axis=0, concat_axis=0, tiled=True)

time: 139 us -> 128 us (0.921)
  Pallas kernels: 32.1 us -> 27.1 us
  waiting for transfers between devices: 22.3 us -> 19.5 us
  starting transfers between devices: 47.9 us -> 45.6 us
    ppermute x18, waiting for transfers between devices: 22.3 us -> 19.5 us  [swap(): lax.ppermute(array, axis, [(i, j) for i, j in pairs if 0 <= j < size])]
    ppermute x18, starting transfers between devices: 47.9 us -> 45.6 us  [swap(): lax.ppermute(array, axis, [(i, j) for i, j in pairs if 0 <= j < size])]
    pallas_call x1, Pallas kernels: 7.8 us -> 6.19 us  [later_round(): pl.pallas_call(functools.partial(later_kernel, first, k, k_next), out_sha...]
    pallas_call x1, Pallas kernels: 9.97 us -> 8.45 us  [last_round(): pl.pallas_call(functools.partial(last_kernel, first, k), out_shape=(jax.S...]
  transfers between devices with their start and end apart: 18 -> 18, of which waited for: 6 -> 4; matrix products, arithmetic and copies ran while one was open for 0% -> 0% of each run, Pallas kernels for 1% -> 0%
where the time goes in v4:
time: 128 us
  starting transfers between devices  45.6 us (36%)
  blocking collectives  34.1 us (27%)
  Pallas kernels  27.1 us (21%)
  waiting for transfers between devices  19.5 us (15%)
    ppermute x18, starting transfers between devices, swap(): lax.ppermute(array, axis, [(i, j) for i, j in pairs if 0 <= j < size])  45.6 us
    all_to_all x1, blocking collectives, shards(): lax.all_to_all(sent, ('gx', 'gy'), split_axis=0, concat_axis=0, tiled=True)  34.1 us
    ppermute x18, waiting for transfers between devices, swap(): lax.ppermute(array, axis, [(i, j) for i, j in pairs if 0 <= j < size])  19.5 us
    pallas_call x1, Pallas kernels, last_round(): pl.pallas_call(functools.partial(last_kernel, first, k), out_shape=(jax.S...  8.45 us
    pallas_call x1, Pallas kernels, first_round(): pl.pallas_call(functools.partial(first_kernel, k, k_next), out_shape=(EXT...  7.18 us
    pallas_call x1, Pallas kernels, later_round(): pl.pallas_call(functools.partial(later_kernel, first, k, k_next), out_sha...  6.19 us
    pallas_call x1, Pallas kernels, pack(): pl.pallas_call(functools.partial(pack_kernel, k), out_shape=(EXT,) * 4 +...  3.22 us
  transfers between devices with their start and end apart: 18, of which 4 were waited for; matrix products, arithmetic and copies ran while one was open for 0% of the time, Pallas kernels for 0%

profile of v4, /device:TPU:1, one launch (start us, length us, event | category | flops | bytes accessed | tf_op | source)
XLA Modules:
  0.0 127.7 jit_solution(1704405138412608640)
XLA Ops:
  0.6 3.2 %pack.1 = (f32[16,40,8,128]{3,2,1,0:T(8,128)S(1)}, f32[16,40,8,128]{3,2,1,0:T(8,128)S(1)}, f32[16,40,8,128]{3,2,1,0:T(8,128)S(1)}, f32[16,40,8,128]{3,2,1,0:T(8,...) custom-call(f32[8,32,1024]{2,1,0:T(8,128)} %g.1, ...), custom_call_target="tpu_custom_call" | custom-call | tf_op jit(solution)/shard_map/pack/pallas_call | solution.py:132
  3.9 1.5 %collective-permute-start = (f32[13,32,8,128]{3,2,1,0:T(8,128)S(1)}, f32[13,32,8,128]{3,2,1,0:T(8,128)S(1)}, u32[]{:S(2)}, u32[]{:S(2)}) collective-permute-start(f32[13,32,8,128]{3,2,1,0:T(8,128)S(1)} %get-tuple-element.38), channel_id=1, source_target_pairs={{0,8},{8,0},{16,24},{24,16},{32,40},{40,32},{48,56},{56,48},{64,72... | collective-permute-start | bytes 5111816 | tf_op jit(solution)/shard_map/ppermute | solution.py:181
  5.4 3.5 %collective-permute-start.1 = (f32[13,32,8,128]{3,2,1,0:T(8,128)S(1)}, f32[13,32,8,128]{3,2,1,0:T(8,128)S(1)}, u32[]{:S(2)}, u32[]{:S(2)}) collective-permute-start(f32[13,32,8,128]{3,2,1,0:T(8,128)S(1)} %get-tuple-element.39), channel_id=1, source_target_pairs={{8,16},{16,8},{24,32},{32,24},{40,48},{48,40},{56,64},{64,56},{72,... | collective-permute-start | bytes 5111816 | tf_op jit(solution)/shard_map/ppermute | solution.py:181
  8.9 1.3 %collective-permute-start.2 = (f32[8,13,8,128]{3,2,1,0:T(8,128)S(1)}, f32[8,13,8,128]{3,2,1,0:T(8,128)S(1)}, u32[]{:S(2)}, u32[]{:S(2)}) collective-permute-start(f32[8,13,8,128]{3,2,1,0:T(8,128)S(1)} %get-tuple-element.40), channel_id=1, source_target_pairs={{0,1},{1,0},{2,3},{3,2},{4,5},{5,4},{6,7},{7,6},{8,9},{9,8},{10,11... | collective-permute-start | bytes 1277960 | tf_op jit(solution)/shard_map/ppermute | solution.py:181
  10.2 0.7 collective-permute-start.3
  10.9 7.4 %collective-permute-done.2.ya = f32[8,13,8,128]{3,2,1,0:T(8,128)S(1)} collective-permute-done((f32[8,13,8,128]{3,2,1,0:T(8,128)S(1)}, f32[8,13,8,128]{3,2,1,0:T(8,128)S(1)}, u32[]{:S(2)}, u32[]{:S(2)}) %collective-permute-start.2) | collective-permute-done | bytes 426016 | tf_op jit(solution)/shard_map/ppermute | solution.py:181
  18.2 0.0 collective-permute-done.3.yb
  18.2 0.4 corners.3
  18.6 0.1 collective-permute-start.4
  18.7 5.5 %collective-permute-start.5 = (f32[2,3,10,8,128]{4,3,2,1,0:T(8,128)S(1)}, f32[2,3,10,8,128]{4,3,2,1,0:T(8,128)S(1)}, u32[]{:S(2)}, u32[]{:S(2)}) collective-permute-start(f32[2,3,10,8,128]{4,3,2,1,0:T(8,128)S(1)} %get-tuple-element.43), channel_id=1, source_target_pairs={{8,16},{16,8},{24,32},{32,24},{40,48},{48,40},{56,64},{64,56},{72,... | collective-permute-start | bytes 737288 | tf_op jit(solution)/shard_map/ppermute | solution.py:181
  24.3 0.0 collective-permute-done.4.ca
  24.3 6.8 %collective-permute-done.5.cb = f32[2,3,10,8,128]{4,3,2,1,0:T(8,128)S(1)} collective-permute-done((f32[2,3,10,8,128]{4,3,2,1,0:T(8,128)S(1)}, f32[2,3,10,8,128]{4,3,2,1,0:T(8,128)S(1)}, u32[]{:S(2)}, u32[]{:S(2)}) %collective-permute-start.5) | collective-permute-done | bytes 245792 | tf_op jit(solution)/shard_map/ppermute | solution.py:181
  31.1 0.0 collective-permute-done.xa
  31.1 0.0 collective-permute-done.1.xb
  31.1 0.0 copy-start.4
  31.1 7.2 %first_round.1 = (f32[16,40,8,128]{3,2,1,0:T(8,128)S(1)}, f32[16,40,8,128]{3,2,1,0:T(8,128)S(1)}, f32[16,40,8,128]{3,2,1,0:T(8,128)S(1)}, f32[16,40,8,128]{3,2,1...) custom-call(f32[16,40,8,128]{3,2,1,0:T(8,128)S(1)} %get-tuple-elemen, ...), custom_call_target="tpu_custom_call", output_to_operand_aliasing={{0}: (0, {}), {1}: (1, {}), {2}: (2, {}), {3}: (3, {})} | custom-call | tf_op jit(solution)/shard_map/first_round/pallas_call | solution.py:316
  38.3 1.4 %collective-permute-start.8 = (f32[8,4,8,128]{3,2,1,0:T(8,128)S(1)}, f32[8,4,8,128]{3,2,1,0:T(8,128)S(1)}, u32[]{:S(2)}, u32[]{:S(2)}) collective-permute-start(f32[8,4,8,128]{3,2,1,0:T(8,128)S(1)} %get-tuple-element.52), channel_id=1, source_target_pairs={{0,1},{1,0},{2,3},{3,2},{4,5},{5,4},{6,7},{7,6},{8,9},{9,8},{10,11... | collective-permute-start | bytes 393224 | tf_op jit(solution)/shard_map/ppermute | solution.py:181
  39.7 0.7 collective-permute-start.9
  40.4 0.0 copy-done.4
  40.4 0.1 collective-permute-start.6
  40.5 0.0 copy-start.3
  40.5 4.0 %collective-permute-start.7 = (f32[4,32,8,128]{3,2,1,0:T(8,128)S(1)}, f32[4,32,8,128]{3,2,1,0:T(8,128)S(1)}, u32[]{:S(2)}, u32[]{:S(2)}) collective-permute-start(f32[4,32,8,128]{3,2,1,0:T(8,128)S(1)} %get-tuple-element.51), channel_id=1, source_target_pairs={{8,16},{16,8},{24,32},{32,24},{40,48},{48,40},{56,64},{64,56},{72,... | collective-permute-start | bytes 1572872 | tf_op jit(solution)/shard_map/ppermute | solution.py:181
  44.5 0.0 collective-permute-done.8.ya
  44.5 0.0 collective-permute-done.9.yb
  44.6 0.1 corners.4
  44.7 0.1 collective-permute-start.10
  44.8 3.9 %collective-permute-start.11 = (f32[2,3,3,8,128]{4,3,2,1,0:T(8,128)S(1)}, f32[2,3,3,8,128]{4,3,2,1,0:T(8,128)S(1)}, u32[]{:S(2)}, u32[]{:S(2)}) collective-permute-start(f32[2,3,3,8,128]{4,3,2,1,0:T(8,128)S(1)} %get-tuple-element.55), channel_id=1, source_target_pairs={{8,16},{16,8},{24,32},{32,24},{40,48},{48,40},{56,64},{64,56},{72,... | collective-permute-start | bytes 221192 | tf_op jit(solution)/shard_map/ppermute | solution.py:181
  48.7 0.0 copy-done.3
  48.7 0.2 convert_reduce_fusion
  48.9 0.0 collective-permute-done.10.ca
  48.9 3.3 %collective-permute-done.11.cb = f32[2,3,3,8,128]{4,3,2,1,0:T(8,128)S(1)} collective-permute-done((f32[2,3,3,8,128]{4,3,2,1,0:T(8,128)S(1)}, f32[2,3,3,8,128]{4,3,2,1,0:T(8,128)S(1)}, u32[]{:S(2)}, u32[]{:S(2)}) %collective-permute-start.11) | collective-permute-done | bytes 73760 | tf_op jit(solution)/shard_map/ppermute | solution.py:181
  52.2 0.0 collective-permute-done.6.xa
  52.2 0.0 collective-permute-done.7.xb
  52.2 6.2 %later_round.1 = (f32[16,40,8,128]{3,2,1,0:T(8,128)S(1)}, f32[8,32,8,128]{3,2,1,0:T(8,128)S(1)}, f32[4,32,8,128]{3,2,1,0:T(8,128)S(1)}, f32[4,32,8,128]{3,2,1,0:...) custom-call(f32[16,40,8,128]{3,2,1,0:T(8,128)S(1)} %get-tuple-elemen, ...), custom_call_target="tpu_custom_call", output_to_operand_aliasing={{0}: (4, {}), {1}: (5, {})} | custom-call | tf_op jit(solution)/shard_map/later_round/pallas_call | solution.py:347
  58.4 5.1 %collective-permute-start.14 = (f32[8,4,8,128]{3,2,1,0:T(8,128)S(1)}, f32[8,4,8,128]{3,2,1,0:T(8,128)S(1)}, u32[]{:S(2)}, u32[]{:S(2)}) collective-permute-start(f32[8,4,8,128]{3,2,1,0:T(8,128)S(1)} %get-tuple-element.60), channel_id=1, source_target_pairs={{0,1},{1,0},{2,3},{3,2},{4,5},{5,4},{6,7},{7,6},{8,9},{9,8},{10,11... | collective-permute-start | bytes 393224 | tf_op jit(solution)/shard_map/ppermute | solution.py:181
  63.5 0.7 collective-permute-start.15
  64.2 0.3 fusion.1.slots
  64.5 0.1 collective-permute-start.12
  64.6 0.0 copy-start.1
  64.6 0.0 copy-start.2
  64.6 11.5 %collective-permute-start.13 = (f32[4,32,8,128]{3,2,1,0:T(8,128)S(1)}, f32[4,32,8,128]{3,2,1,0:T(8,128)S(1)}, u32[]{:S(2)}, u32[]{:S(2)}) collective-permute-start(f32[4,32,8,128]{3,2,1,0:T(8,128)S(1)} %get-tuple-element.59), channel_id=1, source_target_pairs={{8,16},{16,8},{24,32},{32,24},{40,48},{48,40},{56,64},{64,56},{72,... | collective-permute-start | bytes 1572872 | tf_op jit(solution)/shard_map/ppermute | solution.py:181
  76.1 0.0 collective-permute-done.14.ya
  76.1 0.0 collective-permute-done.15.yb
  76.1 0.1 corners.5
  76.3 0.1 collective-permute-start.16
  76.4 5.4 %collective-permute-start.17 = (f32[2,3,3,8,128]{4,3,2,1,0:T(8,128)S(1)}, f32[2,3,3,8,128]{4,3,2,1,0:T(8,128)S(1)}, u32[]{:S(2)}, u32[]{:S(2)}) collective-permute-start(f32[2,3,3,8,128]{4,3,2,1,0:T(8,128)S(1)} %get-tuple-element.63), channel_id=1, source_target_pairs={{8,16},{16,8},{24,32},{32,24},{40,48},{48,40},{56,64},{64,56},{72,... | collective-permute-start | bytes 221192 | tf_op jit(solution)/shard_map/ppermute | solution.py:181
  81.7 0.0 collective-permute-done.16.ca
  81.8 2.0 %collective-permute-done.17.cb = f32[2,3,3,8,128]{4,3,2,1,0:T(8,128)S(1)} collective-permute-done((f32[2,3,3,8,128]{4,3,2,1,0:T(8,128)S(1)}, f32[2,3,3,8,128]{4,3,2,1,0:T(8,128)S(1)}, u32[]{:S(2)}, u32[]{:S(2)}) %collective-permute-start.17) | collective-permute-done | bytes 73760 | tf_op jit(solution)/shard_map/ppermute | solution.py:181
  83.8 0.0 collective-permute-done.12.xa
  83.8 0.0 collective-permute-done.13.xb
  83.8 0.0 copy-done.1
  83.8 0.0 copy-done.2
  83.8 0.0 copy-start
  83.8 8.5 %last_round.1 = (f32[8,32,1024]{2,1,0:T(8,128)}, f32[1152,128]{1,0:T(8,128)S(1)}, f32[16,40,8,128]{3,2,1,0:T(8,128)S(1)}, f32[8,32,8,128]{3,2,1,0:T(8,128)S(1)}) custom-call(s32[256]{0:T(256)S(1)} %copy-done.2, s32[256]{0:T(256)S(1)} %multiply_add_fusion.targets, s32[256,128]{1,0:T(8,128)S(1)} %copy-done.1, ...), custom_call_target="tpu_custom_call", output_to_operand_aliasing={{2}: (8, {}), {3}: (9, {})} | custom-call | tf_op jit(solution)/shard_map/last_round/pallas_call | solution.py:392
  92.2 34.1 %all_to_all.5 = f32[128,1,1152]{2,1,0:T(1,128)S(1)} all-to-all(f32[128,1,1152]{2,1,0:T(1,128)S(1)} %bitcast.4), channel_id=1, replica_groups=mesh['gx'=16,'gy'=8] {'gx','gy'}, dimensions={0} | all-to-all | bytes 1179648 | tf_op jit(solution)/shard_map/all_to_all | solution.py:469
  126.3 0.0 copy-done
  126.3 1.4 %finish.1 = f32[3,256,128]{2,1,0:T(8,128)} custom-call(f32[1152,128]{1,0:T(8,128)S(1)} %bitcast.3, f32[3,256,128]{2,1,0:T(8,128)S(1)} %copy-done), custom_call_target="tpu_custom_call" | custom-call | tf_op jit(solution)/shard_map/finish/pallas_call | solution.py:433
  (2 shorter events, 0.0 us)
Async XLA Ops:
  3.9 27.3 %collective-permute-start = (f32[13,32,8,128]{3,2,1,0:T(8,128)S(1)}, f32[13,32,8,128]{3,2,1,0:T(8,128)S(1)}, u32[]{:S(2)}, u32[]{:S(2)}) collective-permute-start(f32[13,32,8,128]{3,2,1,0:T(8,128)S(1)} %get-tuple-element.38), channel_id=1, source_target_pairs={{0,8},{8,0},{16,24},{24,16},{32,40},{40,32},{48,56},{56,48},{64,72... | collective-permute-start | bytes 5111816 | tf_op jit(solution)/shard_map/ppermute | solution.py:181
  5.4 25.8 %collective-permute-start.1 = (f32[13,32,8,128]{3,2,1,0:T(8,128)S(1)}, f32[13,32,8,128]{3,2,1,0:T(8,128)S(1)}, u32[]{:S(2)}, u32[]{:S(2)}) collective-permute-start(f32[13,32,8,128]{3,2,1,0:T(8,128)S(1)} %get-tuple-element.39), channel_id=1, source_target_pairs={{8,16},{16,8},{24,32},{32,24},{40,48},{48,40},{56,64},{64,56},{72,... | collective-permute-start | bytes 5111816 | tf_op jit(solution)/shard_map/ppermute | solution.py:181
  8.9 9.3 %collective-permute-start.2 = (f32[8,13,8,128]{3,2,1,0:T(8,128)S(1)}, f32[8,13,8,128]{3,2,1,0:T(8,128)S(1)}, u32[]{:S(2)}, u32[]{:S(2)}) collective-permute-start(f32[8,13,8,128]{3,2,1,0:T(8,128)S(1)} %get-tuple-element.40), channel_id=1, source_target_pairs={{0,1},{1,0},{2,3},{3,2},{4,5},{5,4},{6,7},{7,6},{8,9},{9,8},{10,11... | collective-permute-start | bytes 1277960 | tf_op jit(solution)/shard_map/ppermute | solution.py:181
  10.2 8.1 %collective-permute-start.3 = (f32[8,13,8,128]{3,2,1,0:T(8,128)S(1)}, f32[8,13,8,128]{3,2,1,0:T(8,128)S(1)}, u32[]{:S(2)}, u32[]{:S(2)}) collective-permute-start(f32[8,13,8,128]{3,2,1,0:T(8,128)S(1)} %get-tuple-element.41), channel_id=1, source_target_pairs={{1,2},{2,1},{3,4},{4,3},{5,6},{6,5},{9,10},{10,9},{11,12},{12,11},... | collective-permute-start | bytes 1277960 | tf_op jit(solution)/shard_map/ppermute | solution.py:181
  18.6 5.7 %collective-permute-start.4 = (f32[2,3,10,8,128]{4,3,2,1,0:T(8,128)S(1)}, f32[2,3,10,8,128]{4,3,2,1,0:T(8,128)S(1)}, u32[]{:S(2)}, u32[]{:S(2)}) collective-permute-start(f32[2,3,10,8,128]{4,3,2,1,0:T(8,128)S(1)} %get-tuple-element.42), channel_id=1, source_target_pairs={{0,8},{8,0},{16,24},{24,16},{32,40},{40,32},{48,56},{56,48},{64,72... | collective-permute-start | bytes 737288 | tf_op jit(solution)/shard_map/ppermute | solution.py:181
  18.7 12.4 %collective-permute-start.5 = (f32[2,3,10,8,128]{4,3,2,1,0:T(8,128)S(1)}, f32[2,3,10,8,128]{4,3,2,1,0:T(8,128)S(1)}, u32[]{:S(2)}, u32[]{:S(2)}) collective-permute-start(f32[2,3,10,8,128]{4,3,2,1,0:T(8,128)S(1)} %get-tuple-element.43), channel_id=1, source_target_pairs={{8,16},{16,8},{24,32},{32,24},{40,48},{48,40},{56,64},{64,56},{72,... | collective-permute-start | bytes 737288 | tf_op jit(solution)/shard_map/ppermute | solution.py:181
  31.1 9.2 %copy-start.4 = (s32[256]{0:T(256)S(1)}, s32[256]{0:T(256)}, u32[]{:S(2)}) copy-start(s32[256]{0:T(256)} %param.11) | copy-start | bytes 3076
  38.3 6.2 %collective-permute-start.8 = (f32[8,4,8,128]{3,2,1,0:T(8,128)S(1)}, f32[8,4,8,128]{3,2,1,0:T(8,128)S(1)}, u32[]{:S(2)}, u32[]{:S(2)}) collective-permute-start(f32[8,4,8,128]{3,2,1,0:T(8,128)S(1)} %get-tuple-element.52), channel_id=1, source_target_pairs={{0,1},{1,0},{2,3},{3,2},{4,5},{5,4},{6,7},{7,6},{8,9},{9,8},{10,11... | collective-permute-start | bytes 393224 | tf_op jit(solution)/shard_map/ppermute | solution.py:181
  39.7 4.8 %collective-permute-start.9 = (f32[8,4,8,128]{3,2,1,0:T(8,128)S(1)}, f32[8,4,8,128]{3,2,1,0:T(8,128)S(1)}, u32[]{:S(2)}, u32[]{:S(2)}) collective-permute-start(f32[8,4,8,128]{3,2,1,0:T(8,128)S(1)} %get-tuple-element.53), channel_id=1, source_target_pairs={{1,2},{2,1},{3,4},{4,3},{5,6},{6,5},{9,10},{10,9},{11,12},{12,11},... | collective-permute-start | bytes 393224 | tf_op jit(solution)/shard_map/ppermute | solution.py:181
  40.4 11.8 %collective-permute-start.6 = (f32[4,32,8,128]{3,2,1,0:T(8,128)S(1)}, f32[4,32,8,128]{3,2,1,0:T(8,128)S(1)}, u32[]{:S(2)}, u32[]{:S(2)}) collective-permute-start(f32[4,32,8,128]{3,2,1,0:T(8,128)S(1)} %get-tuple-element.50), channel_id=1, source_target_pairs={{0,8},{8,0},{16,24},{24,16},{32,40},{40,32},{48,56},{56,48},{64,72... | collective-permute-start | bytes 1572872 | tf_op jit(solution)/shard_map/ppermute | solution.py:181
  40.5 8.2 %copy-start.3 = (s32[256,1]{0,1:T(1,128)S(1)}, s32[256,1]{0,1:T(1,128)}, u32[]{:S(2)}) copy-start(s32[256,1]{0,1:T(1,128)} %param.10) | copy-start | bytes 3076
  40.5 11.7 %collective-permute-start.7 = (f32[4,32,8,128]{3,2,1,0:T(8,128)S(1)}, f32[4,32,8,128]{3,2,1,0:T(8,128)S(1)}, u32[]{:S(2)}, u32[]{:S(2)}) collective-permute-start(f32[4,32,8,128]{3,2,1,0:T(8,128)S(1)} %get-tuple-element.51), channel_id=1, source_target_pairs={{8,16},{16,8},{24,32},{32,24},{40,48},{48,40},{56,64},{64,56},{72,... | collective-permute-start | bytes 1572872 | tf_op jit(solution)/shard_map/ppermute | solution.py:181
  44.7 4.2 %collective-permute-start.10 = (f32[2,3,3,8,128]{4,3,2,1,0:T(8,128)S(1)}, f32[2,3,3,8,128]{4,3,2,1,0:T(8,128)S(1)}, u32[]{:S(2)}, u32[]{:S(2)}) collective-permute-start(f32[2,3,3,8,128]{4,3,2,1,0:T(8,128)S(1)} %get-tuple-element.54), channel_id=1, source_target_pairs={{0,8},{8,0},{16,24},{24,16},{32,40},{40,32},{48,56},{56,48},{64,72... | collective-permute-start | bytes 221192 | tf_op jit(solution)/shard_map/ppermute | solution.py:181
  44.8 7.4 %collective-permute-start.11 = (f32[2,3,3,8,128]{4,3,2,1,0:T(8,128)S(1)}, f32[2,3,3,8,128]{4,3,2,1,0:T(8,128)S(1)}, u32[]{:S(2)}, u32[]{:S(2)}) collective-permute-start(f32[2,3,3,8,128]{4,3,2,1,0:T(8,128)S(1)} %get-tuple-element.55), channel_id=1, source_target_pairs={{8,16},{16,8},{24,32},{32,24},{40,48},{48,40},{56,64},{64,56},{72,... | collective-permute-start | bytes 221192 | tf_op jit(solution)/shard_map/ppermute | solution.py:181
  58.4 17.7 %collective-permute-start.14 = (f32[8,4,8,128]{3,2,1,0:T(8,128)S(1)}, f32[8,4,8,128]{3,2,1,0:T(8,128)S(1)}, u32[]{:S(2)}, u32[]{:S(2)}) collective-permute-start(f32[8,4,8,128]{3,2,1,0:T(8,128)S(1)} %get-tuple-element.60), channel_id=1, source_target_pairs={{0,1},{1,0},{2,3},{3,2},{4,5},{5,4},{6,7},{7,6},{8,9},{9,8},{10,11... | collective-permute-start | bytes 393224 | tf_op jit(solution)/shard_map/ppermute | solution.py:181
  63.5 12.6 %collective-permute-start.15 = (f32[8,4,8,128]{3,2,1,0:T(8,128)S(1)}, f32[8,4,8,128]{3,2,1,0:T(8,128)S(1)}, u32[]{:S(2)}, u32[]{:S(2)}) collective-permute-start(f32[8,4,8,128]{3,2,1,0:T(8,128)S(1)} %get-tuple-element.61), channel_id=1, source_target_pairs={{1,2},{2,1},{3,4},{4,3},{5,6},{6,5},{9,10},{10,9},{11,12},{12,11},... | collective-permute-start | bytes 393224 | tf_op jit(solution)/shard_map/ppermute | solution.py:181
  64.5 19.2 %collective-permute-start.12 = (f32[4,32,8,128]{3,2,1,0:T(8,128)S(1)}, f32[4,32,8,128]{3,2,1,0:T(8,128)S(1)}, u32[]{:S(2)}, u32[]{:S(2)}) collective-permute-start(f32[4,32,8,128]{3,2,1,0:T(8,128)S(1)} %get-tuple-element.58), channel_id=1, source_target_pairs={{0,8},{8,0},{16,24},{24,16},{32,40},{40,32},{48,56},{56,48},{64,72... | collective-permute-start | bytes 1572872 | tf_op jit(solution)/shard_map/ppermute | solution.py:181
  64.6 19.2 %copy-start.1 = (s32[256,128]{1,0:T(8,128)S(1)}, s32[256,128]{1,0:T(8,128)}, u32[]{:S(2)}) copy-start(s32[256,128]{1,0:T(8,128)} %mask.1) | copy-start | bytes 393220
  64.6 19.2 %copy-start.2 = (s32[256]{0:T(256)S(1)}, s32[256]{0:T(256)}, u32[]{:S(2)}) copy-start(s32[256]{0:T(256)} %tile_rows.1) | copy-start | bytes 3076
  64.6 19.1 %collective-permute-start.13 = (f32[4,32,8,128]{3,2,1,0:T(8,128)S(1)}, f32[4,32,8,128]{3,2,1,0:T(8,128)S(1)}, u32[]{:S(2)}, u32[]{:S(2)}) collective-permute-start(f32[4,32,8,128]{3,2,1,0:T(8,128)S(1)} %get-tuple-element.59), channel_id=1, source_target_pairs={{8,16},{16,8},{24,32},{32,24},{40,48},{48,40},{56,64},{64,56},{72,... | collective-permute-start | bytes 1572872 | tf_op jit(solution)/shard_map/ppermute | solution.py:181
  76.3 5.5 %collective-permute-start.16 = (f32[2,3,3,8,128]{4,3,2,1,0:T(8,128)S(1)}, f32[2,3,3,8,128]{4,3,2,1,0:T(8,128)S(1)}, u32[]{:S(2)}, u32[]{:S(2)}) collective-permute-start(f32[2,3,3,8,128]{4,3,2,1,0:T(8,128)S(1)} %get-tuple-element.62), channel_id=1, source_target_pairs={{0,8},{8,0},{16,24},{24,16},{32,40},{40,32},{48,56},{56,48},{64,72... | collective-permute-start | bytes 221192 | tf_op jit(solution)/shard_map/ppermute | solution.py:181
  76.4 7.4 %collective-permute-start.17 = (f32[2,3,3,8,128]{4,3,2,1,0:T(8,128)S(1)}, f32[2,3,3,8,128]{4,3,2,1,0:T(8,128)S(1)}, u32[]{:S(2)}, u32[]{:S(2)}) collective-permute-start(f32[2,3,3,8,128]{4,3,2,1,0:T(8,128)S(1)} %get-tuple-element.63), channel_id=1, source_target_pairs={{8,16},{16,8},{24,32},{32,24},{40,48},{48,40},{56,64},{64,56},{72,... | collective-permute-start | bytes 221192 | tf_op jit(solution)/shard_map/ppermute | solution.py:181
  83.8 42.6 %copy-start = (f32[3,256,128]{2,1,0:T(8,128)S(1)}, f32[3,256,128]{2,1,0:T(8,128)}, u32[]{:S(2)}) copy-start(f32[3,256,128]{2,1,0:T(8,128)} %heights.1) | copy-start | bytes 1179652

commit v5 on v4

--- a/solution.py
+++ b/solution.py
@@ -78,6 +78,13 @@
         copy.start()
         self.all.append(copy)
 
+    def start_either(self, first, src, other, dst):
+        sem = self.sems.at[len(self.all)]
+        for wanted, ref in ((first, src), (jnp.logical_not(first), other)):
+            copy = pltpu.make_async_copy(ref, dst, sem)
+            pl.when(wanted)(copy.start)
+        self.all.append(copy)
+
     def wait(self):
         for copy in self.all:
             copy.wait()
@@ -87,7 +94,7 @@
     return ((k, k, k - 1), (k + 1, k, k), (k, k + 1, k), (k, k, k - 1))
 
 
-def pack_kernel(k, g, beta, w, bx, by, bz, xa, xb, ya, yb, nat, in_sems, out_sems):
+def pack_kernel(k, g, beta, w, bx, by, bz, xa, xb, xb_z, ya, yb, nat, in_sems, out_sems):
     sides = Sides()
     copies = []
     for x in range(NX):
@@ -120,7 +127,8 @@
             n = in_x if axis == "gx" else in_y
             first = sides.send(axis, ab, n) + K
             if axis == "gx":
-                out.start(field.at[pl.ds(first, n), K : K + NY], strip.at[at : at + n])
+                into = xb_z if ab == "b" and field is bz else strip.at[at : at + n]
+                out.start(field.at[pl.ds(first, n), K : K + NY], into)
             else:
                 out.start(field.at[K : K + NX, pl.ds(first, n)], strip.at[:, at : at + n])
             at += n
@@ -131,9 +139,10 @@
     n = 4 * k + 1
     return pl.pallas_call(
         functools.partial(pack_kernel, k),
-        out_shape=(EXT,) * 4 + (rows_shape(n, NY), rows_shape(n, NY), rows_shape(NX, n), rows_shape(NX, n)),
+        out_shape=(EXT,) * 4
+        + (rows_shape(n, NY), rows_shape(n - k, NY), rows_shape(k, NY), rows_shape(NX, n), rows_shape(NX, n)),
         in_specs=[HBM] * 2,
-        out_specs=(VMEM,) * 4 + (ANY,) * 4,
+        out_specs=(VMEM,) * 4 + (ANY,) * 5,
         scratch_shapes=[
             pltpu.VMEM((4, NX, NY, 1024), F32),
             pltpu.SemaphoreType.DMA((2, NX)),
@@ -170,7 +179,7 @@
         out_specs=(ANY,) * 2,
         scratch_shapes=[pltpu.SemaphoreType.DMA((4 * len(counts),))],
         compiler_params=pltpu.CompilerParams(vmem_limit_bytes=MIB),
-        cost_estimate=pl.CostEstimate(flops=10**10, bytes_accessed=MIB, transcendentals=0),
+        cost_estimate=pl.CostEstimate(flops=10**10 if len(counts) == 1 else 0, bytes_accessed=MIB, transcendentals=0),
         name="corners",
     )(ya, yb)
 
@@ -181,20 +190,52 @@
     return lax.ppermute(array, axis, [(i, j) for i, j in pairs if 0 <= j < size])
 
 
-def exchange(planes, counts, xa, xb, ya, yb):
+def relay_kernel(array, after, out, sem):
+    copy = pltpu.make_async_copy(array, out, sem)
+    copy.start()
+    copy.wait()
+
+
+def relay(array, after):
+    return pl.pallas_call(
+        relay_kernel,
+        out_shape=jax.ShapeDtypeStruct(array.shape, F32),
+        in_specs=[ANY] * 2,
+        out_specs=ANY,
+        scratch_shapes=[pltpu.SemaphoreType.DMA(())],
+        compiler_params=pltpu.CompilerParams(vmem_limit_bytes=MIB),
+        name="relay",
+    )(array, after)
+
+
+def exchange(planes, counts, xa, xb, ya, yb, xb_z=None):
+    size = lax.axis_size("gx")
+    middle = size // 2
+    if xb_z is not None:
+        pairs = [(i, ((i + 1) ^ 1) - 1) for i in range(1, size - 1) if i not in (middle - 1, middle)]
+        xb_z = lax.ppermute(xb_z, "gx", pairs + [(middle - 1, 0), (middle, size - 1)])
     ya, yb = swap(ya, "gy", "a"), swap(yb, "gy", "b")
     xb, xa = swap(xb, "gx", "b"), swap(xa, "gx", "a")
     ca, cb = corners(planes, counts, ya, yb)
     cb, ca = swap(cb, "gx", "b"), swap(ca, "gx", "a")
-    return xa, xb, ya, yb, ca, cb
-
-
-def land_first(k, sides, into, xs, ys, cs, fields):
+    if xb_z is None:
+        return xa, xb, ya, yb, ca, cb
+    onward = lax.ppermute(relay(xb_z, ca), "gx", [(0, middle), (size - 1, middle - 1)])
+    return xa, xb, ya, yb, ca, cb, xb_z, onward
+
+
+def land_first(k, sides, into, xs, ys, cs, routed, fields):
     at_x = at_y = at_c = 0
     for i, (in_x, in_y, in_c) in enumerate(fields_of(k)):
         for ab in ("a", "b"):
             x, y = sides.land("gx", ab, in_x), sides.land("gy", ab, in_y)
-            into.start(xs[ab].at[at_x : at_x + in_x], fields[i].at[pl.ds(x, in_x), K : K + NY])
+            x_halo = fields[i].at[pl.ds(x, in_x), K : K + NY]
+            if ab == "b" and i == 3:
+                me, size = lax.axis_index("gx"), lax.axis_size("gx")
+                by_ends = (me == 0) | (me == size // 2 - 1) | (me == size // 2) | (me == size - 1)
+                into.start_either(by_ends, routed[1], routed[0], x_halo)
+            else:
+                into.start(xs[ab].at[at_x : at_x + in_x], x_halo)
             into.start(ys[ab].at[:, at_y : at_y + in_y], fields[i].at[K : K + NX, pl.ds(y, in_y)])
             x = sides.land("gx", ab, k)
             for j, other in enumerate(("a", "b")):
@@ -291,13 +332,14 @@
 
 def first_kernel(
     k, k_next,
-    w_in, bx_in, by_in, bz_in, xa, xb, ya, yb, ca, cb,
+    w_in, bx_in, by_in, bz_in, xa, xb, ya, yb, ca, cb, z_plain, z_ends,
     w0, bx, by, bz, inv, acc, w1, xa_out, xb_out, ya_out, yb_out,
     in_sems, out_sems,
 ):
     sides = Sides()
     into = Copies(in_sems)
-    land_first(k, sides, into, {"a": xa, "b": xb}, {"a": ya, "b": yb}, {"a": ca, "b": cb}, (w0, bx, by, bz))
+    xs, ys, cs = {"a": xa, "b": xb}, {"a": ya, "b": yb}, {"a": ca, "b": cb}
+    land_first(k, sides, into, xs, ys, cs, (z_plain, z_ends), (w0, bx, by, bz))
     into.wait()
     scale(w0, bx, by, bz, inv)
     w = steps_of(0, k, False, (w0, w1), bx, by, bz, inv, acc)
@@ -316,7 +358,7 @@
     _, bx, by, bz, inv, acc, w, *strips = pl.pallas_call(
         functools.partial(first_kernel, k, k_next),
         out_shape=(EXT,) * 5 + (ACC, EXT) + strips_shape(k_next),
-        in_specs=[VMEM] * 4 + [ANY] * 6,
+        in_specs=[VMEM] * 4 + [ANY] * 8,
         out_specs=(VMEM,) * 7 + (ANY,) * 4,
         scratch_shapes=[pltpu.SemaphoreType.DMA((32,)), pltpu.SemaphoreType.DMA((4,))],
         input_output_aliases={i: i for i in range(4)},
@@ -455,8 +497,9 @@
     peers = lax.axis_size("gx") * lax.axis_size("gy")
     targets, slots = routes(tile_owner, tile_slot, peers)
     k = ROUNDS[0]
-    packed = pack(k, grad_pressure, beta)
-    coeffs, state, strips = first_round(k, ROUNDS[1], *packed[:4], *exchange(k, [f[1:] for f in fields_of(k)], *packed[4:]))
+    *fields, xa, xb, xb_z, ya, yb = pack(k, grad_pressure, beta)
+    counts = [f[1:] for f in fields_of(k)]
+    coeffs, state, strips = first_round(k, ROUNDS[1], *fields, *exchange(k, counts, xa, xb, ya, yb, xb_z))
     done = k
     for k, k_next in zip(ROUNDS[1:-1], ROUNDS[2:]):
         state, strips = later_round(done, k, k_next, *coeffs, *state, *exchange(k - 1, [(k, k - 1)], *strips))

time: 128 us -> 124 us (0.969)
  starting transfers between devices: 45.6 us -> 38.4 us
  waiting for transfers between devices: 19.5 us -> 24.6 us
  blocking collectives: 34.1 us -> 31.8 us
    ppermute x18, starting transfers between devices: 45.6 us -> 35.3 us  [swap(): lax.ppermute(array, axis, [(i, j) for i, j in pairs if 0 <= j < size])]
    ppermute x0 -> x2, waiting for transfers between devices: none -> 9.5 us  [the longest x1 9.5 us: exchange(): lax.ppermute(xb_z, 'gx', pairs + [(middle - 1, 0), (middle, size - 1)])]
    ppermute x18, waiting for transfers between devices: 19.5 us -> 15.1 us  [swap(): lax.ppermute(array, axis, [(i, j) for i, j in pairs if 0 <= j < size])]
    ppermute x0 -> x2, starting transfers between devices: none -> 3.07 us  [the longest x1 2.39 us: exchange(): lax.ppermute(xb_z, 'gx', pairs + [(middle - 1, 0), (middle, size - 1)])]
    all_to_all x1, blocking collectives: 34.1 us -> 31.8 us  [shards(): lax.all_to_all(sent, ('gx', 'gy'), split_axis=0, concat_axis=0, tiled=True)]
  transfers between devices with their start and end apart: 18 -> 20, of which waited for: 4 -> 5; matrix products, arithmetic and copies ran while one was open for 0% -> 0% of each run, Pallas kernels for 0% -> 1%
where the time goes in v5:
time: 124 us
  starting transfers between devices  38.4 us (31%)
  blocking collectives  31.8 us (26%)
  Pallas kernels  27.3 us (22%)
  waiting for transfers between devices  24.6 us (20%)
    ppermute x18, starting transfers between devices, swap(): lax.ppermute(array, axis, [(i, j) for i, j in pairs if 0 <= j < size])  35.3 us
    all_to_all x1, blocking collectives, shards(): lax.all_to_all(sent, ('gx', 'gy'), split_axis=0, concat_axis=0, tiled=True)  31.8 us
    ppermute x18, waiting for transfers between devices, swap(): lax.ppermute(array, axis, [(i, j) for i, j in pairs if 0 <= j < size])  15.1 us
    ppermute x1, waiting for transfers between devices, exchange(): lax.ppermute(xb_z, 'gx', pairs + [(middle - 1, 0), (middle, size - 1)])  9.5 us
    pallas_call x1, Pallas kernels, last_round(): pl.pallas_call(functools.partial(last_kernel, first, k), out_shape=(jax.S...  8.45 us
    pallas_call x1, Pallas kernels, first_round(): pl.pallas_call(functools.partial(first_kernel, k, k_next), out_shape=(EXT...  7.2 us
    pallas_call x1, Pallas kernels, later_round(): pl.pallas_call(functools.partial(later_kernel, first, k, k_next), out_sha...  6.19 us
    pallas_call x1, Pallas kernels, pack(): pl.pallas_call(functools.partial(pack_kernel, k), out_shape=(EXT,) * 4 +...  3.22 us
  transfers between devices with their start and end apart: 20, of which 5 were waited for; matrix products, arithmetic and copies ran while one was open for 0% of the time, Pallas kernels for 1%

profile of v5, /device:TPU:1, one launch (start us, length us, event | category | flops | bytes accessed | tf_op | source)
XLA Modules:
  0.0 123.6 jit_solution(7905042926816926323)
XLA Ops:
  0.6 3.2 %pack.1 = (f32[16,40,8,128]{3,2,1,0:T(8,128)S(1)}, f32[16,40,8,128]{3,2,1,0:T(8,128)S(1)}, f32[16,40,8,128]{3,2,1,0:T(8,128)S(1)}, f32[16,40,8,128]{3,2,1,0:T(8,...) custom-call(f32[8,32,1024]{2,1,0:T(8,128)} %g.1, ...), custom_call_target="tpu_custom_call" | custom-call | tf_op jit(solution)/shard_map/pack/pallas_call | solution.py:140
  3.9 1.5 %collective-permute-start = (f32[13,32,8,128]{3,2,1,0:T(8,128)S(1)}, f32[13,32,8,128]{3,2,1,0:T(8,128)S(1)}, u32[]{:S(2)}, u32[]{:S(2)}) collective-permute-start(f32[13,32,8,128]{3,2,1,0:T(8,128)S(1)} %get-tuple-element.39), channel_id=1, source_target_pairs={{0,8},{8,0},{16,24},{24,16},{32,40},{40,32},{48,56},{56,48},{64,72... | collective-permute-start | bytes 5111816 | tf_op jit(solution)/shard_map/ppermute | solution.py:190
  5.4 3.5 %collective-permute-start.1 = (f32[10,32,8,128]{3,2,1,0:T(8,128)S(1)}, f32[10,32,8,128]{3,2,1,0:T(8,128)S(1)}, u32[]{:S(2)}, u32[]{:S(2)}) collective-permute-start(f32[10,32,8,128]{3,2,1,0:T(8,128)S(1)} %get-tuple-element.40), channel_id=1, source_target_pairs={{8,16},{16,8},{24,32},{32,24},{40,48},{48,40},{56,64},{64,56},{72,... | collective-permute-start | bytes 3932168 | tf_op jit(solution)/shard_map/ppermute | solution.py:190
  8.9 1.3 %collective-permute-start.2 = (f32[8,13,8,128]{3,2,1,0:T(8,128)S(1)}, f32[8,13,8,128]{3,2,1,0:T(8,128)S(1)}, u32[]{:S(2)}, u32[]{:S(2)}) collective-permute-start(f32[8,13,8,128]{3,2,1,0:T(8,128)S(1)} %get-tuple-element.41), channel_id=1, source_target_pairs={{0,1},{1,0},{2,3},{3,2},{4,5},{5,4},{6,7},{7,6},{8,9},{9,8},{10,11... | collective-permute-start | bytes 1277960 | tf_op jit(solution)/shard_map/ppermute | solution.py:190
  10.2 0.7 collective-permute-start.3
  10.9 2.4 %collective-permute-start.6 = (f32[3,32,8,128]{3,2,1,0:T(8,128)S(1)}, f32[3,32,8,128]{3,2,1,0:T(8,128)S(1)}, u32[]{:S(2)}, u32[]{:S(2)}) collective-permute-start(f32[3,32,8,128]{3,2,1,0:T(8,128)S(1)} %get-tuple-element.45), channel_id=1, source_target_pairs={{8,16},{16,8},{24,32},{32,24},{40,48},{48,40},{72,80},{80,72},{88,... | collective-permute-start | bytes 1179656 | tf_op jit(solution)/shard_map/ppermute | solution.py:216
  13.3 5.2 %collective-permute-done.2.ya = f32[8,13,8,128]{3,2,1,0:T(8,128)S(1)} collective-permute-done((f32[8,13,8,128]{3,2,1,0:T(8,128)S(1)}, f32[8,13,8,128]{3,2,1,0:T(8,128)S(1)}, u32[]{:S(2)}, u32[]{:S(2)}) %collective-permute-start.2) | collective-permute-done | bytes 426016 | tf_op jit(solution)/shard_map/ppermute | solution.py:190
  18.5 0.0 collective-permute-done.3.yb
  18.5 0.4 corners.3
  18.9 0.1 collective-permute-start.4
  19.0 9.5 %collective-permute-done.6.array.z_plain = f32[3,32,8,128]{3,2,1,0:T(8,128)S(1)} collective-permute-done((f32[3,32,8,128]{3,2,1,0:T(8,128)S(1)}, f32[3,32,8,128]{3,2,1,0:T(8,128)S(1)}, u32[]{:S(2)}, u32[]{:S(2)}) %collective-permute-start.6) | collective-permute-done | bytes 393248 | tf_op jit(solution)/shard_map/ppermute | solution.py:216
  28.5 0.0 collective-permute-done.4.after.ca
  28.5 0.2 relay.1
  28.7 0.7 collective-permute-start.7
  29.4 3.5 %collective-permute-start.5 = (f32[2,3,10,8,128]{4,3,2,1,0:T(8,128)S(1)}, f32[2,3,10,8,128]{4,3,2,1,0:T(8,128)S(1)}, u32[]{:S(2)}, u32[]{:S(2)}) collective-permute-start(f32[2,3,10,8,128]{4,3,2,1,0:T(8,128)S(1)} %get-tuple-element.44), channel_id=1, source_target_pairs={{8,16},{16,8},{24,32},{32,24},{40,48},{48,40},{56,64},{64,56},{72,... | collective-permute-start | bytes 737288 | tf_op jit(solution)/shard_map/ppermute | solution.py:190
  32.9 4.0 %collective-permute-done.5.cb = f32[2,3,10,8,128]{4,3,2,1,0:T(8,128)S(1)} collective-permute-done((f32[2,3,10,8,128]{4,3,2,1,0:T(8,128)S(1)}, f32[2,3,10,8,128]{4,3,2,1,0:T(8,128)S(1)}, u32[]{:S(2)}, u32[]{:S(2)}) %collective-permute-start.5) | collective-permute-done | bytes 245792 | tf_op jit(solution)/shard_map/ppermute | solution.py:190
  36.9 0.0 collective-permute-done.7.z_ends
  36.9 0.0 collective-permute-done.1.xb
  36.9 0.0 collective-permute-done.xa
  36.9 0.0 copy-start.4
  36.9 7.2 %first_round.1 = (f32[16,40,8,128]{3,2,1,0:T(8,128)S(1)}, f32[16,40,8,128]{3,2,1,0:T(8,128)S(1)}, f32[16,40,8,128]{3,2,1,0:T(8,128)S(1)}, f32[16,40,8,128]{3,2,1...) custom-call(f32[16,40,8,128]{3,2,1,0:T(8,128)S(1)} %get-tuple-elemen, ...), custom_call_target="tpu_custom_call", output_to_operand_aliasing={{0}: (0, {}), {1}: (1, {}), {2}: (2, {}), {3}: (3, {})} | custom-call | tf_op jit(solution)/shard_map/first_round/pallas_call | solution.py:358
  44.1 1.4 %collective-permute-start.10 = (f32[8,4,8,128]{3,2,1,0:T(8,128)S(1)}, f32[8,4,8,128]{3,2,1,0:T(8,128)S(1)}, u32[]{:S(2)}, u32[]{:S(2)}) collective-permute-start(f32[8,4,8,128]{3,2,1,0:T(8,128)S(1)} %get-tuple-element.54), channel_id=1, source_target_pairs={{0,1},{1,0},{2,3},{3,2},{4,5},{5,4},{6,7},{7,6},{8,9},{9,8},{10,11... | collective-permute-start | bytes 393224 | tf_op jit(solution)/shard_map/ppermute | solution.py:190
  45.5 0.7 collective-permute-start.11
  46.2 0.0 copy-done.4
  46.2 0.1 collective-permute-start.8
  46.3 0.0 copy-start.3
  46.3 4.0 %collective-permute-start.9 = (f32[4,32,8,128]{3,2,1,0:T(8,128)S(1)}, f32[4,32,8,128]{3,2,1,0:T(8,128)S(1)}, u32[]{:S(2)}, u32[]{:S(2)}) collective-permute-start(f32[4,32,8,128]{3,2,1,0:T(8,128)S(1)} %get-tuple-element.53), channel_id=1, source_target_pairs={{8,16},{16,8},{24,32},{32,24},{40,48},{48,40},{56,64},{64,56},{72,... | collective-permute-start | bytes 1572872 | tf_op jit(solution)/shard_map/ppermute | solution.py:190
  50.3 0.0 collective-permute-done.10.ya
  50.4 0.0 collective-permute-done.11.yb
  50.4 0.1 corners.4
  50.5 0.1 collective-permute-start.12
  50.6 3.9 %collective-permute-start.13 = (f32[2,3,3,8,128]{4,3,2,1,0:T(8,128)S(1)}, f32[2,3,3,8,128]{4,3,2,1,0:T(8,128)S(1)}, u32[]{:S(2)}, u32[]{:S(2)}) collective-permute-start(f32[2,3,3,8,128]{4,3,2,1,0:T(8,128)S(1)} %get-tuple-element.57), channel_id=1, source_target_pairs={{8,16},{16,8},{24,32},{32,24},{40,48},{48,40},{56,64},{64,56},{72,... | collective-permute-start | bytes 221192 | tf_op jit(solution)/shard_map/ppermute | solution.py:190
  54.5 0.0 copy-done.3
  54.5 0.2 convert_reduce_fusion
  54.7 0.0 collective-permute-done.12.ca
  54.7 3.3 %collective-permute-done.13.cb = f32[2,3,3,8,128]{4,3,2,1,0:T(8,128)S(1)} collective-permute-done((f32[2,3,3,8,128]{4,3,2,1,0:T(8,128)S(1)}, f32[2,3,3,8,128]{4,3,2,1,0:T(8,128)S(1)}, u32[]{:S(2)}, u32[]{:S(2)}) %collective-permute-start.13) | collective-permute-done | bytes 73760 | tf_op jit(solution)/shard_map/ppermute | solution.py:190
  58.0 0.0 collective-permute-done.8.xa
  58.0 0.0 collective-permute-done.9.xb
  58.0 6.2 %later_round.1 = (f32[16,40,8,128]{3,2,1,0:T(8,128)S(1)}, f32[8,32,8,128]{3,2,1,0:T(8,128)S(1)}, f32[4,32,8,128]{3,2,1,0:T(8,128)S(1)}, f32[4,32,8,128]{3,2,1,0:...) custom-call(f32[16,40,8,128]{3,2,1,0:T(8,128)S(1)} %get-tuple-elemen, ...), custom_call_target="tpu_custom_call", output_to_operand_aliasing={{0}: (4, {}), {1}: (5, {})} | custom-call | tf_op jit(solution)/shard_map/later_round/pallas_call | solution.py:389
  64.2 5.1 %collective-permute-start.16 = (f32[8,4,8,128]{3,2,1,0:T(8,128)S(1)}, f32[8,4,8,128]{3,2,1,0:T(8,128)S(1)}, u32[]{:S(2)}, u32[]{:S(2)}) collective-permute-start(f32[8,4,8,128]{3,2,1,0:T(8,128)S(1)} %get-tuple-element.62), channel_id=1, source_target_pairs={{0,1},{1,0},{2,3},{3,2},{4,5},{5,4},{6,7},{7,6},{8,9},{9,8},{10,11... | collective-permute-start | bytes 393224 | tf_op jit(solution)/shard_map/ppermute | solution.py:190
  69.3 0.7 collective-permute-start.17
  70.0 0.3 fusion.1.slots
  70.3 0.1 collective-permute-start.14
  70.4 0.0 copy-start.1
  70.4 0.0 copy-start.2
  70.4 3.2 %collective-permute-start.15 = (f32[4,32,8,128]{3,2,1,0:T(8,128)S(1)}, f32[4,32,8,128]{3,2,1,0:T(8,128)S(1)}, u32[]{:S(2)}, u32[]{:S(2)}) collective-permute-start(f32[4,32,8,128]{3,2,1,0:T(8,128)S(1)} %get-tuple-element.61), channel_id=1, source_target_pairs={{8,16},{16,8},{24,32},{32,24},{40,48},{48,40},{56,64},{64,56},{72,... | collective-permute-start | bytes 1572872 | tf_op jit(solution)/shard_map/ppermute | solution.py:190
  73.6 0.0 collective-permute-done.16.ya
  73.7 0.0 collective-permute-done.17.yb
  73.7 0.1 corners.5
  73.8 0.1 collective-permute-start.18
  73.9 5.4 %collective-permute-start.19 = (f32[2,3,3,8,128]{4,3,2,1,0:T(8,128)S(1)}, f32[2,3,3,8,128]{4,3,2,1,0:T(8,128)S(1)}, u32[]{:S(2)}, u32[]{:S(2)}) collective-permute-start(f32[2,3,3,8,128]{4,3,2,1,0:T(8,128)S(1)} %get-tuple-element.65), channel_id=1, source_target_pairs={{8,16},{16,8},{24,32},{32,24},{40,48},{48,40},{56,64},{64,56},{72,... | collective-permute-start | bytes 221192 | tf_op jit(solution)/shard_map/ppermute | solution.py:190
  79.3 0.0 collective-permute-done.18.ca
  79.3 2.5 %collective-permute-done.19.cb = f32[2,3,3,8,128]{4,3,2,1,0:T(8,128)S(1)} collective-permute-done((f32[2,3,3,8,128]{4,3,2,1,0:T(8,128)S(1)}, f32[2,3,3,8,128]{4,3,2,1,0:T(8,128)S(1)}, u32[]{:S(2)}, u32[]{:S(2)}) %collective-permute-start.19) | collective-permute-done | bytes 73760 | tf_op jit(solution)/shard_map/ppermute | solution.py:190
  81.8 0.0 collective-permute-done.14.xa
  81.8 0.0 collective-permute-done.15.xb
  81.8 0.0 copy-done.1
  81.8 0.0 copy-done.2
  81.9 0.0 copy-start
  81.9 8.5 %last_round.1 = (f32[8,32,1024]{2,1,0:T(8,128)}, f32[1152,128]{1,0:T(8,128)S(1)}, f32[16,40,8,128]{3,2,1,0:T(8,128)S(1)}, f32[8,32,8,128]{3,2,1,0:T(8,128)S(1)}) custom-call(s32[256]{0:T(256)S(1)} %copy-done.2, s32[256]{0:T(256)S(1)} %multiply_add_fusion.targets, s32[256,128]{1,0:T(8,128)S(1)} %copy-done.1, ...), custom_call_target="tpu_custom_call", output_to_operand_aliasing={{2}: (8, {}), {3}: (9, {})} | custom-call | tf_op jit(solution)/shard_map/last_round/pallas_call | solution.py:434
  90.3 31.8 %all_to_all.5 = f32[128,1,1152]{2,1,0:T(1,128)S(1)} all-to-all(f32[128,1,1152]{2,1,0:T(1,128)S(1)} %bitcast.4), channel_id=1, replica_groups=mesh['gx'=16,'gy'=8] {'gx','gy'}, dimensions={0} | all-to-all | bytes 1179648 | tf_op jit(solution)/shard_map/all_to_all | solution.py:512
  122.2 0.0 copy-done
  122.2 1.4 %finish.1 = f32[3,256,128]{2,1,0:T(8,128)} custom-call(f32[1152,128]{1,0:T(8,128)S(1)} %bitcast.3, f32[3,256,128]{2,1,0:T(8,128)S(1)} %copy-done), custom_call_target="tpu_custom_call" | custom-call | tf_op jit(solution)/shard_map/finish/pallas_call | solution.py:475
  (2 shorter events, 0.0 us)
Async XLA Ops:
  3.9 33.1 %collective-permute-start = (f32[13,32,8,128]{3,2,1,0:T(8,128)S(1)}, f32[13,32,8,128]{3,2,1,0:T(8,128)S(1)}, u32[]{:S(2)}, u32[]{:S(2)}) collective-permute-start(f32[13,32,8,128]{3,2,1,0:T(8,128)S(1)} %get-tuple-element.39), channel_id=1, source_target_pairs={{0,8},{8,0},{16,24},{24,16},{32,40},{40,32},{48,56},{56,48},{64,72... | collective-permute-start | bytes 5111816 | tf_op jit(solution)/shard_map/ppermute | solution.py:190
  5.4 31.5 %collective-permute-start.1 = (f32[10,32,8,128]{3,2,1,0:T(8,128)S(1)}, f32[10,32,8,128]{3,2,1,0:T(8,128)S(1)}, u32[]{:S(2)}, u32[]{:S(2)}) collective-permute-start(f32[10,32,8,128]{3,2,1,0:T(8,128)S(1)} %get-tuple-element.40), channel_id=1, source_target_pairs={{8,16},{16,8},{24,32},{32,24},{40,48},{48,40},{56,64},{64,56},{72,... | collective-permute-start | bytes 3932168 | tf_op jit(solution)/shard_map/ppermute | solution.py:190
  8.9 9.6 %collective-permute-start.2 = (f32[8,13,8,128]{3,2,1,0:T(8,128)S(1)}, f32[8,13,8,128]{3,2,1,0:T(8,128)S(1)}, u32[]{:S(2)}, u32[]{:S(2)}) collective-permute-start(f32[8,13,8,128]{3,2,1,0:T(8,128)S(1)} %get-tuple-element.41), channel_id=1, source_target_pairs={{0,1},{1,0},{2,3},{3,2},{4,5},{5,4},{6,7},{7,6},{8,9},{9,8},{10,11... | collective-permute-start | bytes 1277960 | tf_op jit(solution)/shard_map/ppermute | solution.py:190
  10.2 8.3 %collective-permute-start.3 = (f32[8,13,8,128]{3,2,1,0:T(8,128)S(1)}, f32[8,13,8,128]{3,2,1,0:T(8,128)S(1)}, u32[]{:S(2)}, u32[]{:S(2)}) collective-permute-start(f32[8,13,8,128]{3,2,1,0:T(8,128)S(1)} %get-tuple-element.42), channel_id=1, source_target_pairs={{1,2},{2,1},{3,4},{4,3},{5,6},{6,5},{9,10},{10,9},{11,12},{12,11},... | collective-permute-start | bytes 1277960 | tf_op jit(solution)/shard_map/ppermute | solution.py:190
  10.9 17.6 %collective-permute-start.6 = (f32[3,32,8,128]{3,2,1,0:T(8,128)S(1)}, f32[3,32,8,128]{3,2,1,0:T(8,128)S(1)}, u32[]{:S(2)}, u32[]{:S(2)}) collective-permute-start(f32[3,32,8,128]{3,2,1,0:T(8,128)S(1)} %get-tuple-element.45), channel_id=1, source_target_pairs={{8,16},{16,8},{24,32},{32,24},{40,48},{48,40},{72,80},{80,72},{88,... | collective-permute-start | bytes 1179656 | tf_op jit(solution)/shard_map/ppermute | solution.py:216
  18.9 9.6 %collective-permute-start.4 = (f32[2,3,10,8,128]{4,3,2,1,0:T(8,128)S(1)}, f32[2,3,10,8,128]{4,3,2,1,0:T(8,128)S(1)}, u32[]{:S(2)}, u32[]{:S(2)}) collective-permute-start(f32[2,3,10,8,128]{4,3,2,1,0:T(8,128)S(1)} %get-tuple-element.43), channel_id=1, source_target_pairs={{0,8},{8,0},{16,24},{24,16},{32,40},{40,32},{48,56},{56,48},{64,72... | collective-permute-start | bytes 737288 | tf_op jit(solution)/shard_map/ppermute | solution.py:190
  28.7 8.2 %collective-permute-start.7 = (f32[3,32,8,128]{3,2,1,0:T(8,128)S(1)}, f32[3,32,8,128]{3,2,1,0:T(8,128)S(1)}, u32[]{:S(2)}, u32[]{:S(2)}) collective-permute-start(f32[3,32,8,128]{3,2,1,0:T(8,128)S(1)} %relay.1), channel_id=1, source_target_pairs={{0,64},{120,56},{1,65},{121,57},{2,66},{122,58},{3,67},{123,59},{4... | collective-permute-start | bytes 1179656 | tf_op jit(solution)/shard_map/ppermute | solution.py:223
  29.4 7.5 %collective-permute-start.5 = (f32[2,3,10,8,128]{4,3,2,1,0:T(8,128)S(1)}, f32[2,3,10,8,128]{4,3,2,1,0:T(8,128)S(1)}, u32[]{:S(2)}, u32[]{:S(2)}) collective-permute-start(f32[2,3,10,8,128]{4,3,2,1,0:T(8,128)S(1)} %get-tuple-element.44), channel_id=1, source_target_pairs={{8,16},{16,8},{24,32},{32,24},{40,48},{48,40},{56,64},{64,56},{72,... | collective-permute-start | bytes 737288 | tf_op jit(solution)/shard_map/ppermute | solution.py:190
  36.9 9.3 %copy-start.4 = (s32[256]{0:T(256)S(1)}, s32[256]{0:T(256)}, u32[]{:S(2)}) copy-start(s32[256]{0:T(256)} %param.11) | copy-start | bytes 3076
  44.1 6.2 %collective-permute-start.10 = (f32[8,4,8,128]{3,2,1,0:T(8,128)S(1)}, f32[8,4,8,128]{3,2,1,0:T(8,128)S(1)}, u32[]{:S(2)}, u32[]{:S(2)}) collective-permute-start(f32[8,4,8,128]{3,2,1,0:T(8,128)S(1)} %get-tuple-element.54), channel_id=1, source_target_pairs={{0,1},{1,0},{2,3},{3,2},{4,5},{5,4},{6,7},{7,6},{8,9},{9,8},{10,11... | collective-permute-start | bytes 393224 | tf_op jit(solution)/shard_map/ppermute | solution.py:190
  45.5 4.8 %collective-permute-start.11 = (f32[8,4,8,128]{3,2,1,0:T(8,128)S(1)}, f32[8,4,8,128]{3,2,1,0:T(8,128)S(1)}, u32[]{:S(2)}, u32[]{:S(2)}) collective-permute-start(f32[8,4,8,128]{3,2,1,0:T(8,128)S(1)} %get-tuple-element.55), channel_id=1, source_target_pairs={{1,2},{2,1},{3,4},{4,3},{5,6},{6,5},{9,10},{10,9},{11,12},{12,11},... | collective-permute-start | bytes 393224 | tf_op jit(solution)/shard_map/ppermute | solution.py:190
  46.2 11.8 %collective-permute-start.8 = (f32[4,32,8,128]{3,2,1,0:T(8,128)S(1)}, f32[4,32,8,128]{3,2,1,0:T(8,128)S(1)}, u32[]{:S(2)}, u32[]{:S(2)}) collective-permute-start(f32[4,32,8,128]{3,2,1,0:T(8,128)S(1)} %get-tuple-element.52), channel_id=1, source_target_pairs={{0,8},{8,0},{16,24},{24,16},{32,40},{40,32},{48,56},{56,48},{64,72... | collective-permute-start | bytes 1572872 | tf_op jit(solution)/shard_map/ppermute | solution.py:190
  46.3 8.2 %copy-start.3 = (s32[256,1]{0,1:T(1,128)S(1)}, s32[256,1]{0,1:T(1,128)}, u32[]{:S(2)}) copy-start(s32[256,1]{0,1:T(1,128)} %param.10) | copy-start | bytes 3076
  46.3 11.7 %collective-permute-start.9 = (f32[4,32,8,128]{3,2,1,0:T(8,128)S(1)}, f32[4,32,8,128]{3,2,1,0:T(8,128)S(1)}, u32[]{:S(2)}, u32[]{:S(2)}) collective-permute-start(f32[4,32,8,128]{3,2,1,0:T(8,128)S(1)} %get-tuple-element.53), channel_id=1, source_target_pairs={{8,16},{16,8},{24,32},{32,24},{40,48},{48,40},{56,64},{64,56},{72,... | collective-permute-start | bytes 1572872 | tf_op jit(solution)/shard_map/ppermute | solution.py:190
  50.5 4.2 %collective-permute-start.12 = (f32[2,3,3,8,128]{4,3,2,1,0:T(8,128)S(1)}, f32[2,3,3,8,128]{4,3,2,1,0:T(8,128)S(1)}, u32[]{:S(2)}, u32[]{:S(2)}) collective-permute-start(f32[2,3,3,8,128]{4,3,2,1,0:T(8,128)S(1)} %get-tuple-element.56), channel_id=1, source_target_pairs={{0,8},{8,0},{16,24},{24,16},{32,40},{40,32},{48,56},{56,48},{64,72... | collective-permute-start | bytes 221192 | tf_op jit(solution)/shard_map/ppermute | solution.py:190
  50.6 7.4 %collective-permute-start.13 = (f32[2,3,3,8,128]{4,3,2,1,0:T(8,128)S(1)}, f32[2,3,3,8,128]{4,3,2,1,0:T(8,128)S(1)}, u32[]{:S(2)}, u32[]{:S(2)}) collective-permute-start(f32[2,3,3,8,128]{4,3,2,1,0:T(8,128)S(1)} %get-tuple-element.57), channel_id=1, source_target_pairs={{8,16},{16,8},{24,32},{32,24},{40,48},{48,40},{56,64},{64,56},{72,... | collective-permute-start | bytes 221192 | tf_op jit(solution)/shard_map/ppermute | solution.py:190
  64.2 9.5 %collective-permute-start.16 = (f32[8,4,8,128]{3,2,1,0:T(8,128)S(1)}, f32[8,4,8,128]{3,2,1,0:T(8,128)S(1)}, u32[]{:S(2)}, u32[]{:S(2)}) collective-permute-start(f32[8,4,8,128]{3,2,1,0:T(8,128)S(1)} %get-tuple-element.62), channel_id=1, source_target_pairs={{0,1},{1,0},{2,3},{3,2},{4,5},{5,4},{6,7},{7,6},{8,9},{9,8},{10,11... | collective-permute-start | bytes 393224 | tf_op jit(solution)/shard_map/ppermute | solution.py:190
  69.3 4.4 %collective-permute-start.17 = (f32[8,4,8,128]{3,2,1,0:T(8,128)S(1)}, f32[8,4,8,128]{3,2,1,0:T(8,128)S(1)}, u32[]{:S(2)}, u32[]{:S(2)}) collective-permute-start(f32[8,4,8,128]{3,2,1,0:T(8,128)S(1)} %get-tuple-element.63), channel_id=1, source_target_pairs={{1,2},{2,1},{3,4},{4,3},{5,6},{6,5},{9,10},{10,9},{11,12},{12,11},... | collective-permute-start | bytes 393224 | tf_op jit(solution)/shard_map/ppermute | solution.py:190
  70.3 11.5 %collective-permute-start.14 = (f32[4,32,8,128]{3,2,1,0:T(8,128)S(1)}, f32[4,32,8,128]{3,2,1,0:T(8,128)S(1)}, u32[]{:S(2)}, u32[]{:S(2)}) collective-permute-start(f32[4,32,8,128]{3,2,1,0:T(8,128)S(1)} %get-tuple-element.60), channel_id=1, source_target_pairs={{0,8},{8,0},{16,24},{24,16},{32,40},{40,32},{48,56},{56,48},{64,72... | collective-permute-start | bytes 1572872 | tf_op jit(solution)/shard_map/ppermute | solution.py:190
  70.4 11.5 %copy-start.1 = (s32[256,128]{1,0:T(8,128)S(1)}, s32[256,128]{1,0:T(8,128)}, u32[]{:S(2)}) copy-start(s32[256,128]{1,0:T(8,128)} %mask.1) | copy-start | bytes 393220
  70.4 11.4 %copy-start.2 = (s32[256]{0:T(256)S(1)}, s32[256]{0:T(256)}, u32[]{:S(2)}) copy-start(s32[256]{0:T(256)} %tile_rows.1) | copy-start | bytes 3076
  70.4 11.4 %collective-permute-start.15 = (f32[4,32,8,128]{3,2,1,0:T(8,128)S(1)}, f32[4,32,8,128]{3,2,1,0:T(8,128)S(1)}, u32[]{:S(2)}, u32[]{:S(2)}) collective-permute-start(f32[4,32,8,128]{3,2,1,0:T(8,128)S(1)} %get-tuple-element.61), channel_id=1, source_target_pairs={{8,16},{16,8},{24,32},{32,24},{40,48},{48,40},{56,64},{64,56},{72,... | collective-permute-start | bytes 1572872 | tf_op jit(solution)/shard_map/ppermute | solution.py:190
  73.8 5.5 %collective-permute-start.18 = (f32[2,3,3,8,128]{4,3,2,1,0:T(8,128)S(1)}, f32[2,3,3,8,128]{4,3,2,1,0:T(8,128)S(1)}, u32[]{:S(2)}, u32[]{:S(2)}) collective-permute-start(f32[2,3,3,8,128]{4,3,2,1,0:T(8,128)S(1)} %get-tuple-element.64), channel_id=1, source_target_pairs={{0,8},{8,0},{16,24},{24,16},{32,40},{40,32},{48,56},{56,48},{64,72... | collective-permute-start | bytes 221192 | tf_op jit(solution)/shard_map/ppermute | solution.py:190
  73.9 7.9 %collective-permute-start.19 = (f32[2,3,3,8,128]{4,3,2,1,0:T(8,128)S(1)}, f32[2,3,3,8,128]{4,3,2,1,0:T(8,128)S(1)}, u32[]{:S(2)}, u32[]{:S(2)}) collective-permute-start(f32[2,3,3,8,128]{4,3,2,1,0:T(8,128)S(1)} %get-tuple-element.65), channel_id=1, source_target_pairs={{8,16},{16,8},{24,32},{32,24},{40,48},{48,40},{56,64},{64,56},{72,... | collective-permute-start | bytes 221192 | tf_op jit(solution)/shard_map/ppermute | solution.py:190
  81.9 40.3 %copy-start = (f32[3,256,128]{2,1,0:T(8,128)S(1)}, f32[3,256,128]{2,1,0:T(8,128)}, u32[]{:S(2)}) copy-start(f32[3,256,128]{2,1,0:T(8,128)} %heights.1) | copy-start | bytes 1179652

commit v6 on v5

--- a/solution.py
+++ b/solution.py
@@ -224,11 +224,19 @@
     return xa, xb, ya, yb, ca, cb, xb_z, onward
 
 
-def land_first(k, sides, into, xs, ys, cs, routed, fields):
-    at_x = at_y = at_c = 0
-    for i, (in_x, in_y, in_c) in enumerate(fields_of(k)):
+def land_first_y(k, sides, into, ys, fields):
+    at = 0
+    for field, (_, n, _) in zip(fields, fields_of(k)):
         for ab in ("a", "b"):
-            x, y = sides.land("gx", ab, in_x), sides.land("gy", ab, in_y)
+            into.start(ys[ab].at[:, at : at + n], field.at[K : K + NX, pl.ds(sides.land("gy", ab, n), n)])
+        at += n
+
+
+def land_first_x(k, sides, into, xs, cs, routed, fields):
+    at_x = at_c = 0
+    for i, (in_x, _, in_c) in enumerate(fields_of(k)):
+        for ab in ("a", "b"):
+            x = sides.land("gx", ab, in_x)
             x_halo = fields[i].at[pl.ds(x, in_x), K : K + NY]
             if ab == "b" and i == 3:
                 me, size = lax.axis_index("gx"), lax.axis_size("gx")
@@ -236,7 +244,6 @@
                 into.start_either(by_ends, routed[1], routed[0], x_halo)
             else:
                 into.start(xs[ab].at[at_x : at_x + in_x], x_halo)
-            into.start(ys[ab].at[:, at_y : at_y + in_y], fields[i].at[K : K + NX, pl.ds(y, in_y)])
             x = sides.land("gx", ab, k)
             for j, other in enumerate(("a", "b")):
                 y = sides.land("gy", other, in_c)
@@ -244,14 +251,12 @@
                     cs[ab].at[j, :, at_c : at_c + in_c],
                     fields[i].at[pl.ds(x, k), pl.ds(y, in_c)],
                 )
-        at_x, at_y, at_c = at_x + in_x, at_y + in_y, at_c + in_c
-
-
-def land_later(k, sides, into, xs, ys, cs, w):
+        at_x, at_c = at_x + in_x, at_c + in_c
+
+
+def land_later_x(k, sides, into, xs, cs, w):
     for ab in ("a", "b"):
-        x, y = sides.land("gx", ab, k), sides.land("gy", ab, k)
-        into.start(xs[ab], w.at[pl.ds(x, k), K : K + NY])
-        into.start(ys[ab], w.at[K : K + NX, pl.ds(y, k)])
+        into.start(xs[ab], w.at[pl.ds(sides.land("gx", ab, k), k), K : K + NY])
         x = sides.land("gx", ab, k - 1)
         for j, other in enumerate(("a", "b")):
             y = sides.land("gy", other, k - 1)
@@ -262,8 +267,8 @@
     return [(y, min(size, high - y)) for y in range(low, high, size)]
 
 
-def scale(w, bx, by, bz, inv):
-    @pl.loop(K - C, K + NX + C)
+def scale(planes, w, bx, by, bz, inv):
+    @pl.loop(*planes)
     def _(x):
         for y, n in chunks(K - C, K + NY + C):
             b = bz[x, y : y + n]
@@ -278,11 +283,11 @@
             bz[x, y : y + n] = inner
 
 
-def one_step(step, reach, last, w, new, bx, by, bz, inv, acc):
+def one_step(step, reach, last, spans, w, new, bx, by, bz, inv, acc):
     omega = omega_of(step)
-    low, high = K - reach, K + NX + reach
-
-    def walk(y, n, rows_inside):
+
+    def walk(span, y, n, rows_inside):
+        low, high = span
         below = bx[low - 1, pl.ds(y, n)] * w[low - 1, pl.ds(y, n)]
         around = w[low, pl.ds(y - 1, n + 2)]
         for x in range(low, high):
@@ -306,18 +311,33 @@
             below, around = link * centre, above
 
     if reach:
-        walk(K - reach, reach, False)
-        walk(K + NY, reach, False)
+        for span in spans:
+            walk(span, K - reach, reach, False)
+            walk(span, K + NY, reach, False)
 
     @pl.loop(0, NY // 8)
     def _(i):
-        walk(K + i * 8, 8, True)
-
-
-def steps_of(first, k, last, w, bx, by, bz, inv, acc):
+        for span in spans:
+            walk(span, K + i * 8, 8, True)
+
+
+def early_span(i, lead):
+    return K + lead + i, K + NX - 1 - i
+
+
+def early_steps(first, k, lead, w, *arrays):
     for i in range(k):
-        end = last and i == k - 1
-        one_step(first + i, k - 1 - i, end, w[i % 2], w[1 - i % 2], bx, by, bz, inv, acc)
+        low, high = early_span(i, lead)
+        if low < high:
+            one_step(first + i, k - 1 - i, False, [(low, high)], w[i % 2], w[1 - i % 2], *arrays)
+
+
+def other_steps(first, k, lead, last, w, *arrays):
+    for i in range(k):
+        reach = k - 1 - i
+        low, high = early_span(i, lead)
+        spans = [(K - reach, low), (high, K + NX + reach)] if low < high else [(K - reach, K + NX + reach)]
+        one_step(first + i, reach, last and i == k - 1, spans, w[i % 2], w[1 - i % 2], *arrays)
     return w[k % 2]
 
 
@@ -330,89 +350,131 @@
             out.start(w.at[K : K + NX, pl.ds(first, k)], strip)
 
 
+def strips_shape(k):
+    x, y = rows_shape(k, NY), rows_shape(NX, k)
+    return (x, x, y, y)
+
+
+def early_first_kernel(k, w_in, bx_in, by_in, bz_in, ya, yb, w0, bx, by, bz, inv, acc, w1, sems):
+    sides = Sides()
+    into = Copies(sems)
+    land_first_y(k, sides, into, {"a": ya, "b": yb}, (w0, bx, by, bz))
+    into.wait()
+    scale((K + 1, K + NX), w0, bx, by, bz, inv)
+    early_steps(0, k, 2, (w0, w1), bx, by, bz, inv, acc)
+
+
+def early_first(k, fields, ya, yb):
+    return pl.pallas_call(
+        functools.partial(early_first_kernel, k),
+        out_shape=(EXT,) * 5 + (ACC, EXT),
+        in_specs=[VMEM] * 4 + [ANY] * 2,
+        out_specs=(VMEM,) * 7,
+        scratch_shapes=[pltpu.SemaphoreType.DMA((8,))],
+        input_output_aliases={i: i for i in range(4)},
+        compiler_params=pltpu.CompilerParams(vmem_limit_bytes=2 * MIB),
+        name="early_first",
+    )(*fields, ya, yb)
+
+
 def first_kernel(
     k, k_next,
-    w_in, bx_in, by_in, bz_in, xa, xb, ya, yb, ca, cb, z_plain, z_ends,
+    w_in, bx_in, by_in, bz_in, inv_in, acc_in, w1_in, xa, xb, ca, cb, z_plain, z_ends,
     w0, bx, by, bz, inv, acc, w1, xa_out, xb_out, ya_out, yb_out,
     in_sems, out_sems,
 ):
     sides = Sides()
     into = Copies(in_sems)
-    xs, ys, cs = {"a": xa, "b": xb}, {"a": ya, "b": yb}, {"a": ca, "b": cb}
-    land_first(k, sides, into, xs, ys, cs, (z_plain, z_ends), (w0, bx, by, bz))
+    land_first_x(k, sides, into, {"a": xa, "b": xb}, {"a": ca, "b": cb}, (z_plain, z_ends), (w0, bx, by, bz))
     into.wait()
-    scale(w0, bx, by, bz, inv)
-    w = steps_of(0, k, False, (w0, w1), bx, by, bz, inv, acc)
+    scale((K - C, K + 1), w0, bx, by, bz, inv)
+    scale((K + NX, K + NX + C), w0, bx, by, bz, inv)
+    w = other_steps(0, k, 2, False, (w0, w1), bx, by, bz, inv, acc)
     out = Copies(out_sems)
     leave(k_next, sides, out, w, xa_out, xb_out, ya_out, yb_out)
     out.wait()
 
 
-def strips_shape(k):
-    x, y = rows_shape(k, NY), rows_shape(NX, k)
-    return (x, x, y, y)
-
-
 def first_round(k, k_next, *arrays):
-    assert k % 2 == 1
-    _, bx, by, bz, inv, acc, w, *strips = pl.pallas_call(
+    w0, bx, by, bz, inv, acc, w1, *strips = pl.pallas_call(
         functools.partial(first_kernel, k, k_next),
         out_shape=(EXT,) * 5 + (ACC, EXT) + strips_shape(k_next),
-        in_specs=[VMEM] * 4 + [ANY] * 8,
+        in_specs=[VMEM] * 7 + [ANY] * 6,
         out_specs=(VMEM,) * 7 + (ANY,) * 4,
-        scratch_shapes=[pltpu.SemaphoreType.DMA((32,)), pltpu.SemaphoreType.DMA((4,))],
-        input_output_aliases={i: i for i in range(4)},
+        scratch_shapes=[pltpu.SemaphoreType.DMA((24,)), pltpu.SemaphoreType.DMA((4,))],
+        input_output_aliases={i: i for i in range(7)},
         compiler_params=pltpu.CompilerParams(vmem_limit_bytes=2 * MIB),
         name="first_round",
     )(*arrays)
-    return (bx, by, bz, inv), (w, acc), strips
+    return (bx, by, bz, inv), ((w0, w1)[k % 2], (w1, w0)[k % 2], acc), strips
+
+
+def early_kernel(first, k, bx, by, bz, inv, w_in, w1_in, acc_in, ya, yb, w0, w1, acc, sems):
+    sides = Sides()
+    into = Copies(sems)
+    for ab, strip in (("a", ya), ("b", yb)):
+        into.start(strip, w0.at[K : K + NX, pl.ds(sides.land("gy", ab, k), k)])
+    into.wait()
+    early_steps(first, k, 1, (w0, w1), bx, by, bz, inv, acc)
+
+
+def early(first, k, coeffs, state, ya, yb):
+    return pl.pallas_call(
+        functools.partial(early_kernel, first, k),
+        out_shape=(EXT, EXT, ACC),
+        in_specs=[VMEM] * 7 + [ANY] * 2,
+        out_specs=(VMEM,) * 3,
+        scratch_shapes=[pltpu.SemaphoreType.DMA((2,))],
+        input_output_aliases={4: 0, 5: 1, 6: 2},
+        compiler_params=pltpu.CompilerParams(vmem_limit_bytes=2 * MIB),
+        name="early",
+    )(*coeffs, *state, ya, yb)
 
 
 def later_kernel(
     first, k, k_next,
-    bx, by, bz, inv, w_in, acc_in, xa, xb, ya, yb, ca, cb,
-    w0, acc, xa_out, xb_out, ya_out, yb_out,
-    w1, in_sems, out_sems,
+    bx, by, bz, inv, w_in, w1_in, acc_in, xa, xb, ca, cb,
+    w0, w1, acc, xa_out, xb_out, ya_out, yb_out,
+    in_sems, out_sems,
 ):
     sides = Sides()
     into = Copies(in_sems)
-    land_later(k, sides, into, {"a": xa, "b": xb}, {"a": ya, "b": yb}, {"a": ca, "b": cb}, w0)
+    land_later_x(k, sides, into, {"a": xa, "b": xb}, {"a": ca, "b": cb}, w0)
     into.wait()
-    w = steps_of(first, k, False, (w0, w1), bx, by, bz, inv, acc)
+    w = other_steps(first, k, 1, False, (w0, w1), bx, by, bz, inv, acc)
     out = Copies(out_sems)
     leave(k_next, sides, out, w, xa_out, xb_out, ya_out, yb_out)
     out.wait()
 
 
 def later_round(first, k, k_next, *arrays):
-    assert k % 2 == 0
-    w, acc, *strips = pl.pallas_call(
+    w0, w1, acc, *strips = pl.pallas_call(
         functools.partial(later_kernel, first, k, k_next),
-        out_shape=(EXT, ACC) + strips_shape(k_next),
-        in_specs=[VMEM] * 6 + [ANY] * 6,
-        out_specs=(VMEM,) * 2 + (ANY,) * 4,
-        scratch_shapes=[EXT, pltpu.SemaphoreType.DMA((8,)), pltpu.SemaphoreType.DMA((4,))],
-        input_output_aliases={4: 0, 5: 1},
-        compiler_params=pltpu.CompilerParams(vmem_limit_bytes=6 * MIB),
+        out_shape=(EXT, EXT, ACC) + strips_shape(k_next),
+        in_specs=[VMEM] * 7 + [ANY] * 4,
+        out_specs=(VMEM,) * 3 + (ANY,) * 4,
+        scratch_shapes=[pltpu.SemaphoreType.DMA((6,)), pltpu.SemaphoreType.DMA((4,))],
+        input_output_aliases={4: 0, 5: 1, 6: 2},
+        compiler_params=pltpu.CompilerParams(vmem_limit_bytes=2 * MIB),
         name="later_round",
     )(*arrays)
-    return (w, acc), strips
+    return ((w0, w1)[k % 2], (w1, w0)[k % 2], acc), strips
 
 
 def last_kernel(
     first, k,
-    tile_rows, targets, mask, slots, bx, by, bz, inv, w_in, acc_in, xa, xb, ya, yb, ca, cb,
-    grad, sent, w0, acc,
-    w1, in_sems,
+    tile_rows, targets, mask, slots, bx, by, bz, inv, w_in, w1_in, acc_in, xa, xb, ca, cb,
+    grad, sent, w0, w1, acc,
+    in_sems,
 ):
     sides = Sides()
     into = Copies(in_sems)
-    land_later(k, sides, into, {"a": xa, "b": xb}, {"a": ya, "b": yb}, {"a": ca, "b": cb}, w0)
+    land_later_x(k, sides, into, {"a": xa, "b": xb}, {"a": ca, "b": cb}, w0)
     sent[...] = jnp.zeros_like(sent)
     peers = slots.shape[0]
     sent[pl.ds(CAP, peers, stride=CAP + 1), :] = slots[...]
     into.wait()
-    steps_of(first, k, True, (w0, w1), bx, by, bz, inv, acc)
+    other_steps(first, k, 1, True, (w0, w1), bx, by, bz, inv, acc)
     flat = acc.reshape(NX * NY * 8, 128)
 
     @pl.loop(0, mask.shape[0] // 8)
@@ -437,13 +499,14 @@
             jax.ShapeDtypeStruct((NX, NY, 1024), F32),
             jax.ShapeDtypeStruct((peers * (CAP + 1), 128), F32),
             EXT,
+            EXT,
             ACC,
         ),
-        in_specs=[SMEM, SMEM] + [VMEM] * 8 + [ANY] * 6,
-        out_specs=(VMEM,) * 4,
-        scratch_shapes=[EXT, pltpu.SemaphoreType.DMA((8,))],
-        input_output_aliases={8: 2, 9: 3},
-        compiler_params=pltpu.CompilerParams(vmem_limit_bytes=10 * MIB),
+        in_specs=[SMEM, SMEM] + [VMEM] * 9 + [ANY] * 4,
+        out_specs=(VMEM,) * 5,
+        scratch_shapes=[pltpu.SemaphoreType.DMA((6,))],
+        input_output_aliases={8: 2, 9: 3, 10: 4},
+        compiler_params=pltpu.CompilerParams(vmem_limit_bytes=6 * MIB),
         name="last_round",
     )(*arrays)[:2]
 
@@ -499,14 +562,19 @@
     k = ROUNDS[0]
     *fields, xa, xb, xb_z, ya, yb = pack(k, grad_pressure, beta)
     counts = [f[1:] for f in fields_of(k)]
-    coeffs, state, strips = first_round(k, ROUNDS[1], *fields, *exchange(k, counts, xa, xb, ya, yb, xb_z))
+    xa, xb, ya, yb, *corner = exchange(k, counts, xa, xb, ya, yb, xb_z)
+    coeffs, state, strips = first_round(k, ROUNDS[1], *early_first(k, fields, ya, yb), xa, xb, *corner)
     done = k
     for k, k_next in zip(ROUNDS[1:-1], ROUNDS[2:]):
-        state, strips = later_round(done, k, k_next, *coeffs, *state, *exchange(k - 1, [(k, k - 1)], *strips))
+        xa, xb, ya, yb, *corner = exchange(k - 1, [(k, k - 1)], *strips)
+        state = early(done, k, coeffs, state, ya, yb)
+        state, strips = later_round(done, k, k_next, *coeffs, *state, xa, xb, *corner)
         done += k
     k = ROUNDS[-1]
+    xa, xb, ya, yb, *corner = exchange(k - 1, [(k, k - 1)], *strips)
+    state = early(done, k, coeffs, state, ya, yb)
     grad_rhs, sent = last_round(
-        done, k, peers, tile_rows, targets, face_mask, slots, *coeffs, *state, *exchange(k - 1, [(k, k - 1)], *strips)
+        done, k, peers, tile_rows, targets, face_mask, slots, *coeffs, *state, xa, xb, *corner
     )
     sent = sent.reshape(peers, 1, (CAP + 1) * 128)
     received = lax.all_to_all(sent, ("gx", "gy"), split_axis=0, concat_axis=0, tiled=True)

time: 124 us -> 119 us (0.960)
  waiting for transfers between devices: 24.6 us -> 17 us
  Pallas kernels: 27.3 us -> 29.5 us
    ppermute x18, waiting for transfers between devices: 15.1 us -> 7.5 us  [swap(): lax.ppermute(array, axis, [(i, j) for i, j in pairs if 0 <= j < size])]
    pallas_call x0 -> x3, Pallas kernels: none -> 7.49 us  [the longest x2 4.59 us: early(): pl.pallas_call(functools.partial(early_kernel, first, k), out_shape=(EXT,...]
    pallas_call x1, Pallas kernels: 7.2 us -> 4.96 us  [first_round(): pl.pallas_call(functools.partial(first_kernel, k, k_next), out_shape=(EXT...]
    pallas_call x1, Pallas kernels: 8.45 us -> 6.88 us  [last_round(): pl.pallas_call(functools.partial(last_kernel, first, k), out_shape=(jax.S...]
    pallas_call x1, Pallas kernels: 6.19 us -> 4.71 us  [later_round(): pl.pallas_call(functools.partial(later_kernel, first, k, k_next), out_sha...]
  transfers between devices with their start and end apart: 20 -> 20, of which waited for: 5 -> 5; matrix products, arithmetic and copies ran while one was open for 0% -> 0% of each run, Pallas kernels for 1% -> 7%
where the time goes in v6:
time: 119 us; the launch traced here: 118 us
  starting transfers between devices  38.3 us (32%)
  blocking collectives  31.8 us (27%)
  Pallas kernels  29.5 us (25%)
  waiting for transfers between devices  17 us (14%)
    ppermute x18, starting transfers between devices, swap(): lax.ppermute(array, axis, [(i, j) for i, j in pairs if 0 <= j < size])  35.2 us
    all_to_all x1, blocking collectives, shards(): lax.all_to_all(sent, ('gx', 'gy'), split_axis=0, concat_axis=0, tiled=True)  31.8 us
    ppermute x1, waiting for transfers between devices, exchange(): lax.ppermute(xb_z, 'gx', pairs + [(middle - 1, 0), (middle, size - 1)])  9.5 us
    ppermute x18, waiting for transfers between devices, swap(): lax.ppermute(array, axis, [(i, j) for i, j in pairs if 0 <= j < size])  7.5 us
    pallas_call x1, Pallas kernels, last_round(): pl.pallas_call(functools.partial(last_kernel, first, k), out_shape=(jax.S...  6.88 us
    pallas_call x1, Pallas kernels, first_round(): pl.pallas_call(functools.partial(first_kernel, k, k_next), out_shape=(EXT...  4.96 us
    pallas_call x1, Pallas kernels, later_round(): pl.pallas_call(functools.partial(later_kernel, first, k, k_next), out_sha...  4.71 us
    pallas_call x2, Pallas kernels, early(): pl.pallas_call(functools.partial(early_kernel, first, k), out_shape=(EXT,...  4.59 us
  transfers between devices with their start and end apart: 20, of which 5 were waited for; matrix products, arithmetic and copies ran while one was open for 0% of the time, Pallas kernels for 7%

profile of v6, /device:TPU:1, one launch (start us, length us, event | category | flops | bytes accessed | tf_op | source)
XLA Modules:
  0.0 118.1 jit_solution(3770030562115100518)
XLA Ops:
  0.6 3.2 %pack.1 = (f32[16,40,8,128]{3,2,1,0:T(8,128)S(1)}, f32[16,40,8,128]{3,2,1,0:T(8,128)S(1)}, f32[16,40,8,128]{3,2,1,0:T(8,128)S(1)}, f32[16,40,8,128]{3,2,1,0:T(8,...) custom-call(f32[8,32,1024]{2,1,0:T(8,128)} %g.1, ...), custom_call_target="tpu_custom_call" | custom-call | tf_op jit(solution)/shard_map/pack/pallas_call | solution.py:140
  3.9 1.5 %collective-permute-start.2 = (f32[13,32,8,128]{3,2,1,0:T(8,128)S(1)}, f32[13,32,8,128]{3,2,1,0:T(8,128)S(1)}, u32[]{:S(2)}, u32[]{:S(2)}) collective-permute-start(f32[13,32,8,128]{3,2,1,0:T(8,128)S(1)} %get-tuple-element.63), channel_id=1, source_target_pairs={{0,8},{8,0},{16,24},{24,16},{32,40},{40,32},{48,56},{56,48},{64,72... | collective-permute-start | bytes 5111816 | tf_op jit(solution)/shard_map/ppermute | solution.py:190
  5.4 3.5 %collective-permute-start.3 = (f32[10,32,8,128]{3,2,1,0:T(8,128)S(1)}, f32[10,32,8,128]{3,2,1,0:T(8,128)S(1)}, u32[]{:S(2)}, u32[]{:S(2)}) collective-permute-start(f32[10,32,8,128]{3,2,1,0:T(8,128)S(1)} %get-tuple-element.64), channel_id=1, source_target_pairs={{8,16},{16,8},{24,32},{32,24},{40,48},{48,40},{56,64},{64,56},{72,... | collective-permute-start | bytes 3932168 | tf_op jit(solution)/shard_map/ppermute | solution.py:190
  8.9 1.3 %collective-permute-start = (f32[8,13,8,128]{3,2,1,0:T(8,128)S(1)}, f32[8,13,8,128]{3,2,1,0:T(8,128)S(1)}, u32[]{:S(2)}, u32[]{:S(2)}) collective-permute-start(f32[8,13,8,128]{3,2,1,0:T(8,128)S(1)} %get-tuple-element.54), channel_id=1, source_target_pairs={{0,1},{1,0},{2,3},{3,2},{4,5},{5,4},{6,7},{7,6},{8,9},{9,8},{10,11... | collective-permute-start | bytes 1277960 | tf_op jit(solution)/shard_map/ppermute | solution.py:190
  10.2 0.7 collective-permute-start.1
  10.9 2.4 %collective-permute-start.6 = (f32[3,32,8,128]{3,2,1,0:T(8,128)S(1)}, f32[3,32,8,128]{3,2,1,0:T(8,128)S(1)}, u32[]{:S(2)}, u32[]{:S(2)}) collective-permute-start(f32[3,32,8,128]{3,2,1,0:T(8,128)S(1)} %get-tuple-element.67), channel_id=1, source_target_pairs={{8,16},{16,8},{24,32},{32,24},{40,48},{48,40},{72,80},{80,72},{88,... | collective-permute-start | bytes 1179656 | tf_op jit(solution)/shard_map/ppermute | solution.py:216
  13.3 5.2 %collective-permute-done.ya = f32[8,13,8,128]{3,2,1,0:T(8,128)S(1)} collective-permute-done((f32[8,13,8,128]{3,2,1,0:T(8,128)S(1)}, f32[8,13,8,128]{3,2,1,0:T(8,128)S(1)}, u32[]{:S(2)}, u32[]{:S(2)}) %collective-permute-start) | collective-permute-done | bytes 426016 | tf_op jit(solution)/shard_map/ppermute | solution.py:190
  18.5 0.0 collective-permute-done.1.yb
  18.5 0.4 corners.3
  18.9 0.1 collective-permute-start.4
  19.0 9.5 %collective-permute-done.6.array.z_plain = f32[3,32,8,128]{3,2,1,0:T(8,128)S(1)} collective-permute-done((f32[3,32,8,128]{3,2,1,0:T(8,128)S(1)}, f32[3,32,8,128]{3,2,1,0:T(8,128)S(1)}, u32[]{:S(2)}, u32[]{:S(2)}) %collective-permute-start.6) | collective-permute-done | bytes 393248 | tf_op jit(solution)/shard_map/ppermute | solution.py:216
  28.5 0.0 collective-permute-done.4.after.ca
  28.5 0.2 relay.1
  28.7 0.7 collective-permute-start.7
  29.4 3.5 %collective-permute-start.5 = (f32[2,3,10,8,128]{4,3,2,1,0:T(8,128)S(1)}, f32[2,3,10,8,128]{4,3,2,1,0:T(8,128)S(1)}, u32[]{:S(2)}, u32[]{:S(2)}) collective-permute-start(f32[2,3,10,8,128]{4,3,2,1,0:T(8,128)S(1)} %get-tuple-element.66), channel_id=1, source_target_pairs={{8,16},{16,8},{24,32},{32,24},{40,48},{48,40},{56,64},{64,56},{72,... | collective-permute-start | bytes 737288 | tf_op jit(solution)/shard_map/ppermute | solution.py:190
  32.9 2.9 %early_first.1 = (f32[16,40,8,128]{3,2,1,0:T(8,128)S(1)}, f32[16,40,8,128]{3,2,1,0:T(8,128)S(1)}, f32[16,40,8,128]{3,2,1,0:T(8,128)S(1)}, f32[16,40,8,128]{3,2,1...) custom-call(f32[16,40,8,128]{3,2,1,0:T(8,128)S(1)} %get-tuple-elemen, ...), custom_call_target="tpu_custom_call", output_to_operand_aliasing={{0}: (0, {}), {1}: (1, {}), {2}: (2, {}), {3}: (3, {})} | custom-call | tf_op jit(solution)/shard_map/early_first/pallas_call | solution.py:368
  35.8 1.1 collective-permute-done.5.cb
  36.9 0.0 collective-permute-done.7.z_ends
  36.9 0.0 collective-permute-done.3.xb
  36.9 0.0 collective-permute-done.2.xa
  36.9 0.0 copy-start.4
  36.9 5.0 %first_round.1 = (f32[16,40,8,128]{3,2,1,0:T(8,128)S(1)}, f32[16,40,8,128]{3,2,1,0:T(8,128)S(1)}, f32[16,40,8,128]{3,2,1,0:T(8,128)S(1)}, f32[16,40,8,128]{3,2,1...) custom-call(f32[16,40,8,128]{3,2,1,0:T(8,128)S(1)} %get-tuple-elemen, ...), custom_call_target="tpu_custom_call", output_to_operand_aliasing={{0}: (0, {}), {1}: (1, {}), {2}: (2, {}), {3}: (3, {}), {4}... | custom-call | tf_op jit(solution)/shard_map/first_round/pallas_call | solution.py:399
  41.9 1.4 %collective-permute-start.8 = (f32[8,4,8,128]{3,2,1,0:T(8,128)S(1)}, f32[8,4,8,128]{3,2,1,0:T(8,128)S(1)}, u32[]{:S(2)}, u32[]{:S(2)}) collective-permute-start(f32[8,4,8,128]{3,2,1,0:T(8,128)S(1)} %get-tuple-element.75), channel_id=1, source_target_pairs={{0,1},{1,0},{2,3},{3,2},{4,5},{5,4},{6,7},{7,6},{8,9},{9,8},{10,11... | collective-permute-start | bytes 393224 | tf_op jit(solution)/shard_map/ppermute | solution.py:190
  43.3 0.7 collective-permute-start.9
  43.9 0.0 copy-done.4
  44.0 0.1 collective-permute-start.10
  44.0 0.0 copy-start.3
  44.1 4.0 %collective-permute-start.11 = (f32[4,32,8,128]{3,2,1,0:T(8,128)S(1)}, f32[4,32,8,128]{3,2,1,0:T(8,128)S(1)}, u32[]{:S(2)}, u32[]{:S(2)}) collective-permute-start(f32[4,32,8,128]{3,2,1,0:T(8,128)S(1)} %get-tuple-element.81), channel_id=1, source_target_pairs={{8,16},{16,8},{24,32},{32,24},{40,48},{48,40},{56,64},{64,56},{72,... | collective-permute-start | bytes 1572872 | tf_op jit(solution)/shard_map/ppermute | solution.py:190
  48.1 0.0 collective-permute-done.8.ya
  48.1 0.0 collective-permute-done.9.yb
  48.1 0.1 corners.4
  48.3 0.1 collective-permute-start.12
  48.4 3.9 %collective-permute-start.13 = (f32[2,3,3,8,128]{4,3,2,1,0:T(8,128)S(1)}, f32[2,3,3,8,128]{4,3,2,1,0:T(8,128)S(1)}, u32[]{:S(2)}, u32[]{:S(2)}) collective-permute-start(f32[2,3,3,8,128]{4,3,2,1,0:T(8,128)S(1)} %get-tuple-element.83), channel_id=1, source_target_pairs={{8,16},{16,8},{24,32},{32,24},{40,48},{48,40},{56,64},{64,56},{72,... | collective-permute-start | bytes 221192 | tf_op jit(solution)/shard_map/ppermute | solution.py:190
  52.3 0.0 copy-done.3
  52.3 0.2 convert_reduce_fusion
  52.5 2.3 %early.2 = (f32[16,40,8,128]{3,2,1,0:T(8,128)S(1)}, f32[16,40,8,128]{3,2,1,0:T(8,128)S(1)}, f32[8,32,8,128]{3,2,1,0:T(8,128)S(1)}) custom-call(f32[16,40,8,128]{3,2,1,0:T(8,128)S(1)} %get-tuple-element.68.bx, f32[16,40,8,128]{3,2,1,0:T(8,128)S(1)} %get-tuple-element.69.by, ...), custom_call_target="tpu_custom_call", output_to_operand_aliasing={{0}: (4, {}), {1}: (5, {}), {2}: (6, {})} | custom-call | tf_op jit(solution)/shard_map/early/pallas_call | solution.py:422
  54.8 0.0 collective-permute-done.12.ca
  54.8 1.0 collective-permute-done.13.cb
  55.7 0.0 collective-permute-done.10.xa
  55.7 0.0 collective-permute-done.11.xb
  55.7 4.7 %later_round.1 = (f32[16,40,8,128]{3,2,1,0:T(8,128)S(1)}, f32[16,40,8,128]{3,2,1,0:T(8,128)S(1)}, f32[8,32,8,128]{3,2,1,0:T(8,128)S(1)}, f32[4,32,8,128]{3,2,1,0...) custom-call(f32[16,40,8,128]{3,2,1,0:T(8,128)S(1)} %get-tuple-elemen, ...), custom_call_target="tpu_custom_call", output_to_operand_aliasing={{0}: (4, {}), {1}: (5, {}), {2}: (6, {})} | custom-call | tf_op jit(solution)/shard_map/later_round/pallas_call | solution.py:451
  60.5 5.1 %collective-permute-start.14 = (f32[8,4,8,128]{3,2,1,0:T(8,128)S(1)}, f32[8,4,8,128]{3,2,1,0:T(8,128)S(1)}, u32[]{:S(2)}, u32[]{:S(2)}) collective-permute-start(f32[8,4,8,128]{3,2,1,0:T(8,128)S(1)} %get-tuple-element.87), channel_id=1, source_target_pairs={{0,1},{1,0},{2,3},{3,2},{4,5},{5,4},{6,7},{7,6},{8,9},{9,8},{10,11... | collective-permute-start | bytes 393224 | tf_op jit(solution)/shard_map/ppermute | solution.py:190
  65.6 0.7 collective-permute-start.15
  66.2 0.3 fusion.1.slots
  66.6 0.1 collective-permute-start.16
  66.7 3.6 %collective-permute-start.17 = (f32[4,32,8,128]{3,2,1,0:T(8,128)S(1)}, f32[4,32,8,128]{3,2,1,0:T(8,128)S(1)}, u32[]{:S(2)}, u32[]{:S(2)}) collective-permute-start(f32[4,32,8,128]{3,2,1,0:T(8,128)S(1)} %get-tuple-element.93), channel_id=1, source_target_pairs={{8,16},{16,8},{24,32},{32,24},{40,48},{48,40},{56,64},{64,56},{72,... | collective-permute-start | bytes 1572872 | tf_op jit(solution)/shard_map/ppermute | solution.py:190
  70.3 0.0 collective-permute-done.14.ya
  70.3 0.0 collective-permute-done.15.yb
  70.3 0.1 corners.5
  70.5 0.1 collective-permute-start.18
  70.6 4.8 %collective-permute-start.19 = (f32[2,3,3,8,128]{4,3,2,1,0:T(8,128)S(1)}, f32[2,3,3,8,128]{4,3,2,1,0:T(8,128)S(1)}, u32[]{:S(2)}, u32[]{:S(2)}) collective-permute-start(f32[2,3,3,8,128]{4,3,2,1,0:T(8,128)S(1)} %get-tuple-element.95), channel_id=1, source_target_pairs={{8,16},{16,8},{24,32},{32,24},{40,48},{48,40},{56,64},{64,56},{72,... | collective-permute-start | bytes 221192 | tf_op jit(solution)/shard_map/ppermute | solution.py:190
  75.4 0.0 copy-start.1
  75.4 0.0 copy-start.2
  75.4 2.3 %early.3 = (f32[16,40,8,128]{3,2,1,0:T(8,128)S(1)}, f32[16,40,8,128]{3,2,1,0:T(8,128)S(1)}, f32[8,32,8,128]{3,2,1,0:T(8,128)S(1)}) custom-call(f32[16,40,8,128]{3,2,1,0:T(8,128)S(1)} %get-tuple-element.68.bx, f32[16,40,8,128]{3,2,1,0:T(8,128)S(1)} %get-tuple-element.69.by, ...), custom_call_target="tpu_custom_call", output_to_operand_aliasing={{0}: (4, {}), {1}: (5, {}), {2}: (6, {})} | custom-call | tf_op jit(solution)/shard_map/early/pallas_call | solution.py:422
  77.7 0.0 collective-permute-done.18.ca
  77.8 0.2 collective-permute-done.19.cb
  78.0 0.0 collective-permute-done.16.xa
  78.0 0.0 collective-permute-done.17.xb
  78.0 0.0 copy-done.2
  78.0 0.0 copy-start
  78.0 6.9 %last_round.1 = (f32[8,32,1024]{2,1,0:T(8,128)}, f32[1152,128]{1,0:T(8,128)S(1)}, f32[16,40,8,128]{3,2,1,0:T(8,128)S(1)}, f32[16,40,8,128]{3,2,1,0:T(8,128)S(1)}, f32[8,32,8,128]{3,2,1,0:T(8,128)S(1)}) custom-call(s32[256]{0:T(256)S(1)} %copy-done.2, s32[256]{0:T(256)S(1)} %multiply_add_fusion.targets, ...), custom_call_target="tpu_custom_call", output_to_operand_aliasing={{2}: (8, {}), {3}: (9, {}), {4}: (10, {})} | custom-call | tf_op jit(solution)/shard_map/last_round/pallas_call | solution.py:496
  84.9 31.8 %all_to_all.5 = f32[128,1,1152]{2,1,0:T(1,128)S(1)} all-to-all(f32[128,1,1152]{2,1,0:T(1,128)S(1)} %bitcast.4), channel_id=1, replica_groups=mesh['gx'=16,'gy'=8] {'gx','gy'}, dimensions={0} | all-to-all | bytes 1179648 | tf_op jit(solution)/shard_map/all_to_all | solution.py:580
  116.7 0.0 copy-done
  116.7 1.4 %finish.1 = f32[3,256,128]{2,1,0:T(8,128)} custom-call(f32[1152,128]{1,0:T(8,128)S(1)} %bitcast.3, f32[3,256,128]{2,1,0:T(8,128)S(1)} %copy-done), custom_call_target="tpu_custom_call" | custom-call | tf_op jit(solution)/shard_map/finish/pallas_call | solution.py:538
  (3 shorter events, 0.0 us)
Async XLA Ops:
  3.9 33.1 %collective-permute-start.2 = (f32[13,32,8,128]{3,2,1,0:T(8,128)S(1)}, f32[13,32,8,128]{3,2,1,0:T(8,128)S(1)}, u32[]{:S(2)}, u32[]{:S(2)}) collective-permute-start(f32[13,32,8,128]{3,2,1,0:T(8,128)S(1)} %get-tuple-element.63), channel_id=1, source_target_pairs={{0,8},{8,0},{16,24},{24,16},{32,40},{40,32},{48,56},{56,48},{64,72... | collective-permute-start | bytes 5111816 | tf_op jit(solution)/shard_map/ppermute | solution.py:190
  5.4 31.5 %collective-permute-start.3 = (f32[10,32,8,128]{3,2,1,0:T(8,128)S(1)}, f32[10,32,8,128]{3,2,1,0:T(8,128)S(1)}, u32[]{:S(2)}, u32[]{:S(2)}) collective-permute-start(f32[10,32,8,128]{3,2,1,0:T(8,128)S(1)} %get-tuple-element.64), channel_id=1, source_target_pairs={{8,16},{16,8},{24,32},{32,24},{40,48},{48,40},{56,64},{64,56},{72,... | collective-permute-start | bytes 3932168 | tf_op jit(solution)/shard_map/ppermute | solution.py:190
  8.9 9.6 %collective-permute-start = (f32[8,13,8,128]{3,2,1,0:T(8,128)S(1)}, f32[8,13,8,128]{3,2,1,0:T(8,128)S(1)}, u32[]{:S(2)}, u32[]{:S(2)}) collective-permute-start(f32[8,13,8,128]{3,2,1,0:T(8,128)S(1)} %get-tuple-element.54), channel_id=1, source_target_pairs={{0,1},{1,0},{2,3},{3,2},{4,5},{5,4},{6,7},{7,6},{8,9},{9,8},{10,11... | collective-permute-start | bytes 1277960 | tf_op jit(solution)/shard_map/ppermute | solution.py:190
  10.2 8.3 %collective-permute-start.1 = (f32[8,13,8,128]{3,2,1,0:T(8,128)S(1)}, f32[8,13,8,128]{3,2,1,0:T(8,128)S(1)}, u32[]{:S(2)}, u32[]{:S(2)}) collective-permute-start(f32[8,13,8,128]{3,2,1,0:T(8,128)S(1)} %get-tuple-element.55), channel_id=1, source_target_pairs={{1,2},{2,1},{3,4},{4,3},{5,6},{6,5},{9,10},{10,9},{11,12},{12,11},... | collective-permute-start | bytes 1277960 | tf_op jit(solution)/shard_map/ppermute | solution.py:190
  10.9 17.6 %collective-permute-start.6 = (f32[3,32,8,128]{3,2,1,0:T(8,128)S(1)}, f32[3,32,8,128]{3,2,1,0:T(8,128)S(1)}, u32[]{:S(2)}, u32[]{:S(2)}) collective-permute-start(f32[3,32,8,128]{3,2,1,0:T(8,128)S(1)} %get-tuple-element.67), channel_id=1, source_target_pairs={{8,16},{16,8},{24,32},{32,24},{40,48},{48,40},{72,80},{80,72},{88,... | collective-permute-start | bytes 1179656 | tf_op jit(solution)/shard_map/ppermute | solution.py:216
  18.9 9.6 %collective-permute-start.4 = (f32[2,3,10,8,128]{4,3,2,1,0:T(8,128)S(1)}, f32[2,3,10,8,128]{4,3,2,1,0:T(8,128)S(1)}, u32[]{:S(2)}, u32[]{:S(2)}) collective-permute-start(f32[2,3,10,8,128]{4,3,2,1,0:T(8,128)S(1)} %get-tuple-element.65), channel_id=1, source_target_pairs={{0,8},{8,0},{16,24},{24,16},{32,40},{40,32},{48,56},{56,48},{64,72... | collective-permute-start | bytes 737288 | tf_op jit(solution)/shard_map/ppermute | solution.py:190
  28.7 8.2 %collective-permute-start.7 = (f32[3,32,8,128]{3,2,1,0:T(8,128)S(1)}, f32[3,32,8,128]{3,2,1,0:T(8,128)S(1)}, u32[]{:S(2)}, u32[]{:S(2)}) collective-permute-start(f32[3,32,8,128]{3,2,1,0:T(8,128)S(1)} %relay.1), channel_id=1, source_target_pairs={{0,64},{120,56},{1,65},{121,57},{2,66},{122,58},{3,67},{123,59},{4... | collective-permute-start | bytes 1179656 | tf_op jit(solution)/shard_map/ppermute | solution.py:223
  29.4 7.5 %collective-permute-start.5 = (f32[2,3,10,8,128]{4,3,2,1,0:T(8,128)S(1)}, f32[2,3,10,8,128]{4,3,2,1,0:T(8,128)S(1)}, u32[]{:S(2)}, u32[]{:S(2)}) collective-permute-start(f32[2,3,10,8,128]{4,3,2,1,0:T(8,128)S(1)} %get-tuple-element.66), channel_id=1, source_target_pairs={{8,16},{16,8},{24,32},{32,24},{40,48},{48,40},{56,64},{64,56},{72,... | collective-permute-start | bytes 737288 | tf_op jit(solution)/shard_map/ppermute | solution.py:190
  36.9 7.0 %copy-start.4 = (s32[256]{0:T(256)S(1)}, s32[256]{0:T(256)}, u32[]{:S(2)}) copy-start(s32[256]{0:T(256)} %param.11) | copy-start | bytes 3076
  41.9 6.2 %collective-permute-start.8 = (f32[8,4,8,128]{3,2,1,0:T(8,128)S(1)}, f32[8,4,8,128]{3,2,1,0:T(8,128)S(1)}, u32[]{:S(2)}, u32[]{:S(2)}) collective-permute-start(f32[8,4,8,128]{3,2,1,0:T(8,128)S(1)} %get-tuple-element.75), channel_id=1, source_target_pairs={{0,1},{1,0},{2,3},{3,2},{4,5},{5,4},{6,7},{7,6},{8,9},{9,8},{10,11... | collective-permute-start | bytes 393224 | tf_op jit(solution)/shard_map/ppermute | solution.py:190
  43.3 4.8 %collective-permute-start.9 = (f32[8,4,8,128]{3,2,1,0:T(8,128)S(1)}, f32[8,4,8,128]{3,2,1,0:T(8,128)S(1)}, u32[]{:S(2)}, u32[]{:S(2)}) collective-permute-start(f32[8,4,8,128]{3,2,1,0:T(8,128)S(1)} %get-tuple-element.76), channel_id=1, source_target_pairs={{1,2},{2,1},{3,4},{4,3},{5,6},{6,5},{9,10},{10,9},{11,12},{12,11},... | collective-permute-start | bytes 393224 | tf_op jit(solution)/shard_map/ppermute | solution.py:190
  44.0 11.8 %collective-permute-start.10 = (f32[4,32,8,128]{3,2,1,0:T(8,128)S(1)}, f32[4,32,8,128]{3,2,1,0:T(8,128)S(1)}, u32[]{:S(2)}, u32[]{:S(2)}) collective-permute-start(f32[4,32,8,128]{3,2,1,0:T(8,128)S(1)} %get-tuple-element.80), channel_id=1, source_target_pairs={{0,8},{8,0},{16,24},{24,16},{32,40},{40,32},{48,56},{56,48},{64,72... | collective-permute-start | bytes 1572872 | tf_op jit(solution)/shard_map/ppermute | solution.py:190
  44.0 8.2 %copy-start.3 = (s32[256,1]{0,1:T(1,128)S(1)}, s32[256,1]{0,1:T(1,128)}, u32[]{:S(2)}) copy-start(s32[256,1]{0,1:T(1,128)} %param.10) | copy-start | bytes 3076
  44.1 11.7 %collective-permute-start.11 = (f32[4,32,8,128]{3,2,1,0:T(8,128)S(1)}, f32[4,32,8,128]{3,2,1,0:T(8,128)S(1)}, u32[]{:S(2)}, u32[]{:S(2)}) collective-permute-start(f32[4,32,8,128]{3,2,1,0:T(8,128)S(1)} %get-tuple-element.81), channel_id=1, source_target_pairs={{8,16},{16,8},{24,32},{32,24},{40,48},{48,40},{56,64},{64,56},{72,... | collective-permute-start | bytes 1572872 | tf_op jit(solution)/shard_map/ppermute | solution.py:190
  48.3 6.5 %collective-permute-start.12 = (f32[2,3,3,8,128]{4,3,2,1,0:T(8,128)S(1)}, f32[2,3,3,8,128]{4,3,2,1,0:T(8,128)S(1)}, u32[]{:S(2)}, u32[]{:S(2)}) collective-permute-start(f32[2,3,3,8,128]{4,3,2,1,0:T(8,128)S(1)} %get-tuple-element.82), channel_id=1, source_target_pairs={{0,8},{8,0},{16,24},{24,16},{32,40},{40,32},{48,56},{56,48},{64,72... | collective-permute-start | bytes 221192 | tf_op jit(solution)/shard_map/ppermute | solution.py:190
  48.4 7.4 %collective-permute-start.13 = (f32[2,3,3,8,128]{4,3,2,1,0:T(8,128)S(1)}, f32[2,3,3,8,128]{4,3,2,1,0:T(8,128)S(1)}, u32[]{:S(2)}, u32[]{:S(2)}) collective-permute-start(f32[2,3,3,8,128]{4,3,2,1,0:T(8,128)S(1)} %get-tuple-element.83), channel_id=1, source_target_pairs={{8,16},{16,8},{24,32},{32,24},{40,48},{48,40},{56,64},{64,56},{72,... | collective-permute-start | bytes 221192 | tf_op jit(solution)/shard_map/ppermute | solution.py:190
  60.5 9.8 %collective-permute-start.14 = (f32[8,4,8,128]{3,2,1,0:T(8,128)S(1)}, f32[8,4,8,128]{3,2,1,0:T(8,128)S(1)}, u32[]{:S(2)}, u32[]{:S(2)}) collective-permute-start(f32[8,4,8,128]{3,2,1,0:T(8,128)S(1)} %get-tuple-element.87), channel_id=1, source_target_pairs={{0,1},{1,0},{2,3},{3,2},{4,5},{5,4},{6,7},{7,6},{8,9},{9,8},{10,11... | collective-permute-start | bytes 393224 | tf_op jit(solution)/shard_map/ppermute | solution.py:190
  65.6 4.8 %collective-permute-start.15 = (f32[8,4,8,128]{3,2,1,0:T(8,128)S(1)}, f32[8,4,8,128]{3,2,1,0:T(8,128)S(1)}, u32[]{:S(2)}, u32[]{:S(2)}) collective-permute-start(f32[8,4,8,128]{3,2,1,0:T(8,128)S(1)} %get-tuple-element.88), channel_id=1, source_target_pairs={{1,2},{2,1},{3,4},{4,3},{5,6},{6,5},{9,10},{10,9},{11,12},{12,11},... | collective-permute-start | bytes 393224 | tf_op jit(solution)/shard_map/ppermute | solution.py:190
  66.6 11.4 %collective-permute-start.16 = (f32[4,32,8,128]{3,2,1,0:T(8,128)S(1)}, f32[4,32,8,128]{3,2,1,0:T(8,128)S(1)}, u32[]{:S(2)}, u32[]{:S(2)}) collective-permute-start(f32[4,32,8,128]{3,2,1,0:T(8,128)S(1)} %get-tuple-element.92), channel_id=1, source_target_pairs={{0,8},{8,0},{16,24},{24,16},{32,40},{40,32},{48,56},{56,48},{64,72... | collective-permute-start | bytes 1572872 | tf_op jit(solution)/shard_map/ppermute | solution.py:190
  66.7 11.3 %collective-permute-start.17 = (f32[4,32,8,128]{3,2,1,0:T(8,128)S(1)}, f32[4,32,8,128]{3,2,1,0:T(8,128)S(1)}, u32[]{:S(2)}, u32[]{:S(2)}) collective-permute-start(f32[4,32,8,128]{3,2,1,0:T(8,128)S(1)} %get-tuple-element.93), channel_id=1, source_target_pairs={{8,16},{16,8},{24,32},{32,24},{40,48},{48,40},{56,64},{64,56},{72,... | collective-permute-start | bytes 1572872 | tf_op jit(solution)/shard_map/ppermute | solution.py:190
  70.5 7.3 %collective-permute-start.18 = (f32[2,3,3,8,128]{4,3,2,1,0:T(8,128)S(1)}, f32[2,3,3,8,128]{4,3,2,1,0:T(8,128)S(1)}, u32[]{:S(2)}, u32[]{:S(2)}) collective-permute-start(f32[2,3,3,8,128]{4,3,2,1,0:T(8,128)S(1)} %get-tuple-element.94), channel_id=1, source_target_pairs={{0,8},{8,0},{16,24},{24,16},{32,40},{40,32},{48,56},{56,48},{64,72... | collective-permute-start | bytes 221192 | tf_op jit(solution)/shard_map/ppermute | solution.py:190
  70.6 7.4 %collective-permute-start.19 = (f32[2,3,3,8,128]{4,3,2,1,0:T(8,128)S(1)}, f32[2,3,3,8,128]{4,3,2,1,0:T(8,128)S(1)}, u32[]{:S(2)}, u32[]{:S(2)}) collective-permute-start(f32[2,3,3,8,128]{4,3,2,1,0:T(8,128)S(1)} %get-tuple-element.95), channel_id=1, source_target_pairs={{8,16},{16,8},{24,32},{32,24},{40,48},{48,40},{56,64},{64,56},{72,... | collective-permute-start | bytes 221192 | tf_op jit(solution)/shard_map/ppermute | solution.py:190
  75.4 2.5 %copy-start.1 = (s32[256,128]{1,0:T(8,128)S(1)}, s32[256,128]{1,0:T(8,128)}, u32[]{:S(2)}) copy-start(s32[256,128]{1,0:T(8,128)} %mask.1) | copy-start | bytes 393220
  75.4 2.5 %copy-start.2 = (s32[256]{0:T(256)S(1)}, s32[256]{0:T(256)}, u32[]{:S(2)}) copy-start(s32[256]{0:T(256)} %tile_rows.1) | copy-start | bytes 3076
  78.0 38.7 %copy-start = (f32[3,256,128]{2,1,0:T(8,128)S(1)}, f32[3,256,128]{2,1,0:T(8,128)}, u32[]{:S(2)}) copy-start(f32[3,256,128]{2,1,0:T(8,128)} %heights.1) | copy-start | bytes 1179652

commit v7 on v6

--- a/solution.py
+++ b/solution.py
@@ -232,35 +232,29 @@
         at += n
 
 
-def land_first_x(k, sides, into, xs, cs, routed, fields):
+def land_first_x(ab, k, sides, into, strip, corner, routed, fields):
     at_x = at_c = 0
     for i, (in_x, _, in_c) in enumerate(fields_of(k)):
-        for ab in ("a", "b"):
-            x = sides.land("gx", ab, in_x)
-            x_halo = fields[i].at[pl.ds(x, in_x), K : K + NY]
-            if ab == "b" and i == 3:
-                me, size = lax.axis_index("gx"), lax.axis_size("gx")
-                by_ends = (me == 0) | (me == size // 2 - 1) | (me == size // 2) | (me == size - 1)
-                into.start_either(by_ends, routed[1], routed[0], x_halo)
-            else:
-                into.start(xs[ab].at[at_x : at_x + in_x], x_halo)
-            x = sides.land("gx", ab, k)
-            for j, other in enumerate(("a", "b")):
-                y = sides.land("gy", other, in_c)
-                into.start(
-                    cs[ab].at[j, :, at_c : at_c + in_c],
-                    fields[i].at[pl.ds(x, k), pl.ds(y, in_c)],
-                )
+        x_halo = fields[i].at[pl.ds(sides.land("gx", ab, in_x), in_x), K : K + NY]
+        if ab == "b" and i == 3:
+            me, size = lax.axis_index("gx"), lax.axis_size("gx")
+            by_ends = (me == 0) | (me == size // 2 - 1) | (me == size // 2) | (me == size - 1)
+            into.start_either(by_ends, routed[1], routed[0], x_halo)
+        else:
+            into.start(strip.at[at_x : at_x + in_x], x_halo)
+        x = sides.land("gx", ab, k)
+        for j, other in enumerate(("a", "b")):
+            y = sides.land("gy", other, in_c)
+            into.start(corner.at[j, :, at_c : at_c + in_c], fields[i].at[pl.ds(x, k), pl.ds(y, in_c)])
         at_x, at_c = at_x + in_x, at_c + in_c
 
 
-def land_later_x(k, sides, into, xs, cs, w):
-    for ab in ("a", "b"):
-        into.start(xs[ab], w.at[pl.ds(sides.land("gx", ab, k), k), K : K + NY])
-        x = sides.land("gx", ab, k - 1)
-        for j, other in enumerate(("a", "b")):
-            y = sides.land("gy", other, k - 1)
-            into.start(cs[ab].at[j], w.at[pl.ds(x, k - 1), pl.ds(y, k - 1)])
+def land_later_x(ab, k, sides, into, strip, corner, w):
+    into.start(strip, w.at[pl.ds(sides.land("gx", ab, k), k), K : K + NY])
+    x = sides.land("gx", ab, k - 1)
+    for j, other in enumerate(("a", "b")):
+        y = sides.land("gy", other, k - 1)
+        into.start(corner.at[j], w.at[pl.ds(x, k - 1), pl.ds(y, k - 1)])
 
 
 def chunks(low, high, size=8):
@@ -283,11 +277,12 @@
             bz[x, y : y + n] = inner
 
 
-def one_step(step, reach, last, spans, w, new, bx, by, bz, inv, acc):
+def one_step(step, reach, last, span, w, new, bx, by, bz, inv, acc):
     omega = omega_of(step)
 
-    def walk(span, y, n, rows_inside):
-        low, high = span
+    low, high = span
+
+    def walk(y, n, rows_inside):
         below = bx[low - 1, pl.ds(y, n)] * w[low - 1, pl.ds(y, n)]
         around = w[low, pl.ds(y - 1, n + 2)]
         for x in range(low, high):
@@ -311,34 +306,30 @@
             below, around = link * centre, above
 
     if reach:
-        for span in spans:
-            walk(span, K - reach, reach, False)
-            walk(span, K + NY, reach, False)
+        walk(K - reach, reach, False)
+        walk(K + NY, reach, False)
 
     @pl.loop(0, NY // 8)
     def _(i):
-        for span in spans:
-            walk(span, K + i * 8, 8, True)
-
-
-def early_span(i, lead):
-    return K + lead + i, K + NX - 1 - i
-
-
-def early_steps(first, k, lead, w, *arrays):
+        walk(K + i * 8, 8, True)
+
+
+def spans_of(i, k, lead, a_above):
+    low, high = K - (k - 1 - i), K + NX + k - 1 - i
+    cut = K + lead + i if a_above else K + NX - 1 - i
+    return ((cut, high), (low, cut)) if a_above else ((low, cut), (cut, high))
+
+
+def steps_of(first, k, lead, last, late, a_above, w, *arrays):
     for i in range(k):
-        low, high = early_span(i, lead)
-        if low < high:
-            one_step(first + i, k - 1 - i, False, [(low, high)], w[i % 2], w[1 - i % 2], *arrays)
-
-
-def other_steps(first, k, lead, last, w, *arrays):
-    for i in range(k):
-        reach = k - 1 - i
-        low, high = early_span(i, lead)
-        spans = [(K - reach, low), (high, K + NX + reach)] if low < high else [(K - reach, K + NX + reach)]
-        one_step(first + i, reach, last and i == k - 1, spans, w[i % 2], w[1 - i % 2], *arrays)
-    return w[k % 2]
+        span = spans_of(i, k, lead, a_above)[late]
+        one_step(first + i, k - 1 - i, last and i == k - 1, span, w[i % 2], w[1 - i % 2], *arrays)
+
+
+def on_each_side(sides, run):
+    a_above = sides.above["gx", "a"]
+    pl.when(a_above)(functools.partial(run, True))
+    pl.when(jnp.logical_not(a_above))(functools.partial(run, False))
 
 
 def leave(k, sides, out, w, xa, xb, ya, yb):
@@ -355,43 +346,52 @@
     return (x, x, y, y)
 
 
-def early_first_kernel(k, w_in, bx_in, by_in, bz_in, ya, yb, w0, bx, by, bz, inv, acc, w1, sems):
+def early_first_kernel(k, w_in, bx_in, by_in, bz_in, xa, ya, yb, ca, w0, bx, by, bz, inv, acc, w1, sems):
     sides = Sides()
     into = Copies(sems)
-    land_first_y(k, sides, into, {"a": ya, "b": yb}, (w0, bx, by, bz))
+    fields = (w0, bx, by, bz)
+    land_first_y(k, sides, into, {"a": ya, "b": yb}, fields)
+    land_first_x("a", k, sides, into, xa, ca, None, fields)
     into.wait()
-    scale((K + 1, K + NX), w0, bx, by, bz, inv)
-    early_steps(0, k, 2, (w0, w1), bx, by, bz, inv, acc)
-
-
-def early_first(k, fields, ya, yb):
+
+    def run(a_above):
+        scale((K + 1, K + NX + C) if a_above else (K - C, K + NX), w0, bx, by, bz, inv)
+        steps_of(0, k, 2, False, False, a_above, (w0, w1), bx, by, bz, inv, acc)
+
+    on_each_side(sides, run)
+
+
+def early_first(k, fields, *strips):
     return pl.pallas_call(
         functools.partial(early_first_kernel, k),
         out_shape=(EXT,) * 5 + (ACC, EXT),
-        in_specs=[VMEM] * 4 + [ANY] * 2,
+        in_specs=[VMEM] * 4 + [ANY] * 4,
         out_specs=(VMEM,) * 7,
-        scratch_shapes=[pltpu.SemaphoreType.DMA((8,))],
+        scratch_shapes=[pltpu.SemaphoreType.DMA((20,))],
         input_output_aliases={i: i for i in range(4)},
         compiler_params=pltpu.CompilerParams(vmem_limit_bytes=2 * MIB),
         name="early_first",
-    )(*fields, ya, yb)
+    )(*fields, *strips)
 
 
 def first_kernel(
     k, k_next,
-    w_in, bx_in, by_in, bz_in, inv_in, acc_in, w1_in, xa, xb, ca, cb, z_plain, z_ends,
+    w_in, bx_in, by_in, bz_in, inv_in, acc_in, w1_in, xb, cb, z_plain, z_ends,
     w0, bx, by, bz, inv, acc, w1, xa_out, xb_out, ya_out, yb_out,
     in_sems, out_sems,
 ):
     sides = Sides()
     into = Copies(in_sems)
-    land_first_x(k, sides, into, {"a": xa, "b": xb}, {"a": ca, "b": cb}, (z_plain, z_ends), (w0, bx, by, bz))
+    land_first_x("b", k, sides, into, xb, cb, (z_plain, z_ends), (w0, bx, by, bz))
     into.wait()
-    scale((K - C, K + 1), w0, bx, by, bz, inv)
-    scale((K + NX, K + NX + C), w0, bx, by, bz, inv)
-    w = other_steps(0, k, 2, False, (w0, w1), bx, by, bz, inv, acc)
+
+    def run(a_above):
+        scale((K - C, K + 1) if a_above else (K + NX, K + NX + C), w0, bx, by, bz, inv)
+        steps_of(0, k, 2, False, True, a_above, (w0, w1), bx, by, bz, inv, acc)
+
+    on_each_side(sides, run)
     out = Copies(out_sems)
-    leave(k_next, sides, out, w, xa_out, xb_out, ya_out, yb_out)
+    leave(k_next, sides, out, (w0, w1)[k % 2], xa_out, xb_out, ya_out, yb_out)
     out.wait()
 
 
@@ -399,9 +399,9 @@
     w0, bx, by, bz, inv, acc, w1, *strips = pl.pallas_call(
         functools.partial(first_kernel, k, k_next),
         out_shape=(EXT,) * 5 + (ACC, EXT) + strips_shape(k_next),
-        in_specs=[VMEM] * 7 + [ANY] * 6,
+        in_specs=[VMEM] * 7 + [ANY] * 4,
         out_specs=(VMEM,) * 7 + (ANY,) * 4,
-        scratch_shapes=[pltpu.SemaphoreType.DMA((24,)), pltpu.SemaphoreType.DMA((4,))],
+        scratch_shapes=[pltpu.SemaphoreType.DMA((12,)), pltpu.SemaphoreType.DMA((4,))],
         input_output_aliases={i: i for i in range(7)},
         compiler_params=pltpu.CompilerParams(vmem_limit_bytes=2 * MIB),
         name="first_round",
@@ -409,41 +409,42 @@
     return (bx, by, bz, inv), ((w0, w1)[k % 2], (w1, w0)[k % 2], acc), strips
 
 
-def early_kernel(first, k, bx, by, bz, inv, w_in, w1_in, acc_in, ya, yb, w0, w1, acc, sems):
+def early_kernel(first, k, last, bx, by, bz, inv, w_in, w1_in, acc_in, xa, ya, yb, ca, w0, w1, acc, sems):
     sides = Sides()
     into = Copies(sems)
     for ab, strip in (("a", ya), ("b", yb)):
         into.start(strip, w0.at[K : K + NX, pl.ds(sides.land("gy", ab, k), k)])
+    land_later_x("a", k, sides, into, xa, ca, w0)
     into.wait()
-    early_steps(first, k, 1, (w0, w1), bx, by, bz, inv, acc)
-
-
-def early(first, k, coeffs, state, ya, yb):
-    return pl.pallas_call(
-        functools.partial(early_kernel, first, k),
+    on_each_side(sides, lambda a_above: steps_of(first, k, 1, last, False, a_above, (w0, w1), bx, by, bz, inv, acc))
+
+
+def early(first, k, last, coeffs, state, *strips):
+    return pl.pallas_call(
+        functools.partial(early_kernel, first, k, last),
         out_shape=(EXT, EXT, ACC),
-        in_specs=[VMEM] * 7 + [ANY] * 2,
+        in_specs=[VMEM] * 7 + [ANY] * 4,
         out_specs=(VMEM,) * 3,
-        scratch_shapes=[pltpu.SemaphoreType.DMA((2,))],
+        scratch_shapes=[pltpu.SemaphoreType.DMA((5,))],
         input_output_aliases={4: 0, 5: 1, 6: 2},
         compiler_params=pltpu.CompilerParams(vmem_limit_bytes=2 * MIB),
         name="early",
-    )(*coeffs, *state, ya, yb)
+    )(*coeffs, *state, *strips)
 
 
 def later_kernel(
     first, k, k_next,
-    bx, by, bz, inv, w_in, w1_in, acc_in, xa, xb, ca, cb,
+    bx, by, bz, inv, w_in, w1_in, acc_in, xb, cb,
     w0, w1, acc, xa_out, xb_out, ya_out, yb_out,
     in_sems, out_sems,
 ):
     sides = Sides()
     into = Copies(in_sems)
-    land_later_x(k, sides, into, {"a": xa, "b": xb}, {"a": ca, "b": cb}, w0)
+    land_later_x("b", k, sides, into, xb, cb, w0)
     into.wait()
-    w = other_steps(first, k, 1, False, (w0, w1), bx, by, bz, inv, acc)
+    on_each_side(sides, lambda a_above: steps_of(first, k, 1, False, True, a_above, (w0, w1), bx, by, bz, inv, acc))
     out = Copies(out_sems)
-    leave(k_next, sides, out, w, xa_out, xb_out, ya_out, yb_out)
+    leave(k_next, sides, out, (w0, w1)[k % 2], xa_out, xb_out, ya_out, yb_out)
     out.wait()
 
 
@@ -451,9 +452,9 @@
     w0, w1, acc, *strips = pl.pallas_call(
         functools.partial(later_kernel, first, k, k_next),
         out_shape=(EXT, EXT, ACC) + strips_shape(k_next),
-        in_specs=[VMEM] * 7 + [ANY] * 4,
+        in_specs=[VMEM] * 7 + [ANY] * 2,
         out_specs=(VMEM,) * 3 + (ANY,) * 4,
-        scratch_shapes=[pltpu.SemaphoreType.DMA((6,)), pltpu.SemaphoreType.DMA((4,))],
+        scratch_shapes=[pltpu.SemaphoreType.DMA((3,)), pltpu.SemaphoreType.DMA((4,))],
         input_output_aliases={4: 0, 5: 1, 6: 2},
         compiler_params=pltpu.CompilerParams(vmem_limit_bytes=2 * MIB),
         name="later_round",
@@ -463,18 +464,18 @@
 
 def last_kernel(
     first, k,
-    tile_rows, targets, mask, slots, bx, by, bz, inv, w_in, w1_in, acc_in, xa, xb, ca, cb,
+    tile_rows, targets, mask, slots, bx, by, bz, inv, w_in, w1_in, acc_in, xb, cb,
     grad, sent, w0, w1, acc,
     in_sems,
 ):
     sides = Sides()
     into = Copies(in_sems)
-    land_later_x(k, sides, into, {"a": xa, "b": xb}, {"a": ca, "b": cb}, w0)
+    land_later_x("b", k, sides, into, xb, cb, w0)
     sent[...] = jnp.zeros_like(sent)
     peers = slots.shape[0]
     sent[pl.ds(CAP, peers, stride=CAP + 1), :] = slots[...]
     into.wait()
-    other_steps(first, k, 1, True, (w0, w1), bx, by, bz, inv, acc)
+    on_each_side(sides, lambda a_above: steps_of(first, k, 1, True, True, a_above, (w0, w1), bx, by, bz, inv, acc))
     flat = acc.reshape(NX * NY * 8, 128)
 
     @pl.loop(0, mask.shape[0] // 8)
@@ -502,9 +503,9 @@
             EXT,
             ACC,
         ),
-        in_specs=[SMEM, SMEM] + [VMEM] * 9 + [ANY] * 4,
+        in_specs=[SMEM, SMEM] + [VMEM] * 9 + [ANY] * 2,
         out_specs=(VMEM,) * 5,
-        scratch_shapes=[pltpu.SemaphoreType.DMA((6,))],
+        scratch_shapes=[pltpu.SemaphoreType.DMA((3,))],
         input_output_aliases={8: 2, 9: 3, 10: 4},
         compiler_params=pltpu.CompilerParams(vmem_limit_bytes=6 * MIB),
         name="last_round",
@@ -562,20 +563,19 @@
     k = ROUNDS[0]
     *fields, xa, xb, xb_z, ya, yb = pack(k, grad_pressure, beta)
     counts = [f[1:] for f in fields_of(k)]
-    xa, xb, ya, yb, *corner = exchange(k, counts, xa, xb, ya, yb, xb_z)
-    coeffs, state, strips = first_round(k, ROUNDS[1], *early_first(k, fields, ya, yb), xa, xb, *corner)
+    xa, xb, ya, yb, ca, cb, *routed = exchange(k, counts, xa, xb, ya, yb, xb_z)
+    fields = early_first(k, fields, xa, ya, yb, ca)
+    coeffs, state, strips = first_round(k, ROUNDS[1], *fields, xb, cb, *routed)
     done = k
     for k, k_next in zip(ROUNDS[1:-1], ROUNDS[2:]):
-        xa, xb, ya, yb, *corner = exchange(k - 1, [(k, k - 1)], *strips)
-        state = early(done, k, coeffs, state, ya, yb)
-        state, strips = later_round(done, k, k_next, *coeffs, *state, xa, xb, *corner)
+        xa, xb, ya, yb, ca, cb = exchange(k - 1, [(k, k - 1)], *strips)
+        state = early(done, k, False, coeffs, state, xa, ya, yb, ca)
+        state, strips = later_round(done, k, k_next, *coeffs, *state, xb, cb)
         done += k
     k = ROUNDS[-1]
-    xa, xb, ya, yb, *corner = exchange(k - 1, [(k, k - 1)], *strips)
-    state = early(done, k, coeffs, state, ya, yb)
-    grad_rhs, sent = last_round(
-        done, k, peers, tile_rows, targets, face_mask, slots, *coeffs, *state, xa, xb, *corner
-    )
+    xa, xb, ya, yb, ca, cb = exchange(k - 1, [(k, k - 1)], *strips)
+    state = early(done, k, True, coeffs, state, xa, ya, yb, ca)
+    grad_rhs, sent = last_round(done, k, peers, tile_rows, targets, face_mask, slots, *coeffs, *state, xb, cb)
     sent = sent.reshape(peers, 1, (CAP + 1) * 128)
     received = lax.all_to_all(sent, ("gx", "gy"), split_axis=0, concat_axis=0, tiled=True)
     return grad_rhs, finish(received.reshape(peers * (CAP + 1), 128), heights)

time: 119 us -> 114 us (0.958)
  waiting for transfers between devices: 17 us -> 14.8 us
  starting transfers between devices: 38.3 us -> 36.3 us
    pallas_call x2, Pallas kernels: 4.59 us -> 7.7 us  [early(): pl.pallas_call(functools.partial(early_kernel, first, k, last), out_shape...]
    pallas_call x1, Pallas kernels: 4.96 us -> 2.74 us  [first_round(): pl.pallas_call(functools.partial(first_kernel, k, k_next), out_shape=(EXT...]
    ppermute x18, waiting for transfers between devices: 7.5 us -> 5.28 us  [swap(): lax.ppermute(array, axis, [(i, j) for i, j in pairs if 0 <= j < size])]
    ppermute x18, starting transfers between devices: 35.2 us -> 33.2 us  [swap(): lax.ppermute(array, axis, [(i, j) for i, j in pairs if 0 <= j < size])]
    pallas_call x1, Pallas kernels: 2.9 us -> 4.72 us  [early_first(): pl.pallas_call(functools.partial(early_first_kernel, k), out_shape=(EXT,)...]
    pallas_call x1, Pallas kernels: 6.88 us -> 5.06 us  [last_round(): pl.pallas_call(functools.partial(last_kernel, first, k), out_shape=(jax.S...]
    pallas_call x1, Pallas kernels: 4.71 us -> 2.9 us  [later_round(): pl.pallas_call(functools.partial(later_kernel, first, k, k_next), out_sha...]
  transfers between devices with their start and end apart: 20 -> 20, of which waited for: 5 -> 2; matrix products, arithmetic and copies ran while one was open for 0% -> 0% of each run, Pallas kernels for 7% -> 12%
where the time goes in v7:
time: 114 us; the launch traced here: 113 us
  starting transfers between devices  36.3 us (32%)
  blocking collectives  32.1 us (28%)
  Pallas kernels  28.6 us (25%)
  waiting for transfers between devices  14.8 us (13%)
    ppermute x18, starting transfers between devices, swap(): lax.ppermute(array, axis, [(i, j) for i, j in pairs if 0 <= j < size])  33.2 us
    all_to_all x1, blocking collectives, shards(): lax.all_to_all(sent, ('gx', 'gy'), split_axis=0, concat_axis=0, tiled=True)  32.1 us
    ppermute x1, waiting for transfers between devices, exchange(): lax.ppermute(xb_z, 'gx', pairs + [(middle - 1, 0), (middle, size - 1)])  9.5 us
    pallas_call x2, Pallas kernels, early(): pl.pallas_call(functools.partial(early_kernel, first, k, last), out_shape...  7.7 us
    ppermute x18, waiting for transfers between devices, swap(): lax.ppermute(array, axis, [(i, j) for i, j in pairs if 0 <= j < size])  5.28 us
    pallas_call x1, Pallas kernels, last_round(): pl.pallas_call(functools.partial(last_kernel, first, k), out_shape=(jax.S...  5.06 us
    pallas_call x1, Pallas kernels, early_first(): pl.pallas_call(functools.partial(early_first_kernel, k), out_shape=(EXT,)...  4.72 us
    pallas_call x1, Pallas kernels, pack(): pl.pallas_call(functools.partial(pack_kernel, k), out_shape=(EXT,) * 4 +...  3.22 us
  transfers between devices with their start and end apart: 20, of which 2 were waited for; matrix products, arithmetic and copies ran while one was open for 0% of the time, Pallas kernels for 12%

profile of v7, /device:TPU:1, one launch (start us, length us, event | category | flops | bytes accessed | tf_op | source)
XLA Modules:
  0.0 113.4 jit_solution(10297839486569233526)
XLA Ops:
  0.6 3.2 %pack.1 = (f32[16,40,8,128]{3,2,1,0:T(8,128)S(1)}, f32[16,40,8,128]{3,2,1,0:T(8,128)S(1)}, f32[16,40,8,128]{3,2,1,0:T(8,128)S(1)}, f32[16,40,8,128]{3,2,1,0:T(8,...) custom-call(f32[8,32,1024]{2,1,0:T(8,128)} %g.1, ...), custom_call_target="tpu_custom_call" | custom-call | tf_op jit(solution)/shard_map/pack/pallas_call | solution.py:140
  3.9 1.5 %collective-permute-start = (f32[13,32,8,128]{3,2,1,0:T(8,128)S(1)}, f32[13,32,8,128]{3,2,1,0:T(8,128)S(1)}, u32[]{:S(2)}, u32[]{:S(2)}) collective-permute-start(f32[13,32,8,128]{3,2,1,0:T(8,128)S(1)} %get-tuple-element.54), channel_id=1, source_target_pairs={{0,8},{8,0},{16,24},{24,16},{32,40},{40,32},{48,56},{56,48},{64,72... | collective-permute-start | bytes 5111816 | tf_op jit(solution)/shard_map/ppermute | solution.py:190
  5.4 3.5 %collective-permute-start.4 = (f32[10,32,8,128]{3,2,1,0:T(8,128)S(1)}, f32[10,32,8,128]{3,2,1,0:T(8,128)S(1)}, u32[]{:S(2)}, u32[]{:S(2)}) collective-permute-start(f32[10,32,8,128]{3,2,1,0:T(8,128)S(1)} %get-tuple-element.65), channel_id=1, source_target_pairs={{8,16},{16,8},{24,32},{32,24},{40,48},{48,40},{56,64},{64,56},{72,... | collective-permute-start | bytes 3932168 | tf_op jit(solution)/shard_map/ppermute | solution.py:190
  8.9 1.3 %collective-permute-start.1 = (f32[8,13,8,128]{3,2,1,0:T(8,128)S(1)}, f32[8,13,8,128]{3,2,1,0:T(8,128)S(1)}, u32[]{:S(2)}, u32[]{:S(2)}) collective-permute-start(f32[8,13,8,128]{3,2,1,0:T(8,128)S(1)} %get-tuple-element.55), channel_id=1, source_target_pairs={{0,1},{1,0},{2,3},{3,2},{4,5},{5,4},{6,7},{7,6},{8,9},{9,8},{10,11... | collective-permute-start | bytes 1277960 | tf_op jit(solution)/shard_map/ppermute | solution.py:190
  10.2 0.7 collective-permute-start.2
  10.9 2.4 %collective-permute-start.6 = (f32[3,32,8,128]{3,2,1,0:T(8,128)S(1)}, f32[3,32,8,128]{3,2,1,0:T(8,128)S(1)}, u32[]{:S(2)}, u32[]{:S(2)}) collective-permute-start(f32[3,32,8,128]{3,2,1,0:T(8,128)S(1)} %get-tuple-element.67), channel_id=1, source_target_pairs={{8,16},{16,8},{24,32},{32,24},{40,48},{48,40},{72,80},{80,72},{88,... | collective-permute-start | bytes 1179656 | tf_op jit(solution)/shard_map/ppermute | solution.py:216
  13.3 5.2 %collective-permute-done.1.ya = f32[8,13,8,128]{3,2,1,0:T(8,128)S(1)} collective-permute-done((f32[8,13,8,128]{3,2,1,0:T(8,128)S(1)}, f32[8,13,8,128]{3,2,1,0:T(8,128)S(1)}, u32[]{:S(2)}, u32[]{:S(2)}) %collective-permute-start.1) | collective-permute-done | bytes 426016 | tf_op jit(solution)/shard_map/ppermute | solution.py:190
  18.5 0.0 collective-permute-done.2.yb
  18.5 0.4 corners.3
  18.9 0.1 collective-permute-start.3
  19.0 9.5 %collective-permute-done.6.array.z_plain = f32[3,32,8,128]{3,2,1,0:T(8,128)S(1)} collective-permute-done((f32[3,32,8,128]{3,2,1,0:T(8,128)S(1)}, f32[3,32,8,128]{3,2,1,0:T(8,128)S(1)}, u32[]{:S(2)}, u32[]{:S(2)}) %collective-permute-start.6) | collective-permute-done | bytes 393248 | tf_op jit(solution)/shard_map/ppermute | solution.py:216
  28.5 0.0 collective-permute-done.3.ca.after
  28.5 0.2 relay.1
  28.7 0.7 collective-permute-start.7
  29.4 3.5 %collective-permute-start.5 = (f32[2,3,10,8,128]{4,3,2,1,0:T(8,128)S(1)}, f32[2,3,10,8,128]{4,3,2,1,0:T(8,128)S(1)}, u32[]{:S(2)}, u32[]{:S(2)}) collective-permute-start(f32[2,3,10,8,128]{4,3,2,1,0:T(8,128)S(1)} %get-tuple-element.66), channel_id=1, source_target_pairs={{8,16},{16,8},{24,32},{32,24},{40,48},{48,40},{56,64},{64,56},{72,... | collective-permute-start | bytes 737288 | tf_op jit(solution)/shard_map/ppermute | solution.py:190
  32.9 0.0 collective-permute-done.xa
  32.9 4.7 %early_first.1 = (f32[16,40,8,128]{3,2,1,0:T(8,128)S(1)}, f32[16,40,8,128]{3,2,1,0:T(8,128)S(1)}, f32[16,40,8,128]{3,2,1,0:T(8,128)S(1)}, f32[16,40,8,128]{3,2,1...) custom-call(f32[16,40,8,128]{3,2,1,0:T(8,128)S(1)} %get-tuple-elemen, ...), custom_call_target="tpu_custom_call", output_to_operand_aliasing={{0}: (0, {}), {1}: (1, {}), {2}: (2, {}), {3}: (3, {})} | custom-call | tf_op jit(solution)/shard_map/early_first/pallas_call | solution.py:365
  37.7 0.0 collective-permute-done.5.cb
  37.7 0.0 collective-permute-done.7.z_ends
  37.7 0.0 collective-permute-done.4.xb
  37.7 0.0 copy-start.4
  37.7 2.7 %first_round.1 = (f32[16,40,8,128]{3,2,1,0:T(8,128)S(1)}, f32[16,40,8,128]{3,2,1,0:T(8,128)S(1)}, f32[16,40,8,128]{3,2,1,0:T(8,128)S(1)}, f32[16,40,8,128]{3,2,1...) custom-call(f32[16,40,8,128]{3,2,1,0:T(8,128)S(1)} %get-tuple-elemen, ...), custom_call_target="tpu_custom_call", output_to_operand_aliasing={{0}: (0, {}), {1}: (1, {}), {2}: (2, {}), {3}: (3, {}), {4}... | custom-call | tf_op jit(solution)/shard_map/first_round/pallas_call | solution.py:399
  40.5 0.7 collective-permute-start.10
  41.1 3.7 %collective-permute-start.9 = (f32[8,4,8,128]{3,2,1,0:T(8,128)S(1)}, f32[8,4,8,128]{3,2,1,0:T(8,128)S(1)}, u32[]{:S(2)}, u32[]{:S(2)}) collective-permute-start(f32[8,4,8,128]{3,2,1,0:T(8,128)S(1)} %get-tuple-element.76), channel_id=1, source_target_pairs={{0,1},{1,0},{2,3},{3,2},{4,5},{5,4},{6,7},{7,6},{8,9},{9,8},{10,11... | collective-permute-start | bytes 393224 | tf_op jit(solution)/shard_map/ppermute | solution.py:190
  44.9 0.0 copy-done.4
  44.9 0.0 collective-permute-start.8
  44.9 0.0 copy-start.3
  44.9 4.0 %collective-permute-start.12 = (f32[4,32,8,128]{3,2,1,0:T(8,128)S(1)}, f32[4,32,8,128]{3,2,1,0:T(8,128)S(1)}, u32[]{:S(2)}, u32[]{:S(2)}) collective-permute-start(f32[4,32,8,128]{3,2,1,0:T(8,128)S(1)} %get-tuple-element.82), channel_id=1, source_target_pairs={{8,16},{16,8},{24,32},{32,24},{40,48},{48,40},{56,64},{64,56},{72,... | collective-permute-start | bytes 1572872 | tf_op jit(solution)/shard_map/ppermute | solution.py:190
  49.0 0.0 collective-permute-done.10.yb
  49.0 0.0 collective-permute-done.9.ya
  49.0 0.1 corners.4
  49.1 0.1 collective-permute-start.11
  49.2 3.8 %collective-permute-start.13 = (f32[2,3,3,8,128]{4,3,2,1,0:T(8,128)S(1)}, f32[2,3,3,8,128]{4,3,2,1,0:T(8,128)S(1)}, u32[]{:S(2)}, u32[]{:S(2)}) collective-permute-start(f32[2,3,3,8,128]{4,3,2,1,0:T(8,128)S(1)} %get-tuple-element.83), channel_id=1, source_target_pairs={{8,16},{16,8},{24,32},{32,24},{40,48},{48,40},{56,64},{64,56},{72,... | collective-permute-start | bytes 221192 | tf_op jit(solution)/shard_map/ppermute | solution.py:190
  53.0 0.0 copy-done.3
  53.0 0.2 convert_reduce_fusion
  53.2 0.0 collective-permute-done.11.ca
  53.2 0.0 collective-permute-done.8.xa
  53.2 3.8 %early.2 = (f32[16,40,8,128]{3,2,1,0:T(8,128)S(1)}, f32[16,40,8,128]{3,2,1,0:T(8,128)S(1)}, f32[8,32,8,128]{3,2,1,0:T(8,128)S(1)}) custom-call(f32[16,40,8,128]{3,2,1,0:T(8,128)S(1)} %get-tuple-element.68.bx, f32[16,40,8,128]{3,2,1,0:T(8,128)S(1)} %get-tuple-element.69.by, ...), custom_call_target="tpu_custom_call", output_to_operand_aliasing={{0}: (4, {}), {1}: (5, {}), {2}: (6, {})} | custom-call | tf_op jit(solution)/shard_map/early/pallas_call | solution.py:423
  57.0 0.0 collective-permute-done.13.cb
  57.0 0.0 collective-permute-done.12.xb
  57.0 2.9 %later_round.1 = (f32[16,40,8,128]{3,2,1,0:T(8,128)S(1)}, f32[16,40,8,128]{3,2,1,0:T(8,128)S(1)}, f32[8,32,8,128]{3,2,1,0:T(8,128)S(1)}, f32[4,32,8,128]{3,2,1,0...) custom-call(f32[16,40,8,128]{3,2,1,0:T(8,128)S(1)} %get-tuple-elemen, ...), custom_call_target="tpu_custom_call", output_to_operand_aliasing={{0}: (4, {}), {1}: (5, {}), {2}: (6, {})} | custom-call | tf_op jit(solution)/shard_map/later_round/pallas_call | solution.py:452
  59.9 1.5 %collective-permute-start.15 = (f32[8,4,8,128]{3,2,1,0:T(8,128)S(1)}, f32[8,4,8,128]{3,2,1,0:T(8,128)S(1)}, u32[]{:S(2)}, u32[]{:S(2)}) collective-permute-start(f32[8,4,8,128]{3,2,1,0:T(8,128)S(1)} %get-tuple-element.88), channel_id=1, source_target_pairs={{0,1},{1,0},{2,3},{3,2},{4,5},{5,4},{6,7},{7,6},{8,9},{9,8},{10,11... | collective-permute-start | bytes 393224 | tf_op jit(solution)/shard_map/ppermute | solution.py:190
  61.5 0.7 collective-permute-start.16
  62.2 0.3 fusion.1.slots
  62.5 0.3 collective-permute-start.14
  62.8 3.6 %collective-permute-start.18 = (f32[4,32,8,128]{3,2,1,0:T(8,128)S(1)}, f32[4,32,8,128]{3,2,1,0:T(8,128)S(1)}, u32[]{:S(2)}, u32[]{:S(2)}) collective-permute-start(f32[4,32,8,128]{3,2,1,0:T(8,128)S(1)} %get-tuple-element.94), channel_id=1, source_target_pairs={{8,16},{16,8},{24,32},{32,24},{40,48},{48,40},{56,64},{64,56},{72,... | collective-permute-start | bytes 1572872 | tf_op jit(solution)/shard_map/ppermute | solution.py:190
  66.4 0.0 collective-permute-done.15.ya
  66.4 0.0 collective-permute-done.16.yb
  66.4 0.1 corners.5
  66.5 0.1 collective-permute-start.17
  66.6 4.1 %collective-permute-start.19 = (f32[2,3,3,8,128]{4,3,2,1,0:T(8,128)S(1)}, f32[2,3,3,8,128]{4,3,2,1,0:T(8,128)S(1)}, u32[]{:S(2)}, u32[]{:S(2)}) collective-permute-start(f32[2,3,3,8,128]{4,3,2,1,0:T(8,128)S(1)} %get-tuple-element.95), channel_id=1, source_target_pairs={{8,16},{16,8},{24,32},{32,24},{40,48},{48,40},{56,64},{64,56},{72,... | collective-permute-start | bytes 221192 | tf_op jit(solution)/shard_map/ppermute | solution.py:190
  70.8 0.0 collective-permute-done.17.ca
  70.8 0.0 collective-permute-done.14.xa
  70.8 0.0 copy-start.1
  70.8 0.0 copy-start.2
  70.8 3.9 %early.3 = (f32[16,40,8,128]{3,2,1,0:T(8,128)S(1)}, f32[16,40,8,128]{3,2,1,0:T(8,128)S(1)}, f32[8,32,8,128]{3,2,1,0:T(8,128)S(1)}) custom-call(f32[16,40,8,128]{3,2,1,0:T(8,128)S(1)} %get-tuple-element.68.bx, f32[16,40,8,128]{3,2,1,0:T(8,128)S(1)} %get-tuple-element.69.by, ...), custom_call_target="tpu_custom_call", output_to_operand_aliasing={{0}: (4, {}), {1}: (5, {}), {2}: (6, {})} | custom-call | tf_op jit(solution)/shard_map/early/pallas_call | solution.py:423
  74.7 0.0 collective-permute-done.19.cb
  74.7 0.0 collective-permute-done.18.xb
  74.7 0.0 copy-done.1
  74.7 0.0 copy-done.2
  74.8 0.0 copy-start
  74.8 5.1 %last_round.1 = (f32[8,32,1024]{2,1,0:T(8,128)}, f32[1152,128]{1,0:T(8,128)S(1)}, f32[16,40,8,128]{3,2,1,0:T(8,128)S(1)}, f32[16,40,8,128]{3,2,1,0:T(8,128)S(1)}, f32[8,32,8,128]{3,2,1,0:T(8,128)S(1)}) custom-call(s32[256]{0:T(256)S(1)} %copy-done.2, s32[256]{0:T(256)S(1)} %multiply_add_fusion.targets, ...), custom_call_target="tpu_custom_call", output_to_operand_aliasing={{2}: (8, {}), {3}: (9, {}), {4}: (10, {})} | custom-call | tf_op jit(solution)/shard_map/last_round/pallas_call | solution.py:497
  79.8 32.1 %all_to_all.5 = f32[128,1,1152]{2,1,0:T(1,128)S(1)} all-to-all(f32[128,1,1152]{2,1,0:T(1,128)S(1)} %bitcast.4), channel_id=1, replica_groups=mesh['gx'=16,'gy'=8] {'gx','gy'}, dimensions={0} | all-to-all | bytes 1179648 | tf_op jit(solution)/shard_map/all_to_all | solution.py:580
  112.0 1.4 %finish.1 = f32[3,256,128]{2,1,0:T(8,128)} custom-call(f32[1152,128]{1,0:T(8,128)S(1)} %bitcast.3, f32[3,256,128]{2,1,0:T(8,128)S(1)} %copy-done), custom_call_target="tpu_custom_call" | custom-call | tf_op jit(solution)/shard_map/finish/pallas_call | solution.py:539
  (3 shorter events, 0.0 us)
Async XLA Ops:
  3.9 29.1 %collective-permute-start = (f32[13,32,8,128]{3,2,1,0:T(8,128)S(1)}, f32[13,32,8,128]{3,2,1,0:T(8,128)S(1)}, u32[]{:S(2)}, u32[]{:S(2)}) collective-permute-start(f32[13,32,8,128]{3,2,1,0:T(8,128)S(1)} %get-tuple-element.54), channel_id=1, source_target_pairs={{0,8},{8,0},{16,24},{24,16},{32,40},{40,32},{48,56},{56,48},{64,72... | collective-permute-start | bytes 5111816 | tf_op jit(solution)/shard_map/ppermute | solution.py:190
  5.4 32.3 %collective-permute-start.4 = (f32[10,32,8,128]{3,2,1,0:T(8,128)S(1)}, f32[10,32,8,128]{3,2,1,0:T(8,128)S(1)}, u32[]{:S(2)}, u32[]{:S(2)}) collective-permute-start(f32[10,32,8,128]{3,2,1,0:T(8,128)S(1)} %get-tuple-element.65), channel_id=1, source_target_pairs={{8,16},{16,8},{24,32},{32,24},{40,48},{48,40},{56,64},{64,56},{72,... | collective-permute-start | bytes 3932168 | tf_op jit(solution)/shard_map/ppermute | solution.py:190
  8.9 9.6 %collective-permute-start.1 = (f32[8,13,8,128]{3,2,1,0:T(8,128)S(1)}, f32[8,13,8,128]{3,2,1,0:T(8,128)S(1)}, u32[]{:S(2)}, u32[]{:S(2)}) collective-permute-start(f32[8,13,8,128]{3,2,1,0:T(8,128)S(1)} %get-tuple-element.55), channel_id=1, source_target_pairs={{0,1},{1,0},{2,3},{3,2},{4,5},{5,4},{6,7},{7,6},{8,9},{9,8},{10,11... | collective-permute-start | bytes 1277960 | tf_op jit(solution)/shard_map/ppermute | solution.py:190
  10.2 8.3 %collective-permute-start.2 = (f32[8,13,8,128]{3,2,1,0:T(8,128)S(1)}, f32[8,13,8,128]{3,2,1,0:T(8,128)S(1)}, u32[]{:S(2)}, u32[]{:S(2)}) collective-permute-start(f32[8,13,8,128]{3,2,1,0:T(8,128)S(1)} %get-tuple-element.56), channel_id=1, source_target_pairs={{1,2},{2,1},{3,4},{4,3},{5,6},{6,5},{9,10},{10,9},{11,12},{12,11},... | collective-permute-start | bytes 1277960 | tf_op jit(solution)/shard_map/ppermute | solution.py:190
  10.9 17.6 %collective-permute-start.6 = (f32[3,32,8,128]{3,2,1,0:T(8,128)S(1)}, f32[3,32,8,128]{3,2,1,0:T(8,128)S(1)}, u32[]{:S(2)}, u32[]{:S(2)}) collective-permute-start(f32[3,32,8,128]{3,2,1,0:T(8,128)S(1)} %get-tuple-element.67), channel_id=1, source_target_pairs={{8,16},{16,8},{24,32},{32,24},{40,48},{48,40},{72,80},{80,72},{88,... | collective-permute-start | bytes 1179656 | tf_op jit(solution)/shard_map/ppermute | solution.py:216
  18.9 9.6 %collective-permute-start.3 = (f32[2,3,10,8,128]{4,3,2,1,0:T(8,128)S(1)}, f32[2,3,10,8,128]{4,3,2,1,0:T(8,128)S(1)}, u32[]{:S(2)}, u32[]{:S(2)}) collective-permute-start(f32[2,3,10,8,128]{4,3,2,1,0:T(8,128)S(1)} %get-tuple-element.57), channel_id=1, source_target_pairs={{0,8},{8,0},{16,24},{24,16},{32,40},{40,32},{48,56},{56,48},{64,72... | collective-permute-start | bytes 737288 | tf_op jit(solution)/shard_map/ppermute | solution.py:190
  28.7 9.0 %collective-permute-start.7 = (f32[3,32,8,128]{3,2,1,0:T(8,128)S(1)}, f32[3,32,8,128]{3,2,1,0:T(8,128)S(1)}, u32[]{:S(2)}, u32[]{:S(2)}) collective-permute-start(f32[3,32,8,128]{3,2,1,0:T(8,128)S(1)} %relay.1), channel_id=1, source_target_pairs={{0,64},{120,56},{1,65},{121,57},{2,66},{122,58},{3,67},{123,59},{4... | collective-permute-start | bytes 1179656 | tf_op jit(solution)/shard_map/ppermute | solution.py:223
  29.4 8.3 %collective-permute-start.5 = (f32[2,3,10,8,128]{4,3,2,1,0:T(8,128)S(1)}, f32[2,3,10,8,128]{4,3,2,1,0:T(8,128)S(1)}, u32[]{:S(2)}, u32[]{:S(2)}) collective-permute-start(f32[2,3,10,8,128]{4,3,2,1,0:T(8,128)S(1)} %get-tuple-element.66), channel_id=1, source_target_pairs={{8,16},{16,8},{24,32},{32,24},{40,48},{48,40},{56,64},{64,56},{72,... | collective-permute-start | bytes 737288 | tf_op jit(solution)/shard_map/ppermute | solution.py:190
  37.7 7.2 %copy-start.4 = (s32[256]{0:T(256)S(1)}, s32[256]{0:T(256)}, u32[]{:S(2)}) copy-start(s32[256]{0:T(256)} %param.11) | copy-start | bytes 3076
  40.5 8.5 %collective-permute-start.10 = (f32[8,4,8,128]{3,2,1,0:T(8,128)S(1)}, f32[8,4,8,128]{3,2,1,0:T(8,128)S(1)}, u32[]{:S(2)}, u32[]{:S(2)}) collective-permute-start(f32[8,4,8,128]{3,2,1,0:T(8,128)S(1)} %get-tuple-element.77), channel_id=1, source_target_pairs={{1,2},{2,1},{3,4},{4,3},{5,6},{6,5},{9,10},{10,9},{11,12},{12,11},... | collective-permute-start | bytes 393224 | tf_op jit(solution)/shard_map/ppermute | solution.py:190
  41.1 7.8 %collective-permute-start.9 = (f32[8,4,8,128]{3,2,1,0:T(8,128)S(1)}, f32[8,4,8,128]{3,2,1,0:T(8,128)S(1)}, u32[]{:S(2)}, u32[]{:S(2)}) collective-permute-start(f32[8,4,8,128]{3,2,1,0:T(8,128)S(1)} %get-tuple-element.76), channel_id=1, source_target_pairs={{0,1},{1,0},{2,3},{3,2},{4,5},{5,4},{6,7},{7,6},{8,9},{9,8},{10,11... | collective-permute-start | bytes 393224 | tf_op jit(solution)/shard_map/ppermute | solution.py:190
  44.9 8.3 %collective-permute-start.8 = (f32[4,32,8,128]{3,2,1,0:T(8,128)S(1)}, f32[4,32,8,128]{3,2,1,0:T(8,128)S(1)}, u32[]{:S(2)}, u32[]{:S(2)}) collective-permute-start(f32[4,32,8,128]{3,2,1,0:T(8,128)S(1)} %get-tuple-element.75), channel_id=1, source_target_pairs={{0,8},{8,0},{16,24},{24,16},{32,40},{40,32},{48,56},{56,48},{64,72... | collective-permute-start | bytes 1572872 | tf_op jit(solution)/shard_map/ppermute | solution.py:190
  44.9 8.1 %copy-start.3 = (s32[256,1]{0,1:T(1,128)S(1)}, s32[256,1]{0,1:T(1,128)}, u32[]{:S(2)}) copy-start(s32[256,1]{0,1:T(1,128)} %param.10) | copy-start | bytes 3076
  44.9 12.1 %collective-permute-start.12 = (f32[4,32,8,128]{3,2,1,0:T(8,128)S(1)}, f32[4,32,8,128]{3,2,1,0:T(8,128)S(1)}, u32[]{:S(2)}, u32[]{:S(2)}) collective-permute-start(f32[4,32,8,128]{3,2,1,0:T(8,128)S(1)} %get-tuple-element.82), channel_id=1, source_target_pairs={{8,16},{16,8},{24,32},{32,24},{40,48},{48,40},{56,64},{64,56},{72,... | collective-permute-start | bytes 1572872 | tf_op jit(solution)/shard_map/ppermute | solution.py:190
  49.1 4.0 %collective-permute-start.11 = (f32[2,3,3,8,128]{4,3,2,1,0:T(8,128)S(1)}, f32[2,3,3,8,128]{4,3,2,1,0:T(8,128)S(1)}, u32[]{:S(2)}, u32[]{:S(2)}) collective-permute-start(f32[2,3,3,8,128]{4,3,2,1,0:T(8,128)S(1)} %get-tuple-element.78), channel_id=1, source_target_pairs={{0,8},{8,0},{16,24},{24,16},{32,40},{40,32},{48,56},{56,48},{64,72... | collective-permute-start | bytes 221192 | tf_op jit(solution)/shard_map/ppermute | solution.py:190
  49.2 7.8 %collective-permute-start.13 = (f32[2,3,3,8,128]{4,3,2,1,0:T(8,128)S(1)}, f32[2,3,3,8,128]{4,3,2,1,0:T(8,128)S(1)}, u32[]{:S(2)}, u32[]{:S(2)}) collective-permute-start(f32[2,3,3,8,128]{4,3,2,1,0:T(8,128)S(1)} %get-tuple-element.83), channel_id=1, source_target_pairs={{8,16},{16,8},{24,32},{32,24},{40,48},{48,40},{56,64},{64,56},{72,... | collective-permute-start | bytes 221192 | tf_op jit(solution)/shard_map/ppermute | solution.py:190
  59.9 6.4 %collective-permute-start.15 = (f32[8,4,8,128]{3,2,1,0:T(8,128)S(1)}, f32[8,4,8,128]{3,2,1,0:T(8,128)S(1)}, u32[]{:S(2)}, u32[]{:S(2)}) collective-permute-start(f32[8,4,8,128]{3,2,1,0:T(8,128)S(1)} %get-tuple-element.88), channel_id=1, source_target_pairs={{0,1},{1,0},{2,3},{3,2},{4,5},{5,4},{6,7},{7,6},{8,9},{9,8},{10,11... | collective-permute-start | bytes 393224 | tf_op jit(solution)/shard_map/ppermute | solution.py:190
  61.5 4.9 %collective-permute-start.16 = (f32[8,4,8,128]{3,2,1,0:T(8,128)S(1)}, f32[8,4,8,128]{3,2,1,0:T(8,128)S(1)}, u32[]{:S(2)}, u32[]{:S(2)}) collective-permute-start(f32[8,4,8,128]{3,2,1,0:T(8,128)S(1)} %get-tuple-element.89), channel_id=1, source_target_pairs={{1,2},{2,1},{3,4},{4,3},{5,6},{6,5},{9,10},{10,9},{11,12},{12,11},... | collective-permute-start | bytes 393224 | tf_op jit(solution)/shard_map/ppermute | solution.py:190
  62.5 8.3 %collective-permute-start.14 = (f32[4,32,8,128]{3,2,1,0:T(8,128)S(1)}, f32[4,32,8,128]{3,2,1,0:T(8,128)S(1)}, u32[]{:S(2)}, u32[]{:S(2)}) collective-permute-start(f32[4,32,8,128]{3,2,1,0:T(8,128)S(1)} %get-tuple-element.87), channel_id=1, source_target_pairs={{0,8},{8,0},{16,24},{24,16},{32,40},{40,32},{48,56},{56,48},{64,72... | collective-permute-start | bytes 1572872 | tf_op jit(solution)/shard_map/ppermute | solution.py:190
  62.8 12.0 %collective-permute-start.18 = (f32[4,32,8,128]{3,2,1,0:T(8,128)S(1)}, f32[4,32,8,128]{3,2,1,0:T(8,128)S(1)}, u32[]{:S(2)}, u32[]{:S(2)}) collective-permute-start(f32[4,32,8,128]{3,2,1,0:T(8,128)S(1)} %get-tuple-element.94), channel_id=1, source_target_pairs={{8,16},{16,8},{24,32},{32,24},{40,48},{48,40},{56,64},{64,56},{72,... | collective-permute-start | bytes 1572872 | tf_op jit(solution)/shard_map/ppermute | solution.py:190
  66.5 4.2 %collective-permute-start.17 = (f32[2,3,3,8,128]{4,3,2,1,0:T(8,128)S(1)}, f32[2,3,3,8,128]{4,3,2,1,0:T(8,128)S(1)}, u32[]{:S(2)}, u32[]{:S(2)}) collective-permute-start(f32[2,3,3,8,128]{4,3,2,1,0:T(8,128)S(1)} %get-tuple-element.90), channel_id=1, source_target_pairs={{0,8},{8,0},{16,24},{24,16},{32,40},{40,32},{48,56},{56,48},{64,72... | collective-permute-start | bytes 221192 | tf_op jit(solution)/shard_map/ppermute | solution.py:190
  66.6 8.1 %collective-permute-start.19 = (f32[2,3,3,8,128]{4,3,2,1,0:T(8,128)S(1)}, f32[2,3,3,8,128]{4,3,2,1,0:T(8,128)S(1)}, u32[]{:S(2)}, u32[]{:S(2)}) collective-permute-start(f32[2,3,3,8,128]{4,3,2,1,0:T(8,128)S(1)} %get-tuple-element.95), channel_id=1, source_target_pairs={{8,16},{16,8},{24,32},{32,24},{40,48},{48,40},{56,64},{64,56},{72,... | collective-permute-start | bytes 221192 | tf_op jit(solution)/shard_map/ppermute | solution.py:190
  70.8 3.9 %copy-start.1 = (s32[256,128]{1,0:T(8,128)S(1)}, s32[256,128]{1,0:T(8,128)}, u32[]{:S(2)}) copy-start(s32[256,128]{1,0:T(8,128)} %mask.1) | copy-start | bytes 393220
  70.8 3.9 %copy-start.2 = (s32[256]{0:T(256)S(1)}, s32[256]{0:T(256)}, u32[]{:S(2)}) copy-start(s32[256]{0:T(256)} %tile_rows.1) | copy-start | bytes 3076
  74.8 37.2 %copy-start = (f32[3,256,128]{2,1,0:T(8,128)S(1)}, f32[3,256,128]{2,1,0:T(8,128)}, u32[]{:S(2)}) copy-start(f32[3,256,128]{2,1,0:T(8,128)} %heights.1) | copy-start | bytes 1179652

commit v8 on v7

--- a/solution.py
+++ b/solution.py
@@ -153,7 +153,8 @@
     )(*(pltpu.with_memory_space_constraint(array, pltpu.HBM) for array in (g, beta)))
 
 
-def corner_kernel(planes, counts, ya, yb, ca, cb, sems):
+def corner_kernel(planes, counts, ya, yb, *refs):
+    ca, cb, sems = refs[-3:]
     sides = Sides()
     out = Copies(sems)
     for ab, corner in (("b", cb), ("a", ca)):
@@ -170,18 +171,18 @@
     out.wait()
 
 
-def corners(planes, counts, ya, yb):
+def corners(planes, counts, ya, yb, *after):
     shape = rows_shape(2, planes, sum(kept for _, kept in counts))
     return pl.pallas_call(
         functools.partial(corner_kernel, planes, counts),
         out_shape=(shape, shape),
-        in_specs=[ANY] * 2,
+        in_specs=[ANY] * (2 + len(after)),
         out_specs=(ANY,) * 2,
         scratch_shapes=[pltpu.SemaphoreType.DMA((4 * len(counts),))],
         compiler_params=pltpu.CompilerParams(vmem_limit_bytes=MIB),
         cost_estimate=pl.CostEstimate(flops=10**10 if len(counts) == 1 else 0, bytes_accessed=MIB, transcendentals=0),
         name="corners",
-    )(ya, yb)
+    )(ya, yb, *after)
 
 
 def swap(array, axis, ab):
@@ -208,7 +209,7 @@
     )(array, after)
 
 
-def exchange(planes, counts, xa, xb, ya, yb, xb_z=None):
+def exchange(planes, counts, xa, xb, ya, yb, xb_z=None, *after):
     size = lax.axis_size("gx")
     middle = size // 2
     if xb_z is not None:
@@ -216,7 +217,7 @@
         xb_z = lax.ppermute(xb_z, "gx", pairs + [(middle - 1, 0), (middle, size - 1)])
     ya, yb = swap(ya, "gy", "a"), swap(yb, "gy", "b")
     xb, xa = swap(xb, "gx", "b"), swap(xa, "gx", "a")
-    ca, cb = corners(planes, counts, ya, yb)
+    ca, cb = corners(planes, counts, ya, yb, *after)
     cb, ca = swap(cb, "gx", "b"), swap(ca, "gx", "a")
     if xb_z is None:
         return xa, xb, ya, yb, ca, cb
@@ -261,10 +262,10 @@
     return [(y, min(size, high - y)) for y in range(low, high, size)]
 
 
-def scale(planes, w, bx, by, bz, inv):
+def scale(planes, rows, w, bx, by, bz, inv):
     @pl.loop(*planes)
     def _(x):
-        for y, n in chunks(K - C, K + NY + C):
+        for y, n in chunks(*rows):
             b = bz[x, y : y + n]
             sub = lax.broadcasted_iota(jnp.int32, b.shape, 1)
             lane = lax.broadcasted_iota(jnp.int32, b.shape, 2)
@@ -346,7 +347,30 @@
     return (x, x, y, y)
 
 
-def early_first_kernel(k, w_in, bx_in, by_in, bz_in, xa, ya, yb, ca, w0, bx, by, bz, inv, acc, w1, sems):
+ALL_ROWS = (K - C, K + NY + C)
+CORE = (K + 1, K + NX), (K + 1, K + NY)
+
+
+def scale_kernel(w_in, bx, by, bz_in, w, bz, inv):
+    scale(*CORE, w, bx, by, bz, inv)
+
+
+def scale_core(w, bx, by, bz):
+    w, bz, inv = pl.pallas_call(
+        scale_kernel,
+        out_shape=(EXT,) * 3,
+        in_specs=[VMEM] * 4,
+        out_specs=(VMEM,) * 3,
+        input_output_aliases={0: 0, 3: 1},
+        compiler_params=pltpu.CompilerParams(vmem_limit_bytes=2 * MIB),
+        name="scale_core",
+    )(w, bx, by, bz)
+    return w, bx, by, bz, inv
+
+
+def early_first_kernel(
+    k, w_in, bx_in, by_in, bz_in, inv_in, xa, ya, yb, ca, w0, bx, by, bz, inv, acc, w1, sems
+):
     sides = Sides()
     into = Copies(sems)
     fields = (w0, bx, by, bz)
@@ -355,7 +379,10 @@
     into.wait()
 
     def run(a_above):
-        scale((K + 1, K + NX + C) if a_above else (K - C, K + NX), w0, bx, by, bz, inv)
+        arrays = (w0, bx, by, bz, inv)
+        scale(CORE[0], (K - C, K + 1), *arrays)
+        scale(CORE[0], (K + NY, K + NY + C), *arrays)
+        scale((K + NX, K + NX + C) if a_above else (K - C, K + 1), ALL_ROWS, *arrays)
         steps_of(0, k, 2, False, False, a_above, (w0, w1), bx, by, bz, inv, acc)
 
     on_each_side(sides, run)
@@ -365,10 +392,10 @@
     return pl.pallas_call(
         functools.partial(early_first_kernel, k),
         out_shape=(EXT,) * 5 + (ACC, EXT),
-        in_specs=[VMEM] * 4 + [ANY] * 4,
+        in_specs=[VMEM] * 5 + [ANY] * 4,
         out_specs=(VMEM,) * 7,
         scratch_shapes=[pltpu.SemaphoreType.DMA((20,))],
-        input_output_aliases={i: i for i in range(4)},
+        input_output_aliases={i: i for i in range(5)},
         compiler_params=pltpu.CompilerParams(vmem_limit_bytes=2 * MIB),
         name="early_first",
     )(*fields, *strips)
@@ -386,7 +413,7 @@
     into.wait()
 
     def run(a_above):
-        scale((K - C, K + 1) if a_above else (K + NX, K + NX + C), w0, bx, by, bz, inv)
+        scale((K - C, K + 1) if a_above else (K + NX, K + NX + C), ALL_ROWS, w0, bx, by, bz, inv)
         steps_of(0, k, 2, False, True, a_above, (w0, w1), bx, by, bz, inv, acc)
 
     on_each_side(sides, run)
@@ -466,7 +493,7 @@
     first, k,
     tile_rows, targets, mask, slots, bx, by, bz, inv, w_in, w1_in, acc_in, xb, cb,
     grad, sent, w0, w1, acc,
-    in_sems,
+    nat, in_sems, out_sems,
 ):
     sides = Sides()
     into = Copies(in_sems)
@@ -478,6 +505,14 @@
     on_each_side(sides, lambda a_above: steps_of(first, k, 1, True, True, a_above, (w0, w1), bx, by, bz, inv, acc))
     flat = acc.reshape(NX * NY * 8, 128)
 
+    @pl.loop(0, NX)
+    def _(x):
+        for yc in range(0, NY, 8):
+            for s in range(8):
+                at = (x * NY + yc) * 8 + s
+                nat[x, yc : yc + 8, 128 * s : 128 * s + 128] = flat[pl.ds(at, 8, stride=8), :]
+        pltpu.make_async_copy(nat.at[x], grad.at[x], out_sems.at[x]).start()
+
     @pl.loop(0, mask.shape[0] // 8)
     def _(t8):
         for t in range(8):
@@ -485,27 +520,27 @@
             row = flat[pl.ds(tile_rows[at], 1), :] * mask[pl.ds(at, 1), :].astype(F32)
             sent[pl.ds(targets[at], 1), :] = row
 
-    @pl.loop(0, NX)
-    def _(x):
-        for yc in range(0, NY, 8):
-            for s in range(8):
-                at = (x * NY + yc) * 8 + s
-                grad[x, yc : yc + 8, 128 * s : 128 * s + 128] = flat[pl.ds(at, 8, stride=8), :]
+    for x in range(NX):
+        pltpu.make_async_copy(nat.at[x], grad.at[x], out_sems.at[x]).wait()
 
 
 def last_round(first, k, peers, *arrays):
     return pl.pallas_call(
         functools.partial(last_kernel, first, k),
         out_shape=(
-            jax.ShapeDtypeStruct((NX, NY, 1024), F32),
+            pltpu.HBM((NX, NY, 1024), F32),
             jax.ShapeDtypeStruct((peers * (CAP + 1), 128), F32),
             EXT,
             EXT,
             ACC,
         ),
         in_specs=[SMEM, SMEM] + [VMEM] * 9 + [ANY] * 2,
-        out_specs=(VMEM,) * 5,
-        scratch_shapes=[pltpu.SemaphoreType.DMA((3,))],
+        out_specs=(HBM,) + (VMEM,) * 4,
+        scratch_shapes=[
+            pltpu.VMEM((NX, NY, 1024), F32),
+            pltpu.SemaphoreType.DMA((3,)),
+            pltpu.SemaphoreType.DMA((NX,)),
+        ],
         input_output_aliases={8: 2, 9: 3, 10: 4},
         compiler_params=pltpu.CompilerParams(vmem_limit_bytes=6 * MIB),
         name="last_round",
@@ -517,14 +552,14 @@
     slots = received[pl.ds(CAP, peers, stride=CAP + 1), :].T
     n_slots = heights.shape[1]
     ids = lax.broadcasted_iota(jnp.int32, (n_slots, peers), 0).astype(F32)
-    table = jnp.zeros((n_slots, 128), F32)
-    for p in range(CAP):
-        named = (ids == slots[p : p + 1, :]).astype(jnp.bfloat16)
-        rest = received[pl.ds(p, peers, stride=CAP + 1), :]
-        for _ in range(3):
-            part = rest.astype(jnp.bfloat16)
-            rest = rest - part.astype(F32)
-            table = table + jnp.dot(named, part, preferred_element_type=F32)
+    named = jnp.concatenate([(ids == slots[p : p + 1, :]).astype(jnp.bfloat16) for p in range(CAP)], axis=1)
+    rest = jnp.concatenate([received[pl.ds(p, peers, stride=CAP + 1), :] for p in range(CAP)], axis=0)
+    parts = []
+    for _ in range(3):
+        parts.append(rest.astype(jnp.bfloat16))
+        rest = rest - parts[-1].astype(F32)
+    sums = jnp.dot(named, jnp.concatenate(parts, axis=1), preferred_element_type=F32)
+    table = sums[:, :128] + (sums[:, 128:256] + sums[:, 256:])
     slope = 0.5 * (heights[2] - heights[0])
     bend = heights[2] - 2.0 * heights[1] + heights[0]
     denom = 1.0 + slope * slope
@@ -563,7 +598,8 @@
     k = ROUNDS[0]
     *fields, xa, xb, xb_z, ya, yb = pack(k, grad_pressure, beta)
     counts = [f[1:] for f in fields_of(k)]
-    xa, xb, ya, yb, ca, cb, *routed = exchange(k, counts, xa, xb, ya, yb, xb_z)
+    fields = scale_core(*fields)
+    xa, xb, ya, yb, ca, cb, *routed = exchange(k, counts, xa, xb, ya, yb, xb_z, fields[-1])
     fields = early_first(k, fields, xa, ya, yb, ca)
     coeffs, state, strips = first_round(k, ROUNDS[1], *fields, xb, cb, *routed)
     done = k

time: 114 us -> 113 us (level)
    pallas_call x1 -> x2, Pallas kernels: 5.06 us -> 5.33 us  [the longest x1 4.52 us: last_round(): pl.pallas_call(functools.partial(last_kernel, first, k), out_shape=(pltpu...]
  transfers between devices with their start and end apart: 20 -> 20, of which waited for: 2 -> 2; matrix products, arithmetic and copies ran while one was open for 0% -> 0% of each run, Pallas kernels for 12% -> 13%
where the time goes in v8:
time: 113 us
  starting transfers between devices  35.9 us (32%)
  blocking collectives  31.6 us (28%)
  Pallas kernels  29.6 us (26%)
  waiting for transfers between devices  14 us (12%)
    ppermute x18, starting transfers between devices, swap(): lax.ppermute(array, axis, [(i, j) for i, j in pairs if 0 <= j < size])  32.8 us
    all_to_all x1, blocking collectives, shards(): lax.all_to_all(sent, ('gx', 'gy'), split_axis=0, concat_axis=0, tiled=True)  31.6 us
    ppermute x1, waiting for transfers between devices, exchange(): lax.ppermute(xb_z, 'gx', pairs + [(middle - 1, 0), (middle, size - 1)])  9.5 us
    pallas_call x2, Pallas kernels, early(): pl.pallas_call(functools.partial(early_kernel, first, k, last), out_shape...  8.08 us
    pallas_call x1, Pallas kernels, early_first(): pl.pallas_call(functools.partial(early_first_kernel, k), out_shape=(EXT,)...  5.1 us
    pallas_call x1, Pallas kernels, last_round(): pl.pallas_call(functools.partial(last_kernel, first, k), out_shape=(pltpu...  4.52 us
    ppermute x18, waiting for transfers between devices, swap(): lax.ppermute(array, axis, [(i, j) for i, j in pairs if 0 <= j < size])  4.47 us
    pallas_call x1, Pallas kernels, pack(): pl.pallas_call(functools.partial(pack_kernel, k), out_shape=(EXT,) * 4 +...  3.22 us
  transfers between devices with their start and end apart: 20, of which 2 were waited for; matrix products, arithmetic and copies ran while one was open for 0% of the time, Pallas kernels for 13%

profile of v8, /device:TPU:1, one launch (start us, length us, event | category | flops | bytes accessed | tf_op | source)
XLA Modules:
  0.0 112.7 jit_solution(13696751075084442290)
XLA Ops:
  0.6 3.2 %pack.1 = (f32[16,40,8,128]{3,2,1,0:T(8,128)S(1)}, f32[16,40,8,128]{3,2,1,0:T(8,128)S(1)}, f32[16,40,8,128]{3,2,1,0:T(8,128)S(1)}, f32[16,40,8,128]{3,2,1,0:T(8,...) custom-call(f32[8,32,1024]{2,1,0:T(8,128)} %g.1, ...), custom_call_target="tpu_custom_call" | custom-call | tf_op jit(solution)/shard_map/pack/pallas_call | solution.py:140
  3.9 1.5 %collective-permute-start = (f32[13,32,8,128]{3,2,1,0:T(8,128)S(1)}, f32[13,32,8,128]{3,2,1,0:T(8,128)S(1)}, u32[]{:S(2)}, u32[]{:S(2)}) collective-permute-start(f32[13,32,8,128]{3,2,1,0:T(8,128)S(1)} %get-tuple-element.60), channel_id=1, source_target_pairs={{0,8},{8,0},{16,24},{24,16},{32,40},{40,32},{48,56},{56,48},{64,72... | collective-permute-start | bytes 5111816 | tf_op jit(solution)/shard_map/ppermute | solution.py:191
  5.4 3.5 %collective-permute-start.4 = (f32[10,32,8,128]{3,2,1,0:T(8,128)S(1)}, f32[10,32,8,128]{3,2,1,0:T(8,128)S(1)}, u32[]{:S(2)}, u32[]{:S(2)}) collective-permute-start(f32[10,32,8,128]{3,2,1,0:T(8,128)S(1)} %get-tuple-element.71), channel_id=1, source_target_pairs={{8,16},{16,8},{24,32},{32,24},{40,48},{48,40},{56,64},{64,56},{72,... | collective-permute-start | bytes 3932168 | tf_op jit(solution)/shard_map/ppermute | solution.py:191
  8.9 1.3 %collective-permute-start.1 = (f32[8,13,8,128]{3,2,1,0:T(8,128)S(1)}, f32[8,13,8,128]{3,2,1,0:T(8,128)S(1)}, u32[]{:S(2)}, u32[]{:S(2)}) collective-permute-start(f32[8,13,8,128]{3,2,1,0:T(8,128)S(1)} %get-tuple-element.61), channel_id=1, source_target_pairs={{0,1},{1,0},{2,3},{3,2},{4,5},{5,4},{6,7},{7,6},{8,9},{9,8},{10,11... | collective-permute-start | bytes 1277960 | tf_op jit(solution)/shard_map/ppermute | solution.py:191
  10.2 0.7 collective-permute-start.2
  10.9 2.4 %collective-permute-start.6 = (f32[3,32,8,128]{3,2,1,0:T(8,128)S(1)}, f32[3,32,8,128]{3,2,1,0:T(8,128)S(1)}, u32[]{:S(2)}, u32[]{:S(2)}) collective-permute-start(f32[3,32,8,128]{3,2,1,0:T(8,128)S(1)} %get-tuple-element.73), channel_id=1, source_target_pairs={{8,16},{16,8},{24,32},{32,24},{40,48},{48,40},{72,80},{80,72},{88,... | collective-permute-start | bytes 1179656 | tf_op jit(solution)/shard_map/ppermute | solution.py:217
  13.3 0.8 scale_core.1
  14.1 4.4 %collective-permute-done.1.ya = f32[8,13,8,128]{3,2,1,0:T(8,128)S(1)} collective-permute-done((f32[8,13,8,128]{3,2,1,0:T(8,128)S(1)}, f32[8,13,8,128]{3,2,1,0:T(8,128)S(1)}, u32[]{:S(2)}, u32[]{:S(2)}) %collective-permute-start.1) | collective-permute-done | bytes 426016 | tf_op jit(solution)/shard_map/ppermute | solution.py:191
  18.5 0.0 collective-permute-done.2.yb
  18.5 0.4 corners.3
  18.9 0.1 collective-permute-start.3
  19.0 9.5 %collective-permute-done.6.array.z_plain = f32[3,32,8,128]{3,2,1,0:T(8,128)S(1)} collective-permute-done((f32[3,32,8,128]{3,2,1,0:T(8,128)S(1)}, f32[3,32,8,128]{3,2,1,0:T(8,128)S(1)}, u32[]{:S(2)}, u32[]{:S(2)}) %collective-permute-start.6) | collective-permute-done | bytes 393248 | tf_op jit(solution)/shard_map/ppermute | solution.py:217
  28.5 0.0 collective-permute-done.3.ca.after
  28.5 0.2 relay.1
  28.7 0.7 collective-permute-start.7
  29.4 3.5 %collective-permute-start.5 = (f32[2,3,10,8,128]{4,3,2,1,0:T(8,128)S(1)}, f32[2,3,10,8,128]{4,3,2,1,0:T(8,128)S(1)}, u32[]{:S(2)}, u32[]{:S(2)}) collective-permute-start(f32[2,3,10,8,128]{4,3,2,1,0:T(8,128)S(1)} %get-tuple-element.72), channel_id=1, source_target_pairs={{8,16},{16,8},{24,32},{32,24},{40,48},{48,40},{56,64},{64,56},{72,... | collective-permute-start | bytes 737288 | tf_op jit(solution)/shard_map/ppermute | solution.py:191
  32.9 0.0 collective-permute-done.xa
  32.9 5.1 %early_first.1 = (f32[16,40,8,128]{3,2,1,0:T(8,128)S(1)}, f32[16,40,8,128]{3,2,1,0:T(8,128)S(1)}, f32[16,40,8,128]{3,2,1,0:T(8,128)S(1)}, f32[16,40,8,128]{3,2,1...) custom-call(f32[16,40,8,128]{3,2,1,0:T(8,128)S(1)} %get-tuple-elemen, ...), custom_call_target="tpu_custom_call", output_to_operand_aliasing={{0}: (0, {}), {1}: (1, {}), {2}: (2, {}), {3}: (3, {}), {4}... | custom-call | tf_op jit(solution)/shard_map/early_first/pallas_call | solution.py:392
  38.0 0.0 collective-permute-done.5.cb
  38.1 0.0 collective-permute-done.7.z_ends
  38.1 0.0 collective-permute-done.4.xb
  38.1 0.0 copy-start.4
  38.1 2.8 %first_round.1 = (f32[16,40,8,128]{3,2,1,0:T(8,128)S(1)}, f32[16,40,8,128]{3,2,1,0:T(8,128)S(1)}, f32[16,40,8,128]{3,2,1,0:T(8,128)S(1)}, f32[16,40,8,128]{3,2,1...) custom-call(f32[16,40,8,128]{3,2,1,0:T(8,128)S(1)} %get-tuple-elemen, ...), custom_call_target="tpu_custom_call", output_to_operand_aliasing={{0}: (0, {}), {1}: (1, {}), {2}: (2, {}), {3}: (3, {}), {4}... | custom-call | tf_op jit(solution)/shard_map/first_round/pallas_call | solution.py:426
  40.9 0.7 collective-permute-start.10
  41.5 3.7 %collective-permute-start.9 = (f32[8,4,8,128]{3,2,1,0:T(8,128)S(1)}, f32[8,4,8,128]{3,2,1,0:T(8,128)S(1)}, u32[]{:S(2)}, u32[]{:S(2)}) collective-permute-start(f32[8,4,8,128]{3,2,1,0:T(8,128)S(1)} %get-tuple-element.82), channel_id=1, source_target_pairs={{0,1},{1,0},{2,3},{3,2},{4,5},{5,4},{6,7},{7,6},{8,9},{9,8},{10,11... | collective-permute-start | bytes 393224 | tf_op jit(solution)/shard_map/ppermute | solution.py:191
  45.3 0.0 copy-done.4
  45.3 0.0 collective-permute-start.8
  45.3 0.0 copy-start.3
  45.3 4.0 %collective-permute-start.12 = (f32[4,32,8,128]{3,2,1,0:T(8,128)S(1)}, f32[4,32,8,128]{3,2,1,0:T(8,128)S(1)}, u32[]{:S(2)}, u32[]{:S(2)}) collective-permute-start(f32[4,32,8,128]{3,2,1,0:T(8,128)S(1)} %get-tuple-element.88), channel_id=1, source_target_pairs={{8,16},{16,8},{24,32},{32,24},{40,48},{48,40},{56,64},{64,56},{72,... | collective-permute-start | bytes 1572872 | tf_op jit(solution)/shard_map/ppermute | solution.py:191
  49.4 0.0 collective-permute-done.10.yb
  49.4 0.0 collective-permute-done.9.ya
  49.4 0.1 corners.4
  49.5 0.1 collective-permute-start.11
  49.6 3.6 %collective-permute-start.13 = (f32[2,3,3,8,128]{4,3,2,1,0:T(8,128)S(1)}, f32[2,3,3,8,128]{4,3,2,1,0:T(8,128)S(1)}, u32[]{:S(2)}, u32[]{:S(2)}) collective-permute-start(f32[2,3,3,8,128]{4,3,2,1,0:T(8,128)S(1)} %get-tuple-element.89), channel_id=1, source_target_pairs={{8,16},{16,8},{24,32},{32,24},{40,48},{48,40},{56,64},{64,56},{72,... | collective-permute-start | bytes 221192 | tf_op jit(solution)/shard_map/ppermute | solution.py:191
  53.2 0.0 copy-done.3
  53.3 0.2 convert_reduce_fusion
  53.4 0.0 collective-permute-done.11.ca
  53.4 0.0 collective-permute-done.8.xa
  53.5 4.0 %early.2 = (f32[16,40,8,128]{3,2,1,0:T(8,128)S(1)}, f32[16,40,8,128]{3,2,1,0:T(8,128)S(1)}, f32[8,32,8,128]{3,2,1,0:T(8,128)S(1)}) custom-call(f32[16,40,8,128]{3,2,1,0:T(8,128)S(1)} %get-tuple-element.74.bx, f32[16,40,8,128]{3,2,1,0:T(8,128)S(1)} %get-tuple-element.75.by, ...), custom_call_target="tpu_custom_call", output_to_operand_aliasing={{0}: (4, {}), {1}: (5, {}), {2}: (6, {})} | custom-call | tf_op jit(solution)/shard_map/early/pallas_call | solution.py:450
  57.5 0.0 collective-permute-done.13.cb
  57.5 0.0 collective-permute-done.12.xb
  57.5 3.0 %later_round.1 = (f32[16,40,8,128]{3,2,1,0:T(8,128)S(1)}, f32[16,40,8,128]{3,2,1,0:T(8,128)S(1)}, f32[8,32,8,128]{3,2,1,0:T(8,128)S(1)}, f32[4,32,8,128]{3,2,1,0...) custom-call(f32[16,40,8,128]{3,2,1,0:T(8,128)S(1)} %get-tuple-elemen, ...), custom_call_target="tpu_custom_call", output_to_operand_aliasing={{0}: (4, {}), {1}: (5, {}), {2}: (6, {})} | custom-call | tf_op jit(solution)/shard_map/later_round/pallas_call | solution.py:479
  60.5 1.8 %collective-permute-start.15 = (f32[8,4,8,128]{3,2,1,0:T(8,128)S(1)}, f32[8,4,8,128]{3,2,1,0:T(8,128)S(1)}, u32[]{:S(2)}, u32[]{:S(2)}) collective-permute-start(f32[8,4,8,128]{3,2,1,0:T(8,128)S(1)} %get-tuple-element.94), channel_id=1, source_target_pairs={{0,1},{1,0},{2,3},{3,2},{4,5},{5,4},{6,7},{7,6},{8,9},{9,8},{10,11... | collective-permute-start | bytes 393224 | tf_op jit(solution)/shard_map/ppermute | solution.py:191
  62.2 0.8 collective-permute-start.16
  63.1 0.3 fusion.1.slots
  63.4 0.1 collective-permute-start.14
  63.5 3.5 %collective-permute-start.18 = (f32[4,32,8,128]{3,2,1,0:T(8,128)S(1)}, f32[4,32,8,128]{3,2,1,0:T(8,128)S(1)}, u32[]{:S(2)}, u32[]{:S(2)}) collective-permute-start(f32[4,32,8,128]{3,2,1,0:T(8,128)S(1)} %get-tuple-element.100), channel_id=1, source_target_pairs={{8,16},{16,8},{24,32},{32,24},{40,48},{48,40},{56,64},{64,56},{72,... | collective-permute-start | bytes 1572872 | tf_op jit(solution)/shard_map/ppermute | solution.py:191
  67.1 0.0 collective-permute-done.15.ya
  67.1 0.0 collective-permute-done.16.yb
  67.1 0.1 corners.5
  67.2 0.1 collective-permute-start.17
  67.3 3.8 %collective-permute-start.19 = (f32[2,3,3,8,128]{4,3,2,1,0:T(8,128)S(1)}, f32[2,3,3,8,128]{4,3,2,1,0:T(8,128)S(1)}, u32[]{:S(2)}, u32[]{:S(2)}) collective-permute-start(f32[2,3,3,8,128]{4,3,2,1,0:T(8,128)S(1)} %get-tuple-element.101), channel_id=1, source_target_pairs={{8,16},{16,8},{24,32},{32,24},{40,48},{48,40},{56,64},{64,56},{72,... | collective-permute-start | bytes 221192 | tf_op jit(solution)/shard_map/ppermute | solution.py:191
  71.1 0.0 collective-permute-done.17.ca
  71.1 0.0 collective-permute-done.14.xa
  71.1 0.0 copy-start.1
  71.1 0.0 copy-start.2
  71.1 4.1 %early.3 = (f32[16,40,8,128]{3,2,1,0:T(8,128)S(1)}, f32[16,40,8,128]{3,2,1,0:T(8,128)S(1)}, f32[8,32,8,128]{3,2,1,0:T(8,128)S(1)}) custom-call(f32[16,40,8,128]{3,2,1,0:T(8,128)S(1)} %get-tuple-element.74.bx, f32[16,40,8,128]{3,2,1,0:T(8,128)S(1)} %get-tuple-element.75.by, ...), custom_call_target="tpu_custom_call", output_to_operand_aliasing={{0}: (4, {}), {1}: (5, {}), {2}: (6, {})} | custom-call | tf_op jit(solution)/shard_map/early/pallas_call | solution.py:450
  75.2 0.0 collective-permute-done.19.cb
  75.2 0.0 collective-permute-done.18.xb
  75.2 0.0 copy-done.1
  75.2 0.0 copy-start
  75.3 4.5 %last_round.1 = (f32[8,32,1024]{2,1,0:T(8,128)}, f32[1152,128]{1,0:T(8,128)S(1)}, f32[16,40,8,128]{3,2,1,0:T(8,128)S(1)}, f32[16,40,8,128]{3,2,1,0:T(8,128)S(1)}, f32[8,32,8,128]{3,2,1,0:T(8,128)S(1)}) custom-call(s32[256]{0:T(256)S(1)} %copy-done.2, s32[256]{0:T(256)S(1)} %multiply_add_fusion.targets, ...), custom_call_target="tpu_custom_call", output_to_operand_aliasing={{2}: (8, {}), {3}: (9, {}), {4}: (10, {})} | custom-call | tf_op jit(solution)/shard_map/last_round/pallas_call | solution.py:528
  79.8 31.6 %all_to_all.5 = f32[128,1,1152]{2,1,0:T(1,128)S(1)} all-to-all(f32[128,1,1152]{2,1,0:T(1,128)S(1)} %bitcast.4), channel_id=1, replica_groups=mesh['gx'=16,'gy'=8] {'gx','gy'}, dimensions={0} | all-to-all | bytes 1179648 | tf_op jit(solution)/shard_map/all_to_all | solution.py:616
  111.4 1.3 %finish.1 = f32[3,256,128]{2,1,0:T(8,128)} custom-call(f32[1152,128]{1,0:T(8,128)S(1)} %bitcast.3, f32[3,256,128]{2,1,0:T(8,128)S(1)} %copy-done), custom_call_target="tpu_custom_call" | custom-call | tf_op jit(solution)/shard_map/finish/pallas_call | solution.py:574
  (4 shorter events, 0.0 us)
Async XLA Ops:
  3.9 29.1 %collective-permute-start = (f32[13,32,8,128]{3,2,1,0:T(8,128)S(1)}, f32[13,32,8,128]{3,2,1,0:T(8,128)S(1)}, u32[]{:S(2)}, u32[]{:S(2)}) collective-permute-start(f32[13,32,8,128]{3,2,1,0:T(8,128)S(1)} %get-tuple-element.60), channel_id=1, source_target_pairs={{0,8},{8,0},{16,24},{24,16},{32,40},{40,32},{48,56},{56,48},{64,72... | collective-permute-start | bytes 5111816 | tf_op jit(solution)/shard_map/ppermute | solution.py:191
  5.4 32.7 %collective-permute-start.4 = (f32[10,32,8,128]{3,2,1,0:T(8,128)S(1)}, f32[10,32,8,128]{3,2,1,0:T(8,128)S(1)}, u32[]{:S(2)}, u32[]{:S(2)}) collective-permute-start(f32[10,32,8,128]{3,2,1,0:T(8,128)S(1)} %get-tuple-element.71), channel_id=1, source_target_pairs={{8,16},{16,8},{24,32},{32,24},{40,48},{48,40},{56,64},{64,56},{72,... | collective-permute-start | bytes 3932168 | tf_op jit(solution)/shard_map/ppermute | solution.py:191
  8.9 9.6 %collective-permute-start.1 = (f32[8,13,8,128]{3,2,1,0:T(8,128)S(1)}, f32[8,13,8,128]{3,2,1,0:T(8,128)S(1)}, u32[]{:S(2)}, u32[]{:S(2)}) collective-permute-start(f32[8,13,8,128]{3,2,1,0:T(8,128)S(1)} %get-tuple-element.61), channel_id=1, source_target_pairs={{0,1},{1,0},{2,3},{3,2},{4,5},{5,4},{6,7},{7,6},{8,9},{9,8},{10,11... | collective-permute-start | bytes 1277960 | tf_op jit(solution)/shard_map/ppermute | solution.py:191
  10.2 8.3 %collective-permute-start.2 = (f32[8,13,8,128]{3,2,1,0:T(8,128)S(1)}, f32[8,13,8,128]{3,2,1,0:T(8,128)S(1)}, u32[]{:S(2)}, u32[]{:S(2)}) collective-permute-start(f32[8,13,8,128]{3,2,1,0:T(8,128)S(1)} %get-tuple-element.62), channel_id=1, source_target_pairs={{1,2},{2,1},{3,4},{4,3},{5,6},{6,5},{9,10},{10,9},{11,12},{12,11},... | collective-permute-start | bytes 1277960 | tf_op jit(solution)/shard_map/ppermute | solution.py:191
  10.9 17.6 %collective-permute-start.6 = (f32[3,32,8,128]{3,2,1,0:T(8,128)S(1)}, f32[3,32,8,128]{3,2,1,0:T(8,128)S(1)}, u32[]{:S(2)}, u32[]{:S(2)}) collective-permute-start(f32[3,32,8,128]{3,2,1,0:T(8,128)S(1)} %get-tuple-element.73), channel_id=1, source_target_pairs={{8,16},{16,8},{24,32},{32,24},{40,48},{48,40},{72,80},{80,72},{88,... | collective-permute-start | bytes 1179656 | tf_op jit(solution)/shard_map/ppermute | solution.py:217
  18.9 9.6 %collective-permute-start.3 = (f32[2,3,10,8,128]{4,3,2,1,0:T(8,128)S(1)}, f32[2,3,10,8,128]{4,3,2,1,0:T(8,128)S(1)}, u32[]{:S(2)}, u32[]{:S(2)}) collective-permute-start(f32[2,3,10,8,128]{4,3,2,1,0:T(8,128)S(1)} %get-tuple-element.63), channel_id=1, source_target_pairs={{0,8},{8,0},{16,24},{24,16},{32,40},{40,32},{48,56},{56,48},{64,72... | collective-permute-start | bytes 737288 | tf_op jit(solution)/shard_map/ppermute | solution.py:191
  28.7 9.4 %collective-permute-start.7 = (f32[3,32,8,128]{3,2,1,0:T(8,128)S(1)}, f32[3,32,8,128]{3,2,1,0:T(8,128)S(1)}, u32[]{:S(2)}, u32[]{:S(2)}) collective-permute-start(f32[3,32,8,128]{3,2,1,0:T(8,128)S(1)} %relay.1), channel_id=1, source_target_pairs={{0,64},{120,56},{1,65},{121,57},{2,66},{122,58},{3,67},{123,59},{4... | collective-permute-start | bytes 1179656 | tf_op jit(solution)/shard_map/ppermute | solution.py:224
  29.4 8.7 %collective-permute-start.5 = (f32[2,3,10,8,128]{4,3,2,1,0:T(8,128)S(1)}, f32[2,3,10,8,128]{4,3,2,1,0:T(8,128)S(1)}, u32[]{:S(2)}, u32[]{:S(2)}) collective-permute-start(f32[2,3,10,8,128]{4,3,2,1,0:T(8,128)S(1)} %get-tuple-element.72), channel_id=1, source_target_pairs={{8,16},{16,8},{24,32},{32,24},{40,48},{48,40},{56,64},{64,56},{72,... | collective-permute-start | bytes 737288 | tf_op jit(solution)/shard_map/ppermute | solution.py:191
  38.1 7.2 %copy-start.4 = (s32[256]{0:T(256)S(1)}, s32[256]{0:T(256)}, u32[]{:S(2)}) copy-start(s32[256]{0:T(256)} %param.11) | copy-start | bytes 3076
  40.9 8.5 %collective-permute-start.10 = (f32[8,4,8,128]{3,2,1,0:T(8,128)S(1)}, f32[8,4,8,128]{3,2,1,0:T(8,128)S(1)}, u32[]{:S(2)}, u32[]{:S(2)}) collective-permute-start(f32[8,4,8,128]{3,2,1,0:T(8,128)S(1)} %get-tuple-element.83), channel_id=1, source_target_pairs={{1,2},{2,1},{3,4},{4,3},{5,6},{6,5},{9,10},{10,9},{11,12},{12,11},... | collective-permute-start | bytes 393224 | tf_op jit(solution)/shard_map/ppermute | solution.py:191
  41.5 7.8 %collective-permute-start.9 = (f32[8,4,8,128]{3,2,1,0:T(8,128)S(1)}, f32[8,4,8,128]{3,2,1,0:T(8,128)S(1)}, u32[]{:S(2)}, u32[]{:S(2)}) collective-permute-start(f32[8,4,8,128]{3,2,1,0:T(8,128)S(1)} %get-tuple-element.82), channel_id=1, source_target_pairs={{0,1},{1,0},{2,3},{3,2},{4,5},{5,4},{6,7},{7,6},{8,9},{9,8},{10,11... | collective-permute-start | bytes 393224 | tf_op jit(solution)/shard_map/ppermute | solution.py:191
  45.3 8.2 %collective-permute-start.8 = (f32[4,32,8,128]{3,2,1,0:T(8,128)S(1)}, f32[4,32,8,128]{3,2,1,0:T(8,128)S(1)}, u32[]{:S(2)}, u32[]{:S(2)}) collective-permute-start(f32[4,32,8,128]{3,2,1,0:T(8,128)S(1)} %get-tuple-element.81), channel_id=1, source_target_pairs={{0,8},{8,0},{16,24},{24,16},{32,40},{40,32},{48,56},{56,48},{64,72... | collective-permute-start | bytes 1572872 | tf_op jit(solution)/shard_map/ppermute | solution.py:191
  45.3 7.9 %copy-start.3 = (s32[256,1]{0,1:T(1,128)S(1)}, s32[256,1]{0,1:T(1,128)}, u32[]{:S(2)}) copy-start(s32[256,1]{0,1:T(1,128)} %param.10) | copy-start | bytes 3076
  45.3 12.2 %collective-permute-start.12 = (f32[4,32,8,128]{3,2,1,0:T(8,128)S(1)}, f32[4,32,8,128]{3,2,1,0:T(8,128)S(1)}, u32[]{:S(2)}, u32[]{:S(2)}) collective-permute-start(f32[4,32,8,128]{3,2,1,0:T(8,128)S(1)} %get-tuple-element.88), channel_id=1, source_target_pairs={{8,16},{16,8},{24,32},{32,24},{40,48},{48,40},{56,64},{64,56},{72,... | collective-permute-start | bytes 1572872 | tf_op jit(solution)/shard_map/ppermute | solution.py:191
  49.5 3.9 %collective-permute-start.11 = (f32[2,3,3,8,128]{4,3,2,1,0:T(8,128)S(1)}, f32[2,3,3,8,128]{4,3,2,1,0:T(8,128)S(1)}, u32[]{:S(2)}, u32[]{:S(2)}) collective-permute-start(f32[2,3,3,8,128]{4,3,2,1,0:T(8,128)S(1)} %get-tuple-element.84), channel_id=1, source_target_pairs={{0,8},{8,0},{16,24},{24,16},{32,40},{40,32},{48,56},{56,48},{64,72... | collective-permute-start | bytes 221192 | tf_op jit(solution)/shard_map/ppermute | solution.py:191
  49.6 7.9 %collective-permute-start.13 = (f32[2,3,3,8,128]{4,3,2,1,0:T(8,128)S(1)}, f32[2,3,3,8,128]{4,3,2,1,0:T(8,128)S(1)}, u32[]{:S(2)}, u32[]{:S(2)}) collective-permute-start(f32[2,3,3,8,128]{4,3,2,1,0:T(8,128)S(1)} %get-tuple-element.89), channel_id=1, source_target_pairs={{8,16},{16,8},{24,32},{32,24},{40,48},{48,40},{56,64},{64,56},{72,... | collective-permute-start | bytes 221192 | tf_op jit(solution)/shard_map/ppermute | solution.py:191
  60.5 6.6 %collective-permute-start.15 = (f32[8,4,8,128]{3,2,1,0:T(8,128)S(1)}, f32[8,4,8,128]{3,2,1,0:T(8,128)S(1)}, u32[]{:S(2)}, u32[]{:S(2)}) collective-permute-start(f32[8,4,8,128]{3,2,1,0:T(8,128)S(1)} %get-tuple-element.94), channel_id=1, source_target_pairs={{0,1},{1,0},{2,3},{3,2},{4,5},{5,4},{6,7},{7,6},{8,9},{9,8},{10,11... | collective-permute-start | bytes 393224 | tf_op jit(solution)/shard_map/ppermute | solution.py:191
  62.2 4.8 %collective-permute-start.16 = (f32[8,4,8,128]{3,2,1,0:T(8,128)S(1)}, f32[8,4,8,128]{3,2,1,0:T(8,128)S(1)}, u32[]{:S(2)}, u32[]{:S(2)}) collective-permute-start(f32[8,4,8,128]{3,2,1,0:T(8,128)S(1)} %get-tuple-element.95), channel_id=1, source_target_pairs={{1,2},{2,1},{3,4},{4,3},{5,6},{6,5},{9,10},{10,9},{11,12},{12,11},... | collective-permute-start | bytes 393224 | tf_op jit(solution)/shard_map/ppermute | solution.py:191
  63.4 7.7 %collective-permute-start.14 = (f32[4,32,8,128]{3,2,1,0:T(8,128)S(1)}, f32[4,32,8,128]{3,2,1,0:T(8,128)S(1)}, u32[]{:S(2)}, u32[]{:S(2)}) collective-permute-start(f32[4,32,8,128]{3,2,1,0:T(8,128)S(1)} %get-tuple-element.93), channel_id=1, source_target_pairs={{0,8},{8,0},{16,24},{24,16},{32,40},{40,32},{48,56},{56,48},{64,72... | collective-permute-start | bytes 1572872 | tf_op jit(solution)/shard_map/ppermute | solution.py:191
  63.5 11.7 %collective-permute-start.18 = (f32[4,32,8,128]{3,2,1,0:T(8,128)S(1)}, f32[4,32,8,128]{3,2,1,0:T(8,128)S(1)}, u32[]{:S(2)}, u32[]{:S(2)}) collective-permute-start(f32[4,32,8,128]{3,2,1,0:T(8,128)S(1)} %get-tuple-element.100), channel_id=1, source_target_pairs={{8,16},{16,8},{24,32},{32,24},{40,48},{48,40},{56,64},{64,56},{72,... | collective-permute-start | bytes 1572872 | tf_op jit(solution)/shard_map/ppermute | solution.py:191
  67.2 3.9 %collective-permute-start.17 = (f32[2,3,3,8,128]{4,3,2,1,0:T(8,128)S(1)}, f32[2,3,3,8,128]{4,3,2,1,0:T(8,128)S(1)}, u32[]{:S(2)}, u32[]{:S(2)}) collective-permute-start(f32[2,3,3,8,128]{4,3,2,1,0:T(8,128)S(1)} %get-tuple-element.96), channel_id=1, source_target_pairs={{0,8},{8,0},{16,24},{24,16},{32,40},{40,32},{48,56},{56,48},{64,72... | collective-permute-start | bytes 221192 | tf_op jit(solution)/shard_map/ppermute | solution.py:191
  67.3 7.9 %collective-permute-start.19 = (f32[2,3,3,8,128]{4,3,2,1,0:T(8,128)S(1)}, f32[2,3,3,8,128]{4,3,2,1,0:T(8,128)S(1)}, u32[]{:S(2)}, u32[]{:S(2)}) collective-permute-start(f32[2,3,3,8,128]{4,3,2,1,0:T(8,128)S(1)} %get-tuple-element.101), channel_id=1, source_target_pairs={{8,16},{16,8},{24,32},{32,24},{40,48},{48,40},{56,64},{64,56},{72,... | collective-permute-start | bytes 221192 | tf_op jit(solution)/shard_map/ppermute | solution.py:191
  71.1 4.1 %copy-start.1 = (s32[256,128]{1,0:T(8,128)S(1)}, s32[256,128]{1,0:T(8,128)}, u32[]{:S(2)}) copy-start(s32[256,128]{1,0:T(8,128)} %mask.1) | copy-start | bytes 393220
  71.1 4.1 %copy-start.2 = (s32[256]{0:T(256)S(1)}, s32[256]{0:T(256)}, u32[]{:S(2)}) copy-start(s32[256]{0:T(256)} %tile_rows.1) | copy-start | bytes 3076
  75.2 36.2 %copy-start = (f32[3,256,128]{2,1,0:T(8,128)S(1)}, f32[3,256,128]{2,1,0:T(8,128)}, u32[]{:S(2)}) copy-start(f32[3,256,128]{2,1,0:T(8,128)} %heights.1) | copy-start | bytes 1179652

commit v9 on v8

--- a/solution.py
+++ b/solution.py
@@ -209,7 +209,7 @@
     )(array, after)
 
 
-def exchange(planes, counts, xa, xb, ya, yb, xb_z=None, *after):
+def exchange(planes, counts, xa, xb, ya, yb, xb_z=None, meanwhile=None):
     size = lax.axis_size("gx")
     middle = size // 2
     if xb_z is not None:
@@ -217,12 +217,13 @@
         xb_z = lax.ppermute(xb_z, "gx", pairs + [(middle - 1, 0), (middle, size - 1)])
     ya, yb = swap(ya, "gy", "a"), swap(yb, "gy", "b")
     xb, xa = swap(xb, "gx", "b"), swap(xa, "gx", "a")
-    ca, cb = corners(planes, counts, ya, yb, *after)
+    worked = meanwhile(xa) if meanwhile else ()
+    ca, cb = corners(planes, counts, ya, yb, *worked[-1:])
     cb, ca = swap(cb, "gx", "b"), swap(ca, "gx", "a")
     if xb_z is None:
         return xa, xb, ya, yb, ca, cb
     onward = lax.ppermute(relay(xb_z, ca), "gx", [(0, middle), (size - 1, middle - 1)])
-    return xa, xb, ya, yb, ca, cb, xb_z, onward
+    return worked, xb, ya, yb, ca, cb, xb_z, onward
 
 
 def land_first_y(k, sides, into, ys, fields):
@@ -237,16 +238,17 @@
     at_x = at_c = 0
     for i, (in_x, _, in_c) in enumerate(fields_of(k)):
         x_halo = fields[i].at[pl.ds(sides.land("gx", ab, in_x), in_x), K : K + NY]
-        if ab == "b" and i == 3:
+        if strip is not None and ab == "b" and i == 3:
             me, size = lax.axis_index("gx"), lax.axis_size("gx")
             by_ends = (me == 0) | (me == size // 2 - 1) | (me == size // 2) | (me == size - 1)
             into.start_either(by_ends, routed[1], routed[0], x_halo)
-        else:
+        elif strip is not None:
             into.start(strip.at[at_x : at_x + in_x], x_halo)
         x = sides.land("gx", ab, k)
         for j, other in enumerate(("a", "b")):
-            y = sides.land("gy", other, in_c)
-            into.start(corner.at[j, :, at_c : at_c + in_c], fields[i].at[pl.ds(x, k), pl.ds(y, in_c)])
+            if corner is not None:
+                y = sides.land("gy", other, in_c)
+                into.start(corner.at[j, :, at_c : at_c + in_c], fields[i].at[pl.ds(x, k), pl.ds(y, in_c)])
         at_x, at_c = at_x + in_x, at_c + in_c
 
 
@@ -348,41 +350,48 @@
 
 
 ALL_ROWS = (K - C, K + NY + C)
-CORE = (K + 1, K + NX), (K + 1, K + NY)
-
-
-def scale_kernel(w_in, bx, by, bz_in, w, bz, inv):
-    scale(*CORE, w, bx, by, bz, inv)
-
-
-def scale_core(w, bx, by, bz):
-    w, bz, inv = pl.pallas_call(
-        scale_kernel,
-        out_shape=(EXT,) * 3,
-        in_specs=[VMEM] * 4,
-        out_specs=(VMEM,) * 3,
-        input_output_aliases={0: 0, 3: 1},
+CORE_ROWS = (K + 1, K + NY)
+
+
+def early_planes(a_above):
+    return (K + 1, K + NX + C) if a_above else (K - C, K + NX)
+
+
+def scale_kernel(k, w_in, bx_in, by_in, bz_in, xa, w, bx, by, bz, inv, sems):
+    sides = Sides()
+    into = Copies(sems)
+    land_first_x("a", k, sides, into, xa, None, None, (w, bx, by, bz))
+    into.wait()
+    on_each_side(sides, lambda a_above: scale(early_planes(a_above), CORE_ROWS, w, bx, by, bz, inv))
+
+
+def scale_core(k, fields, xa):
+    return pl.pallas_call(
+        functools.partial(scale_kernel, k),
+        out_shape=(EXT,) * 5,
+        in_specs=[VMEM] * 4 + [ANY],
+        out_specs=(VMEM,) * 5,
+        scratch_shapes=[pltpu.SemaphoreType.DMA((4,))],
+        input_output_aliases={i: i for i in range(4)},
         compiler_params=pltpu.CompilerParams(vmem_limit_bytes=2 * MIB),
         name="scale_core",
-    )(w, bx, by, bz)
-    return w, bx, by, bz, inv
+    )(*fields, xa)
 
 
 def early_first_kernel(
-    k, w_in, bx_in, by_in, bz_in, inv_in, xa, ya, yb, ca, w0, bx, by, bz, inv, acc, w1, sems
+    k, w_in, bx_in, by_in, bz_in, inv_in, ya, yb, ca, w0, bx, by, bz, inv, acc, w1, sems
 ):
     sides = Sides()
     into = Copies(sems)
     fields = (w0, bx, by, bz)
     land_first_y(k, sides, into, {"a": ya, "b": yb}, fields)
-    land_first_x("a", k, sides, into, xa, ca, None, fields)
+    land_first_x("a", k, sides, into, None, ca, None, fields)
     into.wait()
 
     def run(a_above):
         arrays = (w0, bx, by, bz, inv)
-        scale(CORE[0], (K - C, K + 1), *arrays)
-        scale(CORE[0], (K + NY, K + NY + C), *arrays)
-        scale((K + NX, K + NX + C) if a_above else (K - C, K + 1), ALL_ROWS, *arrays)
+        scale(early_planes(a_above), (K - C, K + 1), *arrays)
+        scale(early_planes(a_above), (K + NY, K + NY + C), *arrays)
         steps_of(0, k, 2, False, False, a_above, (w0, w1), bx, by, bz, inv, acc)
 
     on_each_side(sides, run)
@@ -392,9 +401,9 @@
     return pl.pallas_call(
         functools.partial(early_first_kernel, k),
         out_shape=(EXT,) * 5 + (ACC, EXT),
-        in_specs=[VMEM] * 5 + [ANY] * 4,
+        in_specs=[VMEM] * 5 + [ANY] * 3,
         out_specs=(VMEM,) * 7,
-        scratch_shapes=[pltpu.SemaphoreType.DMA((20,))],
+        scratch_shapes=[pltpu.SemaphoreType.DMA((16,))],
         input_output_aliases={i: i for i in range(5)},
         compiler_params=pltpu.CompilerParams(vmem_limit_bytes=2 * MIB),
         name="early_first",
@@ -598,9 +607,10 @@
     k = ROUNDS[0]
     *fields, xa, xb, xb_z, ya, yb = pack(k, grad_pressure, beta)
     counts = [f[1:] for f in fields_of(k)]
-    fields = scale_core(*fields)
-    xa, xb, ya, yb, ca, cb, *routed = exchange(k, counts, xa, xb, ya, yb, xb_z, fields[-1])
-    fields = early_first(k, fields, xa, ya, yb, ca)
+    scaled, xb, ya, yb, ca, cb, *routed = exchange(
+        k, counts, xa, xb, ya, yb, xb_z, functools.partial(scale_core, k, fields)
+    )
+    fields = early_first(k, scaled, ya, yb, ca)
     coeffs, state, strips = first_round(k, ROUNDS[1], *fields, xb, cb, *routed)
     done = k
     for k, k_next in zip(ROUNDS[1:-1], ROUNDS[2:]):

time: 113 us -> 113 us (level)
  transfers between devices with their start and end apart: 20 -> 20, of which waited for: 2 -> 2; matrix products, arithmetic and copies ran while one was open for 0% -> 0% of each run, Pallas kernels for 13% -> 14%
where the time goes in v9:
time: 113 us
  starting transfers between devices  36 us (32%)
  blocking collectives  31.6 us (28%)
  Pallas kernels  30.2 us (27%)
  waiting for transfers between devices  13.2 us (12%)
    ppermute x18, starting transfers between devices, swap(): lax.ppermute(array, axis, [(i, j) for i, j in pairs if 0 <= j < size])  32.9 us
    all_to_all x1, blocking collectives, shards(): lax.all_to_all(sent, ('gx', 'gy'), split_axis=0, concat_axis=0, tiled=True)  31.6 us
    ppermute x1, waiting for transfers between devices, exchange(): lax.ppermute(xb_z, 'gx', pairs + [(middle - 1, 0), (middle, size - 1)])  9.5 us
    pallas_call x2, Pallas kernels, early(): pl.pallas_call(functools.partial(early_kernel, first, k, last), out_shape...  8.08 us
    pallas_call x1, Pallas kernels, early_first(): pl.pallas_call(functools.partial(early_first_kernel, k), out_shape=(EXT,)...  5 us
    pallas_call x1, Pallas kernels, last_round(): pl.pallas_call(functools.partial(last_kernel, first, k), out_shape=(pltpu...  4.52 us
    ppermute x18, waiting for transfers between devices, swap(): lax.ppermute(array, axis, [(i, j) for i, j in pairs if 0 <= j < size])  3.71 us
    pallas_call x1, Pallas kernels, pack(): pl.pallas_call(functools.partial(pack_kernel, k), out_shape=(EXT,) * 4 +...  3.22 us
  transfers between devices with their start and end apart: 20, of which 2 were waited for; matrix products, arithmetic and copies ran while one was open for 0% of the time, Pallas kernels for 14%

profile of v9, /device:TPU:1, one launch (start us, length us, event | category | flops | bytes accessed | tf_op | source)
XLA Modules:
  0.0 112.7 jit_solution(1309465331586096879)
XLA Ops:
  0.6 3.2 %pack.1 = (f32[16,40,8,128]{3,2,1,0:T(8,128)S(1)}, f32[16,40,8,128]{3,2,1,0:T(8,128)S(1)}, f32[16,40,8,128]{3,2,1,0:T(8,128)S(1)}, f32[16,40,8,128]{3,2,1,0:T(8,...) custom-call(f32[8,32,1024]{2,1,0:T(8,128)} %g.1, ...), custom_call_target="tpu_custom_call" | custom-call | tf_op jit(solution)/shard_map/pack/pallas_call | solution.py:140
  3.9 1.5 %collective-permute-start = (f32[13,32,8,128]{3,2,1,0:T(8,128)S(1)}, f32[13,32,8,128]{3,2,1,0:T(8,128)S(1)}, u32[]{:S(2)}, u32[]{:S(2)}) collective-permute-start(f32[13,32,8,128]{3,2,1,0:T(8,128)S(1)} %get-tuple-element.59), channel_id=1, source_target_pairs={{0,8},{8,0},{16,24},{24,16},{32,40},{40,32},{48,56},{56,48},{64,72... | collective-permute-start | bytes 5111816 | tf_op jit(solution)/shard_map/ppermute | solution.py:191
  5.4 3.5 %collective-permute-start.4 = (f32[10,32,8,128]{3,2,1,0:T(8,128)S(1)}, f32[10,32,8,128]{3,2,1,0:T(8,128)S(1)}, u32[]{:S(2)}, u32[]{:S(2)}) collective-permute-start(f32[10,32,8,128]{3,2,1,0:T(8,128)S(1)} %get-tuple-element.75), channel_id=1, source_target_pairs={{8,16},{16,8},{24,32},{32,24},{40,48},{48,40},{56,64},{64,56},{72,... | collective-permute-start | bytes 3932168 | tf_op jit(solution)/shard_map/ppermute | solution.py:191
  8.9 1.3 %collective-permute-start.1 = (f32[8,13,8,128]{3,2,1,0:T(8,128)S(1)}, f32[8,13,8,128]{3,2,1,0:T(8,128)S(1)}, u32[]{:S(2)}, u32[]{:S(2)}) collective-permute-start(f32[8,13,8,128]{3,2,1,0:T(8,128)S(1)} %get-tuple-element.65), channel_id=1, source_target_pairs={{0,1},{1,0},{2,3},{3,2},{4,5},{5,4},{6,7},{7,6},{8,9},{9,8},{10,11... | collective-permute-start | bytes 1277960 | tf_op jit(solution)/shard_map/ppermute | solution.py:191
  10.2 0.7 collective-permute-start.2
  10.9 2.4 %collective-permute-start.6 = (f32[3,32,8,128]{3,2,1,0:T(8,128)S(1)}, f32[3,32,8,128]{3,2,1,0:T(8,128)S(1)}, u32[]{:S(2)}, u32[]{:S(2)}) collective-permute-start(f32[3,32,8,128]{3,2,1,0:T(8,128)S(1)} %get-tuple-element.77), channel_id=1, source_target_pairs={{8,16},{16,8},{24,32},{32,24},{40,48},{48,40},{72,80},{80,72},{88,... | collective-permute-start | bytes 1179656 | tf_op jit(solution)/shard_map/ppermute | solution.py:217
  13.3 0.0 collective-permute-done.xa
  13.3 1.6 %scale_core.1 = (f32[16,40,8,128]{3,2,1,0:T(8,128)S(1)}, f32[16,40,8,128]{3,2,1,0:T(8,128)S(1)}, f32[16,40,8,128]{3,2,1,0:T(8,128)S(1)}, f32[16,40,8,128]{3,2,1,0:T(8,128)S(1)}, f32[16,40,8,128]{3,2,1,0:T(8,128)S(1)}) custom-call(f32[16,40,8,128]{3,2,1,0:T(8,128)S(1)} %get-tuple-element.55.w_, ...), custom_call_target="tpu_custom_call", output_to_operand_aliasing={{0}: (0, {}), {1}: (1, {}), {2}: (2, {}), {3}: (3, {})} | custom-call | tf_op jit(solution)/shard_map/scale_core/pallas_call | solution.py:369
  14.8 3.7 %collective-permute-done.1.ya = f32[8,13,8,128]{3,2,1,0:T(8,128)S(1)} collective-permute-done((f32[8,13,8,128]{3,2,1,0:T(8,128)S(1)}, f32[8,13,8,128]{3,2,1,0:T(8,128)S(1)}, u32[]{:S(2)}, u32[]{:S(2)}) %collective-permute-start.1) | collective-permute-done | bytes 426016 | tf_op jit(solution)/shard_map/ppermute | solution.py:191
  18.5 0.0 collective-permute-done.2.yb
  18.5 0.4 corners.3
  18.9 0.1 collective-permute-start.3
  19.0 9.5 %collective-permute-done.6.array.z_plain = f32[3,32,8,128]{3,2,1,0:T(8,128)S(1)} collective-permute-done((f32[3,32,8,128]{3,2,1,0:T(8,128)S(1)}, f32[3,32,8,128]{3,2,1,0:T(8,128)S(1)}, u32[]{:S(2)}, u32[]{:S(2)}) %collective-permute-start.6) | collective-permute-done | bytes 393248 | tf_op jit(solution)/shard_map/ppermute | solution.py:217
  28.5 0.0 collective-permute-done.3.ca.after
  28.5 0.2 relay.1
  28.7 0.7 collective-permute-start.7
  29.4 3.5 %collective-permute-start.5 = (f32[2,3,10,8,128]{4,3,2,1,0:T(8,128)S(1)}, f32[2,3,10,8,128]{4,3,2,1,0:T(8,128)S(1)}, u32[]{:S(2)}, u32[]{:S(2)}) collective-permute-start(f32[2,3,10,8,128]{4,3,2,1,0:T(8,128)S(1)} %get-tuple-element.76), channel_id=1, source_target_pairs={{8,16},{16,8},{24,32},{32,24},{40,48},{48,40},{56,64},{64,56},{72,... | collective-permute-start | bytes 737288 | tf_op jit(solution)/shard_map/ppermute | solution.py:191
  32.9 5.0 %early_first.1 = (f32[16,40,8,128]{3,2,1,0:T(8,128)S(1)}, f32[16,40,8,128]{3,2,1,0:T(8,128)S(1)}, f32[16,40,8,128]{3,2,1,0:T(8,128)S(1)}, f32[16,40,8,128]{3,2,1...) custom-call(f32[16,40,8,128]{3,2,1,0:T(8,128)S(1)} %get-tuple-elemen, ...), custom_call_target="tpu_custom_call", output_to_operand_aliasing={{0}: (0, {}), {1}: (1, {}), {2}: (2, {}), {3}: (3, {}), {4}... | custom-call | tf_op jit(solution)/shard_map/early_first/pallas_call | solution.py:401
  37.9 0.0 collective-permute-done.4.xb
  37.9 0.0 collective-permute-done.5.cb
  38.0 0.0 collective-permute-done.7.z_ends
  38.0 0.0 copy-start.4
  38.0 2.8 %first_round.1 = (f32[16,40,8,128]{3,2,1,0:T(8,128)S(1)}, f32[16,40,8,128]{3,2,1,0:T(8,128)S(1)}, f32[16,40,8,128]{3,2,1,0:T(8,128)S(1)}, f32[16,40,8,128]{3,2,1...) custom-call(f32[16,40,8,128]{3,2,1,0:T(8,128)S(1)} %get-tuple-elemen, ...), custom_call_target="tpu_custom_call", output_to_operand_aliasing={{0}: (0, {}), {1}: (1, {}), {2}: (2, {}), {3}: (3, {}), {4}... | custom-call | tf_op jit(solution)/shard_map/first_round/pallas_call | solution.py:435
  40.8 0.7 collective-permute-start.10
  41.4 3.7 %collective-permute-start.9 = (f32[8,4,8,128]{3,2,1,0:T(8,128)S(1)}, f32[8,4,8,128]{3,2,1,0:T(8,128)S(1)}, u32[]{:S(2)}, u32[]{:S(2)}) collective-permute-start(f32[8,4,8,128]{3,2,1,0:T(8,128)S(1)} %get-tuple-element.86), channel_id=1, source_target_pairs={{0,1},{1,0},{2,3},{3,2},{4,5},{5,4},{6,7},{7,6},{8,9},{9,8},{10,11... | collective-permute-start | bytes 393224 | tf_op jit(solution)/shard_map/ppermute | solution.py:191
  45.2 0.0 copy-done.4
  45.2 0.0 collective-permute-start.8
  45.2 0.0 copy-start.3
  45.2 4.0 %collective-permute-start.12 = (f32[4,32,8,128]{3,2,1,0:T(8,128)S(1)}, f32[4,32,8,128]{3,2,1,0:T(8,128)S(1)}, u32[]{:S(2)}, u32[]{:S(2)}) collective-permute-start(f32[4,32,8,128]{3,2,1,0:T(8,128)S(1)} %get-tuple-element.92), channel_id=1, source_target_pairs={{8,16},{16,8},{24,32},{32,24},{40,48},{48,40},{56,64},{64,56},{72,... | collective-permute-start | bytes 1572872 | tf_op jit(solution)/shard_map/ppermute | solution.py:191
  49.3 0.0 collective-permute-done.10.yb
  49.3 0.0 collective-permute-done.9.ya
  49.3 0.1 corners.4
  49.4 0.1 collective-permute-start.11
  49.5 3.6 %collective-permute-start.13 = (f32[2,3,3,8,128]{4,3,2,1,0:T(8,128)S(1)}, f32[2,3,3,8,128]{4,3,2,1,0:T(8,128)S(1)}, u32[]{:S(2)}, u32[]{:S(2)}) collective-permute-start(f32[2,3,3,8,128]{4,3,2,1,0:T(8,128)S(1)} %get-tuple-element.93), channel_id=1, source_target_pairs={{8,16},{16,8},{24,32},{32,24},{40,48},{48,40},{56,64},{64,56},{72,... | collective-permute-start | bytes 221192 | tf_op jit(solution)/shard_map/ppermute | solution.py:191
  53.1 0.0 copy-done.3
  53.1 0.2 convert_reduce_fusion
  53.3 0.0 collective-permute-done.11.ca
  53.3 0.0 collective-permute-done.8.xa
  53.3 4.0 %early.2 = (f32[16,40,8,128]{3,2,1,0:T(8,128)S(1)}, f32[16,40,8,128]{3,2,1,0:T(8,128)S(1)}, f32[8,32,8,128]{3,2,1,0:T(8,128)S(1)}) custom-call(f32[16,40,8,128]{3,2,1,0:T(8,128)S(1)} %get-tuple-element.78.bx, f32[16,40,8,128]{3,2,1,0:T(8,128)S(1)} %get-tuple-element.79.by, ...), custom_call_target="tpu_custom_call", output_to_operand_aliasing={{0}: (4, {}), {1}: (5, {}), {2}: (6, {})} | custom-call | tf_op jit(solution)/shard_map/early/pallas_call | solution.py:459
  57.4 0.0 collective-permute-done.13.cb
  57.4 0.0 collective-permute-done.12.xb
  57.4 3.0 %later_round.1 = (f32[16,40,8,128]{3,2,1,0:T(8,128)S(1)}, f32[16,40,8,128]{3,2,1,0:T(8,128)S(1)}, f32[8,32,8,128]{3,2,1,0:T(8,128)S(1)}, f32[4,32,8,128]{3,2,1,0...) custom-call(f32[16,40,8,128]{3,2,1,0:T(8,128)S(1)} %get-tuple-elemen, ...), custom_call_target="tpu_custom_call", output_to_operand_aliasing={{0}: (4, {}), {1}: (5, {}), {2}: (6, {})} | custom-call | tf_op jit(solution)/shard_map/later_round/pallas_call | solution.py:488
  60.4 1.7 %collective-permute-start.15 = (f32[8,4,8,128]{3,2,1,0:T(8,128)S(1)}, f32[8,4,8,128]{3,2,1,0:T(8,128)S(1)}, u32[]{:S(2)}, u32[]{:S(2)}) collective-permute-start(f32[8,4,8,128]{3,2,1,0:T(8,128)S(1)} %get-tuple-element.98), channel_id=1, source_target_pairs={{0,1},{1,0},{2,3},{3,2},{4,5},{5,4},{6,7},{7,6},{8,9},{9,8},{10,11... | collective-permute-start | bytes 393224 | tf_op jit(solution)/shard_map/ppermute | solution.py:191
  62.1 0.8 collective-permute-start.16
  62.9 0.3 fusion.1.slots
  63.2 0.1 collective-permute-start.14
  63.3 3.6 %collective-permute-start.18 = (f32[4,32,8,128]{3,2,1,0:T(8,128)S(1)}, f32[4,32,8,128]{3,2,1,0:T(8,128)S(1)}, u32[]{:S(2)}, u32[]{:S(2)}) collective-permute-start(f32[4,32,8,128]{3,2,1,0:T(8,128)S(1)} %get-tuple-element.104), channel_id=1, source_target_pairs={{8,16},{16,8},{24,32},{32,24},{40,48},{48,40},{56,64},{64,56},{72,... | collective-permute-start | bytes 1572872 | tf_op jit(solution)/shard_map/ppermute | solution.py:191
  66.9 0.0 collective-permute-done.15.ya
  67.0 0.0 collective-permute-done.16.yb
  67.0 0.1 corners.5
  67.1 0.1 collective-permute-start.17
  67.2 3.8 %collective-permute-start.19 = (f32[2,3,3,8,128]{4,3,2,1,0:T(8,128)S(1)}, f32[2,3,3,8,128]{4,3,2,1,0:T(8,128)S(1)}, u32[]{:S(2)}, u32[]{:S(2)}) collective-permute-start(f32[2,3,3,8,128]{4,3,2,1,0:T(8,128)S(1)} %get-tuple-element.105), channel_id=1, source_target_pairs={{8,16},{16,8},{24,32},{32,24},{40,48},{48,40},{56,64},{64,56},{72,... | collective-permute-start | bytes 221192 | tf_op jit(solution)/shard_map/ppermute | solution.py:191
  71.0 0.0 collective-permute-done.17.ca
  71.1 0.0 collective-permute-done.14.xa
  71.1 0.0 copy-start.1
  71.1 0.0 copy-start.2
  71.1 4.1 %early.3 = (f32[16,40,8,128]{3,2,1,0:T(8,128)S(1)}, f32[16,40,8,128]{3,2,1,0:T(8,128)S(1)}, f32[8,32,8,128]{3,2,1,0:T(8,128)S(1)}) custom-call(f32[16,40,8,128]{3,2,1,0:T(8,128)S(1)} %get-tuple-element.78.bx, f32[16,40,8,128]{3,2,1,0:T(8,128)S(1)} %get-tuple-element.79.by, ...), custom_call_target="tpu_custom_call", output_to_operand_aliasing={{0}: (4, {}), {1}: (5, {}), {2}: (6, {})} | custom-call | tf_op jit(solution)/shard_map/early/pallas_call | solution.py:459
  75.2 0.0 collective-permute-done.19.cb
  75.2 0.0 collective-permute-done.18.xb
  75.2 0.0 copy-start
  75.2 4.5 %last_round.1 = (f32[8,32,1024]{2,1,0:T(8,128)}, f32[1152,128]{1,0:T(8,128)S(1)}, f32[16,40,8,128]{3,2,1,0:T(8,128)S(1)}, f32[16,40,8,128]{3,2,1,0:T(8,128)S(1)}, f32[8,32,8,128]{3,2,1,0:T(8,128)S(1)}) custom-call(s32[256]{0:T(256)S(1)} %copy-done.2, s32[256]{0:T(256)S(1)} %multiply_add_fusion.targets, ...), custom_call_target="tpu_custom_call", output_to_operand_aliasing={{2}: (8, {}), {3}: (9, {}), {4}: (10, {})} | custom-call | tf_op jit(solution)/shard_map/last_round/pallas_call | solution.py:537
  79.7 31.6 %all_to_all.5 = f32[128,1,1152]{2,1,0:T(1,128)S(1)} all-to-all(f32[128,1,1152]{2,1,0:T(1,128)S(1)} %bitcast.4), channel_id=1, replica_groups=mesh['gx'=16,'gy'=8] {'gx','gy'}, dimensions={0} | all-to-all | bytes 1179648 | tf_op jit(solution)/shard_map/all_to_all | solution.py:626
  111.4 0.0 copy-done
  111.4 1.3 %finish.1 = f32[3,256,128]{2,1,0:T(8,128)} custom-call(f32[1152,128]{1,0:T(8,128)S(1)} %bitcast.3, f32[3,256,128]{2,1,0:T(8,128)S(1)} %copy-done), custom_call_target="tpu_custom_call" | custom-call | tf_op jit(solution)/shard_map/finish/pallas_call | solution.py:583
  (4 shorter events, 0.0 us)
Async XLA Ops:
  3.9 9.4 %collective-permute-start = (f32[13,32,8,128]{3,2,1,0:T(8,128)S(1)}, f32[13,32,8,128]{3,2,1,0:T(8,128)S(1)}, u32[]{:S(2)}, u32[]{:S(2)}) collective-permute-start(f32[13,32,8,128]{3,2,1,0:T(8,128)S(1)} %get-tuple-element.59), channel_id=1, source_target_pairs={{0,8},{8,0},{16,24},{24,16},{32,40},{40,32},{48,56},{56,48},{64,72... | collective-permute-start | bytes 5111816 | tf_op jit(solution)/shard_map/ppermute | solution.py:191
  5.4 32.6 %collective-permute-start.4 = (f32[10,32,8,128]{3,2,1,0:T(8,128)S(1)}, f32[10,32,8,128]{3,2,1,0:T(8,128)S(1)}, u32[]{:S(2)}, u32[]{:S(2)}) collective-permute-start(f32[10,32,8,128]{3,2,1,0:T(8,128)S(1)} %get-tuple-element.75), channel_id=1, source_target_pairs={{8,16},{16,8},{24,32},{32,24},{40,48},{48,40},{56,64},{64,56},{72,... | collective-permute-start | bytes 3932168 | tf_op jit(solution)/shard_map/ppermute | solution.py:191
  8.9 9.6 %collective-permute-start.1 = (f32[8,13,8,128]{3,2,1,0:T(8,128)S(1)}, f32[8,13,8,128]{3,2,1,0:T(8,128)S(1)}, u32[]{:S(2)}, u32[]{:S(2)}) collective-permute-start(f32[8,13,8,128]{3,2,1,0:T(8,128)S(1)} %get-tuple-element.65), channel_id=1, source_target_pairs={{0,1},{1,0},{2,3},{3,2},{4,5},{5,4},{6,7},{7,6},{8,9},{9,8},{10,11... | collective-permute-start | bytes 1277960 | tf_op jit(solution)/shard_map/ppermute | solution.py:191
  10.2 8.3 %collective-permute-start.2 = (f32[8,13,8,128]{3,2,1,0:T(8,128)S(1)}, f32[8,13,8,128]{3,2,1,0:T(8,128)S(1)}, u32[]{:S(2)}, u32[]{:S(2)}) collective-permute-start(f32[8,13,8,128]{3,2,1,0:T(8,128)S(1)} %get-tuple-element.66), channel_id=1, source_target_pairs={{1,2},{2,1},{3,4},{4,3},{5,6},{6,5},{9,10},{10,9},{11,12},{12,11},... | collective-permute-start | bytes 1277960 | tf_op jit(solution)/shard_map/ppermute | solution.py:191
  10.9 17.6 %collective-permute-start.6 = (f32[3,32,8,128]{3,2,1,0:T(8,128)S(1)}, f32[3,32,8,128]{3,2,1,0:T(8,128)S(1)}, u32[]{:S(2)}, u32[]{:S(2)}) collective-permute-start(f32[3,32,8,128]{3,2,1,0:T(8,128)S(1)} %get-tuple-element.77), channel_id=1, source_target_pairs={{8,16},{16,8},{24,32},{32,24},{40,48},{48,40},{72,80},{80,72},{88,... | collective-permute-start | bytes 1179656 | tf_op jit(solution)/shard_map/ppermute | solution.py:217
  18.9 9.6 %collective-permute-start.3 = (f32[2,3,10,8,128]{4,3,2,1,0:T(8,128)S(1)}, f32[2,3,10,8,128]{4,3,2,1,0:T(8,128)S(1)}, u32[]{:S(2)}, u32[]{:S(2)}) collective-permute-start(f32[2,3,10,8,128]{4,3,2,1,0:T(8,128)S(1)} %get-tuple-element.67), channel_id=1, source_target_pairs={{0,8},{8,0},{16,24},{24,16},{32,40},{40,32},{48,56},{56,48},{64,72... | collective-permute-start | bytes 737288 | tf_op jit(solution)/shard_map/ppermute | solution.py:191
  28.7 9.3 %collective-permute-start.7 = (f32[3,32,8,128]{3,2,1,0:T(8,128)S(1)}, f32[3,32,8,128]{3,2,1,0:T(8,128)S(1)}, u32[]{:S(2)}, u32[]{:S(2)}) collective-permute-start(f32[3,32,8,128]{3,2,1,0:T(8,128)S(1)} %relay.1), channel_id=1, source_target_pairs={{0,64},{120,56},{1,65},{121,57},{2,66},{122,58},{3,67},{123,59},{4... | collective-permute-start | bytes 1179656 | tf_op jit(solution)/shard_map/ppermute | solution.py:225
  29.4 8.6 %collective-permute-start.5 = (f32[2,3,10,8,128]{4,3,2,1,0:T(8,128)S(1)}, f32[2,3,10,8,128]{4,3,2,1,0:T(8,128)S(1)}, u32[]{:S(2)}, u32[]{:S(2)}) collective-permute-start(f32[2,3,10,8,128]{4,3,2,1,0:T(8,128)S(1)} %get-tuple-element.76), channel_id=1, source_target_pairs={{8,16},{16,8},{24,32},{32,24},{40,48},{48,40},{56,64},{64,56},{72,... | collective-permute-start | bytes 737288 | tf_op jit(solution)/shard_map/ppermute | solution.py:191
  38.0 7.2 %copy-start.4 = (s32[256]{0:T(256)S(1)}, s32[256]{0:T(256)}, u32[]{:S(2)}) copy-start(s32[256]{0:T(256)} %param.11) | copy-start | bytes 3076
  40.8 8.5 %collective-permute-start.10 = (f32[8,4,8,128]{3,2,1,0:T(8,128)S(1)}, f32[8,4,8,128]{3,2,1,0:T(8,128)S(1)}, u32[]{:S(2)}, u32[]{:S(2)}) collective-permute-start(f32[8,4,8,128]{3,2,1,0:T(8,128)S(1)} %get-tuple-element.87), channel_id=1, source_target_pairs={{1,2},{2,1},{3,4},{4,3},{5,6},{6,5},{9,10},{10,9},{11,12},{12,11},... | collective-permute-start | bytes 393224 | tf_op jit(solution)/shard_map/ppermute | solution.py:191
  41.4 7.8 %collective-permute-start.9 = (f32[8,4,8,128]{3,2,1,0:T(8,128)S(1)}, f32[8,4,8,128]{3,2,1,0:T(8,128)S(1)}, u32[]{:S(2)}, u32[]{:S(2)}) collective-permute-start(f32[8,4,8,128]{3,2,1,0:T(8,128)S(1)} %get-tuple-element.86), channel_id=1, source_target_pairs={{0,1},{1,0},{2,3},{3,2},{4,5},{5,4},{6,7},{7,6},{8,9},{9,8},{10,11... | collective-permute-start | bytes 393224 | tf_op jit(solution)/shard_map/ppermute | solution.py:191
  45.2 8.2 %collective-permute-start.8 = (f32[4,32,8,128]{3,2,1,0:T(8,128)S(1)}, f32[4,32,8,128]{3,2,1,0:T(8,128)S(1)}, u32[]{:S(2)}, u32[]{:S(2)}) collective-permute-start(f32[4,32,8,128]{3,2,1,0:T(8,128)S(1)} %get-tuple-element.85), channel_id=1, source_target_pairs={{0,8},{8,0},{16,24},{24,16},{32,40},{40,32},{48,56},{56,48},{64,72... | collective-permute-start | bytes 1572872 | tf_op jit(solution)/shard_map/ppermute | solution.py:191
  45.2 7.9 %copy-start.3 = (s32[256,1]{0,1:T(1,128)S(1)}, s32[256,1]{0,1:T(1,128)}, u32[]{:S(2)}) copy-start(s32[256,1]{0,1:T(1,128)} %param.10) | copy-start | bytes 3076
  45.2 12.2 %collective-permute-start.12 = (f32[4,32,8,128]{3,2,1,0:T(8,128)S(1)}, f32[4,32,8,128]{3,2,1,0:T(8,128)S(1)}, u32[]{:S(2)}, u32[]{:S(2)}) collective-permute-start(f32[4,32,8,128]{3,2,1,0:T(8,128)S(1)} %get-tuple-element.92), channel_id=1, source_target_pairs={{8,16},{16,8},{24,32},{32,24},{40,48},{48,40},{56,64},{64,56},{72,... | collective-permute-start | bytes 1572872 | tf_op jit(solution)/shard_map/ppermute | solution.py:191
  49.4 3.9 %collective-permute-start.11 = (f32[2,3,3,8,128]{4,3,2,1,0:T(8,128)S(1)}, f32[2,3,3,8,128]{4,3,2,1,0:T(8,128)S(1)}, u32[]{:S(2)}, u32[]{:S(2)}) collective-permute-start(f32[2,3,3,8,128]{4,3,2,1,0:T(8,128)S(1)} %get-tuple-element.88), channel_id=1, source_target_pairs={{0,8},{8,0},{16,24},{24,16},{32,40},{40,32},{48,56},{56,48},{64,72... | collective-permute-start | bytes 221192 | tf_op jit(solution)/shard_map/ppermute | solution.py:191
  49.5 7.9 %collective-permute-start.13 = (f32[2,3,3,8,128]{4,3,2,1,0:T(8,128)S(1)}, f32[2,3,3,8,128]{4,3,2,1,0:T(8,128)S(1)}, u32[]{:S(2)}, u32[]{:S(2)}) collective-permute-start(f32[2,3,3,8,128]{4,3,2,1,0:T(8,128)S(1)} %get-tuple-element.93), channel_id=1, source_target_pairs={{8,16},{16,8},{24,32},{32,24},{40,48},{48,40},{56,64},{64,56},{72,... | collective-permute-start | bytes 221192 | tf_op jit(solution)/shard_map/ppermute | solution.py:191
  60.4 6.6 %collective-permute-start.15 = (f32[8,4,8,128]{3,2,1,0:T(8,128)S(1)}, f32[8,4,8,128]{3,2,1,0:T(8,128)S(1)}, u32[]{:S(2)}, u32[]{:S(2)}) collective-permute-start(f32[8,4,8,128]{3,2,1,0:T(8,128)S(1)} %get-tuple-element.98), channel_id=1, source_target_pairs={{0,1},{1,0},{2,3},{3,2},{4,5},{5,4},{6,7},{7,6},{8,9},{9,8},{10,11... | collective-permute-start | bytes 393224 | tf_op jit(solution)/shard_map/ppermute | solution.py:191
  62.1 4.9 %collective-permute-start.16 = (f32[8,4,8,128]{3,2,1,0:T(8,128)S(1)}, f32[8,4,8,128]{3,2,1,0:T(8,128)S(1)}, u32[]{:S(2)}, u32[]{:S(2)}) collective-permute-start(f32[8,4,8,128]{3,2,1,0:T(8,128)S(1)} %get-tuple-element.99), channel_id=1, source_target_pairs={{1,2},{2,1},{3,4},{4,3},{5,6},{6,5},{9,10},{10,9},{11,12},{12,11},... | collective-permute-start | bytes 393224 | tf_op jit(solution)/shard_map/ppermute | solution.py:191
  63.2 7.8 %collective-permute-start.14 = (f32[4,32,8,128]{3,2,1,0:T(8,128)S(1)}, f32[4,32,8,128]{3,2,1,0:T(8,128)S(1)}, u32[]{:S(2)}, u32[]{:S(2)}) collective-permute-start(f32[4,32,8,128]{3,2,1,0:T(8,128)S(1)} %get-tuple-element.97), channel_id=1, source_target_pairs={{0,8},{8,0},{16,24},{24,16},{32,40},{40,32},{48,56},{56,48},{64,72... | collective-permute-start | bytes 1572872 | tf_op jit(solution)/shard_map/ppermute | solution.py:191
  63.3 11.9 %collective-permute-start.18 = (f32[4,32,8,128]{3,2,1,0:T(8,128)S(1)}, f32[4,32,8,128]{3,2,1,0:T(8,128)S(1)}, u32[]{:S(2)}, u32[]{:S(2)}) collective-permute-start(f32[4,32,8,128]{3,2,1,0:T(8,128)S(1)} %get-tuple-element.104), channel_id=1, source_target_pairs={{8,16},{16,8},{24,32},{32,24},{40,48},{48,40},{56,64},{64,56},{72,... | collective-permute-start | bytes 1572872 | tf_op jit(solution)/shard_map/ppermute | solution.py:191
  67.1 3.9 %collective-permute-start.17 = (f32[2,3,3,8,128]{4,3,2,1,0:T(8,128)S(1)}, f32[2,3,3,8,128]{4,3,2,1,0:T(8,128)S(1)}, u32[]{:S(2)}, u32[]{:S(2)}) collective-permute-start(f32[2,3,3,8,128]{4,3,2,1,0:T(8,128)S(1)} %get-tuple-element.100), channel_id=1, source_target_pairs={{0,8},{8,0},{16,24},{24,16},{32,40},{40,32},{48,56},{56,48},{64,72... | collective-permute-start | bytes 221192 | tf_op jit(solution)/shard_map/ppermute | solution.py:191
  67.2 8.0 %collective-permute-start.19 = (f32[2,3,3,8,128]{4,3,2,1,0:T(8,128)S(1)}, f32[2,3,3,8,128]{4,3,2,1,0:T(8,128)S(1)}, u32[]{:S(2)}, u32[]{:S(2)}) collective-permute-start(f32[2,3,3,8,128]{4,3,2,1,0:T(8,128)S(1)} %get-tuple-element.105), channel_id=1, source_target_pairs={{8,16},{16,8},{24,32},{32,24},{40,48},{48,40},{56,64},{64,56},{72,... | collective-permute-start | bytes 221192 | tf_op jit(solution)/shard_map/ppermute | solution.py:191
  71.1 4.1 %copy-start.1 = (s32[256,128]{1,0:T(8,128)S(1)}, s32[256,128]{1,0:T(8,128)}, u32[]{:S(2)}) copy-start(s32[256,128]{1,0:T(8,128)} %mask.1) | copy-start | bytes 393220
  71.1 4.1 %copy-start.2 = (s32[256]{0:T(256)S(1)}, s32[256]{0:T(256)}, u32[]{:S(2)}) copy-start(s32[256]{0:T(256)} %tile_rows.1) | copy-start | bytes 3076
  75.2 36.2 %copy-start = (f32[3,256,128]{2,1,0:T(8,128)S(1)}, f32[3,256,128]{2,1,0:T(8,128)}, u32[]{:S(2)}) copy-start(f32[3,256,128]{2,1,0:T(8,128)} %heights.1) | copy-start | bytes 1179652
